TPU v7x, 32 devices: a whole 2x2x4 slice. The times are simulated.
32 devices in a mesh: section: 2 (over y), tensor: 4 (over x, core), dp: 4 (over z).
Axes of the slice: x: 2, y: 2, z: 4, core: 2. Of those that a mesh axis runs over, the one named last changes fastest.
Arguments:
- block_input: bfloat16 [8, 256, 768], P('dp', 'tensor'), may hold values from -6 to 6
- segments: int32 [8, 256], P('dp'), may hold values from 0 to 2, as said below
- out_grad: bfloat16 [8, 256, 768], P('dp', 'tensor'), may hold values from -6 to 6
- query_key_value_weight: bfloat16 [2, 768, 3, 768], P('section', None, None, 'tensor'), may hold values from -0.21875 to 0.21875
- b_qv: bfloat16 [2, 2, 768], P('section', None, 'tensor'), may hold values from -3 to 3
- attention_output_weight: bfloat16 [2, 768, 768], P('section', 'tensor'), may hold values from -0.625 to 0.625
- attention_out_bias: bfloat16 [2, 768], P('section'), may hold values from -2 to 2
- ln_gain: bfloat16 [2, 2, 768], P('section'), may hold values from 0.5 to 1.5
- ln_bias: bfloat16 [2, 2, 768], P('section'), may hold values from -2 to 2
- up_projection_weight: bfloat16 [2, 768, 3072], P('section', None, 'tensor'), may hold values from -0.21875 to 0.21875
- up_proj_bias: bfloat16 [2, 3072], P('section', 'tensor'), may hold values from -3 to 3
- down_projection_weight: bfloat16 [2, 3072, 768], P('section', 'tensor'), may hold values from -0.15625 to 0.15625
- down_proj_bias: bfloat16 [2, 768], P('section'), may hold values from -2 to 2
Outputs:
- layer_outputs: bfloat16 [2, 8, 256, 768], P('section', 'dp', 'tensor')
- input_grads: bfloat16 [2, 8, 256, 768], P('section', 'dp', 'tensor')
- grad_w_qkv: float32 [2, 768, 3, 768], P('section', None, None, 'tensor')
- grad_b_qv: float32 [2, 2, 768], P('section', None, 'tensor')
- grad_w_out: float32 [2, 768, 768], P('section', 'tensor')
- grad_b_out: float32 [2, 768], P('section')
- grad_ln_gain: float32 [2, 2, 768], P('section')
- grad_ln_bias: float32 [2, 2, 768], P('section')
- grad_w_up: float32 [2, 768, 3072], P('section', None, 'tensor')
- grad_b_up: float32 [2, 3072], P('section', 'tensor')
- grad_w_down: float32 [2, 3072, 768], P('section', 'tensor')
- grad_b_down: float32 [2, 768], P('section')
Inputs may be any that keep to these rules, and one draw needn't show every extreme that they name: `segments`: along each sequence the document numbers never fall; document 1 begins at a position below 64 and ends at or after position 192; documents 0 and 2 are the pieces before and after it.
All inputs are finite; a program needn't handle non-finite values.
Results may differ from a plain program's by a relative error of at most 0.022.
Values may be sent and summed in bfloat16 or wider, within the bound.
No kernel may reach another device: no remote copies, remote signals or barrier semaphores. Data moves between devices by JAX's collectives and lax.ppermute only.
A program may use at most 128 MiB of HBM per device.

v0:
```python
import jax
import jax.numpy as jnp
from jax import lax
from jax.sharding import PartitionSpec as P

HEAD_DIM = 64
MICRO = 2


EPSILON = 1e-06
BIG_NEGATIVE = -1e30


def from_behind(value, axis, steps):
    count = lax.axis_size(axis)
    first, last = (max(0, -steps), min(count, count - steps))
    return lax.ppermute(value, axis, [(source, source + steps) for source in range(first, last)])


def normalize(values, gain, shift):
    centred = values - jnp.mean(values, -1, keepdims=True)
    spread = jnp.mean(centred * centred, -1, keepdims=True)
    return centred * lax.rsqrt(spread + EPSILON) * gain + shift


def norm_back(values, gain, shift, upstream):
    result, pullback = jax.vjp(normalize, values, gain, shift)
    return pullback(upstream)


def gelu_exact(values):
    return jax.nn.gelu(values, approximate=False)


def masked_scores(query, key_rows, seg_rows, score_scale):
    scores = (
        jnp.einsum("sqhe,skhe->shqk", query, key_rows, preferred_element_type=jnp.float32)
        * score_scale
    )
    same = (seg_rows[:, :, None] == seg_rows[:, None, :])[:, None]
    return jnp.where(same, scores, BIG_NEGATIVE)


def attend_forward(query, key_rows, value, seg_rows, score_scale):
    scores = masked_scores(query, key_rows, seg_rows, score_scale)
    peak = jnp.max(scores, -1, keepdims=True)
    weights = jnp.exp(scores - peak)
    total = jnp.sum(weights, -1, keepdims=True)
    probs = (weights / total).astype(jnp.bfloat16)
    mixed_heads = jnp.einsum("shqk,skhe->sqhe", probs, value, preferred_element_type=jnp.float32)
    return (mixed_heads, peak + jnp.log(total))


def attend_backward(query, key_rows, value, seg_rows, log_total, grad_mixed, score_scale):
    scores = masked_scores(query, key_rows, seg_rows, score_scale)
    probs = jnp.exp(scores - log_total)
    grad_probs = jnp.einsum(
        "sqhe,skhe->shqk", grad_mixed, value, preferred_element_type=jnp.float32
    )
    row_dot = jnp.sum(probs * grad_probs, -1, keepdims=True)
    grad_scores = (probs * (grad_probs - row_dot)).astype(jnp.bfloat16)
    grad_query = (
        jnp.einsum("shqk,skhe->sqhe", grad_scores, key_rows, preferred_element_type=jnp.float32)
        * score_scale
    )
    grad_key = (
        jnp.einsum("shqk,sqhe->skhe", grad_scores, query, preferred_element_type=jnp.float32)
        * score_scale
    )
    grad_value = jnp.einsum(
        "shqk,sqhe->skhe",
        probs.astype(jnp.bfloat16),
        grad_mixed,
        preferred_element_type=jnp.float32,
    )
    return (grad_query, grad_key, grad_value)


def when_active(active, work, blanks):

    def spare():
        return tuple((jnp.zeros(extent, kind) for extent, kind in blanks))

    return lax.cond(active, work, spare)


def place(buffers, slot, values, active):

    def update_one(buffer, value):
        current = lax.dynamic_index_in_dim(buffer, slot, 0, keepdims=False)
        return lax.dynamic_update_index_in_dim(buffer, jnp.where(active, value, current), slot, 0)

    return jax.tree.map(update_one, buffers, values)


def fetch(buffers, slot):
    return jax.tree.map(
        lambda buffer: lax.dynamic_index_in_dim(buffer, slot, 0, keepdims=False), buffers
    )


def blank_like(values):
    return jax.tree.map(lambda item: jnp.zeros((MICRO,) + item.shape, item.dtype), values)


def shards(
    block_input,
    segments,
    out_grad,
    query_key_value_weight,
    b_qv,
    attention_output_weight,
    attention_out_bias,
    ln_gain,
    ln_bias,
    up_projection_weight,
    up_proj_bias,
    down_projection_weight,
    down_proj_bias,
):
    single_float = jnp.float32
    bf16 = jnp.bfloat16
    section_index = lax.axis_index("section")
    seq_dev, part_rows, width = block_input.shape
    full_len = segments.shape[1]
    per_micro = seq_dev // MICRO
    local_width = query_key_value_weight.shape[3]
    local_hidden = up_projection_weight.shape[2]
    head_local = local_width // HEAD_DIM
    score_scale = HEAD_DIM ** (-0.5)
    query_key_value_matrix = query_key_value_weight[0]
    qv_bias = b_qv[0].astype(single_float)
    output_matrix = attention_output_weight[0]
    out_bias = attention_out_bias[0].astype(single_float)
    gain_pair = ln_gain[0].astype(single_float)
    shift_pair = ln_bias[0].astype(single_float)
    up_matrix = up_projection_weight[0]
    up_bias = up_proj_bias[0].astype(single_float)
    down_matrix = down_projection_weight[0]
    down_bias = down_proj_bias[0].astype(single_float)
    micro_in = block_input.reshape(MICRO, per_micro, part_rows, width)
    micro_grad = out_grad.reshape(MICRO, per_micro, part_rows, width)
    micro_seg = segments.reshape(MICRO, per_micro, full_len)
    act_shape = (per_micro, part_rows, width)
    seq_shape = (per_micro, full_len, width)
    heads_shape = (per_micro, full_len, head_local, HEAD_DIM)
    store = None
    received = jnp.zeros(act_shape, bf16)
    for tick in range(MICRO + 1):
        micro_index = tick - section_index
        active = (micro_index >= 0) & (micro_index < MICRO)
        slot = jnp.clip(micro_index, 0, MICRO - 1)
        own = micro_in[tick] if tick < MICRO else jnp.zeros(act_shape, bf16)
        layer_entry = jnp.where(section_index == 0, own, received)
        seg_rows = lax.dynamic_index_in_dim(micro_seg, slot, 0, keepdims=False)
        row_total_whole = lax.all_gather(layer_entry, "tensor", axis=1, tiled=True)

        def attention_part():
            projected = jnp.einsum(
                "qhj,jpv->qhpv",
                row_total_whole,
                query_key_value_matrix,
                preferred_element_type=single_float,
            )
            query = (projected[:, :, 0] + qv_bias[0]).astype(bf16)
            key_rows = projected[:, :, 1].astype(bf16)
            value = (projected[:, :, 2] + qv_bias[1]).astype(bf16)
            mixed_heads, log_total = attend_forward(
                query.reshape(heads_shape),
                key_rows.reshape(heads_shape),
                value.reshape(heads_shape),
                seg_rows,
                score_scale,
            )
            mixed_heads_reduced = mixed_heads.reshape(per_micro, full_len, local_width).astype(bf16)
            summand_terms = jnp.einsum(
                "hmy,yv->hmv",
                mixed_heads_reduced,
                output_matrix,
                preferred_element_type=single_float,
            )
            return (
                jnp.stack([query, key_rows, value], 2),
                log_total,
                mixed_heads_reduced,
                summand_terms,
            )

        proj_low, log_total, mixed_heads_reduced, summand_terms = when_active(
            active,
            attention_part,
            (
                ((per_micro, full_len, 3, local_width), bf16),
                ((per_micro, head_local, full_len, 1), single_float),
                ((per_micro, full_len, local_width), bf16),
                (seq_shape, single_float),
            ),
        )
        first_res = layer_entry.astype(single_float) + (
            lax.psum_scatter(
                summand_terms.astype(jnp.bfloat16), "tensor", scatter_dimension=1, tiled=True
            ).astype(jnp.float32)
            + out_bias
        )
        first_layer = normalize(first_res, gain_pair[0], shift_pair[0])
        first_low = first_layer.astype(bf16)
        first_layer_whole = lax.all_gather(first_low, "tensor", axis=1, tiled=True)

        def mlp_part():
            hidden_pre = (
                jnp.einsum(
                    "xjg,gq->xjq", first_layer_whole, up_matrix, preferred_element_type=single_float
                )
                + up_bias
            )
            activation_reduced = gelu_exact(hidden_pre).astype(bf16)
            return (
                hidden_pre,
                activation_reduced,
                jnp.einsum(
                    "bxz,zp->bxp",
                    activation_reduced,
                    down_matrix,
                    preferred_element_type=single_float,
                ),
            )

        hidden_pre, activation_reduced, summand_terms = when_active(
            active,
            mlp_part,
            (
                ((per_micro, full_len, local_hidden), single_float),
                ((per_micro, full_len, local_hidden), bf16),
                (seq_shape, single_float),
            ),
        )
        second_res = first_layer + (
            lax.psum_scatter(
                summand_terms.astype(jnp.bfloat16), "tensor", scatter_dimension=1, tiled=True
            ).astype(jnp.float32)
            + down_bias
        )
        output = normalize(second_res, gain_pair[1], shift_pair[1]).astype(bf16)
        saved = {
            "entry": layer_entry,
            "proj": proj_low,
            "log_total": log_total,
            "mixed": mixed_heads_reduced,
            "first_res": first_res,
            "first_low": first_low,
            "hidden_pre": hidden_pre,
            "act_low": activation_reduced,
            "second_res": second_res,
            "output": output,
        }
        if tick == 0:
            store = blank_like(saved)
        store = place(store, slot, saved, active)
        if tick < MICRO:
            received = from_behind(output, "section", 1)
    back_store = None
    small = {
        "out_bias": jnp.zeros((width,), single_float),
        "down_bias": jnp.zeros((width,), single_float),
        "gain_grad": jnp.zeros((2, width), single_float),
        "shift_grad": jnp.zeros((2, width), single_float),
        "qv_grad": jnp.zeros((2, local_width), single_float),
        "up_grad": jnp.zeros((local_hidden,), single_float),
    }
    received = jnp.zeros(act_shape, bf16)
    for tick in range(MICRO + 1):
        micro_index = tick - (1 - section_index)
        active = (micro_index >= 0) & (micro_index < MICRO)
        slot = jnp.clip(micro_index, 0, MICRO - 1)
        own = micro_grad[tick] if tick < MICRO else jnp.zeros(act_shape, bf16)
        grad_out = jnp.where(section_index == 1, own, received)
        kept = fetch(store, slot)
        seg_rows = lax.dynamic_index_in_dim(micro_seg, slot, 0, keepdims=False)
        grad_second, grad_gain_b, grad_shift_b = norm_back(
            kept["second_res"], gain_pair[1], shift_pair[1], grad_out.astype(single_float)
        )
        grad_y_low = grad_second.astype(bf16)
        output_gradient_whole = lax.all_gather(grad_y_low, "tensor", axis=1, tiled=True)

        def mlp_back():
            grad_act = jnp.einsum(
                "jmp,qp->jmq",
                output_gradient_whole,
                down_matrix,
                preferred_element_type=single_float,
            )
            unused, pullback = jax.vjp(gelu_exact, kept["hidden_pre"])
            hidden_gradient = pullback(grad_act)[0].astype(bf16)
            return (
                hidden_gradient,
                jnp.einsum(
                    "xjn,qn->xjq", hidden_gradient, up_matrix, preferred_element_type=single_float
                ),
            )

        hidden_gradient, summand_terms = when_active(
            active,
            mlp_back,
            (((per_micro, full_len, local_hidden), bf16), (seq_shape, single_float)),
        )
        grad_first = grad_second + lax.psum_scatter(
            summand_terms.astype(jnp.bfloat16), "tensor", scatter_dimension=1, tiled=True
        ).astype(jnp.float32)
        grad_first_res, grad_gain_a, grad_shift_a = norm_back(
            kept["first_res"], gain_pair[0], shift_pair[0], grad_first
        )
        grad_branch_low = grad_first_res.astype(bf16)
        branch_gradient_whole = lax.all_gather(grad_branch_low, "tensor", axis=1, tiled=True)

        def attention_back():
            grad_mixed = jnp.einsum(
                "unh,jh->unj",
                branch_gradient_whole,
                output_matrix,
                preferred_element_type=single_float,
            ).astype(bf16)
            proj_kept = kept["proj"]
            grad_parts = attend_backward(
                proj_kept[:, :, 0].reshape(heads_shape),
                proj_kept[:, :, 1].reshape(heads_shape),
                proj_kept[:, :, 2].reshape(heads_shape),
                seg_rows,
                kept["log_total"],
                grad_mixed.reshape(heads_shape),
                score_scale,
            )
            projected_gradient = jnp.stack(
                [item.reshape(per_micro, full_len, local_width) for item in grad_parts], 2
            ).astype(bf16)
            return (
                projected_gradient,
                jnp.einsum(
                    "bugj,agj->bua",
                    projected_gradient,
                    query_key_value_matrix,
                    preferred_element_type=single_float,
                ),
            )

        projected_gradient, summand_terms = when_active(
            active,
            attention_back,
            (((per_micro, full_len, 3, local_width), bf16), (seq_shape, single_float)),
        )
        grad_entry = grad_first_res + lax.psum_scatter(
            summand_terms.astype(jnp.bfloat16), "tensor", scatter_dimension=1, tiled=True
        ).astype(jnp.float32)
        grad_entry_low = grad_entry.astype(bf16)
        update = {
            "out_bias": jnp.sum(grad_branch_low, (0, 1), dtype=single_float),
            "down_bias": jnp.sum(grad_y_low, (0, 1), dtype=single_float),
            "gain_grad": jnp.stack([grad_gain_a, grad_gain_b]),
            "shift_grad": jnp.stack([grad_shift_a, grad_shift_b]),
            "qv_grad": jnp.stack(
                [
                    jnp.sum(projected_gradient[:, :, 0], (0, 1), dtype=single_float),
                    jnp.sum(projected_gradient[:, :, 2], (0, 1), dtype=single_float),
                ]
            ),
            "up_grad": jnp.sum(hidden_gradient, (0, 1), dtype=single_float),
        }
        small = jax.tree.map(
            lambda total, item: total + jnp.where(active, item, jnp.zeros_like(item)), small, update
        )
        saved_back = {
            "grad_proj": projected_gradient,
            "grad_branch_full": branch_gradient_whole,
            "grad_hidden": hidden_gradient,
            "grad_y_full": output_gradient_whole,
            "entry_grad": grad_entry_low,
        }
        if tick == 0:
            back_store = blank_like(saved_back)
        back_store = place(back_store, slot, saved_back, active)
        if tick < MICRO:
            received = from_behind(grad_entry_low, "section", -1)
    rows_all, first_all_rows = (
        lax.all_gather(store["entry"], "tensor", axis=2, tiled=True),
        lax.all_gather(store["first_low"], "tensor", axis=2, tiled=True),
    )
    grad_down = jnp.einsum(
        "mozk,mozh->kh",
        store["act_low"],
        back_store["grad_y_full"],
        preferred_element_type=single_float,
    )
    grad_out_w = jnp.einsum(
        "maxz,maxi->zi",
        store["mixed"],
        back_store["grad_branch_full"],
        preferred_element_type=single_float,
    )
    grad_up = jnp.einsum(
        "mowy,mowg->yg",
        first_all_rows,
        back_store["grad_hidden"],
        preferred_element_type=single_float,
    )
    grad_up_bias = small["up_grad"]
    grad_qkv = jnp.einsum(
        "mzbo,mzbuk->ouk", rows_all, back_store["grad_proj"], preferred_element_type=single_float
    )
    grad_qv_bias = small["qv_grad"]
    grad_qkv, grad_qv_bias, grad_out_w, grad_up, grad_up_bias, grad_down = (
        lax.psum(grad_qkv.astype(jnp.bfloat16), "dp").astype(jnp.float32),
        lax.psum(grad_qv_bias.astype(jnp.bfloat16), "dp").astype(jnp.float32),
        lax.psum(grad_out_w.astype(jnp.bfloat16), "dp").astype(jnp.float32),
        lax.psum(grad_up.astype(jnp.bfloat16), "dp").astype(jnp.float32),
        lax.psum(grad_up_bias.astype(jnp.bfloat16), "dp").astype(jnp.float32),
        lax.psum(grad_down.astype(jnp.bfloat16), "dp").astype(jnp.float32),
    )
    grad_out_bias, grad_down_bias, grad_gains, grad_shifts = lax.psum(
        (small["out_bias"], small["down_bias"], small["gain_grad"], small["shift_grad"]),
        ("tensor", "dp"),
    )
    layer_outputs = store["output"].reshape(1, seq_dev, part_rows, width)
    input_grads = back_store["entry_grad"].reshape(1, seq_dev, part_rows, width)
    return (
        layer_outputs,
        input_grads,
        grad_qkv[None],
        grad_qv_bias[None],
        grad_out_w[None],
        grad_out_bias[None],
        grad_gains[None],
        grad_shifts[None],
        grad_up[None],
        grad_up_bias[None],
        grad_down[None],
        grad_down_bias[None],
    )


def solution(mesh):
    return jax.shard_map(
        shards,
        mesh=mesh,
        in_specs=(
            P("dp", "tensor", None),
            P("dp", None),
            P("dp", "tensor", None),
            P("section", None, None, "tensor"),
            P("section", None, "tensor"),
            P("section", "tensor", None),
            P("section", None),
            P("section", None, None),
            P("section", None, None),
            P("section", None, "tensor"),
            P("section", "tensor"),
            P("section", "tensor", None),
            P("section", None),
        ),
        out_specs=(
            P("section", "dp", "tensor", None),
            P("section", "dp", "tensor", None),
            P("section", None, None, "tensor"),
            P("section", None, "tensor"),
            P("section", "tensor", None),
            P("section", None),
            P("section", None, None),
            P("section", None, None),
            P("section", None, "tensor"),
            P("section", "tensor"),
            P("section", "tensor", None),
            P("section", None),
        ),
        check_vma=False,
    )
```

profile of v0, /device:TPU:0, one launch (start us, length us, event | category | flops | bytes accessed | tf_op | source)
XLA Modules:
  0.0 654.2 jit_solution(15851410355924757204)
XLA Ops:
  8.2 7.9 %all_gather.42 = bf16[1,256,768]{2,1,0:T(8,128)(2,1)S(1)} all-gather(bf16[1,64,768]{2,1,0:T(8,128)(2,1)S(1)} %get-tuple-element.566), channel_id=1, replica_groups=mesh['section'=2,'tensor'=4,'dp'=4] {'tensor'}, dimensions={1}, use_global_device_ids=true | all-gather | bytes 491520 | tf_op jit(solution)/shard_map/all_gather | solution.py:156
  17.4 5.6 conditional.12
  29.5 15.2 %reduce-scatter.13.cloned.1.call-done = bf16[1,64,768]{2,1,0:T(8,128)(2,1)} async-done(((bf16[1,256,768]{2,1,0:T(8,128)(2,1)}), bf16[1,64,768]{2,1,0:T(8,128)(2,1)}) %reduce-scatter.13.cloned.1.call-update) | async-done | bytes 98320 | tf_op jit(solution)/shard_map/reduce_scatter | solution.py:200
  48.0 6.1 all_gather.43
  70.0 9.7 %reduce-scatter.15.cloned.1.call-done = bf16[1,64,768]{2,1,0:T(8,128)(2,1)} async-done(((bf16[1,256,768]{2,1,0:T(8,128)(2,1)}), bf16[1,64,768]{2,1,0:T(8,128)(2,1)}) %reduce-scatter.15.cloned.1.call-update) | async-done | bytes 98320 | tf_op jit(solution)/shard_map/reduce_scatter | solution.py:238
  91.7 6.1 all_gather.44
  97.9 14.5 %conditional.14 = (bf16[1,256,3,192]{1,3,2,0:T(8,128)(2,1)}, f32[1,3,256,1]{2,1,3,0:T(4,128)}, bf16[1,256,192]{1,2,0:T(8,128)(2,1)}, bf16[1,256,768]{2,1,0:T(8,128)(2,1)}) conditional(s32[]{:T(128)} %convert_element_type.701, () %tuple.132, (bf16[1,256,768]{2,1,0:T(8,128)(2,1)S(1)}, bf16[768,3,192]{0,2,1:T(8,128)(2,1)S(1)}, f32[2,192]{1,0:T(2,128)}, ...), branch_computations={%region_12.13_spmd, %region_13.16_spmd} | conditional | flops 354696448 | bytes 11105940 | solution.py:84
  122.1 12.5 %reduce-scatter.17.cloned.1.call-done = bf16[1,64,768]{2,1,0:T(8,128)(2,1)} async-done(((bf16[1,256,768]{2,1,0:T(8,128)(2,1)}), bf16[1,64,768]{2,1,0:T(8,128)(2,1)}) %reduce-scatter.17.cloned.1.call-update) | async-done | bytes 98320 | tf_op jit(solution)/shard_map/reduce_scatter | solution.py:200
  138.5 6.3 all_gather.45
  165.3 6.0 reduce-scatter.19.cloned.1.call-done
  183.7 6.1 all_gather.46
  197.3 9.2 %all_gather.54 = bf16[2,1,256,768]{3,2,0,1:T(8,128)(2,1)} all-gather(bf16[2,1,64,768]{3,2,0,1:T(8,128)(2,1)S(1)} %copy-done.50), channel_id=1, replica_groups=mesh['section'=2,'tensor'=4,'dp'=4] {'tensor'}, dimensions={2}, use_global_device_ids=true | all-gather | bytes 983040 | tf_op jit(solution)/shard_map/all_gather | solution.py:383
  206.5 20.1 %reduce-scatter.21.cloned.1.call-done = bf16[1,64,768]{2,1,0:T(8,128)(2,1)} async-done(((bf16[1,256,768]{2,1,0:T(8,128)(2,1)}), bf16[1,64,768]{2,1,0:T(8,128)(2,1)}) %reduce-scatter.21.cloned.1.call-update) | async-done | bytes 98320 | tf_op jit(solution)/shard_map/reduce_scatter | solution.py:200
  230.5 6.1 all_gather.47
  245.8 9.2 %all_gather.55 = bf16[2,1,256,768]{3,2,0,1:T(8,128)(2,1)} all-gather(bf16[2,1,64,768]{3,2,0,1:T(8,128)(2,1)S(1)} %copy-done.52), channel_id=1, replica_groups=mesh['section'=2,'tensor'=4,'dp'=4] {'tensor'}, dimensions={2}, use_global_device_ids=true | all-gather | bytes 983040 | tf_op jit(solution)/shard_map/all_gather | solution.py:384
  255.0 8.2 %reduce-scatter.23.cloned.1.call-done = bf16[1,64,768]{2,1,0:T(8,128)(2,1)} async-done(((bf16[1,256,768]{2,1,0:T(8,128)(2,1)}), bf16[1,64,768]{2,1,0:T(8,128)(2,1)}) %reduce-scatter.23.cloned.1.call-update) | async-done | bytes 98320 | tf_op jit(solution)/shard_map/reduce_scatter | solution.py:238
  267.7 6.1 all_gather.48
  292.1 9.2 %reduce-scatter.25.cloned.1.call-done = bf16[1,64,768]{2,1,0:T(8,128)(2,1)} async-done(((bf16[1,256,768]{2,1,0:T(8,128)(2,1)}), bf16[1,64,768]{2,1,0:T(8,128)(2,1)}) %reduce-scatter.25.cloned.1.call-update) | async-done | bytes 98320 | tf_op jit(solution)/shard_map/reduce_scatter | solution.py:306
  305.1 6.1 all_gather.49
  322.4 15.8 %reduce-scatter.27.cloned.1.call-done = bf16[1,64,768]{2,1,0:T(8,128)(2,1)} async-done(((bf16[1,256,768]{2,1,0:T(8,128)(2,1)}), bf16[1,64,768]{2,1,0:T(8,128)(2,1)}) %reduce-scatter.27.cloned.1.call-update) | async-done | bytes 98320 | tf_op jit(solution)/shard_map/reduce_scatter | solution.py:350
  349.9 6.6 %all_gather.50 = bf16[1,256,768]{2,1,0:T(8,128)(2,1)} all-gather(bf16[1,64,768]{2,1,0:T(8,128)(2,1)S(1)} %get-tuple-element.546), channel_id=1, replica_groups=mesh['section'=2,'tensor'=4,'dp'=4] {'tensor'}, dimensions={1}, use_global_device_ids=true | all-gather | bytes 491520 | tf_op jit(solution)/shard_map/all_gather | solution.py:283
  356.5 6.2 conditional.20
  387.7 7.0 %all_gather.51 = bf16[1,256,768]{2,1,0:T(8,128)(2,1)} all-gather(bf16[1,64,768]{2,1,0:T(8,128)(2,1)S(1)} %get-tuple-element.552), channel_id=1, replica_groups=mesh['section'=2,'tensor'=4,'dp'=4] {'tensor'}, dimensions={1}, use_global_device_ids=true | all-gather | bytes 491520 | tf_op jit(solution)/shard_map/all_gather | solution.py:313
  394.7 5.8 conditional.21
  411.1 10.8 %reduce-scatter.31.cloned.1.call-done = bf16[1,64,768]{2,1,0:T(8,128)(2,1)} async-done(((bf16[1,256,768]{2,1,0:T(8,128)(2,1)}), bf16[1,64,768]{2,1,0:T(8,128)(2,1)}) %reduce-scatter.31.cloned.1.call-update) | async-done | bytes 98320 | tf_op jit(solution)/shard_map/reduce_scatter | solution.py:350
  433.2 6.6 %all_gather.52 = bf16[1,256,768]{2,1,0:T(8,128)(2,1)} all-gather(bf16[1,64,768]{2,1,0:T(8,128)(2,1)S(1)} %get-tuple-element.548), channel_id=1, replica_groups=mesh['section'=2,'tensor'=4,'dp'=4] {'tensor'}, dimensions={1}, use_global_device_ids=true | all-gather | bytes 491520 | tf_op jit(solution)/shard_map/all_gather | solution.py:283
  439.8 5.3 conditional.22
  455.3 11.0 %reduce-scatter.33.cloned.1.call-done = bf16[1,64,768]{2,1,0:T(8,128)(2,1)} async-done(((bf16[1,256,768]{2,1,0:T(8,128)(2,1)}), bf16[1,64,768]{2,1,0:T(8,128)(2,1)}) %reduce-scatter.33.cloned.1.call-update) | async-done | bytes 98320 | tf_op jit(solution)/shard_map/reduce_scatter | solution.py:306
  468.7 6.1 all_gather.53
  493.5 11.7 %all-reduce.1 = (bf16[1,2,192]{2,1,0:T(2,128)(2,1)S(1)}, bf16[1,768]{1,0:T(2,128)(2,1)S(1)}) all-reduce(bf16[1,2,192]{2,1,0:T(2,128)(2,1)S(1)} %fusion.226, bf16[1,768]{1,0:T(2,128)(2,1)S(1)} %broadcast_in_dim.408), channel_id=1, replica_groups=mesh['section'=2,'tensor'=4,'dp'=4] {'dp'}, use_global_device_ids=true, to_apply=%region_88.89 | all-reduce | flops 1152 | bytes 4608 | tf_op jit(solution)/shard_map/psum | solution.py:411
  506.5 63.2 %all-reduce = (f32[1,768]{1,0:T(1,128)}, f32[1,2,768]{2,1,0:T(2,128)}, f32[1,2,768]{2,1,0:T(2,128)}, f32[1,768]{1,0:T(1,128)}) all-reduce(f32[1,768]{1,0:T(1,128)S(1)} %broadcast_in_dim.398, f32[1,2,768]{2,1,0:T(2,128)S(1)} %fusion.213, ...), channel_id=1, replica_groups=mesh['section'=2,'tensor'=4,'dp'=4] {'tensor','dp'}, use_global_device_ids=true, to_apply=%region_93.94 | all-reduce | flops 4608 | bytes 36864 | tf_op jit(solution)/shard_map/psum | solution.py:417
  570.7 70.1 %all-reduce.5.cloned.1.call-done = (bf16[1,768,3,192]{1,3,2,0:T(8,128)(2,1)}, bf16[1,192,768]{2,1,0:T(8,128)(2,1)}, bf16[1,768,768]{2,1,0:T(8,128)(2,1)}, bf16[1,768,768]{2,1,0:T(8,128)(2,1)}) async-done(((bf16[1,768,3,192]{1,3,2,0:T(8,128)(2,1)}, bf16[1,192,768]{2,1,0:T(8,128)(2,1)}, bf16[1,768,768]{2,1,0:T(8,128)(2,1)}, bf16[1,768,768]{2,1,0:T(8,128)(2,1)}), (bf16[1,768,3,192]{1,3,2,0:T(8,128)(2,1)}, ...) | async-done | bytes 3538960 | tf_op jit(solution)/shard_map/psum | solution.py:410
  (571 shorter events, 300.2 us)
Async XLA Ops:
  7.2 37.6 %reduce-scatter.13.cloned.1.call-start = ((), (), s32[]{:S(2)}) async-start(), calls=%async_computation.12 | async-start | bytes 491520 | tf_op jit(solution)/shard_map/reduce_scatter | solution.py:200
  23.8 56.0 %reduce-scatter.15.cloned.1.call-start = ((), (), s32[]{:S(2)}) async-start(), calls=%async_computation.13 | async-start | bytes 491520 | tf_op jit(solution)/shard_map/reduce_scatter | solution.py:238
  26.8 27.3 %copy-start.97 = (f32[768]{0:T(1024)}, f32[768]{0:T(1024)S(1)}, u32[]{:S(2)}) copy-start(f32[768]{0:T(1024)S(1)} %convert_reduce_fusion.19) | copy-start | bytes 9220
  27.5 26.6 %copy-start.3 = (bf16[1,768,768]{2,1,0:T(8,128)(2,1)S(1)}, bf16[1,768,768]{2,1,0:T(8,128)(2,1)}, u32[]{:S(2)}) copy-start(bf16[1,768,768]{2,1,0:T(8,128)(2,1)} %param.46) | copy-start | bytes 3538948
  27.6 26.6 %copy-start.9 = (bf16[2,1,256,3,192]{2,4,3,1,0:T(8,128)(2,1)}, bf16[2,1,256,3,192]{2,4,3,1,0:T(8,128)(2,1)S(1)}, u32[]{:S(2)}) copy-start(bf16[2,1,256,3,192]{2,4,3,1,0:T(8,128)(2,1)S(1)} %bitcast_dynamic-update-slice_fusion.7) | copy-start | bytes 1769476
  27.6 26.5 %copy-start.2 = (bf16[1,768,768]{2,1,0:T(8,128)(2,1)S(1)}, bf16[1,768,768]{2,1,0:T(8,128)(2,1)}, u32[]{:S(2)}) copy-start(bf16[1,768,768]{2,1,0:T(8,128)(2,1)} %param.48) | copy-start | bytes 3538948
  59.4 75.2 %reduce-scatter.17.cloned.1.call-start = ((), (), s32[]{:S(2)}) async-start(), calls=%async_computation.14 | async-start | bytes 491520 | tf_op jit(solution)/shard_map/reduce_scatter | solution.py:200
  84.5 5.6 collective-permute-start
  112.4 59.0 %reduce-scatter.19.cloned.1.call-start = ((), (), s32[]{:S(2)}) async-start(), calls=%async_computation.15 | async-start | bytes 491520 | tf_op jit(solution)/shard_map/reduce_scatter | solution.py:238
  150.1 76.5 %reduce-scatter.21.cloned.1.call-start = ((), (), s32[]{:S(2)}) async-start(), calls=%async_computation.16 | async-start | bytes 491520 | tf_op jit(solution)/shard_map/reduce_scatter | solution.py:200
  178.1 5.6 collective-permute-start.1
  192.6 70.6 %reduce-scatter.23.cloned.1.call-start = ((), (), s32[]{:S(2)}) async-start(), calls=%async_computation.17 | async-start | bytes 491520 | tf_op jit(solution)/shard_map/reduce_scatter | solution.py:238
  239.2 62.0 %reduce-scatter.25.cloned.1.call-start = ((), (), s32[]{:S(2)}) async-start(), calls=%async_computation.18 | async-start | bytes 491520 | tf_op jit(solution)/shard_map/reduce_scatter | solution.py:306
  266.8 23.7 %copy-start.110 = (f32[64]{0:T(128)}, f32[64]{0:T(128)S(1)}, u32[]{:S(2)}) copy-start(f32[64]{0:T(128)S(1)} %get-tuple-element.510) | copy-start | bytes 772
  276.4 61.7 %reduce-scatter.27.cloned.1.call-start = ((), (), s32[]{:S(2)}) async-start(), calls=%async_computation.19 | async-start | bytes 491520 | tf_op jit(solution)/shard_map/reduce_scatter | solution.py:350
  290.5 21.5 %copy-start.96 = (f32[64]{0:T(128)}, f32[64]{0:T(128)S(1)}, u32[]{:S(2)}) copy-start(f32[64]{0:T(128)S(1)} %broadcast_multiply_fusion.2) | copy-start | bytes 772
  303.0 18.8 %copy-start.111 = (f32[64]{0:T(128)}, f32[64]{0:T(128)S(1)}, u32[]{:S(2)}) copy-start(f32[64]{0:T(128)S(1)} %get-tuple-element.509) | copy-start | bytes 772
  313.5 69.5 %reduce-scatter.29.cloned.1.call-start = ((), (), s32[]{:S(2)}) async-start(), calls=%async_computation.20 | async-start | bytes 491520 | tf_op jit(solution)/shard_map/reduce_scatter | solution.py:306
  339.2 17.2 %copy-start.17 = (f32[2,1,256,768]{3,2,1,0:T(8,128)S(1)}, f32[2,1,256,768]{3,2,1,0:T(8,128)}, u32[]{:S(2)}) copy-start(f32[2,1,256,768]{3,2,1,0:T(8,128)} %bitcast_dynamic-update-slice_fusion) | copy-start | bytes 4718596
  339.3 6.6 %collective-permute-start.2 = (bf16[1,64,768]{2,1,0:T(8,128)(2,1)S(1)}, bf16[1,64,768]{2,1,0:T(8,128)(2,1)S(1)}, u32[]{:S(2)}, u32[]{:S(2)}) collective-permute-start(bf16[1,64,768]{2,1,0:T(8,128)(2,1)S(1)} %get-tuple-element.579), channel_id=1, source_target_pairs={{16,0},{17,1},{18,2},{19,3},{20,4},{21,5},{22,6},{23,7},{24,8},{25... | collective-permute-start | bytes 294920 | tf_op jit(solution)/shard_map/ppermute | solution.py:17
  362.6 59.2 %reduce-scatter.31.cloned.1.call-start = ((), (), s32[]{:S(2)}) async-start(), calls=%async_computation.21 | async-start | bytes 491520 | tf_op jit(solution)/shard_map/reduce_scatter | solution.py:350
  400.5 65.8 %reduce-scatter.33.cloned.1.call-start = ((), (), s32[]{:S(2)}) async-start(), calls=%async_computation.22 | async-start | bytes 491520 | tf_op jit(solution)/shard_map/reduce_scatter | solution.py:306
  423.6 6.7 %collective-permute-start.3 = (bf16[1,64,768]{2,1,0:T(8,128)(2,1)}, bf16[1,64,768]{2,1,0:T(8,128)(2,1)S(1)}, u32[]{:S(2)}, u32[]{:S(2)}) collective-permute-start(bf16[1,64,768]{2,1,0:T(8,128)(2,1)} %get-tuple-element.572), channel_id=1, source_target_pairs={{16,0},{17,1},{18,2},{19,3},{20,4},{21,5},{22,6},{23,7},{24,8},{25... | collective-permute-start | bytes 294920 | tf_op jit(solution)/shard_map/ppermute | solution.py:17
  445.9 123.7 %reduce-scatter.35.cloned.1.call-start = ((), (), s32[]{:S(2)}) async-start(), calls=%async_computation.23 | async-start | bytes 491520 | tf_op jit(solution)/shard_map/reduce_scatter | solution.py:350
  455.3 19.6 %copy-start.8 = (bf16[1,768,3,192]{1,3,2,0:T(8,128)(2,1)S(1)}, bf16[1,768,3,192]{1,3,2,0:T(8,128)(2,1)}, u32[]{:S(2)}) copy-start(bf16[1,768,3,192]{1,3,2,0:T(8,128)(2,1)} %param.40) | copy-start | bytes 2654212
  455.3 19.6 %copy-start.12 = (bf16[2,1,256,3,192]{2,4,3,1,0:T(8,128)(2,1)S(1)}, bf16[2,1,256,3,192]{2,4,3,1,0:T(8,128)(2,1)}, u32[]{:S(2)}) copy-start(bf16[2,1,256,3,192]{2,4,3,1,0:T(8,128)(2,1)} %bitcast_dynamic-update-slice_fusion.5) | copy-start | bytes 1769476
  479.7 161.0 %all-reduce.5.cloned.1.call-start = ((), (), s32[]{:S(2)}) async-start(), calls=%async_computation.24 | async-start | bytes 7077888 | tf_op jit(solution)/shard_map/psum | solution.py:410
  487.5 18.3 %copy-start.87 = (f32[768]{0:T(1024)S(1)}, f32[768]{0:T(1024)}, u32[]{:S(2)}) copy-start(f32[768]{0:T(1024)} %get-tuple-element.549) | copy-start | bytes 9220
  487.5 18.2 %copy-start.89 = (f32[768]{0:T(1024)S(1)}, f32[768]{0:T(1024)}, u32[]{:S(2)}) copy-start(f32[768]{0:T(1024)} %get-tuple-element.551) | copy-start | bytes 9220
  487.5 82.1 %copy-start.44 = (f32[1,64,768]{2,1,0:T(8,128)S(1)}, f32[1,64,768]{2,1,0:T(8,128)}, u32[]{:S(2)}) copy-start(f32[1,64,768]{2,1,0:T(8,128)} %copy-done.43) | copy-start | bytes 589828
  487.7 82.9 %copy-start.69 = (bf16[1,2,64,768]{3,2,1,0:T(8,128)(2,1)}, bf16[1,2,64,768]{3,2,1,0:T(8,128)(2,1)S(1)}, u32[]{:S(2)}) copy-start(bf16[1,2,64,768]{3,2,1,0:T(8,128)(2,1)S(1)} %fusion.206) | copy-start | bytes 589828
  570.6 72.8 %copy-start.68 = (bf16[1,2,64,768]{3,2,1,0:T(8,128)(2,1)}, bf16[1,2,64,768]{3,2,1,0:T(8,128)(2,1)S(1)}, u32[]{:S(2)}) copy-start(bf16[1,2,64,768]{3,2,1,0:T(8,128)(2,1)S(1)} %fusion.209) | copy-start | bytes 589828
  (94 other events, 525.0 us)
Sparse Core Ops, SparseCore 0:
  23.9 20.8 reduce-scatter.12
  59.5 20.1 reduce-scatter.14
  112.5 22.0 reduce-scatter.16
  150.2 21.1 reduce-scatter.18
  192.8 33.8 reduce-scatter.20
  239.3 23.7 reduce-scatter.22
  276.5 24.6 reduce-scatter.24
  313.7 24.4 reduce-scatter.26
  362.8 20.1 reduce-scatter.28
  400.6 21.1 reduce-scatter.30
  446.1 20.2 reduce-scatter.32
  479.8 20.2 reduce-scatter.34
  503.9 136.8 all-reduce.4
where the time goes:
time: 665 us; the launch traced here: 654 us
  waiting for transfers between devices  199 us (30%)
  blocking collectives  171 us (26%)
  other arithmetic  112 us (17%)
  local copies, waits for them, and re-layouts  102 us (15%)
  matrix products  43.7 us (7%)
  between operations  15.8 us (2%)
  starting transfers between devices  10.2 us (2%)
    reduce_scatter x12, waiting for transfers between devices, shards(): lax.psum_scatter(summand_terms.astype(jnp.bfloat16), 'tensor', scatter_di...  119 us
    psum x1, waiting for transfers between devices, shards(): lax.psum(grad_qkv.astype(jnp.bfloat16), 'dp').astype(jnp.float32)  70.1 us
    psum x1, blocking collectives, shards(): lax.psum((small['out_bias'], small['down_bias'], small['gain_grad'], smal...  63.2 us
    dynamic_slice x32, local copies, waits for them, and re-layouts, update_one(): current = lax.dynamic_index_in_dim(buffer, slot, 0, keepdims=False)  40.3 us
    dynamic_update_slice x31, other arithmetic, update_one(): lax.dynamic_update_index_in_dim(buffer, jnp.where(active, value, current)...  37.2 us
    all_gather x3, blocking collectives, shards(): row_total_whole = lax.all_gather(layer_entry, 'tensor', axis=1, tiled=True)  20.2 us
    all_gather x3, blocking collectives, shards(): lax.all_gather(grad_y_low, 'tensor', axis=1, tiled=True)  19.3 us
    all_gather x3, blocking collectives, shards(): lax.all_gather(grad_branch_low, 'tensor', axis=1, tiled=True)  19.3 us
  transfers between devices with their start and end apart: 17, of which 16 were waited for; matrix products, arithmetic and copies ran while one was open for 20% of the time, Pallas kernels for 0%

commit v1 on v0

v1 whole, which is shorter than its diff:
```python
import functools

import jax
import jax.numpy as jnp
from jax import lax
from jax.experimental import pallas as pl
from jax.experimental.pallas import tpu as pltpu
from jax.sharding import PartitionSpec as P

HEAD_DIM = 64
EPSILON = 1e-06
BIG_NEGATIVE = -1e30
VMEM_BYTES = 40 * 1024 * 1024
EXTRA_ROWS = 16
SQRT_HALF = 0.7071067811865476
INV_SQRT_TAU = 0.3989422804014327

f32 = jnp.float32
bf16 = jnp.bfloat16


def dot_nn(left, right):
    return lax.dot_general(left, right, (((1,), (0,)), ((), ())), preferred_element_type=f32)


def dot_nt(left, right):
    return lax.dot_general(left, right, (((1,), (1,)), ((), ())), preferred_element_type=f32)


def dot_tn(left, right):
    return lax.dot_general(left, right, (((0,), (0,)), ((), ())), preferred_element_type=f32)


def shape(dims, kind):
    return jax.ShapeDtypeStruct(dims, kind)


def run(kernel, outs, args, flops, name, **grid):
    moved = sum(item.size * item.dtype.itemsize for item in (*args, *outs))
    return pl.pallas_call(
        kernel,
        out_shape=outs,
        name=name,
        compiler_params=pltpu.CompilerParams(vmem_limit_bytes=VMEM_BYTES),
        cost_estimate=pl.CostEstimate(flops=flops, bytes_accessed=moved, transcendentals=0),
        **grid,
    )(*args)


def heads_forward(rows, w, bias, same):
    query = ((dot_nn(rows, w[0]) + bias[0:1]).astype(bf16) * HEAD_DIM**-0.5).astype(bf16)
    key = dot_nn(rows, w[1]).astype(bf16)
    value = (dot_nn(rows, w[2]) + bias[1:2]).astype(bf16)
    probs, mixed = [], []
    for start in range(0, query.shape[1], HEAD_DIM):
        head = slice(start, start + HEAD_DIM)
        scores = jnp.where(same, dot_nt(query[:, head], key[:, head]), BIG_NEGATIVE)
        weights = jnp.exp(scores - jnp.max(scores, -1, keepdims=True))
        total = jnp.sum(weights, -1, keepdims=True)
        low = (weights * (1.0 / total)).astype(bf16)
        probs.append(low)
        mixed.append(dot_nn(low, value[:, head]).astype(bf16))
    return query, key, value, probs, jnp.concatenate(mixed, 1)


def heads_backward(query, key, value, probs, grad_mixed):
    parts = [], [], []
    for number, low in enumerate(probs):
        head = slice(number * HEAD_DIM, (number + 1) * HEAD_DIM)
        upstream = grad_mixed[:, head]
        wide = low.astype(f32)
        product = wide * dot_nt(upstream, value[:, head])
        scores = (product - wide * jnp.sum(product, -1, keepdims=True)).astype(bf16)
        parts[0].append((dot_nn(scores, key[:, head]) * HEAD_DIM**-0.5).astype(bf16))
        parts[1].append(dot_tn(scores, query[:, head]).astype(bf16))
        parts[2].append(dot_tn(low, upstream).astype(bf16))
    return [jnp.concatenate(part, 1) for part in parts]


def attend_kernel(own, other, w_own, w_far, b_own, b_far, o_own, o_far, seg_row, seg_col, *outs):
    keep, send = outs[:2]
    rows = jnp.concatenate([own[...], other[...]], 0)
    same = seg_col[...] == seg_row[...]
    total = None
    for group, (w, bias, out) in enumerate(((w_own, b_own, o_own), (w_far, b_far, o_far))):
        query, key, value, probs, mixed = heads_forward(rows, w, bias, same)
        if len(outs) > 2:
            qkv, kept = outs[2:]
            qkv[group, 0], qkv[group, 1], qkv[group, 2] = query, key, value
            for number, low in enumerate(probs):
                kept[group, number] = low
        term = dot_nn(mixed, out[...])
        total = term if total is None else total + term
    half = own.shape[0]
    keep[...] = total[:half]
    send[...] = total[half:].astype(bf16)


def attend_back_kernel(own, other, w_own, w_far, o_own, o_far, qkv, kept, keep, send):
    rows = jnp.concatenate([own[...], other[...]], 0)
    total = None
    for group, (w, out) in enumerate(((w_own, o_own), (w_far, o_far))):
        grad_mixed = dot_nt(rows, out[...]).astype(bf16)
        probs = [kept[group, number] for number in range(kept.shape[1])]
        parts = heads_backward(qkv[group, 0], qkv[group, 1], qkv[group, 2], probs, grad_mixed)
        for number, part in enumerate(parts):
            term = dot_nt(part, w[number])
            total = term if total is None else total + term
    half = own.shape[0]
    keep[...] = total[:half]
    send[...] = total[half:].astype(bf16)


def standard(values):
    centred = values - jnp.mean(values, -1, keepdims=True)
    spread = lax.rsqrt(jnp.mean(centred * centred, -1, keepdims=True) + EPSILON)
    return centred * spread, spread


def norm_kernel(arrived, kept, residual, bias, gain, shift, *outs):
    summed = residual[...].astype(f32) + (arrived[...].astype(f32) + kept[...] + bias[...])
    result = standard(summed)[0] * gain[...] + shift[...]
    outs[0][...] = result.astype(bf16)
    if len(outs) > 1:
        outs[1][...] = result
    if len(outs) > 2:
        outs[2][...] = summed


def norm_grads(values, gain, upstream):
    normal, spread = standard(values)
    scaled = upstream * gain
    along = jnp.mean(scaled * normal, -1, keepdims=True)
    grad = (scaled - jnp.mean(scaled, -1, keepdims=True) - normal * along) * spread
    return grad, jnp.sum(upstream * normal, 0, keepdims=True), jnp.sum(upstream, 0, keepdims=True)


def norm_back_kernel(upstream, values, gain, grad, low, gain_bias):
    result, grad_gain, grad_shift = norm_grads(values[...], gain[...], upstream[...].astype(f32))
    grad[...] = result
    low[...] = result.astype(bf16)
    gain_bias[0:1] = grad_gain
    gain_bias[1:2] = grad_shift


def norm_back_sum_kernel(arrived, kept, residual, values, gain, others, grad, low):
    upstream = residual[...] + (arrived[...].astype(f32) + kept[...])
    result, grad_gain, grad_shift = norm_grads(values[...], gain[...], upstream)
    rows = result.shape[0]
    grad[...] = result
    low[0:rows] = result.astype(bf16)
    small = jnp.concatenate([grad_gain, grad_shift, others[0:2]], 0)
    high = small.astype(bf16)
    rest = (small - high.astype(f32)).astype(bf16)
    blank = jnp.zeros((EXTRA_ROWS - 8, result.shape[1]), bf16)
    low[rows : rows + EXTRA_ROWS] = jnp.concatenate([high, rest, blank], 0)


def feed_kernel(one, two, three, four, up, up_bias, down, keep, send, *saved):
    part = one.shape[0]
    rows = jnp.concatenate([one[...], two[...], three[...], four[...]], 0)
    hidden = dot_nn(rows, up[...]) + up_bias[...]
    phi = 0.5 * (1.0 + lax.erf(hidden * SQRT_HALF))
    if saved:
        slope = phi + hidden * (jnp.exp(-0.5 * hidden * hidden) * INV_SQRT_TAU)
        saved[0][...] = slope.astype(bf16)
    total = dot_nn((hidden * phi).astype(bf16), down[...])
    keep[...] = total[: 2 * part]
    send[...] = total[2 * part :].astype(bf16)


def feed_back_kernel(one, two, three, four, slope, up, down, keep, send):
    part = one.shape[0]
    rows = jnp.concatenate([one[...], two[...], three[...], four[...]], 0)
    hidden = (dot_nt(rows, down[...]) * slope[...].astype(f32)).astype(bf16)
    total = dot_nt(hidden, up[...])
    keep[...] = total[: 2 * part]
    send[...] = total[2 * part :].astype(bf16)


def halves_kernel(arrived, kept, keep, send):
    part = keep.shape[0]
    total = arrived[...].astype(f32) + kept[...]
    keep[...] = total[:part]
    send[...] = total[part:].astype(bf16)


def entry_grad_kernel(arrived, kept, residual, low):
    low[...] = (residual[...] + (arrived[...].astype(f32) + kept[...])).astype(bf16)


def attend_all_kernel(rows, w, bias, seg_row, seg_col, qkv, kept, mixed):
    part = rows.shape[1] - EXTRA_ROWS
    whole = jnp.concatenate([rows[0, :part], rows[1, :part]], 0)
    same = seg_col[0] == seg_row[0]
    query, key, value, probs, heads = heads_forward(whole, w, bias, same)
    qkv[0, 0], qkv[0, 1], qkv[0, 2] = query, key, value
    for number, low in enumerate(probs):
        kept[0, number] = low
    mixed[0] = heads


def attend_grads_kernel(rows, grads, out, qkv, kept, mixed, g_w, g_b, g_out, g_out_b):
    @pl.when(pl.program_id(0) == 0)
    def _():
        g_w[...] = jnp.zeros_like(g_w)
        g_b[...] = jnp.zeros_like(g_b)
        g_out[...] = jnp.zeros_like(g_out)
        g_out_b[...] = jnp.zeros_like(g_out_b)

    part = rows.shape[1] - EXTRA_ROWS
    entry = jnp.concatenate([rows[0, :part], rows[1, :part]], 0)
    branch = jnp.concatenate([grads[0, :part], grads[1, :part]], 0)
    grad_mixed = dot_nt(branch, out[...]).astype(bf16)
    probs = [kept[0, number] for number in range(kept.shape[1])]
    parts = heads_backward(qkv[0, 0], qkv[0, 1], qkv[0, 2], probs, grad_mixed)
    for number, item in enumerate(parts):
        g_w[number] += dot_tn(entry, item)
    g_b[0:1] += jnp.sum(parts[0].astype(f32), 0, keepdims=True)
    g_b[1:2] += jnp.sum(parts[2].astype(f32), 0, keepdims=True)
    g_out[...] += dot_tn(mixed[0], branch)
    g_out_b[...] += jnp.sum(branch.astype(f32), 0, keepdims=True)


def feed_grads_kernel(rows, grads, up, up_bias, down, g_up, g_up_b, g_down, g_down_b):
    @pl.when(pl.program_id(0) == 0)
    def _():
        g_up[...] = jnp.zeros_like(g_up)
        g_up_b[...] = jnp.zeros_like(g_up_b)
        g_down[...] = jnp.zeros_like(g_down)
        g_down_b[...] = jnp.zeros_like(g_down_b)

    first, grad = rows[...], grads[...]
    hidden = dot_nn(first, up[...]) + up_bias[...]
    phi = 0.5 * (1.0 + lax.erf(hidden * SQRT_HALF))
    slope = phi + hidden * (jnp.exp(-0.5 * hidden * hidden) * INV_SQRT_TAU)
    act = (hidden * phi).astype(bf16)
    grad_hidden = (dot_nt(grad, down[...]) * slope).astype(bf16)
    g_down[...] += dot_tn(act, grad)
    g_up[...] += dot_tn(first, grad_hidden)
    g_up_b[...] += jnp.sum(grad_hidden.astype(f32), 0, keepdims=True)
    g_down_b[...] += jnp.sum(grad.astype(f32), 0, keepdims=True)


def whole(item):
    return pl.BlockSpec(item.shape, lambda step: (0,) * len(item.shape))


def leading(item, count):
    rest = len(item.shape) - 1
    return pl.BlockSpec((count,) + item.shape[1:], lambda step: (step,) + (0,) * rest)


def shards(
    block_input,
    segments,
    out_grad,
    query_key_value_weight,
    b_qv,
    attention_output_weight,
    attention_out_bias,
    ln_gain,
    ln_bias,
    up_projection_weight,
    up_proj_bias,
    down_projection_weight,
    down_proj_bias,
):
    assert lax.axis_size("tensor") == 4 and block_input.shape[0] == 2
    groups = lax.axis_size("dp")
    section = lax.axis_index("section")
    place = lax.axis_index("tensor")
    a, b = place // 2, place % 2
    seqs, quarter, width = block_input.shape
    length = segments.shape[1]
    part = length // 2
    local = query_key_value_weight.shape[3]
    hidden_local = up_projection_weight.shape[2]
    heads = local // HEAD_DIM

    beside = [(i, i ^ 1) for i in range(4)]
    across = [(i, i ^ 2) for i in range(4)]
    turn = [(2 * s + c, 2 * c + s) for s in range(2) for c in range(2)]
    twist = [(2 * s + c, 2 * c + 1 - s) for s in range(2) for c in range(2)]
    untwist = [(target, source) for source, target in twist]

    def swap(value, pairs):
        return lax.ppermute(value, "tensor", pairs)

    def pieces_of(block):
        one = swap(jnp.where(b == 0, block[0], block[1]), turn)
        two = swap(jnp.where(b == 0, block[1], block[0]), untwist)
        return jnp.where(a == 0, jnp.concatenate([one, two]), jnp.concatenate([two, one]))

    def blocks_of(piece):
        one = swap(jnp.where(a == 0, piece[:quarter], piece[quarter:]), turn)
        two = swap(jnp.where(a == 0, piece[quarter:], piece[:quarter]), twist)
        return jnp.where(b == 0, jnp.stack([one, two]), jnp.stack([two, one]))

    w_own = jnp.transpose(query_key_value_weight[0], (1, 0, 2))
    o_own = attention_output_weight[0]
    b_own = b_qv[0].astype(f32)
    entry_input = pieces_of(block_input)
    w_far = swap(w_own, across)
    o_far = swap(o_own, across)
    b_far = swap(b_own, across)
    cotangent = pieces_of(out_grad)
    out_bias = attention_out_bias.astype(f32)
    gain = ln_gain[0].astype(f32)
    shift = ln_bias[0].astype(f32)
    up, down = up_projection_weight[0], down_projection_weight[0]
    up_bias = up_proj_bias.astype(f32)
    down_bias = down_proj_bias.astype(f32)

    seg_own = segments[0] if seqs == 1 else jnp.where(a == 0, segments[0], segments[1])
    seg_own = seg_own.astype(f32)
    seg_turned = jnp.where(b == 0, seg_own, jnp.roll(seg_own, part))
    seg_row, seg_col = seg_turned[None, :], seg_turned[:, None]

    piece_f, piece_h = shape((part, width), f32), shape((part, width), bf16)
    pair_f, pair_h = shape((2 * part, width), f32), shape((2 * part, width), bf16)
    weights_macs = length * width * 4 * local * 2
    scores_macs = 2 * heads * length * length * HEAD_DIM
    feed_macs = 4 * part * width * hidden_local * 2

    def forward(entry, save):
        outs = [piece_f, piece_h]
        if save:
            outs += [
                shape((2, 3, length, local), bf16),
                shape((2, heads, length, length), bf16),
            ]
        args = (entry, swap(entry, beside), w_own, w_far, b_own, b_far, o_own, o_far, seg_row, seg_col)
        flops = 2 * weights_macs + 4 * scores_macs
        keep, send, *kept = run(attend_kernel, outs, args, flops, "attend")
        args = (swap(send, beside), keep, entry, out_bias, gain[0:1], shift[0:1])
        first_low, first, *first_res = run(
            norm_kernel, [piece_h, piece_f] + [piece_f] * save, args, 0, "first_norm"
        )
        far = swap(first_low, across)
        near, far_near = swap(first_low, beside), None
        far_near = swap(far, beside)
        outs = [pair_f, pair_h] + [shape((4 * part, hidden_local), bf16)] * save
        args = (first_low, far, near, far_near, up, up_bias, down)
        keep, send, *slope = run(feed_kernel, outs, args, 2 * feed_macs, "feed")
        keep, send = run(halves_kernel, [piece_f, piece_h], (swap(send, beside), keep), 0, "halves")
        args = (swap(send, across), keep, first, down_bias, gain[1:2], shift[1:2])
        output, *second = run(
            norm_kernel, [piece_h] + [piece_f, piece_f] * save, args, 0, "second_norm"
        )
        if not save:
            return output
        return output, kept, first_low, first_res[0], slope[0], second[1]

    def backward(upstream, saved):
        kept, first_res, slope, second_res = saved
        grad_second, grad_y, gain_bias = run(
            norm_back_kernel,
            [piece_f, piece_h, shape((2, width), f32)],
            (upstream, second_res, gain[1:2]),
            0,
            "second_norm_back",
        )
        far = swap(grad_y, across)
        near = swap(grad_y, beside)
        far_near = swap(far, beside)
        args = (grad_y, far, near, far_near, slope, up, down)
        keep, send = run(feed_back_kernel, [pair_f, pair_h], args, 2 * feed_macs, "feed_back")
        keep, send = run(halves_kernel, [piece_f, piece_h], (swap(send, beside), keep), 0, "halves")
        args = (swap(send, across), keep, grad_second, first_res, gain[0:1], gain_bias)
        grad_first, grad_branch = run(
            norm_back_sum_kernel,
            [piece_f, shape((part + EXTRA_ROWS, width), bf16)],
            args,
            0,
            "first_norm_back",
        )
        branch = grad_branch[:part]
        args = (branch, swap(branch, beside), w_own, w_far, o_own, o_far, *kept)
        flops = 2 * weights_macs + 10 * scores_macs
        keep, send = run(attend_back_kernel, [piece_f, piece_h], args, flops, "attend_back")
        args = (swap(send, beside), keep, grad_first)
        grad_entry = run(entry_grad_kernel, [piece_h], args, 0, "entry_grad")[0]
        return grad_entry, grad_y, grad_branch

    middle = lax.ppermute(forward(entry_input, False), "section", [(0, 1)])
    entry = jnp.where(section == 0, entry_input, middle)
    output, kept, first_low, first_res, slope, second_res = forward(entry, True)
    saved = (kept, first_res, slope, second_res)
    middle = lax.ppermute(backward(cotangent, saved)[0], "section", [(1, 0)])
    grad_entry, grad_y, grad_branch = backward(jnp.where(section == 1, cotangent, middle), saved)

    wide = groups <= 4
    axes = ("dp", "tensor") if wide else ("tensor",)
    seg_line = jnp.where(b == 0, seg_own[:part], seg_own[part:]).astype(bf16)
    seg_line = jnp.pad(seg_line[None], ((0, EXTRA_ROWS - 1), (0, width - part)))
    entry_all = lax.all_gather(jnp.concatenate([entry, seg_line]), axes)
    first_all = lax.all_gather(first_low, axes)
    grad_y_all = lax.all_gather(grad_y, axes)
    grad_branch_all = lax.all_gather(grad_branch, axes)
    count = entry_all.shape[0] // 2

    seg_all = entry_all[:, part, :part].astype(f32).reshape(count, length)
    args = (entry_all, w_own, b_own, seg_all[:, None, :], seg_all[:, :, None])
    outs = [
        shape((count, 3, length, local), bf16),
        shape((count, heads, length, length), bf16),
        shape((count, length, local), bf16),
    ]
    qkv_all, kept_all, mixed_all = run(
        attend_all_kernel,
        outs,
        args,
        count * (weights_macs + 2 * scores_macs),
        "attend_all",
        grid=(count,),
        in_specs=[leading(args[0], 2), whole(w_own), whole(b_own), leading(args[3], 1), leading(args[4], 1)],
        out_specs=[leading(item, 1) for item in outs],
    )

    args = (
        first_all.reshape(-1, width),
        grad_y_all.reshape(-1, width),
        up,
        up_bias,
        down,
    )
    outs = [
        shape((width, hidden_local), f32),
        shape((1, hidden_local), f32),
        shape((hidden_local, width), f32),
        shape((1, width), f32),
    ]
    block = 2 * length
    g_up, g_up_b, g_down, g_down_b = run(
        feed_grads_kernel,
        outs,
        args,
        count * feed_macs * 2,
        "feed_grads",
        grid=(args[0].shape[0] // block,),
        in_specs=[leading(args[0], block), leading(args[1], block), whole(up), whole(up_bias), whole(down)],
        out_specs=[whole(item) for item in outs],
    )

    args = (entry_all, grad_branch_all, o_own, qkv_all, kept_all, mixed_all)
    outs = [
        shape((3, width, local), f32),
        shape((2, local), f32),
        shape((local, width), f32),
        shape((1, width), f32),
    ]
    g_w, g_b, g_out, g_out_b = run(
        attend_grads_kernel,
        outs,
        args,
        count * (weights_macs + 5 * scores_macs),
        "attend_grads",
        grid=(count,),
        in_specs=[leading(args[0], 2), leading(args[1], 2), whole(o_own)]
        + [leading(item, 1) for item in args[3:]],
        out_specs=[whole(item) for item in outs],
    )
    small = jnp.sum(grad_branch_all[:, part : part + 8].astype(f32), 0)
    small = small[:4] + small[4:]
    totals = (g_w, g_b, g_out, g_up, g_up_b, g_down)
    if not wide:
        totals = [lax.psum(item.astype(bf16), "dp").astype(f32) for item in totals]
        g_out_b, g_down_b, small = lax.psum((g_out_b, g_down_b, small), "dp")
    g_w, g_b, g_out, g_up, g_up_b, g_down = totals
    return (
        blocks_of(output)[None],
        blocks_of(grad_entry)[None],
        jnp.transpose(g_w, (1, 0, 2))[None],
        g_b[None],
        g_out[None],
        g_out_b,
        jnp.stack([small[0], small[2]])[None],
        jnp.stack([small[1], small[3]])[None],
        g_up[None],
        g_up_b,
        g_down[None],
        g_down_b,
    )


def solution(mesh):
    return jax.shard_map(
        shards,
        mesh=mesh,
        in_specs=(
            P("dp", "tensor", None),
            P("dp", None),
            P("dp", "tensor", None),
            P("section", None, None, "tensor"),
            P("section", None, "tensor"),
            P("section", "tensor", None),
            P("section", None),
            P("section", None, None),
            P("section", None, None),
            P("section", None, "tensor"),
            P("section", "tensor"),
            P("section", "tensor", None),
            P("section", None),
        ),
        out_specs=(
            P("section", "dp", "tensor", None),
            P("section", "dp", "tensor", None),
            P("section", None, None, "tensor"),
            P("section", None, "tensor"),
            P("section", "tensor", None),
            P("section", None),
            P("section", None, None),
            P("section", None, None),
            P("section", None, "tensor"),
            P("section", "tensor"),
            P("section", "tensor", None),
            P("section", None),
        ),
        check_vma=False,
    )
```

time: 665 us -> 312 us (0.47); the launches traced: 654 us -> 310 us
  blocking collectives: 171 us -> 0 us
  other arithmetic: 112 us -> 11 us
  Pallas kernels: 0 us -> 67 us
  waiting for transfers between devices: 199 us -> 139 us
  local copies, waits for them, and re-layouts: 102 us -> 46.1 us
  matrix products: 43.7 us -> 0 us
  starting transfers between devices: 10.2 us -> 32.8 us
    reduce_scatter x12 -> x0, waiting for transfers between devices: 119 us -> none  [shards(): lax.psum_scatter(summand_terms.astype(jnp.bfloat16), 'tensor', scatter_di...]
    ppermute x4 -> x41, waiting for transfers between devices: 9.91 us -> 109 us  [the longest x39 97.3 us: swap(): return lax.ppermute(value, 'tensor', pairs)]
    all_gather x14 -> x0, blocking collectives: 95.7 us -> none  [the longest x3 20.2 us: shards(): row_total_whole = lax.all_gather(layer_entry, 'tensor', axis=1, tiled=True)]
    psum x2 -> x0, blocking collectives: 74.9 us -> none  [the longest x1 63.2 us: shards(): lax.psum((small['out_bias'], small['down_bias'], small['gain_grad'], smal...]
    psum x1 -> x0, waiting for transfers between devices: 70.1 us -> none  [shards(): lax.psum(grad_qkv.astype(jnp.bfloat16), 'dp').astype(jnp.float32)]
    pallas_call x0 -> x25, Pallas kernels: none -> 67 us  [run(): pl.pallas_call(kernel, out_shape=outs, name=name, compiler_params=pltpu.C...]
    dot_general x32 -> x0, matrix products: 41.6 us -> none  [the longest x2 7.73 us: mlp_back(): jnp.einsum('jmp,qp->jmq', output_gradient_whole, down_matrix, preferred_e...]
    dynamic_slice x32 -> x0, local copies, waits for them, and re-layouts: 40.3 us -> none  [update_one(): current = lax.dynamic_index_in_dim(buffer, slot, 0, keepdims=False)]
  transfers between devices with their start and end apart: 17 -> 45, of which waited for: 16 -> 30; matrix products, arithmetic and copies ran while one was open for 20% -> 4% of each run, Pallas kernels for 0% -> 14%
where the time goes in v1:
time: 312 us; the launch traced here: 310 us
  waiting for transfers between devices  139 us (45%)
  Pallas kernels  67 us (21%)
  local copies, waits for them, and re-layouts  46.1 us (15%)
  starting transfers between devices  32.8 us (11%)
  between operations  14.4 us (5%)
  other arithmetic  11 us (4%)
    ppermute x39, waiting for transfers between devices, swap(): return lax.ppermute(value, 'tensor', pairs)  97.3 us
    pallas_call x25, Pallas kernels, run(): pl.pallas_call(kernel, out_shape=outs, name=name, compiler_params=pltpu.C...  67 us
    unnamed x114, local copies, waits for them, and re-layouts  42.4 us
    all_gather x1, waiting for transfers between devices, shards(): grad_branch_all = lax.all_gather(grad_branch, axes)  28.4 us
    ppermute x39, starting transfers between devices, swap(): return lax.ppermute(value, 'tensor', pairs)  27 us
    ppermute x1, waiting for transfers between devices, shards(): middle = lax.ppermute(backward(cotangent, saved)[0], 'section', [(1, 0)])  7.86 us
  transfers between devices with their start and end apart: 45, of which 30 were waited for; matrix products, arithmetic and copies ran while one was open for 4% of the time, Pallas kernels for 14%

profile of v1, /device:TPU:0, one launch (start us, length us, event | category | flops | bytes accessed | tf_op | source)
XLA Modules:
  0.0 310.4 jit_solution(9503471691703896955)
XLA Ops:
  8.2 3.0 collective-permute-start.1
  20.9 13.4 %collective-permute-done.3 = bf16[3,768,192]{1,2,0:T(8,128)(2,1)} collective-permute-done((bf16[3,768,192]{1,2,0:T(8,128)(2,1)}, bf16[3,768,192]{1,2,0:T(8,128)(2,1)}, u32[]{:S(2)}, u32[]{:S(2)}) %collective-permute-start.3) | collective-permute-done | bytes 884768 | tf_op jit(solution)/shard_map/ppermute | solution.py:288
  35.9 4.7 %collective-permute-done.5.o_far = bf16[192,768]{1,0:T(8,128)(2,1)S(1)} collective-permute-done((bf16[192,768]{1,0:T(8,128)(2,1)}, bf16[192,768]{1,0:T(8,128)(2,1)S(1)}, u32[]{:S(2)}, u32[]{:S(2)}) %collective-permute-start.5) | collective-permute-done | bytes 294944 | tf_op jit(solution)/shard_map/ppermute | solution.py:288
  40.6 3.0 attend.2
  47.8 5.4 %collective-permute-done.7.two = bf16[128,768]{1,0:T(8,128)(2,1)S(1)} collective-permute-done((bf16[128,768]{1,0:T(8,128)(2,1)S(1)}, bf16[128,768]{1,0:T(8,128)(2,1)S(1)}, u32[]{:S(2)}, u32[]{:S(2)}) %collective-permute-start.7) | collective-permute-done | bytes 196640 | tf_op jit(solution)/shard_map/ppermute | solution.py:288
  61.0 5.6 %collective-permute-done.11.arrived = bf16[128,768]{1,0:T(8,128)(2,1)S(1)} collective-permute-done((bf16[128,768]{1,0:T(8,128)(2,1)}, bf16[128,768]{1,0:T(8,128)(2,1)S(1)}, u32[]{:S(2)}, u32[]{:S(2)}) %collective-permute-start.11) | collective-permute-done | bytes 196640 | tf_op jit(solution)/shard_map/ppermute | solution.py:288
  68.9 4.4 %collective-permute-start.12 = (bf16[128,768]{1,0:T(8,128)(2,1)S(1)}, bf16[128,768]{1,0:T(8,128)(2,1)S(1)}, u32[]{:S(2)}, u32[]{:S(2)}) collective-permute-start(bf16[128,768]{1,0:T(8,128)(2,1)S(1)} %second_norm.2), channel_id=1, source_target_pairs={{0,16},{1,17},{2,18},{3,19},{4,20},{5,21},{6,22},{7,23},{8,24},{9,... | collective-permute-start | bytes 589832 | tf_op jit(solution)/shard_map/ppermute | solution.py:386
  73.3 3.6 %collective-permute-done.12 = bf16[128,768]{1,0:T(8,128)(2,1)S(1)} collective-permute-done((bf16[128,768]{1,0:T(8,128)(2,1)S(1)}, bf16[128,768]{1,0:T(8,128)(2,1)S(1)}, u32[]{:S(2)}, u32[]{:S(2)}) %collective-permute-start.12) | collective-permute-done | bytes 196640 | tf_op jit(solution)/shard_map/ppermute | solution.py:386
  79.2 3.1 attend.3
  88.9 7.7 %collective-permute-done.15.two = bf16[128,768]{1,0:T(8,128)(2,1)S(1)} collective-permute-done((bf16[128,768]{1,0:T(8,128)(2,1)}, bf16[128,768]{1,0:T(8,128)(2,1)S(1)}, u32[]{:S(2)}, u32[]{:S(2)}) %collective-permute-start.15) | collective-permute-done | bytes 196640 | tf_op jit(solution)/shard_map/ppermute | solution.py:288
  100.5 2.8 feed.3
  105.2 2.8 collective-permute-start.19
  108.0 12.5 %collective-permute-done.19.arrived = bf16[128,768]{1,0:T(8,128)(2,1)S(1)} collective-permute-done((bf16[128,768]{1,0:T(8,128)(2,1)S(1)}, bf16[128,768]{1,0:T(8,128)(2,1)S(1)}, u32[]{:S(2)}, u32[]{:S(2)}) %collective-permute-start.19) | collective-permute-done | bytes 196640 | tf_op jit(solution)/shard_map/ppermute | solution.py:288
  122.0 5.6 %collective-permute-done.24.two = bf16[128,768]{1,0:T(8,128)(2,1)S(1)} collective-permute-done((bf16[128,768]{1,0:T(8,128)(2,1)S(1)}, bf16[128,768]{1,0:T(8,128)(2,1)S(1)}, u32[]{:S(2)}, u32[]{:S(2)}) %collective-permute-start.24) | collective-permute-done | bytes 196640 | tf_op jit(solution)/shard_map/ppermute | solution.py:288
  134.0 5.6 %collective-permute-done.28.arrived = bf16[128,768]{1,0:T(8,128)(2,1)S(1)} collective-permute-done((bf16[128,768]{1,0:T(8,128)(2,1)S(1)}, bf16[128,768]{1,0:T(8,128)(2,1)S(1)}, u32[]{:S(2)}, u32[]{:S(2)}) %collective-permute-start.28) | collective-permute-done | bytes 196640 | tf_op jit(solution)/shard_map/ppermute | solution.py:288
  141.4 3.3 %attend_back.2 = (f32[128,768]{1,0:T(8,128)S(1)}, bf16[128,768]{1,0:T(8,128)(2,1)S(1)}) custom-call(bf16[128,768]{1,0:T(8,128)(2,1)S(1)} %slice.130.own, bf16[128,768]{1,0:T(8,128)(2,1)S(1)} %collective-permute-done.29.other, bf16[3,768,192]{2,1,0:T(8,128)(2,1)S(1)} %bitcast.52, bf16[3,768,192]{2,1,0:T(8,128)(2,1)S(1)} %copy.42.w_far, ...), custom_call_target="tpu_custom_call" | custom-call | flops 855638016 | bytes 4718592 | tf_op jit(solution)/shard_map/attend_back/pallas_call | solution.py:40
  148.3 7.9 %collective-permute-done.31 = bf16[128,768]{1,0:T(8,128)(2,1)} collective-permute-done((bf16[128,768]{1,0:T(8,128)(2,1)}, bf16[128,768]{1,0:T(8,128)(2,1)}, u32[]{:S(2)}, u32[]{:S(2)}) %collective-permute-start.31) | collective-permute-done | bytes 196640 | tf_op jit(solution)/shard_map/ppermute | solution.py:390
  160.4 9.4 %collective-permute-done.32.two = bf16[128,768]{1,0:T(8,128)(2,1)S(1)} collective-permute-done((bf16[128,768]{1,0:T(8,128)(2,1)}, bf16[128,768]{1,0:T(8,128)(2,1)S(1)}, u32[]{:S(2)}, u32[]{:S(2)}) %collective-permute-start.32) | collective-permute-done | bytes 196640 | tf_op jit(solution)/shard_map/ppermute | solution.py:288
  179.3 2.2 collective-permute-start.36
  181.5 5.2 %collective-permute-done.36.arrived = bf16[128,768]{1,0:T(8,128)(2,1)S(1)} collective-permute-done((bf16[128,768]{1,0:T(8,128)(2,1)S(1)}, bf16[128,768]{1,0:T(8,128)(2,1)S(1)}, u32[]{:S(2)}, u32[]{:S(2)}) %collective-permute-start.36) | collective-permute-done | bytes 196640 | tf_op jit(solution)/shard_map/ppermute | solution.py:288
  193.3 3.3 %attend_back.3 = (f32[128,768]{1,0:T(8,128)S(1)}, bf16[128,768]{1,0:T(8,128)(2,1)S(1)}) custom-call(bf16[128,768]{1,0:T(8,128)(2,1)S(1)} %slice.131.own, bf16[128,768]{1,0:T(8,128)(2,1)S(1)} %collective-permute-done.37.other, bf16[3,768,192]{2,1,0:T(8,128)(2,1)S(1)} %bitcast.53, bf16[3,768,192]{2,1,0:T(8,128)(2,1)S(1)} %copy.42.w_far, ...), custom_call_target="tpu_custom_call" | custom-call | flops 855638016 | bytes 4718592 | tf_op jit(solution)/shard_map/attend_back/pallas_call | solution.py:40
  198.2 2.8 collective-permute-start.40
  202.6 3.2 %collective-permute-done.40 = bf16[64,768]{1,0:T(8,128)(2,1)S(1)} collective-permute-done((bf16[64,768]{1,0:T(8,128)(2,1)S(1)}, bf16[64,768]{1,0:T(8,128)(2,1)S(1)}, u32[]{:S(2)}, u32[]{:S(2)}) %collective-permute-start.40) | collective-permute-done | bytes 98336 | tf_op jit(solution)/shard_map/ppermute | solution.py:288
  209.0 2.3 copy-done.1
  211.3 11.6 %attend_all.1 = (bf16[8,3,256,192]{3,2,1,0:T(8,128)(2,1)S(1)}, bf16[8,3,256,256]{3,2,1,0:T(8,128)(2,1)S(1)}, bf16[8,256,192]{2,1,0:T(8,128)(2,1)S(1)}) custom-call(bf16[16,144,768]{2,1,0:T(8,128)(2,1)S(1)} %bitcast.63, bf16[3,768,192]{2,1,0:T(8,128)(2,1)S(1)} %bitcast.54, f32[2,192]{1,0:T(2,128)S(1)} %copy-done.34, f32[8,1,256]{2,1,0:T(1,128)S(1)} %bitcast.66, ...), custom_call_target="tpu_custom_call" | custom-call | flops 2818572288 | bytes 10733056 | tf_op jit(solution)/shard_map/attend_all/pallas_call | solution.py:40
  229.1 1.9 copy-done.37
  231.0 1.9 copy-done.38
  235.4 13.4 %feed_grads.1 = (f32[768,768]{1,0:T(8,128)}, f32[1,768]{1,0:T(1,128)}, f32[768,768]{1,0:T(8,128)}, f32[1,768]{1,0:T(1,128)}) custom-call(bf16[2048,768]{1,0:T(8,128)(2,1)S(1)} %copy-done.37, bf16[2048,768]{1,0:T(8,128)(2,1)S(1)} %copy-done.38, bf16[768,768]{1,0:T(8,128)(2,1)S(1)} %bitcast.71, f32[1,768]{1,0:T(1,128)S(1)} %copy-done.36, ...), custom_call_target="tpu_custom_call" | custom-call | flops 9663676416 | bytes 13378560 | tf_op jit(solution)/shard_map/feed_grads/pallas_call | solution.py:40
  248.8 28.4 %all-gather.11.cloned.1.call-done = bf16[2304,768]{1,0:T(8,128)(2,1)} async-done(((bf16[144,768]{1,0:T(8,128)(2,1)}), bf16[2304,768]{1,0:T(8,128)(2,1)}) %all-gather.11.cloned.1.call-update) | async-done | bytes 3538960 | tf_op jit(solution)/shard_map/all_gather | solution.py:400
  278.2 2.0 copy-done.2
  280.2 1.9 copy-done.4
  285.2 16.2 %attend_grads.1 = (f32[3,768,192]{2,1,0:T(8,128)S(1)}, f32[2,192]{1,0:T(2,128)}, f32[192,768]{1,0:T(8,128)}, f32[1,768]{1,0:T(1,128)}) custom-call(bf16[16,144,768]{2,1,0:T(8,128)(2,1)S(1)} %bitcast.64, bf16[16,144,768]{2,1,0:T(8,128)(2,1)} %bitcast.78, bf16[192,768]{1,0:T(8,128)(2,1)S(1)} %bitcast.60, bf16[8,3,256,192]{3,2,1,0:T(8,128)(2,1)S(1)} %copy-done.4, ...), custom_call_target="tpu_custom_call" | custom-call | flops 3422552064 | bytes 16028160 | tf_op jit(solution)/shard_map/attend_grads/pallas_call | solution.py:40
  (239 shorter events, 96.1 us)
Async XLA Ops:
  7.2 199.3 %all-gather.9.cloned.1.call-start = ((), (), s32[]{:S(2)}) async-start(), calls=%async_computation | async-start | bytes 3760128 | tf_op jit(solution)/shard_map/all_gather | solution.py:397
  8.2 10.2 %collective-permute-start.1 = (bf16[64,768]{1,0:T(8,128)(2,1)S(1)}, bf16[64,768]{1,0:T(8,128)(2,1)S(1)}, u32[]{:S(2)}, u32[]{:S(2)}) collective-permute-start(bf16[64,768]{1,0:T(8,128)(2,1)S(1)} %get-tuple-element.165), channel_id=1, source_target_pairs={{4,0},{12,4},{0,8},{8,12},{5,1},{13,5},{1,9},{9,13},{6,2},{14,6},{... | collective-permute-start | bytes 294920 | tf_op jit(solution)/shard_map/ppermute | solution.py:288
  11.2 7.3 %collective-permute-start = (bf16[64,768]{1,0:T(8,128)(2,1)S(1)}, bf16[64,768]{1,0:T(8,128)(2,1)S(1)}, u32[]{:S(2)}, u32[]{:S(2)}) collective-permute-start(bf16[64,768]{1,0:T(8,128)(2,1)S(1)} %get-tuple-element.164), channel_id=1, source_target_pairs={{0,0},{4,8},{8,4},{12,12},{1,1},{5,9},{9,5},{13,13},{2,2},{6,10},{... | collective-permute-start | bytes 294920 | tf_op jit(solution)/shard_map/ppermute | solution.py:288
  11.8 22.4 %collective-permute-start.3 = (bf16[3,768,192]{1,2,0:T(8,128)(2,1)}, bf16[3,768,192]{1,2,0:T(8,128)(2,1)}, u32[]{:S(2)}, u32[]{:S(2)}) collective-permute-start(bf16[3,768,192]{1,2,0:T(8,128)(2,1)} %bitcast.79), channel_id=1, source_target_pairs={{0,8},{4,12},{8,0},{12,4},{1,9},{5,13},{9,1},{13,5},{2,10},{6,14},... | collective-permute-start | bytes 2654216 | tf_op jit(solution)/shard_map/ppermute | solution.py:288
  13.9 22.0 %collective-permute-start.4 = (f32[2,192]{1,0:T(2,128)S(1)}, f32[2,192]{1,0:T(2,128)S(1)}, u32[]{:S(2)}, u32[]{:S(2)}) collective-permute-start(f32[2,192]{1,0:T(2,128)S(1)} %bitcast_convert_fusion.b_own.bias), channel_id=1, source_target_pairs={{0,8},{4,12},{8,0},{12,4},{1,9},{5,13},{9,1},{13,5},{2,10},{6,14},... | collective-permute-start | bytes 4616 | tf_op jit(solution)/shard_map/ppermute | solution.py:288
  14.6 25.9 %collective-permute-start.5 = (bf16[192,768]{1,0:T(8,128)(2,1)}, bf16[192,768]{1,0:T(8,128)(2,1)S(1)}, u32[]{:S(2)}, u32[]{:S(2)}) collective-permute-start(bf16[192,768]{1,0:T(8,128)(2,1)} %bitcast.55), channel_id=1, source_target_pairs={{0,8},{4,12},{8,0},{12,4},{1,9},{5,13},{9,1},{13,5},{2,10},{6,14},... | collective-permute-start | bytes 884744 | tf_op jit(solution)/shard_map/ppermute | solution.py:288
  18.5 17.3 %collective-permute-start.2 = (bf16[128,768]{1,0:T(8,128)(2,1)S(1)}, bf16[128,768]{1,0:T(8,128)(2,1)S(1)}, u32[]{:S(2)}, u32[]{:S(2)}) collective-permute-start(bf16[128,768]{1,0:T(8,128)(2,1)S(1)} %maximum_select_fusion.own.residual), channel_id=1, source_target_pairs={{0,4},{4,0},{8,12},{12,8},{1,5},{5,1},{9,13},{13,9},{2,6},{6,2},{1... | collective-permute-start | bytes 589832 | tf_op jit(solution)/shard_map/ppermute | solution.py:288
  46.1 7.1 %collective-permute-start.7 = (bf16[128,768]{1,0:T(8,128)(2,1)S(1)}, bf16[128,768]{1,0:T(8,128)(2,1)S(1)}, u32[]{:S(2)}, u32[]{:S(2)}) collective-permute-start(bf16[128,768]{1,0:T(8,128)(2,1)S(1)} %get-tuple-element.69.one), channel_id=1, source_target_pairs={{0,8},{4,12},{8,0},{12,4},{1,9},{5,13},{9,1},{13,5},{2,10},{6,14},... | collective-permute-start | bytes 589832 | tf_op jit(solution)/shard_map/ppermute | solution.py:288
  47.8 5.4 %collective-permute-start.8 = (bf16[128,768]{1,0:T(8,128)(2,1)S(1)}, bf16[128,768]{1,0:T(8,128)(2,1)S(1)}, u32[]{:S(2)}, u32[]{:S(2)}) collective-permute-start(bf16[128,768]{1,0:T(8,128)(2,1)S(1)} %get-tuple-element.69.one), channel_id=1, source_target_pairs={{0,4},{4,0},{8,12},{12,8},{1,5},{5,1},{9,13},{13,9},{2,6},{6,2},{1... | collective-permute-start | bytes 589832 | tf_op jit(solution)/shard_map/ppermute | solution.py:288
  56.2 1.8 collective-permute-start.10
  59.5 7.2 %collective-permute-start.11 = (bf16[128,768]{1,0:T(8,128)(2,1)}, bf16[128,768]{1,0:T(8,128)(2,1)S(1)}, u32[]{:S(2)}, u32[]{:S(2)}) collective-permute-start(bf16[128,768]{1,0:T(8,128)(2,1)} %get-tuple-element.72), channel_id=1, source_target_pairs={{0,8},{4,12},{8,0},{12,4},{1,9},{5,13},{9,1},{13,5},{2,10},{6,14},... | collective-permute-start | bytes 589832 | tf_op jit(solution)/shard_map/ppermute | solution.py:288
  68.9 8.0 %collective-permute-start.12 = (bf16[128,768]{1,0:T(8,128)(2,1)S(1)}, bf16[128,768]{1,0:T(8,128)(2,1)S(1)}, u32[]{:S(2)}, u32[]{:S(2)}) collective-permute-start(bf16[128,768]{1,0:T(8,128)(2,1)S(1)} %second_norm.2), channel_id=1, source_target_pairs={{0,16},{1,17},{2,18},{3,19},{4,20},{5,21},{6,22},{7,23},{8,24},{9,... | collective-permute-start | bytes 589832 | tf_op jit(solution)/shard_map/ppermute | solution.py:386
  77.6 149.6 %all-gather.13.cloned.1.call-start = ((), (), s32[]{:S(2)}) async-start(), calls=%async_computation.2 | async-start | bytes 3342336 | tf_op jit(solution)/shard_map/all_gather | solution.py:398
  87.9 141.2 %all-gather.15.cloned.1.call-start = ((), (), s32[]{:S(2)}) async-start(), calls=%async_computation.3 | async-start | bytes 3342336 | tf_op jit(solution)/shard_map/all_gather | solution.py:399
  88.0 8.6 %collective-permute-start.15 = (bf16[128,768]{1,0:T(8,128)(2,1)}, bf16[128,768]{1,0:T(8,128)(2,1)S(1)}, u32[]{:S(2)}, u32[]{:S(2)}) collective-permute-start(bf16[128,768]{1,0:T(8,128)(2,1)} %get-tuple-element.77.one), channel_id=1, source_target_pairs={{0,8},{4,12},{8,0},{12,4},{1,9},{5,13},{9,1},{13,5},{2,10},{6,14},... | collective-permute-start | bytes 589832 | tf_op jit(solution)/shard_map/ppermute | solution.py:288
  88.9 7.7 %collective-permute-start.16 = (bf16[128,768]{1,0:T(8,128)(2,1)}, bf16[128,768]{1,0:T(8,128)(2,1)S(1)}, u32[]{:S(2)}, u32[]{:S(2)}) collective-permute-start(bf16[128,768]{1,0:T(8,128)(2,1)} %get-tuple-element.77.one), channel_id=1, source_target_pairs={{0,4},{4,0},{8,12},{12,8},{1,5},{5,1},{9,13},{13,9},{2,6},{6,2},{1... | collective-permute-start | bytes 589832 | tf_op jit(solution)/shard_map/ppermute | solution.py:288
  103.4 1.8 collective-permute-start.18
  103.6 4.4 %collective-permute-start.23 = (bf16[64,768]{1,0:T(8,128)(2,1)S(1)}, bf16[64,768]{1,0:T(8,128)(2,1)S(1)}, u32[]{:S(2)}, u32[]{:S(2)}) collective-permute-start(bf16[64,768]{1,0:T(8,128)(2,1)S(1)} %get-tuple-element.161), channel_id=1, source_target_pairs={{4,0},{12,4},{0,8},{8,12},{5,1},{13,5},{1,9},{9,13},{6,2},{14,6},{... | collective-permute-start | bytes 294920 | tf_op jit(solution)/shard_map/ppermute | solution.py:288
  103.9 4.1 %collective-permute-start.22 = (bf16[64,768]{1,0:T(8,128)(2,1)S(1)}, bf16[64,768]{1,0:T(8,128)(2,1)S(1)}, u32[]{:S(2)}, u32[]{:S(2)}) collective-permute-start(bf16[64,768]{1,0:T(8,128)(2,1)S(1)} %get-tuple-element.160), channel_id=1, source_target_pairs={{0,0},{4,8},{8,4},{12,12},{1,1},{5,9},{9,5},{13,13},{2,2},{6,10},{... | collective-permute-start | bytes 294920 | tf_op jit(solution)/shard_map/ppermute | solution.py:288
  105.2 15.3 %collective-permute-start.19 = (bf16[128,768]{1,0:T(8,128)(2,1)S(1)}, bf16[128,768]{1,0:T(8,128)(2,1)S(1)}, u32[]{:S(2)}, u32[]{:S(2)}) collective-permute-start(bf16[128,768]{1,0:T(8,128)(2,1)S(1)} %get-tuple-element.80), channel_id=1, source_target_pairs={{0,8},{4,12},{8,0},{12,4},{1,9},{5,13},{9,1},{13,5},{2,10},{6,14},... | collective-permute-start | bytes 589832 | tf_op jit(solution)/shard_map/ppermute | solution.py:288
  121.9 5.7 %collective-permute-start.24 = (bf16[128,768]{1,0:T(8,128)(2,1)S(1)}, bf16[128,768]{1,0:T(8,128)(2,1)S(1)}, u32[]{:S(2)}, u32[]{:S(2)}) collective-permute-start(bf16[128,768]{1,0:T(8,128)(2,1)S(1)} %get-tuple-element.85.one), channel_id=1, source_target_pairs={{0,8},{4,12},{8,0},{12,4},{1,9},{5,13},{9,1},{13,5},{2,10},{6,14},... | collective-permute-start | bytes 589832 | tf_op jit(solution)/shard_map/ppermute | solution.py:288
  122.0 5.7 %collective-permute-start.25 = (bf16[128,768]{1,0:T(8,128)(2,1)S(1)}, bf16[128,768]{1,0:T(8,128)(2,1)S(1)}, u32[]{:S(2)}, u32[]{:S(2)}) collective-permute-start(bf16[128,768]{1,0:T(8,128)(2,1)S(1)} %get-tuple-element.85.one), channel_id=1, source_target_pairs={{0,4},{4,0},{8,12},{12,8},{1,5},{5,1},{9,13},{13,9},{2,6},{6,2},{1... | collective-permute-start | bytes 589832 | tf_op jit(solution)/shard_map/ppermute | solution.py:288
  132.5 7.0 %collective-permute-start.28 = (bf16[128,768]{1,0:T(8,128)(2,1)S(1)}, bf16[128,768]{1,0:T(8,128)(2,1)S(1)}, u32[]{:S(2)}, u32[]{:S(2)}) collective-permute-start(bf16[128,768]{1,0:T(8,128)(2,1)S(1)} %get-tuple-element.89), channel_id=1, source_target_pairs={{0,8},{4,12},{8,0},{12,4},{1,9},{5,13},{9,1},{13,5},{2,10},{6,14},... | collective-permute-start | bytes 589832 | tf_op jit(solution)/shard_map/ppermute | solution.py:288
  147.0 9.1 %collective-permute-start.31 = (bf16[128,768]{1,0:T(8,128)(2,1)}, bf16[128,768]{1,0:T(8,128)(2,1)}, u32[]{:S(2)}, u32[]{:S(2)}) collective-permute-start(bf16[128,768]{1,0:T(8,128)(2,1)} %entry_grad.2), channel_id=1, source_target_pairs={{16,0},{17,1},{18,2},{19,3},{20,4},{21,5},{22,6},{23,7},{24,8},{25... | collective-permute-start | bytes 589832 | tf_op jit(solution)/shard_map/ppermute | solution.py:390
  158.9 118.3 %all-gather.11.cloned.1.call-start = ((), (), s32[]{:S(2)}) async-start(), calls=%async_computation.1 | async-start | bytes 3760128 | tf_op jit(solution)/shard_map/all_gather | solution.py:400
  159.0 10.9 %collective-permute-start.32 = (bf16[128,768]{1,0:T(8,128)(2,1)}, bf16[128,768]{1,0:T(8,128)(2,1)S(1)}, u32[]{:S(2)}, u32[]{:S(2)}) collective-permute-start(bf16[128,768]{1,0:T(8,128)(2,1)} %copy-done.31), channel_id=1, source_target_pairs={{0,8},{4,12},{8,0},{12,4},{1,9},{5,13},{9,1},{13,5},{2,10},{6,14},... | collective-permute-start | bytes 589832 | tf_op jit(solution)/shard_map/ppermute | solution.py:288
  160.4 9.5 %collective-permute-start.33 = (bf16[128,768]{1,0:T(8,128)(2,1)}, bf16[128,768]{1,0:T(8,128)(2,1)S(1)}, u32[]{:S(2)}, u32[]{:S(2)}) collective-permute-start(bf16[128,768]{1,0:T(8,128)(2,1)} %copy-done.31), channel_id=1, source_target_pairs={{0,4},{4,0},{8,12},{12,8},{1,5},{5,1},{9,13},{13,9},{2,6},{6,2},{1... | collective-permute-start | bytes 589832 | tf_op jit(solution)/shard_map/ppermute | solution.py:288
  179.3 7.4 %collective-permute-start.36 = (bf16[128,768]{1,0:T(8,128)(2,1)S(1)}, bf16[128,768]{1,0:T(8,128)(2,1)S(1)}, u32[]{:S(2)}, u32[]{:S(2)}) collective-permute-start(bf16[128,768]{1,0:T(8,128)(2,1)S(1)} %get-tuple-element.103), channel_id=1, source_target_pairs={{0,8},{4,12},{8,0},{12,4},{1,9},{5,13},{9,1},{13,5},{2,10},{6,14},... | collective-permute-start | bytes 589832 | tf_op jit(solution)/shard_map/ppermute | solution.py:288
  196.9 5.1 %collective-permute-start.21 = (bf16[64,768]{1,0:T(8,128)(2,1)S(1)}, bf16[64,768]{1,0:T(8,128)(2,1)S(1)}, u32[]{:S(2)}, u32[]{:S(2)}) collective-permute-start(bf16[64,768]{1,0:T(8,128)(2,1)S(1)} %get-tuple-element.163), channel_id=1, source_target_pairs={{0,4},{4,12},{8,0},{12,8},{1,5},{5,13},{9,1},{13,9},{2,6},{6,14},{... | collective-permute-start | bytes 294920 | tf_op jit(solution)/shard_map/ppermute | solution.py:288
  197.2 4.7 %collective-permute-start.20 = (bf16[64,768]{1,0:T(8,128)(2,1)S(1)}, bf16[64,768]{1,0:T(8,128)(2,1)S(1)}, u32[]{:S(2)}, u32[]{:S(2)}) collective-permute-start(bf16[64,768]{1,0:T(8,128)(2,1)S(1)} %get-tuple-element.162), channel_id=1, source_target_pairs={{0,0},{4,8},{8,4},{12,12},{1,1},{5,9},{9,5},{13,13},{2,2},{6,10},{... | collective-permute-start | bytes 294920 | tf_op jit(solution)/shard_map/ppermute | solution.py:288
  198.2 7.6 %collective-permute-start.40 = (bf16[64,768]{1,0:T(8,128)(2,1)S(1)}, bf16[64,768]{1,0:T(8,128)(2,1)S(1)}, u32[]{:S(2)}, u32[]{:S(2)}) collective-permute-start(bf16[64,768]{1,0:T(8,128)(2,1)S(1)} %get-tuple-element.159), channel_id=1, source_target_pairs={{0,4},{4,12},{8,0},{12,8},{1,5},{5,13},{9,1},{13,9},{2,6},{6,14},{... | collective-permute-start | bytes 294920 | tf_op jit(solution)/shard_map/ppermute | solution.py:288
  201.0 4.8 %collective-permute-start.39 = (bf16[64,768]{1,0:T(8,128)(2,1)S(1)}, bf16[64,768]{1,0:T(8,128)(2,1)S(1)}, u32[]{:S(2)}, u32[]{:S(2)}) collective-permute-start(bf16[64,768]{1,0:T(8,128)(2,1)S(1)} %get-tuple-element.158), channel_id=1, source_target_pairs={{0,0},{4,8},{8,4},{12,12},{1,1},{5,9},{9,5},{13,13},{2,2},{6,10},{... | collective-permute-start | bytes 294920 | tf_op jit(solution)/shard_map/ppermute | solution.py:288
  (69 other events, 607.9 us)
Sparse Core Ops, SparseCore 0:
  77.7 54.0 all-gather.8
  134.1 48.5 all-gather.12
  184.9 44.0 all-gather.14
  231.2 45.9 all-gather.10

commit v2 on v1

--- a/solution.py
+++ b/solution.py
@@ -10,7 +10,7 @@
 HEAD_DIM = 64
 EPSILON = 1e-06
 BIG_NEGATIVE = -1e30
-VMEM_BYTES = 40 * 1024 * 1024
+MIB = 1024 * 1024
 EXTRA_ROWS = 16
 SQRT_HALF = 0.7071067811865476
 INV_SQRT_TAU = 0.3989422804014327
@@ -35,13 +35,13 @@
     return jax.ShapeDtypeStruct(dims, kind)
 
 
-def run(kernel, outs, args, flops, name, **grid):
+def run(kernel, outs, args, flops, name, mib=16, **grid):
     moved = sum(item.size * item.dtype.itemsize for item in (*args, *outs))
     return pl.pallas_call(
         kernel,
         out_shape=outs,
         name=name,
-        compiler_params=pltpu.CompilerParams(vmem_limit_bytes=VMEM_BYTES),
+        compiler_params=pltpu.CompilerParams(vmem_limit_bytes=mib * MIB),
         cost_estimate=pl.CostEstimate(flops=flops, bytes_accessed=moved, transcendentals=0),
         **grid,
     )(*args)
@@ -189,40 +189,52 @@
     low[...] = (residual[...] + (arrived[...].astype(f32) + kept[...])).astype(bf16)
 
 
-def attend_all_kernel(rows, w, bias, seg_row, seg_col, qkv, kept, mixed):
-    part = rows.shape[1] - EXTRA_ROWS
-    whole = jnp.concatenate([rows[0, :part], rows[1, :part]], 0)
+def attend_all_kernel(mine, other, w, bias, seg_row, seg_col, qkv, kept, mixed):
+    part = mine.shape[1] - EXTRA_ROWS
+    rows = jnp.concatenate([mine[0, :part], other[0, :part]], 0)
     same = seg_col[0] == seg_row[0]
-    query, key, value, probs, heads = heads_forward(whole, w, bias, same)
+    query, key, value, probs, heads = heads_forward(rows, w, bias, same)
     qkv[0, 0], qkv[0, 1], qkv[0, 2] = query, key, value
     for number, low in enumerate(probs):
         kept[0, number] = low
     mixed[0] = heads
 
 
-def attend_grads_kernel(rows, grads, out, qkv, kept, mixed, g_w, g_b, g_out, g_out_b):
-    @pl.when(pl.program_id(0) == 0)
-    def _():
-        g_w[...] = jnp.zeros_like(g_w)
-        g_b[...] = jnp.zeros_like(g_b)
-        g_out[...] = jnp.zeros_like(g_out)
-        g_out_b[...] = jnp.zeros_like(g_out_b)
-
-    part = rows.shape[1] - EXTRA_ROWS
-    entry = jnp.concatenate([rows[0, :part], rows[1, :part]], 0)
-    branch = jnp.concatenate([grads[0, :part], grads[1, :part]], 0)
-    grad_mixed = dot_nt(branch, out[...]).astype(bf16)
-    probs = [kept[0, number] for number in range(kept.shape[1])]
-    parts = heads_backward(qkv[0, 0], qkv[0, 1], qkv[0, 2], probs, grad_mixed)
-    for number, item in enumerate(parts):
-        g_w[number] += dot_tn(entry, item)
-    g_b[0:1] += jnp.sum(parts[0].astype(f32), 0, keepdims=True)
-    g_b[1:2] += jnp.sum(parts[2].astype(f32), 0, keepdims=True)
-    g_out[...] += dot_tn(mixed[0], branch)
-    g_out_b[...] += jnp.sum(branch.astype(f32), 0, keepdims=True)
-
-
-def feed_grads_kernel(rows, grads, up, up_bias, down, g_up, g_up_b, g_down, g_down_b):
+def attend_grads_kernel(group, mine, other, one, two, three, four, out, qkv, kept, mixed, *refs):
+    g_w, g_b, g_out, g_out_b, g_small = refs[-5:]
+    part = mine.shape[1] - EXTRA_ROWS
+    sums = None
+    for seq, (low_half, high_half) in enumerate(((one, two), (three, four))):
+        entry = jnp.concatenate([mine[seq, :part], other[seq, :part]], 0)
+        branch = jnp.concatenate([low_half[:part], high_half[:part]], 0)
+        grad_mixed = dot_nt(branch, out[...]).astype(bf16)
+        probs = [kept[seq, number] for number in range(kept.shape[1])]
+        parts = heads_backward(qkv[seq, 0], qkv[seq, 1], qkv[seq, 2], probs, grad_mixed)
+        small = low_half[part:].astype(f32) + high_half[part:].astype(f32)
+        terms = [dot_tn(entry, item) for item in parts]
+        terms += [jnp.sum(parts[0].astype(f32), 0, keepdims=True)]
+        terms += [jnp.sum(parts[2].astype(f32), 0, keepdims=True)]
+        terms += [dot_tn(mixed[seq], branch), jnp.sum(branch.astype(f32), 0, keepdims=True)]
+        terms += [small[:4] + small[4:8]]
+        sums = terms if sums is None else [old + new for old, new in zip(sums, terms)]
+    before = refs[:-5]
+    for number, item in enumerate(sums):
+        name = (0, 0, 0, 1, 1, 2, 3, 4)[number]
+        spot = ((0,), (1,), (2,), (slice(0, 1),), (slice(1, 2),), (), (), ())[number]
+        spot = spot if spot else (...,)
+        refs[name - 5][spot] = item + before[name][spot] if before else item
+
+
+def feed_all_kernel(rows, up, up_bias, act, slope):
+    hidden = dot_nn(rows[...], up[...]) + up_bias[...]
+    phi = 0.5 * (1.0 + lax.erf(hidden * SQRT_HALF))
+    act[...] = (hidden * phi).astype(bf16)
+    slope[...] = (phi + hidden * (jnp.exp(-0.5 * hidden * hidden) * INV_SQRT_TAU)).astype(bf16)
+
+
+def feed_grads_kernel(*refs):
+    down, g_up, g_up_b, g_down, g_down_b = refs[8:]
+
     @pl.when(pl.program_id(0) == 0)
     def _():
         g_up[...] = jnp.zeros_like(g_up)
@@ -230,12 +242,10 @@
         g_down[...] = jnp.zeros_like(g_down)
         g_down_b[...] = jnp.zeros_like(g_down_b)
 
-    first, grad = rows[...], grads[...]
-    hidden = dot_nn(first, up[...]) + up_bias[...]
-    phi = 0.5 * (1.0 + lax.erf(hidden * SQRT_HALF))
-    slope = phi + hidden * (jnp.exp(-0.5 * hidden * hidden) * INV_SQRT_TAU)
-    act = (hidden * phi).astype(bf16)
-    grad_hidden = (dot_nt(grad, down[...]) * slope).astype(bf16)
+    first, grad, act, slope = (
+        jnp.concatenate([refs[i][...], refs[i + 4][...]], 0) for i in range(4)
+    )
+    grad_hidden = (dot_nt(grad, down[...]) * slope.astype(f32)).astype(bf16)
     g_down[...] += dot_tn(act, grad)
     g_up[...] += dot_tn(first, grad_hidden)
     g_up_b[...] += jnp.sum(grad_hidden.astype(f32), 0, keepdims=True)
@@ -350,7 +360,7 @@
         )
         if not save:
             return output
-        return output, kept, first_low, first_res[0], slope[0], second[1]
+        return output, kept, (first_low, far), first_res[0], slope[0], second[1]
 
     def backward(upstream, saved):
         kept, first_res, slope, second_res = saved
@@ -381,88 +391,130 @@
         keep, send = run(attend_back_kernel, [piece_f, piece_h], args, flops, "attend_back")
         args = (swap(send, beside), keep, grad_first)
         grad_entry = run(entry_grad_kernel, [piece_h], args, 0, "entry_grad")[0]
-        return grad_entry, grad_y, grad_branch
-
-    middle = lax.ppermute(forward(entry_input, False), "section", [(0, 1)])
+        return grad_entry, (grad_y, far), grad_branch
+
+    sections = [(0, 1), (1, 0)]
+    middle = lax.ppermute(forward(entry_input, False), "section", sections)
     entry = jnp.where(section == 0, entry_input, middle)
-    output, kept, first_low, first_res, slope, second_res = forward(entry, True)
+    output, kept, first, first_res, slope, second_res = forward(entry, True)
     saved = (kept, first_res, slope, second_res)
-    middle = lax.ppermute(backward(cotangent, saved)[0], "section", [(1, 0)])
-    grad_entry, grad_y, grad_branch = backward(jnp.where(section == 1, cotangent, middle), saved)
-
-    wide = groups <= 4
-    axes = ("dp", "tensor") if wide else ("tensor",)
+    middle = lax.ppermute(backward(cotangent, saved)[0], "section", sections)
+    grad_entry, grad_y, branch = backward(jnp.where(section == 1, cotangent, middle), saved)
+
+    wide = groups in (2, 4)
+    count = groups if wide else 1
+
+    def gather(pair):
+        pair = jnp.stack(pair)
+        mine = lax.all_gather(pair, "dp") if wide else pair[None]
+        return mine, swap(mine, beside)
+
     seg_line = jnp.where(b == 0, seg_own[:part], seg_own[part:]).astype(bf16)
     seg_line = jnp.pad(seg_line[None], ((0, EXTRA_ROWS - 1), (0, width - part)))
-    entry_all = lax.all_gather(jnp.concatenate([entry, seg_line]), axes)
-    first_all = lax.all_gather(first_low, axes)
-    grad_y_all = lax.all_gather(grad_y, axes)
-    grad_branch_all = lax.all_gather(grad_branch, axes)
-    count = entry_all.shape[0] // 2
-
-    seg_all = entry_all[:, part, :part].astype(f32).reshape(count, length)
-    args = (entry_all, w_own, b_own, seg_all[:, None, :], seg_all[:, :, None])
+    entry_long = jnp.concatenate([entry, seg_line])
+    entries = [
+        item.reshape(2 * count, part + EXTRA_ROWS, width)
+        for item in gather((entry_long, swap(entry_long, across)))
+    ]
+    firsts = [item.reshape(-1, width) for item in gather(first)]
+    grads_y = [item.reshape(-1, width) for item in gather(grad_y)]
+
+    seg_all = jnp.concatenate([item[:, part, :part] for item in entries], 1).astype(f32)
+    args = (*entries, w_own, b_own, seg_all[:, None, :], seg_all[:, :, None])
     outs = [
-        shape((count, 3, length, local), bf16),
-        shape((count, heads, length, length), bf16),
-        shape((count, length, local), bf16),
+        shape((2 * count, 3, length, local), bf16),
+        shape((2 * count, heads, length, length), bf16),
+        shape((2 * count, length, local), bf16),
     ]
-    qkv_all, kept_all, mixed_all = run(
+    attended = run(
         attend_all_kernel,
         outs,
         args,
-        count * (weights_macs + 2 * scores_macs),
+        2 * count * (weights_macs + 2 * scores_macs),
         "attend_all",
-        grid=(count,),
-        in_specs=[leading(args[0], 2), whole(w_own), whole(b_own), leading(args[3], 1), leading(args[4], 1)],
+        grid=(2 * count,),
+        in_specs=[leading(args[0], 1)] * 2
+        + [whole(w_own), whole(b_own), leading(args[4], 1), leading(args[5], 1)],
         out_specs=[leading(item, 1) for item in outs],
     )
 
-    args = (
-        first_all.reshape(-1, width),
-        grad_y_all.reshape(-1, width),
-        up,
-        up_bias,
-        down,
-    )
+    block = 2 * part
+    tall = firsts[0].shape[0]
+    units = shape((tall, hidden_local), bf16)
+    acts = [
+        run(
+            feed_all_kernel,
+            [units, units],
+            (item, up, up_bias),
+            tall * width * hidden_local * 2,
+            "feed_all",
+            grid=(tall // block,),
+            in_specs=[leading(item, block), whole(up), whole(up_bias)],
+            out_specs=[leading(units, block)] * 2,
+        )
+        for item in firsts
+    ]
+    args = (firsts[0], grads_y[0], *acts[0], firsts[1], grads_y[1], *acts[1], down)
     outs = [
         shape((width, hidden_local), f32),
         shape((1, hidden_local), f32),
         shape((hidden_local, width), f32),
         shape((1, width), f32),
     ]
-    block = 2 * length
     g_up, g_up_b, g_down, g_down_b = run(
         feed_grads_kernel,
         outs,
         args,
-        count * feed_macs * 2,
+        2 * tall * width * hidden_local * 6,
         "feed_grads",
-        grid=(args[0].shape[0] // block,),
-        in_specs=[leading(args[0], block), leading(args[1], block), whole(up), whole(up_bias), whole(down)],
+        mib=28,
+        grid=(tall // block,),
+        in_specs=[leading(item, block) for item in args[:8]] + [whole(down)],
         out_specs=[whole(item) for item in outs],
     )
 
-    args = (entry_all, grad_branch_all, o_own, qkv_all, kept_all, mixed_all)
     outs = [
         shape((3, width, local), f32),
         shape((2, local), f32),
         shape((local, width), f32),
         shape((1, width), f32),
+        shape((4, width), f32),
     ]
-    g_w, g_b, g_out, g_out_b = run(
-        attend_grads_kernel,
-        outs,
-        args,
-        count * (weights_macs + 5 * scores_macs),
-        "attend_grads",
-        grid=(count,),
-        in_specs=[leading(args[0], 2), leading(args[1], 2), whole(o_own)]
-        + [leading(item, 1) for item in args[3:]],
-        out_specs=[whole(item) for item in outs],
-    )
-    small = jnp.sum(grad_branch_all[:, part : part + 8].astype(f32), 0)
-    small = small[:4] + small[4:]
+    sums = []
+    for step in range(count):
+        if step == 0:
+            piece = branch
+        else:
+            piece = lax.ppermute(branch, "dp", [(i, i ^ step) for i in range(groups)])
+        far = swap(piece, across)
+        args = (*entries, piece, swap(piece, beside), far, swap(far, beside), o_own, *attended, *sums)
+        args = ((lax.axis_index("dp") ^ step if wide else jnp.int32(0)).reshape(1), *args)
+
+        def picked(item):
+            rest = len(item.shape) - 1
+            return pl.BlockSpec((2,) + item.shape[1:], lambda i, group: (group[0],) + (0,) * rest)
+
+        def fixed(item):
+            rest = len(item.shape)
+            return pl.BlockSpec(item.shape, lambda i, group: (0,) * rest)
+
+        specs = [picked(item) for item in args[1:3]] + [fixed(item) for item in args[3:8]]
+        specs += [picked(item) for item in args[8:11]] + [fixed(item) for item in args[11:]]
+        sums = run(
+            attend_grads_kernel,
+            outs,
+            args,
+            2 * (weights_macs + 5 * scores_macs),
+            "attend_grads",
+            grid_spec=pltpu.PrefetchScalarGridSpec(
+                num_scalar_prefetch=1,
+                grid=(1,),
+                in_specs=specs,
+                out_specs=[fixed(item) for item in outs],
+            ),
+            input_output_aliases={11 + i: i for i in range(len(sums))},
+        )
+    g_w, g_b, g_out, g_out_b, small = sums
     totals = (g_w, g_b, g_out, g_up, g_up_b, g_down)
     if not wide:
         totals = [lax.psum(item.astype(bf16), "dp").astype(f32) for item in totals]

time: 312 us -> 332 us (1.064); the launches traced: 310 us -> 326 us
  waiting for transfers between devices: 139 us -> 116 us
  Pallas kernels: 67 us -> 88.5 us
  starting transfers between devices: 32.8 us -> 47.7 us
    all_gather x4 -> x3, waiting for transfers between devices: 30.2 us -> 0.62 us  [gather(): mine = lax.all_gather(pair, 'dp') if wide else pair[None]]
    pallas_call x25 -> x30, Pallas kernels: 67 us -> 88.5 us  [run(): pl.pallas_call(kernel, out_shape=outs, name=name, compiler_params=pltpu.C...]
    ppermute x39 -> x55, starting transfers between devices: 27 us -> 34.8 us  [swap(): return lax.ppermute(value, 'tensor', pairs)]
    ppermute x2 -> x5, starting transfers between devices: 5.65 us -> 12.4 us  [the longest x3 8.31 us: shards(): piece = lax.ppermute(branch, 'dp', [(i, i ^ step) for i in range(groups)])]
    ppermute x39 -> x55, waiting for transfers between devices: 97.3 us -> 102 us  [swap(): return lax.ppermute(value, 'tensor', pairs)]
    ppermute x2 -> x5, waiting for transfers between devices: 11.4 us -> 13.6 us  [the longest x1 5.66 us: shards(): middle = lax.ppermute(backward(cotangent, saved)[0], 'section', sections)]
    unnamed x114 -> x130, local copies, waits for them, and re-layouts: 42.4 us -> 41.7 us
  transfers between devices with their start and end apart: 45 -> 63, of which waited for: 30 -> 30; matrix products, arithmetic and copies ran while one was open for 4% -> 5% of each run, Pallas kernels for 14% -> 22%
where the time goes in v2:
time: 332 us; the launch traced here: 326 us
  waiting for transfers between devices  116 us (35%)
  Pallas kernels  88.5 us (27%)
  starting transfers between devices  47.7 us (14%)
  local copies, waits for them, and re-layouts  45.4 us (14%)
  between operations  14.7 us (4%)
  other arithmetic  13.7 us (4%)
    ppermute x55, waiting for transfers between devices, swap(): return lax.ppermute(value, 'tensor', pairs)  102 us
    pallas_call x30, Pallas kernels, run(): pl.pallas_call(kernel, out_shape=outs, name=name, compiler_params=pltpu.C...  88.5 us
    unnamed x130, local copies, waits for them, and re-layouts  41.7 us
    ppermute x55, starting transfers between devices, swap(): return lax.ppermute(value, 'tensor', pairs)  34.8 us
    ppermute x3, starting transfers between devices, shards(): piece = lax.ppermute(branch, 'dp', [(i, i ^ step) for i in range(groups)])  8.31 us
  transfers between devices with their start and end apart: 63, of which 30 were waited for; matrix products, arithmetic and copies ran while one was open for 5% of the time, Pallas kernels for 22%

profile of v2, /device:TPU:0, one launch (start us, length us, event | category | flops | bytes accessed | tf_op | source)
XLA Modules:
  0.0 326.2 jit_solution(3264610537473525074)
XLA Ops:
  8.3 3.0 collective-permute-start.1
  20.1 14.2 %collective-permute-done.3 = bf16[3,768,192]{1,2,0:T(8,128)(2,1)} collective-permute-done((bf16[3,768,192]{1,2,0:T(8,128)(2,1)}, bf16[3,768,192]{1,2,0:T(8,128)(2,1)}, u32[]{:S(2)}, u32[]{:S(2)}) %collective-permute-start.3) | collective-permute-done | bytes 884768 | tf_op jit(solution)/shard_map/ppermute | solution.py:298
  35.9 4.7 %collective-permute-done.5.o_far = bf16[192,768]{1,0:T(8,128)(2,1)S(1)} collective-permute-done((bf16[192,768]{1,0:T(8,128)(2,1)}, bf16[192,768]{1,0:T(8,128)(2,1)S(1)}, u32[]{:S(2)}, u32[]{:S(2)}) %collective-permute-start.5) | collective-permute-done | bytes 294944 | tf_op jit(solution)/shard_map/ppermute | solution.py:298
  40.6 3.1 attend.2
  47.9 5.4 %collective-permute-done.7.two = bf16[128,768]{1,0:T(8,128)(2,1)S(1)} collective-permute-done((bf16[128,768]{1,0:T(8,128)(2,1)S(1)}, bf16[128,768]{1,0:T(8,128)(2,1)S(1)}, u32[]{:S(2)}, u32[]{:S(2)}) %collective-permute-start.7) | collective-permute-done | bytes 196640 | tf_op jit(solution)/shard_map/ppermute | solution.py:298
  61.1 5.6 %collective-permute-done.11.arrived = bf16[128,768]{1,0:T(8,128)(2,1)S(1)} collective-permute-done((bf16[128,768]{1,0:T(8,128)(2,1)}, bf16[128,768]{1,0:T(8,128)(2,1)S(1)}, u32[]{:S(2)}, u32[]{:S(2)}) %collective-permute-start.11) | collective-permute-done | bytes 196640 | tf_op jit(solution)/shard_map/ppermute | solution.py:298
  71.4 4.4 %collective-permute-done.12 = bf16[128,768]{1,0:T(8,128)(2,1)S(1)} collective-permute-done((bf16[128,768]{1,0:T(8,128)(2,1)S(1)}, bf16[128,768]{1,0:T(8,128)(2,1)S(1)}, u32[]{:S(2)}, u32[]{:S(2)}) %collective-permute-start.12) | collective-permute-done | bytes 196640 | tf_op jit(solution)/shard_map/ppermute | solution.py:397
  76.8 5.2 %collective-permute-done.41 = bf16[144,768]{1,0:T(8,128)(2,1)S(1)} collective-permute-done((bf16[144,768]{1,0:T(8,128)(2,1)S(1)}, bf16[144,768]{1,0:T(8,128)(2,1)S(1)}, u32[]{:S(2)}, u32[]{:S(2)}) %collective-permute-start.41) | collective-permute-done | bytes 221216 | tf_op jit(solution)/shard_map/ppermute | solution.py:298
  84.4 3.1 attend.3
  93.2 6.2 %collective-permute-done.15.two = bf16[128,768]{1,0:T(8,128)(2,1)S(1)} collective-permute-done((bf16[128,768]{1,0:T(8,128)(2,1)S(1)}, bf16[128,768]{1,0:T(8,128)(2,1)S(1)}, u32[]{:S(2)}, u32[]{:S(2)}) %collective-permute-start.15) | collective-permute-done | bytes 196640 | tf_op jit(solution)/shard_map/ppermute | solution.py:298
  110.6 3.9 %collective-permute-done.19.arrived = bf16[128,768]{1,0:T(8,128)(2,1)S(1)} collective-permute-done((bf16[128,768]{1,0:T(8,128)(2,1)S(1)}, bf16[128,768]{1,0:T(8,128)(2,1)S(1)}, u32[]{:S(2)}, u32[]{:S(2)}) %collective-permute-start.19) | collective-permute-done | bytes 196640 | tf_op jit(solution)/shard_map/ppermute | solution.py:298
  120.4 5.8 %collective-permute-done.24.two = bf16[128,768]{1,0:T(8,128)(2,1)S(1)} collective-permute-done((bf16[128,768]{1,0:T(8,128)(2,1)S(1)}, bf16[128,768]{1,0:T(8,128)(2,1)S(1)}, u32[]{:S(2)}, u32[]{:S(2)}) %collective-permute-start.24) | collective-permute-done | bytes 196640 | tf_op jit(solution)/shard_map/ppermute | solution.py:298
  134.0 6.4 %collective-permute-done.28.arrived = bf16[128,768]{1,0:T(8,128)(2,1)S(1)} collective-permute-done((bf16[128,768]{1,0:T(8,128)(2,1)S(1)}, bf16[128,768]{1,0:T(8,128)(2,1)S(1)}, u32[]{:S(2)}, u32[]{:S(2)}) %collective-permute-start.28) | collective-permute-done | bytes 196640 | tf_op jit(solution)/shard_map/ppermute | solution.py:298
  142.4 3.3 %attend_back.2 = (f32[128,768]{1,0:T(8,128)S(1)}, bf16[128,768]{1,0:T(8,128)(2,1)S(1)}) custom-call(bf16[128,768]{1,0:T(8,128)(2,1)S(1)} %slice.124.own, bf16[128,768]{1,0:T(8,128)(2,1)S(1)} %collective-permute-done.29.other, bf16[3,768,192]{2,1,0:T(8,128)(2,1)S(1)} %bitcast.75, bf16[3,768,192]{2,1,0:T(8,128)(2,1)S(1)} %copy.81.w_far, ...), custom_call_target="tpu_custom_call" | custom-call | flops 855638016 | bytes 4718592 | tf_op jit(solution)/shard_map/attend_back/pallas_call | solution.py:40
  149.5 5.7 %collective-permute-done.31 = bf16[128,768]{1,0:T(8,128)(2,1)} collective-permute-done((bf16[128,768]{1,0:T(8,128)(2,1)}, bf16[128,768]{1,0:T(8,128)(2,1)}, u32[]{:S(2)}, u32[]{:S(2)}) %collective-permute-start.31) | collective-permute-done | bytes 196640 | tf_op jit(solution)/shard_map/ppermute | solution.py:401
  157.8 5.6 %collective-permute-done.32.two = bf16[128,768]{1,0:T(8,128)(2,1)S(1)} collective-permute-done((bf16[128,768]{1,0:T(8,128)(2,1)S(1)}, bf16[128,768]{1,0:T(8,128)(2,1)S(1)}, u32[]{:S(2)}, u32[]{:S(2)}) %collective-permute-start.32) | collective-permute-done | bytes 196640 | tf_op jit(solution)/shard_map/ppermute | solution.py:298
  165.3 3.1 collective-permute-done.33.three
  177.2 6.7 %collective-permute-done.36.arrived = bf16[128,768]{1,0:T(8,128)(2,1)S(1)} collective-permute-done((bf16[128,768]{1,0:T(8,128)(2,1)S(1)}, bf16[128,768]{1,0:T(8,128)(2,1)S(1)}, u32[]{:S(2)}, u32[]{:S(2)}) %collective-permute-start.36) | collective-permute-done | bytes 196640 | tf_op jit(solution)/shard_map/ppermute | solution.py:298
  186.9 3.3 %attend_back.3 = (f32[128,768]{1,0:T(8,128)S(1)}, bf16[128,768]{1,0:T(8,128)(2,1)S(1)}) custom-call(bf16[128,768]{1,0:T(8,128)(2,1)S(1)} %slice.125.own, bf16[128,768]{1,0:T(8,128)(2,1)S(1)} %collective-permute-done.37.other, bf16[3,768,192]{2,1,0:T(8,128)(2,1)S(1)} %bitcast.76, bf16[3,768,192]{2,1,0:T(8,128)(2,1)S(1)} %copy.81.w_far, ...), custom_call_target="tpu_custom_call" | custom-call | flops 855638016 | bytes 4718592 | tf_op jit(solution)/shard_map/attend_back/pallas_call | solution.py:40
  195.7 3.7 %collective-permute-start.43 = (bf16[144,768]{1,0:T(8,128)(2,1)S(1)}, bf16[144,768]{1,0:T(8,128)(2,1)}, u32[]{:S(2)}, u32[]{:S(2)}) collective-permute-start(bf16[144,768]{1,0:T(8,128)(2,1)S(1)} %get-tuple-element.127.one), channel_id=1, source_target_pairs={{0,3},{1,2},{2,1},{3,0},{4,7},{5,6},{6,5},{7,4},{8,11},{9,10},{10,... | collective-permute-start | bytes 663560 | tf_op jit(solution)/shard_map/ppermute | solution.py:488
  202.6 3.6 %collective-permute-done.43.one = bf16[144,768]{1,0:T(8,128)(2,1)} collective-permute-done((bf16[144,768]{1,0:T(8,128)(2,1)S(1)}, bf16[144,768]{1,0:T(8,128)(2,1)}, u32[]{:S(2)}, u32[]{:S(2)}) %collective-permute-start.43) | collective-permute-done | bytes 221216 | tf_op jit(solution)/shard_map/ppermute | solution.py:488
  209.5 2.7 feed_all.2
  214.5 4.3 %collective-permute-start.47 = (bf16[144,768]{1,0:T(8,128)(2,1)S(1)}, bf16[144,768]{1,0:T(8,128)(2,1)}, u32[]{:S(2)}, u32[]{:S(2)}) collective-permute-start(bf16[144,768]{1,0:T(8,128)(2,1)S(1)} %get-tuple-element.127.one), channel_id=1, source_target_pairs={{0,2},{1,3},{2,0},{3,1},{4,6},{5,7},{6,4},{7,5},{8,10},{9,11},{10,... | collective-permute-start | bytes 663560 | tf_op jit(solution)/shard_map/ppermute | solution.py:488
  222.8 4.0 %feed_all.3 = (bf16[1024,768]{1,0:T(8,128)(2,1)S(1)}, bf16[1024,768]{1,0:T(8,128)(2,1)S(1)}) custom-call(bf16[1024,768]{1,0:T(8,128)(2,1)} %bitcast.45.rows.refs_4_, bf16[768,768]{1,0:T(8,128)(2,1)S(1)} %bitcast.102, f32[1,768]{1,0:T(1,128)S(1)} %copy-done.32), custom_call_target="tpu_custom_call" | custom-call | flops 1207959552 | bytes 5901312 | tf_op jit(solution)/shard_map/feed_all/pallas_call | solution.py:40
  234.1 9.4 %collective-permute-done.45.three = bf16[144,768]{1,0:T(8,128)(2,1)} collective-permute-done((bf16[144,768]{1,0:T(8,128)(2,1)}, bf16[144,768]{1,0:T(8,128)(2,1)}, u32[]{:S(2)}, u32[]{:S(2)}) %collective-permute-start.45) | collective-permute-done | bytes 221216 | tf_op jit(solution)/shard_map/ppermute | solution.py:298
  243.5 4.2 %collective-permute-done.49.three = bf16[144,768]{1,0:T(8,128)(2,1)} collective-permute-done((bf16[144,768]{1,0:T(8,128)(2,1)}, bf16[144,768]{1,0:T(8,128)(2,1)}, u32[]{:S(2)}, u32[]{:S(2)}) %collective-permute-start.49) | collective-permute-done | bytes 221216 | tf_op jit(solution)/shard_map/ppermute | solution.py:298
  249.7 21.3 %attend_all.1 = (bf16[8,3,256,192]{3,2,1,0:T(8,128)(2,1)S(1)}, bf16[8,3,256,256]{3,2,1,0:T(8,128)(2,1)S(1)}, bf16[8,256,192]{2,1,0:T(8,128)(2,1)S(1)}) custom-call(bf16[8,144,768]{2,1,0:T(8,128)(2,1)S(1)} %copy-done, bf16[8,144,768]{2,1,0:T(8,128)(2,1)} %bitcast.28.other, bf16[3,768,192]{2,1,0:T(8,128)(2,1)S(1)} %bitcast.77, f32[2,192]{1,0:T(2,128)S(1)} %copy-done.30, ...), custom_call_target="tpu_custom_call" | custom-call | flops 2818572288 | bytes 10733056 | tf_op jit(solution)/shard_map/attend_all/pallas_call | solution.py:40
  271.6 5.3 %attend_grads.4 = (f32[3,768,192]{2,1,0:T(8,128)S(1)}, f32[2,192]{1,0:T(2,128)}, f32[192,768]{1,0:T(8,128)}, f32[1,768]{1,0:T(1,128)}, f32[4,768]{1,0:T(4,128)S(1)}) custom-call(s32[1]{0:T(128)} %bitcast.31.group, bf16[8,144,768]{2,1,0:T(8,128)(2,1)S(1)} %copy-done, bf16[8,144,768]{2,1,0:T(8,128)(2,1)} %bitcast.28.other, ...), custom_call_target="tpu_custom_call" | custom-call | flops 855638016 | bytes 13386244 | tf_op jit(solution)/shard_map/attend_grads/pallas_call | solution.py:40
  277.0 6.2 %attend_grads.5 = (f32[3,768,192]{2,1,0:T(8,128)S(1)}, f32[2,192]{1,0:T(2,128)}, f32[192,768]{1,0:T(8,128)}, f32[1,768]{1,0:T(1,128)}, f32[4,768]{1,0:T(4,128)S(1)}) custom-call(s32[1]{0:T(128)} %bitcast.30.group, bf16[8,144,768]{2,1,0:T(8,128)(2,1)S(1)} %copy-done, ...), custom_call_target="tpu_custom_call", output_to_operand_aliasing={{0}: (11, {}), {1}: (12, {}), {2}: (13, {}), {3}: (14, {}),... | custom-call | flops 855638016 | bytes 15762436 | tf_op jit(solution)/shard_map/attend_grads/pallas_call | solution.py:40
  283.2 6.2 %attend_grads.6 = (f32[3,768,192]{2,1,0:T(8,128)S(1)}, f32[2,192]{1,0:T(2,128)}, f32[192,768]{1,0:T(8,128)}, f32[1,768]{1,0:T(1,128)}, f32[4,768]{1,0:T(4,128)S(1)}) custom-call(s32[1]{0:T(128)} %bitcast.29.group, bf16[8,144,768]{2,1,0:T(8,128)(2,1)S(1)} %copy-done, ...), custom_call_target="tpu_custom_call", output_to_operand_aliasing={{0}: (11, {}), {1}: (12, {}), {2}: (13, {}), {3}: (14, {}),... | custom-call | flops 855638016 | bytes 15762436 | tf_op jit(solution)/shard_map/attend_grads/pallas_call | solution.py:40
  289.5 6.4 %attend_grads.7 = (f32[3,768,192]{2,1,0:T(8,128)S(1)}, f32[2,192]{1,0:T(2,128)}, f32[192,768]{1,0:T(8,128)}, f32[1,768]{1,0:T(1,128)}, f32[4,768]{1,0:T(4,128)S(1)}) custom-call(s32[1]{0:T(128)} %bitcast.24.group, bf16[8,144,768]{2,1,0:T(8,128)(2,1)S(1)} %copy-done, ...), custom_call_target="tpu_custom_call", output_to_operand_aliasing={{0}: (11, {}), {1}: (12, {}), {2}: (13, {}), {3}: (14, {}),... | custom-call | flops 855638016 | bytes 15762436 | tf_op jit(solution)/shard_map/attend_grads/pallas_call | solution.py:40
  308.0 11.4 %feed_grads.1 = (f32[768,768]{1,0:T(8,128)}, f32[1,768]{1,0:T(1,128)}, f32[768,768]{1,0:T(8,128)}, f32[1,768]{1,0:T(1,128)}) custom-call(bf16[1024,768]{1,0:T(8,128)(2,1)S(1)} %bitcast.94, bf16[1024,768]{1,0:T(8,128)(2,1)S(1)} %bitcast.96, bf16[1024,768]{1,0:T(8,128)(2,1)S(1)} %copy-done.50, bf16[1024,768]{1,0:T(8,128)(2,1)S(1)} %copy-done.52, ...), custom_call_target="tpu_custom_call" | custom-call | flops 7247757312 | bytes 18487296 | tf_op jit(solution)/shard_map/feed_grads/pallas_call | solution.py:40
  (298 shorter events, 124.3 us)
Async XLA Ops:
  7.2 157.0 %all-gather.7.cloned.1.call-start = ((), (), s32[]{:S(2)}) async-start(), calls=%async_computation | async-start | bytes 2211840 | tf_op jit(solution)/shard_map/all_gather | solution.py:409
  8.3 10.2 %collective-permute-start.1 = (bf16[64,768]{1,0:T(8,128)(2,1)S(1)}, bf16[64,768]{1,0:T(8,128)(2,1)S(1)}, u32[]{:S(2)}, u32[]{:S(2)}) collective-permute-start(bf16[64,768]{1,0:T(8,128)(2,1)S(1)} %get-tuple-element.231), channel_id=1, source_target_pairs={{4,0},{12,4},{0,8},{8,12},{5,1},{13,5},{1,9},{9,13},{6,2},{14,6},{... | collective-permute-start | bytes 294920 | tf_op jit(solution)/shard_map/ppermute | solution.py:298
  11.2 7.3 %collective-permute-start = (bf16[64,768]{1,0:T(8,128)(2,1)S(1)}, bf16[64,768]{1,0:T(8,128)(2,1)S(1)}, u32[]{:S(2)}, u32[]{:S(2)}) collective-permute-start(bf16[64,768]{1,0:T(8,128)(2,1)S(1)} %get-tuple-element.230), channel_id=1, source_target_pairs={{0,0},{4,8},{8,4},{12,12},{1,1},{5,9},{9,5},{13,13},{2,2},{6,10},{... | collective-permute-start | bytes 294920 | tf_op jit(solution)/shard_map/ppermute | solution.py:298
  11.9 22.4 %collective-permute-start.3 = (bf16[3,768,192]{1,2,0:T(8,128)(2,1)}, bf16[3,768,192]{1,2,0:T(8,128)(2,1)}, u32[]{:S(2)}, u32[]{:S(2)}) collective-permute-start(bf16[3,768,192]{1,2,0:T(8,128)(2,1)} %bitcast.109), channel_id=1, source_target_pairs={{0,8},{4,12},{8,0},{12,4},{1,9},{5,13},{9,1},{13,5},{2,10},{6,14},... | collective-permute-start | bytes 2654216 | tf_op jit(solution)/shard_map/ppermute | solution.py:298
  13.9 21.9 %collective-permute-start.4 = (f32[2,192]{1,0:T(2,128)S(1)}, f32[2,192]{1,0:T(2,128)S(1)}, u32[]{:S(2)}, u32[]{:S(2)}) collective-permute-start(f32[2,192]{1,0:T(2,128)S(1)} %bitcast_convert_fusion.b_own.bias), channel_id=1, source_target_pairs={{0,8},{4,12},{8,0},{12,4},{1,9},{5,13},{9,1},{13,5},{2,10},{6,14},... | collective-permute-start | bytes 4616 | tf_op jit(solution)/shard_map/ppermute | solution.py:298
  14.7 25.9 %collective-permute-start.5 = (bf16[192,768]{1,0:T(8,128)(2,1)}, bf16[192,768]{1,0:T(8,128)(2,1)S(1)}, u32[]{:S(2)}, u32[]{:S(2)}) collective-permute-start(bf16[192,768]{1,0:T(8,128)(2,1)} %bitcast.79), channel_id=1, source_target_pairs={{0,8},{4,12},{8,0},{12,4},{1,9},{5,13},{9,1},{13,5},{2,10},{6,14},... | collective-permute-start | bytes 884744 | tf_op jit(solution)/shard_map/ppermute | solution.py:298
  18.6 17.3 %collective-permute-start.2 = (bf16[128,768]{1,0:T(8,128)(2,1)S(1)}, bf16[128,768]{1,0:T(8,128)(2,1)S(1)}, u32[]{:S(2)}, u32[]{:S(2)}) collective-permute-start(bf16[128,768]{1,0:T(8,128)(2,1)S(1)} %maximum_select_fusion.own.residual), channel_id=1, source_target_pairs={{0,4},{4,0},{8,12},{12,8},{1,5},{5,1},{9,13},{13,9},{2,6},{6,2},{1... | collective-permute-start | bytes 589832 | tf_op jit(solution)/shard_map/ppermute | solution.py:298
  82.8 82.1 %all-gather.9.cloned.1.call-start = ((), (), s32[]{:S(2)}) async-start(), calls=%async_computation.1 | async-start | bytes 1966080 | tf_op jit(solution)/shard_map/all_gather | solution.py:409
  109.2 92.8 %all-gather.11.cloned.1.call-start = ((), (), s32[]{:S(2)}) async-start(), calls=%async_computation.2 | async-start | bytes 1966080 | tf_op jit(solution)/shard_map/all_gather | solution.py:409
  164.2 57.4 %collective-permute-start.42 = (bf16[4,2,144,768]{3,2,1,0:T(8,128)(2,1)}, bf16[4,2,144,768]{3,2,1,0:T(8,128)(2,1)}, u32[]{:S(2)}, u32[]{:S(2)}) collective-permute-start(bf16[4,2,144,768]{3,2,1,0:T(8,128)(2,1)} %bitcast.78), channel_id=1, source_target_pairs={{0,4},{4,0},{8,12},{12,8},{1,5},{5,1},{9,13},{13,9},{2,6},{6,2},{1... | collective-permute-start | bytes 5308424 | tf_op jit(solution)/shard_map/ppermute | solution.py:298
  164.9 54.2 %collective-permute-start.58 = (bf16[4,2,128,768]{3,2,1,0:T(8,128)(2,1)}, bf16[4,2,128,768]{3,2,1,0:T(8,128)(2,1)}, u32[]{:S(2)}, u32[]{:S(2)}) collective-permute-start(bf16[4,2,128,768]{3,2,1,0:T(8,128)(2,1)} %bitcast.92), channel_id=1, source_target_pairs={{0,4},{4,0},{8,12},{12,8},{1,5},{5,1},{9,13},{13,9},{2,6},{6,2},{1... | collective-permute-start | bytes 4718600 | tf_op jit(solution)/shard_map/ppermute | solution.py:298
  185.1 8.1 %collective-permute-start.21 = (bf16[64,768]{1,0:T(8,128)(2,1)}, bf16[64,768]{1,0:T(8,128)(2,1)}, u32[]{:S(2)}, u32[]{:S(2)}) collective-permute-start(bf16[64,768]{1,0:T(8,128)(2,1)} %get-tuple-element.229), channel_id=1, source_target_pairs={{0,4},{4,12},{8,0},{12,8},{1,5},{5,13},{9,1},{13,9},{2,6},{6,14},{... | collective-permute-start | bytes 294920 | tf_op jit(solution)/shard_map/ppermute | solution.py:298
  185.6 7.6 %collective-permute-start.20 = (bf16[64,768]{1,0:T(8,128)(2,1)S(1)}, bf16[64,768]{1,0:T(8,128)(2,1)}, u32[]{:S(2)}, u32[]{:S(2)}) collective-permute-start(bf16[64,768]{1,0:T(8,128)(2,1)S(1)} %get-tuple-element.228), channel_id=1, source_target_pairs={{0,0},{4,8},{8,4},{12,12},{1,1},{5,9},{9,5},{13,13},{2,2},{6,10},{... | collective-permute-start | bytes 294920 | tf_op jit(solution)/shard_map/ppermute | solution.py:298
  190.9 8.5 %collective-permute-start.38 = (bf16[128,768]{1,0:T(8,128)(2,1)S(1)}, bf16[128,768]{1,0:T(8,128)(2,1)S(1)}, u32[]{:S(2)}, u32[]{:S(2)}) collective-permute-start(bf16[128,768]{1,0:T(8,128)(2,1)S(1)} %get-tuple-element.128), channel_id=1, source_target_pairs={{0,4},{4,0},{8,12},{12,8},{1,5},{5,1},{9,13},{13,9},{2,6},{6,2},{1... | collective-permute-start | bytes 589832 | tf_op jit(solution)/shard_map/ppermute | solution.py:298
  195.7 10.5 %collective-permute-start.43 = (bf16[144,768]{1,0:T(8,128)(2,1)S(1)}, bf16[144,768]{1,0:T(8,128)(2,1)}, u32[]{:S(2)}, u32[]{:S(2)}) collective-permute-start(bf16[144,768]{1,0:T(8,128)(2,1)S(1)} %get-tuple-element.127.one), channel_id=1, source_target_pairs={{0,3},{1,2},{2,1},{3,0},{4,7},{5,6},{6,5},{7,4},{8,11},{9,10},{10,... | collective-permute-start | bytes 663560 | tf_op jit(solution)/shard_map/ppermute | solution.py:488
  202.1 96.3 %collective-permute-start.59 = (bf16[4,2,128,768]{3,2,1,0:T(8,128)(2,1)}, bf16[4,2,128,768]{3,2,1,0:T(8,128)(2,1)}, u32[]{:S(2)}, u32[]{:S(2)}) collective-permute-start(bf16[4,2,128,768]{3,2,1,0:T(8,128)(2,1)} %bitcast.95), channel_id=1, source_target_pairs={{0,4},{4,0},{8,12},{12,8},{1,5},{5,1},{9,13},{13,9},{2,6},{6,2},{1... | collective-permute-start | bytes 4718600 | tf_op jit(solution)/shard_map/ppermute | solution.py:298
  202.1 12.4 %collective-permute-start.40 = (bf16[64,768]{1,0:T(8,128)(2,1)S(1)}, bf16[64,768]{1,0:T(8,128)(2,1)S(1)}, u32[]{:S(2)}, u32[]{:S(2)}) collective-permute-start(bf16[64,768]{1,0:T(8,128)(2,1)S(1)} %get-tuple-element.225), channel_id=1, source_target_pairs={{0,4},{4,12},{8,0},{12,8},{1,5},{5,13},{9,1},{13,9},{2,6},{6,14},{... | collective-permute-start | bytes 294920 | tf_op jit(solution)/shard_map/ppermute | solution.py:298
  206.2 12.6 %collective-permute-start.39 = (bf16[64,768]{1,0:T(8,128)(2,1)S(1)}, bf16[64,768]{1,0:T(8,128)(2,1)S(1)}, u32[]{:S(2)}, u32[]{:S(2)}) collective-permute-start(bf16[64,768]{1,0:T(8,128)(2,1)S(1)} %get-tuple-element.224), channel_id=1, source_target_pairs={{0,0},{4,8},{8,4},{12,12},{1,1},{5,9},{9,5},{13,13},{2,2},{6,10},{... | collective-permute-start | bytes 294920 | tf_op jit(solution)/shard_map/ppermute | solution.py:298
  214.5 15.7 %collective-permute-start.47 = (bf16[144,768]{1,0:T(8,128)(2,1)S(1)}, bf16[144,768]{1,0:T(8,128)(2,1)}, u32[]{:S(2)}, u32[]{:S(2)}) collective-permute-start(bf16[144,768]{1,0:T(8,128)(2,1)S(1)} %get-tuple-element.127.one), channel_id=1, source_target_pairs={{0,2},{1,3},{2,0},{3,1},{4,6},{5,7},{6,4},{7,5},{8,10},{9,11},{10,... | collective-permute-start | bytes 663560 | tf_op jit(solution)/shard_map/ppermute | solution.py:488
  218.8 11.1 %collective-permute-start.51 = (bf16[144,768]{1,0:T(8,128)(2,1)S(1)}, bf16[144,768]{1,0:T(8,128)(2,1)}, u32[]{:S(2)}, u32[]{:S(2)}) collective-permute-start(bf16[144,768]{1,0:T(8,128)(2,1)S(1)} %get-tuple-element.127.one), channel_id=1, source_target_pairs={{0,1},{1,0},{2,3},{3,2},{4,5},{5,4},{6,7},{7,6},{8,9},{9,8},{10,11... | collective-permute-start | bytes 663560 | tf_op jit(solution)/shard_map/ppermute | solution.py:488
  219.1 12.6 %collective-permute-start.55 = (bf16[144,768]{1,0:T(8,128)(2,1)S(1)}, bf16[144,768]{1,0:T(8,128)(2,1)S(1)}, u32[]{:S(2)}, u32[]{:S(2)}) collective-permute-start(bf16[144,768]{1,0:T(8,128)(2,1)S(1)} %get-tuple-element.127.one), channel_id=1, source_target_pairs={{0,4},{4,0},{8,12},{12,8},{1,5},{5,1},{9,13},{13,9},{2,6},{6,2},{1... | collective-permute-start | bytes 663560 | tf_op jit(solution)/shard_map/ppermute | solution.py:298
  221.6 10.6 %collective-permute-start.56 = (bf16[144,768]{1,0:T(8,128)(2,1)S(1)}, bf16[144,768]{1,0:T(8,128)(2,1)S(1)}, u32[]{:S(2)}, u32[]{:S(2)}) collective-permute-start(bf16[144,768]{1,0:T(8,128)(2,1)S(1)} %get-tuple-element.127.one), channel_id=1, source_target_pairs={{0,8},{4,12},{8,0},{12,4},{1,9},{5,13},{9,1},{13,5},{2,10},{6,14},... | collective-permute-start | bytes 663560 | tf_op jit(solution)/shard_map/ppermute | solution.py:298
  229.9 17.7 %collective-permute-start.52 = (bf16[144,768]{1,0:T(8,128)(2,1)}, bf16[144,768]{1,0:T(8,128)(2,1)}, u32[]{:S(2)}, u32[]{:S(2)}) collective-permute-start(bf16[144,768]{1,0:T(8,128)(2,1)} %collective-permute-done.51.one), channel_id=1, source_target_pairs={{0,4},{4,0},{8,12},{12,8},{1,5},{5,1},{9,13},{13,9},{2,6},{6,2},{1... | collective-permute-start | bytes 663560 | tf_op jit(solution)/shard_map/ppermute | solution.py:298
  230.1 18.0 %collective-permute-start.53 = (bf16[144,768]{1,0:T(8,128)(2,1)}, bf16[144,768]{1,0:T(8,128)(2,1)}, u32[]{:S(2)}, u32[]{:S(2)}) collective-permute-start(bf16[144,768]{1,0:T(8,128)(2,1)} %collective-permute-done.51.one), channel_id=1, source_target_pairs={{0,8},{4,12},{8,0},{12,4},{1,9},{5,13},{9,1},{13,5},{2,10},{6,14},... | collective-permute-start | bytes 663560 | tf_op jit(solution)/shard_map/ppermute | solution.py:298
  231.6 11.8 %collective-permute-start.45 = (bf16[144,768]{1,0:T(8,128)(2,1)}, bf16[144,768]{1,0:T(8,128)(2,1)}, u32[]{:S(2)}, u32[]{:S(2)}) collective-permute-start(bf16[144,768]{1,0:T(8,128)(2,1)} %collective-permute-done.43.one), channel_id=1, source_target_pairs={{0,8},{4,12},{8,0},{12,4},{1,9},{5,13},{9,1},{13,5},{2,10},{6,14},... | collective-permute-start | bytes 663560 | tf_op jit(solution)/shard_map/ppermute | solution.py:298
  232.2 15.4 %collective-permute-start.49 = (bf16[144,768]{1,0:T(8,128)(2,1)}, bf16[144,768]{1,0:T(8,128)(2,1)}, u32[]{:S(2)}, u32[]{:S(2)}) collective-permute-start(bf16[144,768]{1,0:T(8,128)(2,1)} %collective-permute-done.47.one), channel_id=1, source_target_pairs={{0,8},{4,12},{8,0},{12,4},{1,9},{5,13},{9,1},{13,5},{2,10},{6,14},... | collective-permute-start | bytes 663560 | tf_op jit(solution)/shard_map/ppermute | solution.py:298
  243.4 39.8 %collective-permute-start.48 = (bf16[144,768]{1,0:T(8,128)(2,1)}, bf16[144,768]{1,0:T(8,128)(2,1)S(1)}, u32[]{:S(2)}, u32[]{:S(2)}) collective-permute-start(bf16[144,768]{1,0:T(8,128)(2,1)} %collective-permute-done.47.one), channel_id=1, source_target_pairs={{0,4},{4,0},{8,12},{12,8},{1,5},{5,1},{9,13},{13,9},{2,6},{6,2},{1... | collective-permute-start | bytes 663560 | tf_op jit(solution)/shard_map/ppermute | solution.py:298
  247.6 23.4 %collective-permute-start.57 = (bf16[144,768]{1,0:T(8,128)(2,1)S(1)}, bf16[144,768]{1,0:T(8,128)(2,1)S(1)}, u32[]{:S(2)}, u32[]{:S(2)}) collective-permute-start(bf16[144,768]{1,0:T(8,128)(2,1)S(1)} %collective-permute-done.56.three), channel_id=1, source_target_pairs={{0,4},{4,0},{8,12},{12,8},{1,5},{5,1},{9,13},{13,9},{2,6},{6,2},{1... | collective-permute-start | bytes 663560 | tf_op jit(solution)/shard_map/ppermute | solution.py:298
  247.6 35.6 %collective-permute-start.50 = (bf16[144,768]{1,0:T(8,128)(2,1)}, bf16[144,768]{1,0:T(8,128)(2,1)S(1)}, u32[]{:S(2)}, u32[]{:S(2)}) collective-permute-start(bf16[144,768]{1,0:T(8,128)(2,1)} %collective-permute-done.49.three), channel_id=1, source_target_pairs={{0,4},{4,0},{8,12},{12,8},{1,5},{5,1},{9,13},{13,9},{2,6},{6,2},{1... | collective-permute-start | bytes 663560 | tf_op jit(solution)/shard_map/ppermute | solution.py:298
  248.1 23.4 %collective-permute-start.54 = (bf16[144,768]{1,0:T(8,128)(2,1)}, bf16[144,768]{1,0:T(8,128)(2,1)S(1)}, u32[]{:S(2)}, u32[]{:S(2)}) collective-permute-start(bf16[144,768]{1,0:T(8,128)(2,1)} %collective-permute-done.53.three), channel_id=1, source_target_pairs={{0,4},{4,0},{8,12},{12,8},{1,5},{5,1},{9,13},{13,9},{2,6},{6,2},{1... | collective-permute-start | bytes 663560 | tf_op jit(solution)/shard_map/ppermute | solution.py:298
  271.1 18.4 %collective-permute-start.44 = (bf16[144,768]{1,0:T(8,128)(2,1)}, bf16[144,768]{1,0:T(8,128)(2,1)S(1)}, u32[]{:S(2)}, u32[]{:S(2)}) collective-permute-start(bf16[144,768]{1,0:T(8,128)(2,1)} %collective-permute-done.43.one), channel_id=1, source_target_pairs={{0,4},{4,0},{8,12},{12,8},{1,5},{5,1},{9,13},{13,9},{2,6},{6,2},{1... | collective-permute-start | bytes 663560 | tf_op jit(solution)/shard_map/ppermute | solution.py:298
  271.6 17.9 %collective-permute-start.46 = (bf16[144,768]{1,0:T(8,128)(2,1)}, bf16[144,768]{1,0:T(8,128)(2,1)S(1)}, u32[]{:S(2)}, u32[]{:S(2)}) collective-permute-start(bf16[144,768]{1,0:T(8,128)(2,1)} %collective-permute-done.45.three), channel_id=1, source_target_pairs={{0,4},{4,0},{8,12},{12,8},{1,5},{5,1},{9,13},{13,9},{2,6},{6,2},{1... | collective-permute-start | bytes 663560 | tf_op jit(solution)/shard_map/ppermute | solution.py:298
  (94 other events, 596.6 us)
Sparse Core Ops, SparseCore 0:
  82.9 41.0 all-gather.6
  125.6 35.9 all-gather.8
  164.3 37.7 all-gather.10

commit v3 on v1

v3 whole, which is shorter than its diff:
```python
import functools

import jax
import jax.numpy as jnp
from jax import lax
from jax.experimental import pallas as pl
from jax.experimental.pallas import tpu as pltpu
from jax.sharding import PartitionSpec as P

HEAD_DIM = 64
EPSILON = 1e-06
BIG_NEGATIVE = -1e30
MIB = 1024 * 1024
EXTRA_ROWS = 16
GAIN, SHIFT, OUT_BIAS, UP_BIAS, DOWN_BIAS, QV_OWN, QV_FAR, TABLE_ROWS = 0, 2, 4, 5, 6, 7, 9, 16
SQRT_HALF = 0.7071067811865476
INV_SQRT_TAU = 0.3989422804014327

f32 = jnp.float32
bf16 = jnp.bfloat16


def dot_nn(left, right):
    return lax.dot_general(left, right, (((1,), (0,)), ((), ())), preferred_element_type=f32)


def dot_nt(left, right):
    return lax.dot_general(left, right, (((1,), (1,)), ((), ())), preferred_element_type=f32)


def dot_tn(left, right):
    return lax.dot_general(left, right, (((0,), (0,)), ((), ())), preferred_element_type=f32)


def shape(dims, kind):
    return jax.ShapeDtypeStruct(dims, kind)


def run(kernel, outs, args, us, name, mib=16, after=(), grid=None, in_specs=None, out_specs=None,
        scalars=0, aliases=None):
    count = len(args)
    if in_specs is None:
        in_specs = [pl.BlockSpec(memory_space=pltpu.VMEM)] * count
    if out_specs is None:
        out_specs = [pl.BlockSpec(memory_space=pltpu.VMEM)] * len(outs)
    waits = [pl.BlockSpec(memory_space=pl.ANY)] * len(after)

    def body(*refs):
        kernel(*refs[:count], *refs[count + len(after) :])

    moved = sum(item.size * item.dtype.itemsize for item in (*args, *outs))
    return pl.pallas_call(
        body,
        out_shape=outs,
        grid_spec=pltpu.PrefetchScalarGridSpec(
            num_scalar_prefetch=scalars,
            grid=grid or (),
            in_specs=[*in_specs, *waits],
            out_specs=out_specs,
        ),
        name=name,
        input_output_aliases=aliases or {},
        compiler_params=pltpu.CompilerParams(vmem_limit_bytes=mib * MIB),
        cost_estimate=pl.CostEstimate(
            flops=int(us * 1.15e9), bytes_accessed=moved, transcendentals=0
        ),
    )(*args, *after)


def heads_forward(rows, w, table, line, same):
    local = w.shape[-1]
    query = dot_nn(rows, w[0]) + table[line : line + 1, :local]
    query = (query.astype(bf16) * HEAD_DIM**-0.5).astype(bf16)
    key = dot_nn(rows, w[1]).astype(bf16)
    value = (dot_nn(rows, w[2]) + table[line + 1 : line + 2, :local]).astype(bf16)
    probs, mixed = [], []
    for start in range(0, query.shape[1], HEAD_DIM):
        head = slice(start, start + HEAD_DIM)
        scores = jnp.where(same, dot_nt(query[:, head], key[:, head]), BIG_NEGATIVE)
        weights = jnp.exp(scores - jnp.max(scores, -1, keepdims=True))
        total = jnp.sum(weights, -1, keepdims=True)
        low = (weights * (1.0 / total)).astype(bf16)
        probs.append(low)
        mixed.append(dot_nn(low, value[:, head]).astype(bf16))
    return query, key, value, probs, jnp.concatenate(mixed, 1)


def heads_backward(query, key, value, probs, grad_mixed):
    parts = [], [], []
    for number, low in enumerate(probs):
        head = slice(number * HEAD_DIM, (number + 1) * HEAD_DIM)
        upstream = grad_mixed[:, head]
        wide = low.astype(f32)
        product = wide * dot_nt(upstream, value[:, head])
        scores = (product - wide * jnp.sum(product, -1, keepdims=True)).astype(bf16)
        parts[0].append((dot_nn(scores, key[:, head]) * HEAD_DIM**-0.5).astype(bf16))
        parts[1].append(dot_tn(scores, query[:, head]).astype(bf16))
        parts[2].append(dot_tn(low, upstream).astype(bf16))
    return [jnp.concatenate(part, 1) for part in parts]


def attend_kernel(
    own, other, w_own, w_far, o_own, o_far, table, seg_row, seg_col, *outs
):
    keep, send = outs[:2]
    rows = jnp.concatenate([own[...], other[...]], 0)
    same = seg_col[...] == seg_row[...]
    total = None
    for group, (w, out) in enumerate(((w_own, o_own), (w_far, o_far))):
        query, key, value, probs, mixed = heads_forward(rows, w, table, QV_OWN + 2 * group, same)
        if len(outs) > 2:
            qkv, kept = outs[2:]
            qkv[group, 0], qkv[group, 1], qkv[group, 2] = query, key, value
            for number, low in enumerate(probs):
                kept[group, number] = low
        term = dot_nn(mixed, out[...])
        total = term if total is None else total + term
    half = own.shape[0]
    keep[...] = own[...].astype(f32) + (total[:half] + table[OUT_BIAS : OUT_BIAS + 1])
    send[...] = total[half:].astype(bf16)


def attend_back_kernel(own, other, w_own, w_far, o_own, o_far, qkv, kept, residual, keep, send):
    half = own.shape[0] - EXTRA_ROWS
    rows = jnp.concatenate([own[:half], other[:half]], 0)
    total = None
    for group, (w, out) in enumerate(((w_own, o_own), (w_far, o_far))):
        grad_mixed = dot_nt(rows, out[...]).astype(bf16)
        probs = [kept[group, number] for number in range(kept.shape[1])]
        parts = heads_backward(qkv[group, 0], qkv[group, 1], qkv[group, 2], probs, grad_mixed)
        for number, part in enumerate(parts):
            term = dot_nt(part, w[number])
            total = term if total is None else total + term
    keep[...] = total[:half] + residual[...]
    send[...] = total[half:].astype(bf16)


def standard(values):
    centred = values - jnp.mean(values, -1, keepdims=True)
    spread = lax.rsqrt(jnp.mean(centred * centred, -1, keepdims=True) + EPSILON)
    return centred * spread, spread


def norm_kernel(which, arrived, kept, table, *outs):
    summed = arrived[...].astype(f32) + kept[...]
    gain, shift = table[GAIN + which : GAIN + which + 1], table[SHIFT + which : SHIFT + which + 1]
    outs[0][...] = (standard(summed)[0] * gain + shift).astype(bf16)
    if len(outs) > 1:
        outs[1][...] = summed


def norm_grads(values, gain, upstream):
    normal, spread = standard(values)
    scaled = upstream * gain
    along = jnp.mean(scaled * normal, -1, keepdims=True)
    grad = (scaled - jnp.mean(scaled, -1, keepdims=True) - normal * along) * spread
    return grad, jnp.sum(upstream * normal, 0, keepdims=True), jnp.sum(upstream, 0, keepdims=True)


def norm_back_kernel(upstream, values, table, grad, low, gain_bias):
    result, grad_gain, grad_shift = norm_grads(
        values[...], table[GAIN + 1 : GAIN + 2], upstream[...].astype(f32)
    )
    grad[...] = result
    low[...] = result.astype(bf16)
    gain_bias[0:1] = grad_gain
    gain_bias[1:2] = grad_shift


def norm_back_sum_kernel(arrived, kept, values, table, others, grad, low):
    upstream = arrived[...].astype(f32) + kept[...]
    result, grad_gain, grad_shift = norm_grads(values[...], table[GAIN : GAIN + 1], upstream)
    rows = result.shape[0]
    grad[...] = result
    low[0:rows] = result.astype(bf16)
    small = jnp.concatenate([grad_gain, grad_shift, others[0:2]], 0)
    high = small.astype(bf16)
    rest = (small - high.astype(f32)).astype(bf16)
    blank = jnp.zeros((EXTRA_ROWS - 8, result.shape[1]), bf16)
    low[rows : rows + EXTRA_ROWS] = jnp.concatenate([high, rest, blank], 0)


def feed_kernel(one, two, three, four, up, down, table, keep, send, *saved):
    part = one.shape[0]
    rows = jnp.concatenate([one[...], two[...], three[...], four[...]], 0)
    hidden = dot_nn(rows, up[...]) + table[UP_BIAS : UP_BIAS + 1]
    phi = 0.5 * (1.0 + lax.erf(hidden * SQRT_HALF))
    if saved:
        slope = phi + hidden * (jnp.exp(-0.5 * hidden * hidden) * INV_SQRT_TAU)
        saved[0][...] = slope.astype(bf16)
    total = dot_nn((hidden * phi).astype(bf16), down[...])
    keep[:part] = one[...].astype(f32) + (total[:part] + table[DOWN_BIAS : DOWN_BIAS + 1])
    keep[part:] = total[part : 2 * part]
    send[...] = total[2 * part :].astype(bf16)


def feed_back_kernel(one, two, three, four, slope, up, down, residual, keep, send):
    part = one.shape[0]
    rows = jnp.concatenate([one[...], two[...], three[...], four[...]], 0)
    hidden = (dot_nt(rows, down[...]) * slope[...].astype(f32)).astype(bf16)
    total = dot_nt(hidden, up[...])
    keep[:part] = total[:part] + residual[...]
    keep[part:] = total[part : 2 * part]
    send[...] = total[2 * part :].astype(bf16)


def halves_kernel(arrived, kept, keep, send):
    part = keep.shape[0]
    total = arrived[...].astype(f32) + kept[...]
    keep[...] = total[:part]
    send[...] = total[part:].astype(bf16)


def entry_grad_kernel(arrived, kept, low):
    low[...] = (arrived[...].astype(f32) + kept[...]).astype(bf16)


def copy_kernel(source, target):
    target[...] = source[...]


def pair_kernel(*refs):
    for number, ref in enumerate(refs[:-1]):
        refs[-1][number] = ref[...]


def group_forward(entry, w, table, seg_row, seg_col):
    local, length = w.shape[1], entry.shape[0] // 2
    bias = jnp.transpose(table[QV_OWN : QV_OWN + 2, :local])
    query = ((dot_nt(w[0], entry) + bias[:, 0:1]).astype(bf16) * HEAD_DIM**-0.5).astype(bf16)
    key = dot_nt(w[1], entry).astype(bf16)
    value = (dot_nt(w[2], entry) + bias[:, 1:2]).astype(bf16)
    probs, mixed = [], []
    for seq in range(2):
        span = slice(length * seq, length * (seq + 1))
        same = seg_col[seq] == seg_row[seq]
        for start in range(0, local, HEAD_DIM):
            head = slice(start, start + HEAD_DIM)
            scores = jnp.where(same, dot_tn(key[head, span], query[head, span]), BIG_NEGATIVE)
            weights = jnp.exp(scores - jnp.max(scores, 0, keepdims=True))
            weights = weights * (1.0 / jnp.sum(weights, 0, keepdims=True))
            probs.append(weights.astype(bf16))
            mixed.append(dot_nn(value[head, span], probs[-1]).astype(bf16))
    heads = len(probs) // 2
    columns = [jnp.concatenate(mixed[heads * seq : heads * (seq + 1)], 0) for seq in range(2)]
    return query, key, value, probs, jnp.concatenate(columns, 1)


def attend_group_kernel(one, two, three, four, w, table, seg_row, seg_col, lines, kept):
    entry = jnp.concatenate([one[...], two[...], three[...], four[...]], 0)
    *parts, probs, mixed = group_forward(entry, w, table, seg_row, seg_col)
    for number, item in enumerate((*parts, mixed)):
        lines[number] = item
    for number, item in enumerate(probs):
        kept[number] = item


def unpack_kernel(total, g_w, g_out, small):
    local = g_out.shape[0]
    for number in range(3):
        g_w[number] = total[local * number : local * (number + 1)].astype(f32)
    g_out[...] = total[3 * local : 4 * local].astype(f32)
    rest = total[4 * local :].astype(f32)
    small[...] = rest + jnp.concatenate([rest[7:], rest[:7]], 0)


def attend_grads_kernel(*refs):
    lines, kept, out, total = refs[8:]
    entry = jnp.concatenate([item[...] for item in refs[:4]], 0)
    pieces = [item[...] for item in refs[4:8]]
    part = refs[0].shape[0]
    local = out.shape[0]
    query, key, value, mixed = (lines[number] for number in range(4))
    probs = [kept[number] for number in range(kept.shape[0])]
    branch = jnp.concatenate([item[:part] for item in pieces], 0)
    grad_mixed = dot_nt(out[...], branch).astype(bf16)
    columns = []
    heads = len(probs) // 2
    for seq in range(2):
        span = slice(2 * part * seq, 2 * part * (seq + 1))
        rows = [], [], []
        for number in range(heads):
            head = slice(HEAD_DIM * number, HEAD_DIM * (number + 1))
            low = probs[heads * seq + number]
            q, k, v, upstream = (item[head, span] for item in (query, key, value, grad_mixed))
            wide = low.astype(f32)
            grads = wide * dot_tn(v, upstream)
            grads = (grads - wide * jnp.sum(grads, 0, keepdims=True)).astype(bf16)
            rows[0].append((dot_nn(k, grads) * HEAD_DIM**-0.5).astype(bf16))
            rows[1].append(dot_nt(q, grads).astype(bf16))
            rows[2].append(dot_nt(upstream, low).astype(bf16))
        columns.append([jnp.concatenate(item, 0) for item in rows])
    parts = [jnp.concatenate(pair, 1) for pair in zip(*columns)]
    for number, item in enumerate(parts):
        total[local * number : local * (number + 1)] = dot_nn(item, entry).astype(bf16)
    total[3 * local : 4 * local] = dot_nn(mixed, branch).astype(bf16)
    ones = jnp.ones((8, entry.shape[0]), bf16)
    blank = jnp.zeros((2, entry.shape[1] - local), f32)
    sums = jnp.concatenate([dot_nt(ones, parts[0])[:1], dot_nt(ones, parts[2])[:1]], 0)
    small = sum(item[part:].astype(f32) for item in pieces)
    sums = [jnp.concatenate([sums, blank], 1), dot_nn(ones, branch)[:1], small[:4] + small[4:8]]
    sums = jnp.concatenate(sums, 0)
    high = sums.astype(bf16)
    rest = (sums - high.astype(f32)).astype(bf16)
    blank = jnp.zeros((EXTRA_ROWS - 14, sums.shape[1]), bf16)
    total[4 * local : 4 * local + EXTRA_ROWS] = jnp.concatenate([high, rest, blank], 0)


def feed_grads_kernel(*refs):
    up, down, table, g_up, g_up_b, g_down, g_down_b = refs[4:]

    @pl.when(pl.program_id(0) == 0)
    def _():
        g_up[...] = jnp.zeros_like(g_up)
        g_up_b[...] = jnp.zeros_like(g_up_b)
        g_down[...] = jnp.zeros_like(g_down)
        g_down_b[...] = jnp.zeros_like(g_down_b)

    first, grad = (jnp.concatenate([refs[i][...], refs[i + 2][...]], 0) for i in range(2))
    hidden = dot_nn(first, up[...]) + table[UP_BIAS : UP_BIAS + 1]
    phi = 0.5 * (1.0 + lax.erf(hidden * SQRT_HALF))
    slope = phi + hidden * (jnp.exp(-0.5 * hidden * hidden) * INV_SQRT_TAU)
    act = (hidden * phi).astype(bf16)
    grad_hidden = (dot_nt(grad, down[...]) * slope).astype(bf16)
    g_down[...] += dot_tn(act, grad)
    g_up[...] += dot_tn(first, grad_hidden)
    g_up_b[...] += jnp.sum(grad_hidden.astype(f32), 0, keepdims=True)
    g_down_b[...] += jnp.sum(grad.astype(f32), 0, keepdims=True)


def whole(item):
    return pl.BlockSpec(item.shape, lambda step: (0,) * len(item.shape))


def leading(item, count):
    rest = len(item.shape) - 1
    return pl.BlockSpec((count,) + item.shape[1:], lambda step: (step,) + (0,) * rest)


def shards(
    block_input,
    segments,
    out_grad,
    query_key_value_weight,
    b_qv,
    attention_output_weight,
    attention_out_bias,
    ln_gain,
    ln_bias,
    up_projection_weight,
    up_proj_bias,
    down_projection_weight,
    down_proj_bias,
):
    assert lax.axis_size("tensor") == 4 and block_input.shape[0] == 2
    groups = lax.axis_size("dp")
    section = lax.axis_index("section")
    place = lax.axis_index("tensor")
    a, b = place // 2, place % 2
    seqs, quarter, width = block_input.shape
    length = segments.shape[1]
    part = length // 2
    local = query_key_value_weight.shape[3]
    hidden_local = up_projection_weight.shape[2]
    heads = local // HEAD_DIM

    beside = [(i, i ^ 1) for i in range(4)]
    across = [(i, i ^ 2) for i in range(4)]
    turn = [(2 * s + c, 2 * c + s) for s in range(2) for c in range(2)]
    twist = [(2 * s + c, 2 * c + 1 - s) for s in range(2) for c in range(2)]
    untwist = [(target, source) for source, target in twist]

    def swap(value, pairs):
        return lax.ppermute(value, "tensor", pairs)

    def pieces_of(block):
        one = swap(jnp.where(b == 0, block[0], block[1]), turn)
        two = swap(jnp.where(b == 0, block[1], block[0]), untwist)
        return jnp.where(a == 0, jnp.concatenate([one, two]), jnp.concatenate([two, one]))

    def blocks_of(piece):
        one = swap(jnp.where(a == 0, piece[:quarter], piece[quarter:]), turn)
        two = swap(jnp.where(a == 0, piece[quarter:], piece[:quarter]), twist)
        return jnp.where(b == 0, jnp.stack([one, two]), jnp.stack([two, one]))

    w_own = jnp.transpose(query_key_value_weight[0], (1, 0, 2))
    w_turned = jnp.transpose(query_key_value_weight[0], (1, 2, 0))
    o_own = attention_output_weight[0]
    b_own = b_qv[0].astype(f32)
    entry_input = pieces_of(block_input)
    w_far = swap(w_own, across)
    o_far = swap(o_own, across)
    cotangent = pieces_of(out_grad)
    up, down = up_projection_weight[0], down_projection_weight[0]

    def lines(item):
        return jnp.pad(item, ((0, 0), (0, width - item.shape[1])))

    b_own = lines(b_qv[0])
    table = [ln_gain[0], ln_bias[0], attention_out_bias, lines(up_proj_bias), down_proj_bias]
    table += [b_own, swap(b_own, across)]
    table = jnp.concatenate(table).astype(f32)
    table = jnp.pad(table, ((0, TABLE_ROWS - table.shape[0]), (0, 0)))

    seg_own = segments[0] if seqs == 1 else jnp.where(a == 0, segments[0], segments[1])
    seg_own = seg_own.astype(f32)
    seg_turned = jnp.where(b == 0, seg_own, jnp.roll(seg_own, part))
    seg_row, seg_col = seg_turned[None, :], seg_turned[:, None]
    seg_far = jnp.where(a == 0, segments[1], segments[0]).astype(f32)
    seg_far = jnp.where(b == 0, seg_far, jnp.roll(seg_far, part))
    seg_both = jnp.stack([seg_turned, seg_far])

    piece_f, piece_h = shape((part, width), f32), shape((part, width), bf16)
    pair_f, pair_h = shape((2 * part, width), f32), shape((2 * part, width), bf16)

    def forward(entry, save, after=()):
        outs = [piece_f, piece_h]
        if save:
            outs += [
                shape((2, 3, length, local), bf16),
                shape((2, heads, length, length), bf16),
            ]
        args = (entry, swap(entry, beside), w_own, w_far, o_own, o_far, table, seg_row, seg_col)
        keep, branch, *kept = run(attend_kernel, outs, args, 3.0, "attend")
        args = (swap(branch, beside), keep, table)
        first, *first_res = run(
            functools.partial(norm_kernel, 0), [piece_h] + [piece_f] * save, args, 0, "first_norm"
        )
        far = swap(first, across)
        near, far_near = swap(first, beside), swap(far, beside)
        outs = [pair_f, pair_h] + [shape((4 * part, hidden_local), bf16)] * save
        args = (first, far, near, far_near, up, down, table)
        keep, send, *slope = run(feed_kernel, outs, args, 1.6, "feed")
        keep, send = run(halves_kernel, [piece_f, piece_h], (swap(send, beside), keep), 0, "halves")
        args = (swap(send, across), keep, table)
        output, *second_res = run(
            functools.partial(norm_kernel, 1),
            [piece_h] + [piece_f] * save,
            args,
            0,
            "second_norm",
            after=after,
        )
        if not save:
            return output
        return output, (kept, first_res[0], slope[0], second_res[0]), (first, far), branch

    def backward(upstream, saved, after=(), later=()):
        kept, first_res, slope, second_res = saved
        grad_second, grad_y, gain_bias = run(
            norm_back_kernel,
            [piece_f, piece_h, shape((2, width), f32)],
            (upstream, second_res, table),
            0,
            "second_norm_back",
            after=after,
        )
        far = swap(grad_y, across)
        near, far_near = swap(grad_y, beside), swap(far, beside)
        args = (grad_y, far, near, far_near, slope, up, down, grad_second)
        keep, gate = run(feed_back_kernel, [pair_f, pair_h], args, 1.5, "feed_back")
        keep, send = run(halves_kernel, [piece_f, piece_h], (swap(gate, beside), keep), 0, "halves")
        args = (swap(send, across), keep, first_res, table, gain_bias)
        outs = [piece_f, shape((part + EXTRA_ROWS, width), bf16)]
        grad_first, branch = run(norm_back_sum_kernel, outs, args, 0, "first_norm_back", after=later)
        near = swap(branch, beside)

        args = (branch, near, w_own, w_far, o_own, o_far, *kept, grad_first)
        keep, send = run(attend_back_kernel, [piece_f, piece_h], args, 3.2, "attend_back")
        args = (swap(send, beside), keep)
        grad_entry = run(entry_grad_kernel, [piece_h], args, 0, "entry_grad")[0]
        return grad_entry, (grad_y, far), branch, near, send

    wide = groups in (2, 4)
    count = groups if wide else 1

    def gather(pair):
        mine = lax.all_gather(pair, "dp") if wide else pair[None]
        return mine, swap(mine, beside)

    sections = [(0, 1), (1, 0)]
    middle = lax.ppermute(forward(entry_input, False, (cotangent,)), "section", sections)
    entry = jnp.where(section == 0, entry_input, middle)
    output, saved, first_pair, token = forward(entry, True)

    entry_far = swap(entry, across)
    entries = (entry, swap(entry, beside), entry_far, swap(entry_far, beside))

    grad = backward(cotangent, saved)[0]
    firsts = [item.reshape(-1, width) for item in gather(jnp.stack(first_pair))]
    layer_output = blocks_of(output)
    args = (*entries, w_turned, table, seg_both[:, None, :], seg_both[:, :, None])
    outs = [shape((4, local, 2 * length), bf16), shape((2 * heads, length, length), bf16)]
    attended = run(attend_group_kernel, outs, args, 4.0, "attend_group", mib=24)
    middle = lax.ppermute(grad, "section", sections)
    grad_entry, grad_y, branch, near, token = backward(
        jnp.where(section == 1, cotangent, middle), saved, (layer_output, firsts[0]), tuple(attended[:1])
    )
    grad_y = jnp.stack(grad_y)
    grad_y = lax.all_gather(grad_y, "dp") if wide else grad_y[None]

    far = run(copy_kernel, [shape(branch.shape, bf16)], (swap(branch, across),), 0, "far", after=(token,))[0]
    total = run(
        attend_grads_kernel,
        [shape((4 * local + EXTRA_ROWS, width), bf16)],
        (*entries, branch, near, far, swap(far, beside), *attended, o_own),
        5.0,
        "attend_grads",
        mib=56,
    )[0]
    local_total = total
    total = lax.psum(total, "dp")
    grad_y = run(copy_kernel, [shape(grad_y.shape, bf16)], (grad_y,), 0, "gathered", after=(local_total,))[0]
    grads_y = [item.reshape(-1, width) for item in (grad_y, swap(grad_y, beside))]
    args = (firsts[0], grads_y[0], firsts[1], grads_y[1], up, down, table)
    outs = [
        shape((width, hidden_local), f32),
        shape((1, hidden_local), f32),
        shape((hidden_local, width), f32),
        shape((1, width), f32),
    ]
    block, tall = 2 * part, firsts[0].shape[0]
    g_up, g_up_b, g_down, g_down_b = run(
        feed_grads_kernel,
        outs,
        args,
        5.0,
        "feed_grads",
        mib=56,
        grid=(tall // block,),
        in_specs=[leading(item, block) for item in args[:4]] + [whole(item) for item in args[4:]],
        out_specs=[whole(item) for item in outs],
    )
    held = run(copy_kernel, [piece_h], (grad_entry,), 0, "held", after=(g_down,))[0]
    input_grad = blocks_of(held)
    if not wide:
        g_up, g_up_b, g_down = [
            lax.psum(item.astype(bf16), "dp").astype(f32) for item in (g_up, g_up_b, g_down)
        ]
        g_down_b = lax.psum(g_down_b, "dp")
    outs = [shape((3, local, width), f32), shape((local, width), f32), shape((EXTRA_ROWS, width), f32)]
    g_w, g_out, small = run(unpack_kernel, outs, (total,), 1.0, "unpack", after=(g_down, input_grad))
    g_b, g_out_b, small = small[:2, :local], small[2:3], small[3:7]
    return (
        layer_output[None],
        input_grad[None],
        jnp.transpose(g_w, (2, 0, 1))[None],
        g_b[None],
        g_out[None],
        g_out_b,
        jnp.stack([small[0], small[2]])[None],
        jnp.stack([small[1], small[3]])[None],
        g_up[None],
        g_up_b,
        g_down[None],
        g_down_b,
    )


def solution(mesh):
    return jax.shard_map(
        shards,
        mesh=mesh,
        in_specs=(
            P("dp", "tensor", None),
            P("dp", None),
            P("dp", "tensor", None),
            P("section", None, None, "tensor"),
            P("section", None, "tensor"),
            P("section", "tensor", None),
            P("section", None),
            P("section", None, None),
            P("section", None, None),
            P("section", None, "tensor"),
            P("section", "tensor"),
            P("section", "tensor", None),
            P("section", None),
        ),
        out_specs=(
            P("section", "dp", "tensor", None),
            P("section", "dp", "tensor", None),
            P("section", None, None, "tensor"),
            P("section", None, "tensor"),
            P("section", "tensor", None),
            P("section", None),
            P("section", None, None),
            P("section", None, None),
            P("section", None, "tensor"),
            P("section", "tensor"),
            P("section", "tensor", None),
            P("section", None),
        ),
        check_vma=False,
    )
```

time: 312 us -> 271 us (0.87)
  local copies, waits for them, and re-layouts: 46.1 us -> 28.9 us
  Pallas kernels: 67 us -> 56.3 us
  waiting for transfers between devices: 139 us -> 130 us
  other arithmetic: 11 us -> 6.94 us
    psum x0 -> x1, waiting for transfers between devices: none -> 33.2 us  [shards(): total = lax.psum(total, 'dp')]
    all_gather x4 -> x2, waiting for transfers between devices: 30.2 us -> 3.57 us  [the longest x1 3.44 us: gather(): mine = lax.all_gather(pair, 'dp') if wide else pair[None]]
    unnamed x114 -> x115, local copies, waits for them, and re-layouts: 42.4 us -> 24.2 us
    ppermute x39 -> x45, waiting for transfers between devices: 97.3 us -> 85 us  [swap(): return lax.ppermute(value, 'tensor', pairs)]
    pallas_call x25 -> x29, Pallas kernels: 67 us -> 56.3 us  [run(): pl.pallas_call(body, out_shape=outs, grid_spec=pltpu.PrefetchScalarGridSp...]
    ppermute x2, waiting for transfers between devices: 11.4 us -> 7.58 us  [the longest x1 4.54 us: shards(): lax.ppermute(forward(entry_input, False, (cotangent,)), 'section', sections)]
    convert_element_type x11 -> x1, other arithmetic: 4.47 us -> 0.76 us  [shards(): seg_far = jnp.where(a == 0, segments[1], segments[0]).astype(f32)]
    ppermute x39 -> x45, starting transfers between devices: 27 us -> 27.8 us  [swap(): return lax.ppermute(value, 'tensor', pairs)]
  transfers between devices with their start and end apart: 45 -> 50, of which waited for: 30 -> 29; matrix products, arithmetic and copies ran while one was open for 4% -> 3% of each run, Pallas kernels for 14% -> 15%
where the time goes in v3:
time: 271 us; the launch traced here: 270 us
  waiting for transfers between devices  130 us (48%)
  Pallas kernels  56.3 us (21%)
  starting transfers between devices  33.6 us (12%)
  local copies, waits for them, and re-layouts  28.9 us (11%)
  between operations  14.6 us (5%)
  other arithmetic  6.94 us (3%)
    ppermute x45, waiting for transfers between devices, swap(): return lax.ppermute(value, 'tensor', pairs)  85 us
    pallas_call x29, Pallas kernels, run(): pl.pallas_call(body, out_shape=outs, grid_spec=pltpu.PrefetchScalarGridSp...  56.3 us
    psum x1, waiting for transfers between devices, shards(): total = lax.psum(total, 'dp')  33.2 us
    ppermute x45, starting transfers between devices, swap(): return lax.ppermute(value, 'tensor', pairs)  27.8 us
    unnamed x115, local copies, waits for them, and re-layouts  24.2 us
  transfers between devices with their start and end apart: 50, of which 29 were waited for; matrix products, arithmetic and copies ran while one was open for 3% of the time, Pallas kernels for 15%

profile of v3, /device:TPU:0, one launch (start us, length us, event | category | flops | bytes accessed | tf_op | source)
XLA Modules:
  0.0 270.0 jit_solution(5886129422839539757)
XLA Ops:
  8.3 3.0 %collective-permute-start.1 = (bf16[64,768]{1,0:T(8,128)(2,1)S(1)}, bf16[64,768]{1,0:T(8,128)(2,1)S(1)}, u32[]{:S(2)}, u32[]{:S(2)}) collective-permute-start(bf16[64,768]{1,0:T(8,128)(2,1)S(1)} %get-tuple-element.119), channel_id=1, source_target_pairs={{4,0},{12,4},{0,8},{8,12},{5,1},{13,5},{1,9},{9,13},{6,2},{14,6},{... | collective-permute-start | bytes 294920 | tf_op jit(solution)/shard_map/ppermute | solution.py:374
  17.9 22.8 %collective-permute-done.5 = bf16[2,768]{1,0:T(2,128)(2,1)S(1)} collective-permute-done((bf16[2,768]{1,0:T(2,128)(2,1)S(1)}, bf16[2,768]{1,0:T(2,128)(2,1)S(1)}, u32[]{:S(2)}, u32[]{:S(2)}) %collective-permute-start.5) | collective-permute-done | bytes 3104 | tf_op jit(solution)/shard_map/ppermute | solution.py:374
  42.5 4.4 %attend.2 = (f32[128,768]{1,0:T(8,128)S(1)}, bf16[128,768]{1,0:T(8,128)(2,1)S(1)}) custom-call(bf16[128,768]{1,0:T(8,128)(2,1)S(1)} %maximum_select_fusion.refs_0_, bf16[128,768]{1,0:T(8,128)(2,1)S(1)} %collective-permute-done.2.refs_1_, bf16[3,768,192]{2,1,0:T(8,128)(2,1)S(1)} %bitcast.63, bf16[3,768,192]{2,1,0:T(8,128)(2,1)S(1)} %copy.40.refs_3_, ...), custom_call_target="tpu_custom_call" | custom-call | flops 3449999872 | bytes 3393536 | tf_op jit(solution)/shard_map/attend/pallas_call | solution.py:52
  48.7 1.8 collective-permute-start.7
  50.4 5.4 %collective-permute-done.7.refs_1_ = bf16[128,768]{1,0:T(8,128)(2,1)S(1)} collective-permute-done((bf16[128,768]{1,0:T(8,128)(2,1)S(1)}, bf16[128,768]{1,0:T(8,128)(2,1)S(1)}, u32[]{:S(2)}, u32[]{:S(2)}) %collective-permute-start.7) | collective-permute-done | bytes 196640 | tf_op jit(solution)/shard_map/ppermute | solution.py:374
  61.4 1.9 collective-permute-start.11
  63.3 6.5 %collective-permute-done.11.refs_0_ = bf16[128,768]{1,0:T(8,128)(2,1)S(1)} collective-permute-done((bf16[128,768]{1,0:T(8,128)(2,1)S(1)}, bf16[128,768]{1,0:T(8,128)(2,1)S(1)}, u32[]{:S(2)}, u32[]{:S(2)}) %collective-permute-start.11) | collective-permute-done | bytes 196640 | tf_op jit(solution)/shard_map/ppermute | solution.py:374
  70.0 2.6 collective-permute-start.14
  72.6 4.5 %collective-permute-done.14 = bf16[128,768]{1,0:T(8,128)(2,1)} collective-permute-done((bf16[128,768]{1,0:T(8,128)(2,1)S(1)}, bf16[128,768]{1,0:T(8,128)(2,1)}, u32[]{:S(2)}, u32[]{:S(2)}) %collective-permute-start.14) | collective-permute-done | bytes 196640 | tf_op jit(solution)/shard_map/ppermute | solution.py:482
  77.9 1.6 collective-permute-done.15.refs_1_
  79.6 4.2 %attend.3 = (f32[128,768]{1,0:T(8,128)S(1)}, bf16[128,768]{1,0:T(8,128)(2,1)S(1)}, bf16[2,3,256,192]{3,2,1,0:T(8,128)(2,1)S(1)}, bf16[2,3,256,256]{3,2,1,0:T(8,128)(2,1)S(1)}) custom-call(bf16[128,768]{1,0:T(8,128)(2,1)} %broadcast_select_fusion.1.refs_0_, bf16[128,768]{1,0:T(8,128)(2,1)S(1)} %collective-permute-done.15.refs_1_, ...), custom_call_target="tpu_custom_call" | custom-call | flops 3449999872 | bytes 4769792 | tf_op jit(solution)/shard_map/attend/pallas_call | solution.py:52
  88.5 5.8 %collective-permute-done.17.refs_1_ = bf16[128,768]{1,0:T(8,128)(2,1)S(1)} collective-permute-done((bf16[128,768]{1,0:T(8,128)(2,1)S(1)}, bf16[128,768]{1,0:T(8,128)(2,1)S(1)}, u32[]{:S(2)}, u32[]{:S(2)}) %collective-permute-start.17) | collective-permute-done | bytes 196640 | tf_op jit(solution)/shard_map/ppermute | solution.py:374
  95.7 1.7 feed.3
  100.6 5.8 %collective-permute-done.21.refs_0_ = bf16[128,768]{1,0:T(8,128)(2,1)S(1)} collective-permute-done((bf16[128,768]{1,0:T(8,128)(2,1)S(1)}, bf16[128,768]{1,0:T(8,128)(2,1)S(1)}, u32[]{:S(2)}, u32[]{:S(2)}) %collective-permute-start.21) | collective-permute-done | bytes 196640 | tf_op jit(solution)/shard_map/ppermute | solution.py:374
  109.9 4.1 %collective-permute-done.24.refs_1_ = bf16[128,768]{1,0:T(8,128)(2,1)} collective-permute-done((bf16[128,768]{1,0:T(8,128)(2,1)}, bf16[128,768]{1,0:T(8,128)(2,1)}, u32[]{:S(2)}, u32[]{:S(2)}) %collective-permute-start.24) | collective-permute-done | bytes 196640 | tf_op jit(solution)/shard_map/ppermute | solution.py:374
  119.5 2.7 feed_back.2
  125.2 5.9 %collective-permute-done.28.refs_0_ = bf16[128,768]{1,0:T(8,128)(2,1)S(1)} collective-permute-done((bf16[128,768]{1,0:T(8,128)(2,1)S(1)}, bf16[128,768]{1,0:T(8,128)(2,1)S(1)}, u32[]{:S(2)}, u32[]{:S(2)}) %collective-permute-start.28) | collective-permute-done | bytes 196640 | tf_op jit(solution)/shard_map/ppermute | solution.py:374
  133.0 4.2 %attend_back.2 = (f32[128,768]{1,0:T(8,128)S(1)}, bf16[128,768]{1,0:T(8,128)(2,1)S(1)}) custom-call(bf16[144,768]{1,0:T(8,128)(2,1)S(1)} %get-tuple-element.86.refs_0_, bf16[144,768]{1,0:T(8,128)(2,1)S(1)} %collective-permute-done.29.refs_1_, bf16[3,768,192]{2,1,0:T(8,128)(2,1)S(1)} %bitcast.65, bf16[3,768,192]{2,1,0:T(8,128)(2,1)S(1)} %copy-done.9, ...), custom_call_target="tpu_custom_call" | custom-call | flops 3680000000 | bytes 5160960 | tf_op jit(solution)/shard_map/attend_back/pallas_call | solution.py:52
  138.8 2.7 %collective-permute-start.31 = (bf16[128,768]{1,0:T(8,128)(2,1)S(1)}, bf16[128,768]{1,0:T(8,128)(2,1)S(1)}, u32[]{:S(2)}, u32[]{:S(2)}) collective-permute-start(bf16[128,768]{1,0:T(8,128)(2,1)S(1)} %entry_grad.2), channel_id=1, source_target_pairs={{0,16},{16,0},{1,17},{17,1},{2,18},{18,2},{3,19},{19,3},{4,20},{20... | collective-permute-start | bytes 589832 | tf_op jit(solution)/shard_map/ppermute | solution.py:495
  142.1 3.0 %collective-permute-done.31 = bf16[128,768]{1,0:T(8,128)(2,1)S(1)} collective-permute-done((bf16[128,768]{1,0:T(8,128)(2,1)S(1)}, bf16[128,768]{1,0:T(8,128)(2,1)S(1)}, u32[]{:S(2)}, u32[]{:S(2)}) %collective-permute-start.31) | collective-permute-done | bytes 196640 | tf_op jit(solution)/shard_map/ppermute | solution.py:495
  145.2 3.4 %all-gather.5.cloned.1.call-done = bf16[8,128,768]{2,1,0:T(8,128)(2,1)} async-done(((bf16[2,128,768]{2,1,0:T(8,128)(2,1)}), bf16[8,128,768]{2,1,0:T(8,128)(2,1)}) %all-gather.5.cloned.1.call-update) | async-done | bytes 1572880 | tf_op jit(solution)/shard_map/all_gather | solution.py:478
  152.6 5.1 %collective-permute-done.32.refs_1_ = bf16[128,768]{1,0:T(8,128)(2,1)S(1)} collective-permute-done((bf16[128,768]{1,0:T(8,128)(2,1)S(1)}, bf16[128,768]{1,0:T(8,128)(2,1)S(1)}, u32[]{:S(2)}, u32[]{:S(2)}) %collective-permute-start.32) | collective-permute-done | bytes 196640 | tf_op jit(solution)/shard_map/ppermute | solution.py:374
  166.4 2.3 feed_back.3
  174.3 4.1 %attend_group.1 = (bf16[4,192,512]{2,1,0:T(8,128)(2,1)S(1)}, bf16[6,256,256]{2,1,0:T(8,128)(2,1)S(1)}) custom-call(bf16[128,768]{1,0:T(8,128)(2,1)} %broadcast_select_fusion.1.refs_0_, bf16[128,768]{1,0:T(8,128)(2,1)S(1)} %copy-done.33, bf16[128,768]{1,0:T(8,128)(2,1)} %collective-permute-done.37.refs_2_, bf16[128,768]{1,0:T(8,128)(2,1)} %collective-permute-done.38.refs_3_, ...), custom_call_target="tpu_custom_call" | custom-call | flops 4600000000 | bytes 3297280 | tf_op jit(solution)/shard_map/attend_group/pallas_call | solution.py:52
  180.5 4.4 %attend_back.3 = (f32[128,768]{1,0:T(8,128)S(1)}, bf16[128,768]{1,0:T(8,128)(2,1)S(1)}) custom-call(bf16[144,768]{1,0:T(8,128)(2,1)S(1)} %get-tuple-element.100.refs_0_.refs_4_, bf16[144,768]{1,0:T(8,128)(2,1)S(1)} %collective-permute-done.39.refs_1_.refs_5_, bf16[3,768,192]{2,1,0:T(8,128)(2,1)S(1)} %bitcast.66, bf16[3,768,192]{2,1,0:T(8,128)(2,1)S(1)} %copy-done.10, ...), custom_call_target="tpu_custom_call" | custom-call | flops 3680000000 | bytes 5160960 | tf_op jit(solution)/shard_map/attend_back/pallas_call | solution.py:52
  185.0 1.8 collective-permute-done.41.refs_0_
  189.1 6.1 %attend_grads.1.refs_1_ = bf16[784,768]{1,0:T(8,128)(2,1)} custom-call(bf16[128,768]{1,0:T(8,128)(2,1)} %broadcast_select_fusion.1.refs_0_, bf16[128,768]{1,0:T(8,128)(2,1)} %copy-done.32, bf16[128,768]{1,0:T(8,128)(2,1)} %collective-permute-done.37.refs_2_, bf16[128,768]{1,0:T(8,128)(2,1)} %collective-permute-done.38.refs_3_, bf16[144,768]{1,0:T(8,128)(2,1)} %copy-done.30, ...), custom_call_target="tpu_custom_call" | custom-call | flops 5750000128 | bytes 4743168 | tf_op jit(solution)/shard_map/attend_grads/pallas_call | solution.py:52
  199.1 3.3 %collective-permute-done.40.refs_0_ = bf16[128,768]{1,0:T(8,128)(2,1)S(1)} collective-permute-done((bf16[128,768]{1,0:T(8,128)(2,1)}, bf16[128,768]{1,0:T(8,128)(2,1)S(1)}, u32[]{:S(2)}, u32[]{:S(2)}) %collective-permute-start.40) | collective-permute-done | bytes 196640 | tf_op jit(solution)/shard_map/ppermute | solution.py:374
  202.4 15.6 %feed_grads.1 = (f32[768,768]{1,0:T(8,128)}, f32[1,768]{1,0:T(1,128)}, f32[768,768]{1,0:T(8,128)}, f32[1,768]{1,0:T(1,128)}) custom-call(bf16[1024,768]{1,0:T(8,128)(2,1)} %bitcast.58, bf16[1024,768]{1,0:T(8,128)(2,1)} %bitcast.62, bf16[1024,768]{1,0:T(8,128)(2,1)} %bitcast.32.refs_2_, bf16[1024,768]{1,0:T(8,128)(2,1)} %bitcast.33.refs_3_, ...), custom_call_target="tpu_custom_call" | custom-call | flops 5750000128 | bytes 13424640 | tf_op jit(solution)/shard_map/feed_grads/pallas_call | solution.py:52
  218.1 1.7 copy-done.2
  221.5 3.0 %collective-permute-done.46 = bf16[64,768]{1,0:T(8,128)(2,1)S(1)} collective-permute-done((bf16[64,768]{1,0:T(8,128)(2,1)S(1)}, bf16[64,768]{1,0:T(8,128)(2,1)S(1)}, u32[]{:S(2)}, u32[]{:S(2)}) %collective-permute-start.46) | collective-permute-done | bytes 98336 | tf_op jit(solution)/shard_map/ppermute | solution.py:374
  224.4 33.2 %all-reduce.4.cloned.1.call-done.refs_0_ = bf16[784,768]{1,0:T(8,128)(2,1)} async-done(((bf16[784,768]{1,0:T(8,128)(2,1)}), bf16[784,768]{1,0:T(8,128)(2,1)}) %all-reduce.4.cloned.1.call-update) | async-done | bytes 1204240 | tf_op jit(solution)/shard_map/psum | solution.py:512
  (248 shorter events, 76.9 us)
Async XLA Ops:
  7.2 141.4 %all-gather.5.cloned.1.call-start = ((), (), s32[]{:S(2)}) async-start(), calls=%async_computation.1 | async-start | bytes 1966080 | tf_op jit(solution)/shard_map/all_gather | solution.py:478
  8.3 8.8 %collective-permute-start.1 = (bf16[64,768]{1,0:T(8,128)(2,1)S(1)}, bf16[64,768]{1,0:T(8,128)(2,1)S(1)}, u32[]{:S(2)}, u32[]{:S(2)}) collective-permute-start(bf16[64,768]{1,0:T(8,128)(2,1)S(1)} %get-tuple-element.119), channel_id=1, source_target_pairs={{4,0},{12,4},{0,8},{8,12},{5,1},{13,5},{1,9},{9,13},{6,2},{14,6},{... | collective-permute-start | bytes 294920 | tf_op jit(solution)/shard_map/ppermute | solution.py:374
  11.2 5.9 %collective-permute-start = (bf16[64,768]{1,0:T(8,128)(2,1)S(1)}, bf16[64,768]{1,0:T(8,128)(2,1)S(1)}, u32[]{:S(2)}, u32[]{:S(2)}) collective-permute-start(bf16[64,768]{1,0:T(8,128)(2,1)S(1)} %get-tuple-element.118), channel_id=1, source_target_pairs={{0,0},{4,8},{8,4},{12,12},{1,1},{5,9},{9,5},{13,13},{2,2},{6,10},{... | collective-permute-start | bytes 294920 | tf_op jit(solution)/shard_map/ppermute | solution.py:374
  11.9 29.0 %collective-permute-start.3 = (bf16[3,768,192]{1,2,0:T(8,128)(2,1)}, bf16[3,768,192]{1,2,0:T(8,128)(2,1)}, u32[]{:S(2)}, u32[]{:S(2)}) collective-permute-start(bf16[3,768,192]{1,2,0:T(8,128)(2,1)} %bitcast.67), channel_id=1, source_target_pairs={{0,8},{4,12},{8,0},{12,4},{1,9},{5,13},{9,1},{13,5},{2,10},{6,14},... | collective-permute-start | bytes 2654216 | tf_op jit(solution)/shard_map/ppermute | solution.py:374
  13.2 29.2 %collective-permute-start.4 = (bf16[192,768]{1,0:T(8,128)(2,1)}, bf16[192,768]{1,0:T(8,128)(2,1)}, u32[]{:S(2)}, u32[]{:S(2)}) collective-permute-start(bf16[192,768]{1,0:T(8,128)(2,1)} %bitcast.83), channel_id=1, source_target_pairs={{0,8},{4,12},{8,0},{12,4},{1,9},{5,13},{9,1},{13,5},{2,10},{6,14},... | collective-permute-start | bytes 884744 | tf_op jit(solution)/shard_map/ppermute | solution.py:374
  14.7 26.0 %collective-permute-start.5 = (bf16[2,768]{1,0:T(2,128)(2,1)S(1)}, bf16[2,768]{1,0:T(2,128)(2,1)S(1)}, u32[]{:S(2)}, u32[]{:S(2)}) collective-permute-start(bf16[2,768]{1,0:T(2,128)(2,1)S(1)} %pad.10), channel_id=1, source_target_pairs={{0,8},{4,12},{8,0},{12,4},{1,9},{5,13},{9,1},{13,5},{2,10},{6,14},... | collective-permute-start | bytes 9224 | tf_op jit(solution)/shard_map/ppermute | solution.py:374
  17.2 25.3 %collective-permute-start.2 = (bf16[128,768]{1,0:T(8,128)(2,1)S(1)}, bf16[128,768]{1,0:T(8,128)(2,1)S(1)}, u32[]{:S(2)}, u32[]{:S(2)}) collective-permute-start(bf16[128,768]{1,0:T(8,128)(2,1)S(1)} %maximum_select_fusion.refs_0_), channel_id=1, source_target_pairs={{0,4},{4,0},{8,12},{12,8},{1,5},{5,1},{9,13},{13,9},{2,6},{6,2},{1... | collective-permute-start | bytes 589832 | tf_op jit(solution)/shard_map/ppermute | solution.py:374
  48.7 7.2 %collective-permute-start.7 = (bf16[128,768]{1,0:T(8,128)(2,1)S(1)}, bf16[128,768]{1,0:T(8,128)(2,1)S(1)}, u32[]{:S(2)}, u32[]{:S(2)}) collective-permute-start(bf16[128,768]{1,0:T(8,128)(2,1)S(1)} %first_norm.2.refs_0_), channel_id=1, source_target_pairs={{0,8},{4,12},{8,0},{12,4},{1,9},{5,13},{9,1},{13,5},{2,10},{6,14},... | collective-permute-start | bytes 589832 | tf_op jit(solution)/shard_map/ppermute | solution.py:374
  50.4 5.4 %collective-permute-start.8 = (bf16[128,768]{1,0:T(8,128)(2,1)S(1)}, bf16[128,768]{1,0:T(8,128)(2,1)S(1)}, u32[]{:S(2)}, u32[]{:S(2)}) collective-permute-start(bf16[128,768]{1,0:T(8,128)(2,1)S(1)} %first_norm.2.refs_0_), channel_id=1, source_target_pairs={{0,4},{4,0},{8,12},{12,8},{1,5},{5,1},{9,13},{13,9},{2,6},{6,2},{1... | collective-permute-start | bytes 589832 | tf_op jit(solution)/shard_map/ppermute | solution.py:374
  59.1 4.2 %collective-permute-start.13 = (bf16[64,768]{1,0:T(8,128)(2,1)S(1)}, bf16[64,768]{1,0:T(8,128)(2,1)S(1)}, u32[]{:S(2)}, u32[]{:S(2)}) collective-permute-start(bf16[64,768]{1,0:T(8,128)(2,1)S(1)} %get-tuple-element.117), channel_id=1, source_target_pairs={{4,0},{12,4},{0,8},{8,12},{5,1},{13,5},{1,9},{9,13},{6,2},{14,6},{... | collective-permute-start | bytes 294920 | tf_op jit(solution)/shard_map/ppermute | solution.py:374
  61.4 8.5 %collective-permute-start.11 = (bf16[128,768]{1,0:T(8,128)(2,1)S(1)}, bf16[128,768]{1,0:T(8,128)(2,1)S(1)}, u32[]{:S(2)}, u32[]{:S(2)}) collective-permute-start(bf16[128,768]{1,0:T(8,128)(2,1)S(1)} %get-tuple-element.66), channel_id=1, source_target_pairs={{0,8},{4,12},{8,0},{12,4},{1,9},{5,13},{9,1},{13,5},{2,10},{6,14},... | collective-permute-start | bytes 589832 | tf_op jit(solution)/shard_map/ppermute | solution.py:374
  70.0 7.1 %collective-permute-start.14 = (bf16[128,768]{1,0:T(8,128)(2,1)S(1)}, bf16[128,768]{1,0:T(8,128)(2,1)}, u32[]{:S(2)}, u32[]{:S(2)}) collective-permute-start(bf16[128,768]{1,0:T(8,128)(2,1)S(1)} %second_norm.2), channel_id=1, source_target_pairs={{0,16},{16,0},{1,17},{17,1},{2,18},{18,2},{3,19},{19,3},{4,20},{20... | collective-permute-start | bytes 589832 | tf_op jit(solution)/shard_map/ppermute | solution.py:482
  87.2 7.0 %collective-permute-start.17 = (bf16[128,768]{1,0:T(8,128)(2,1)S(1)}, bf16[128,768]{1,0:T(8,128)(2,1)S(1)}, u32[]{:S(2)}, u32[]{:S(2)}) collective-permute-start(bf16[128,768]{1,0:T(8,128)(2,1)S(1)} %get-tuple-element.70.refs_0_), channel_id=1, source_target_pairs={{0,8},{4,12},{8,0},{12,4},{1,9},{5,13},{9,1},{13,5},{2,10},{6,14},... | collective-permute-start | bytes 589832 | tf_op jit(solution)/shard_map/ppermute | solution.py:374
  88.5 5.8 %collective-permute-start.18 = (bf16[128,768]{1,0:T(8,128)(2,1)S(1)}, bf16[128,768]{1,0:T(8,128)(2,1)S(1)}, u32[]{:S(2)}, u32[]{:S(2)}) collective-permute-start(bf16[128,768]{1,0:T(8,128)(2,1)S(1)} %get-tuple-element.70.refs_0_), channel_id=1, source_target_pairs={{0,4},{4,0},{8,12},{12,8},{1,5},{5,1},{9,13},{13,9},{2,6},{6,2},{1... | collective-permute-start | bytes 589832 | tf_op jit(solution)/shard_map/ppermute | solution.py:374
  99.3 7.0 %collective-permute-start.21 = (bf16[128,768]{1,0:T(8,128)(2,1)S(1)}, bf16[128,768]{1,0:T(8,128)(2,1)S(1)}, u32[]{:S(2)}, u32[]{:S(2)}) collective-permute-start(bf16[128,768]{1,0:T(8,128)(2,1)S(1)} %get-tuple-element.73), channel_id=1, source_target_pairs={{0,8},{4,12},{8,0},{12,4},{1,9},{5,13},{9,1},{13,5},{2,10},{6,14},... | collective-permute-start | bytes 589832 | tf_op jit(solution)/shard_map/ppermute | solution.py:374
  107.6 6.4 %collective-permute-start.24 = (bf16[128,768]{1,0:T(8,128)(2,1)}, bf16[128,768]{1,0:T(8,128)(2,1)}, u32[]{:S(2)}, u32[]{:S(2)}) collective-permute-start(bf16[128,768]{1,0:T(8,128)(2,1)} %get-tuple-element.77.refs_0_), channel_id=1, source_target_pairs={{0,8},{4,12},{8,0},{12,4},{1,9},{5,13},{9,1},{13,5},{2,10},{6,14},... | collective-permute-start | bytes 589832 | tf_op jit(solution)/shard_map/ppermute | solution.py:374
  109.6 85.7 %all-gather.7.cloned.1.call-start = ((), (), s32[]{:S(2)}) async-start(), calls=%async_computation.2 | async-start | bytes 1966080 | tf_op jit(solution)/shard_map/all_gather | solution.py:500
  109.8 4.2 %collective-permute-start.25 = (bf16[128,768]{1,0:T(8,128)(2,1)}, bf16[128,768]{1,0:T(8,128)(2,1)S(1)}, u32[]{:S(2)}, u32[]{:S(2)}) collective-permute-start(bf16[128,768]{1,0:T(8,128)(2,1)} %get-tuple-element.77.refs_0_), channel_id=1, source_target_pairs={{0,4},{4,0},{8,12},{12,8},{1,5},{5,1},{9,13},{13,9},{2,6},{6,2},{1... | collective-permute-start | bytes 589832 | tf_op jit(solution)/shard_map/ppermute | solution.py:374
  124.0 7.0 %collective-permute-start.28 = (bf16[128,768]{1,0:T(8,128)(2,1)S(1)}, bf16[128,768]{1,0:T(8,128)(2,1)S(1)}, u32[]{:S(2)}, u32[]{:S(2)}) collective-permute-start(bf16[128,768]{1,0:T(8,128)(2,1)S(1)} %get-tuple-element.82), channel_id=1, source_target_pairs={{0,8},{4,12},{8,0},{12,4},{1,9},{5,13},{9,1},{13,5},{2,10},{6,14},... | collective-permute-start | bytes 589832 | tf_op jit(solution)/shard_map/ppermute | solution.py:374
  137.4 4.6 %collective-permute-start.23 = (bf16[64,768]{1,0:T(8,128)(2,1)S(1)}, bf16[64,768]{1,0:T(8,128)(2,1)S(1)}, u32[]{:S(2)}, u32[]{:S(2)}) collective-permute-start(bf16[64,768]{1,0:T(8,128)(2,1)S(1)} %get-tuple-element.115), channel_id=1, source_target_pairs={{0,4},{4,12},{8,0},{12,8},{1,5},{5,13},{9,1},{13,9},{2,6},{6,14},{... | collective-permute-start | bytes 294920 | tf_op jit(solution)/shard_map/ppermute | solution.py:374
  137.8 4.2 %collective-permute-start.22 = (bf16[64,768]{1,0:T(8,128)(2,1)S(1)}, bf16[64,768]{1,0:T(8,128)(2,1)S(1)}, u32[]{:S(2)}, u32[]{:S(2)}) collective-permute-start(bf16[64,768]{1,0:T(8,128)(2,1)S(1)} %get-tuple-element.114), channel_id=1, source_target_pairs={{0,0},{4,8},{8,4},{12,12},{1,1},{5,9},{9,5},{13,13},{2,2},{6,10},{... | collective-permute-start | bytes 294920 | tf_op jit(solution)/shard_map/ppermute | solution.py:374
  138.8 6.4 %collective-permute-start.31 = (bf16[128,768]{1,0:T(8,128)(2,1)S(1)}, bf16[128,768]{1,0:T(8,128)(2,1)S(1)}, u32[]{:S(2)}, u32[]{:S(2)}) collective-permute-start(bf16[128,768]{1,0:T(8,128)(2,1)S(1)} %entry_grad.2), channel_id=1, source_target_pairs={{0,16},{16,0},{1,17},{17,1},{2,18},{18,2},{3,19},{19,3},{4,20},{20... | collective-permute-start | bytes 589832 | tf_op jit(solution)/shard_map/ppermute | solution.py:495
  151.1 6.5 %collective-permute-start.32 = (bf16[128,768]{1,0:T(8,128)(2,1)S(1)}, bf16[128,768]{1,0:T(8,128)(2,1)S(1)}, u32[]{:S(2)}, u32[]{:S(2)}) collective-permute-start(bf16[128,768]{1,0:T(8,128)(2,1)S(1)} %get-tuple-element.92.refs_0_), channel_id=1, source_target_pairs={{0,8},{4,12},{8,0},{12,4},{1,9},{5,13},{9,1},{13,5},{2,10},{6,14},... | collective-permute-start | bytes 589832 | tf_op jit(solution)/shard_map/ppermute | solution.py:374
  152.6 7.5 %collective-permute-start.33 = (bf16[128,768]{1,0:T(8,128)(2,1)S(1)}, bf16[128,768]{1,0:T(8,128)(2,1)S(1)}, u32[]{:S(2)}, u32[]{:S(2)}) collective-permute-start(bf16[128,768]{1,0:T(8,128)(2,1)S(1)} %get-tuple-element.92.refs_0_), channel_id=1, source_target_pairs={{0,4},{4,0},{8,12},{12,8},{1,5},{5,1},{9,13},{13,9},{2,6},{6,2},{1... | collective-permute-start | bytes 589832 | tf_op jit(solution)/shard_map/ppermute | solution.py:374
  158.5 10.4 %collective-permute-start.37 = (bf16[128,768]{1,0:T(8,128)(2,1)}, bf16[128,768]{1,0:T(8,128)(2,1)}, u32[]{:S(2)}, u32[]{:S(2)}) collective-permute-start(bf16[128,768]{1,0:T(8,128)(2,1)} %broadcast_select_fusion.1.refs_0_), channel_id=1, source_target_pairs={{0,8},{4,12},{8,0},{12,4},{1,9},{5,13},{9,1},{13,5},{2,10},{6,14},... | collective-permute-start | bytes 589832 | tf_op jit(solution)/shard_map/ppermute | solution.py:374
  170.7 7.8 %collective-permute-start.36 = (bf16[128,768]{1,0:T(8,128)(2,1)S(1)}, bf16[128,768]{1,0:T(8,128)(2,1)S(1)}, u32[]{:S(2)}, u32[]{:S(2)}) collective-permute-start(bf16[128,768]{1,0:T(8,128)(2,1)S(1)} %get-tuple-element.96), channel_id=1, source_target_pairs={{0,8},{4,12},{8,0},{12,4},{1,9},{5,13},{9,1},{13,5},{2,10},{6,14},... | collective-permute-start | bytes 589832 | tf_op jit(solution)/shard_map/ppermute | solution.py:374
  179.0 7.8 %collective-permute-start.41 = (bf16[144,768]{1,0:T(8,128)(2,1)S(1)}, bf16[144,768]{1,0:T(8,128)(2,1)S(1)}, u32[]{:S(2)}, u32[]{:S(2)}) collective-permute-start(bf16[144,768]{1,0:T(8,128)(2,1)S(1)} %get-tuple-element.100.refs_0_.refs_4_), channel_id=1, source_target_pairs={{0,8},{4,12},{8,0},{12,4},{1,9},{5,13},{9,1},{13,5},{2,10},{6,14},... | collective-permute-start | bytes 663560 | tf_op jit(solution)/shard_map/ppermute | solution.py:374
  186.9 15.5 %collective-permute-start.43 = (bf16[4,2,128,768]{3,2,1,0:T(8,128)(2,1)S(1)}, bf16[4,2,128,768]{3,2,1,0:T(8,128)(2,1)}, u32[]{:S(2)}, u32[]{:S(2)}) collective-permute-start(bf16[4,2,128,768]{3,2,1,0:T(8,128)(2,1)S(1)} %bitcast.60), channel_id=1, source_target_pairs={{0,4},{4,0},{8,12},{12,8},{1,5},{5,1},{9,13},{13,9},{2,6},{6,2},{1... | collective-permute-start | bytes 4718600 | tf_op jit(solution)/shard_map/ppermute | solution.py:374
  198.1 59.5 %all-reduce.4.cloned.1.call-start = ((), (), s32[]{:S(2)}) async-start(), calls=%async_computation | async-start | bytes 2408448 | tf_op jit(solution)/shard_map/psum | solution.py:512
  198.4 4.0 %collective-permute-start.44 = (bf16[4,2,128,768]{3,2,1,0:T(8,128)(2,1)S(1)}, bf16[4,2,128,768]{3,2,1,0:T(8,128)(2,1)}, u32[]{:S(2)}, u32[]{:S(2)}) collective-permute-start(bf16[4,2,128,768]{3,2,1,0:T(8,128)(2,1)S(1)} %gathered.1), channel_id=1, source_target_pairs={{0,4},{4,0},{8,12},{12,8},{1,5},{5,1},{9,13},{13,9},{2,6},{6,2},{1... | collective-permute-start | bytes 4718600 | tf_op jit(solution)/shard_map/ppermute | solution.py:374
  219.8 4.6 %collective-permute-start.46 = (bf16[64,768]{1,0:T(8,128)(2,1)S(1)}, bf16[64,768]{1,0:T(8,128)(2,1)S(1)}, u32[]{:S(2)}, u32[]{:S(2)}) collective-permute-start(bf16[64,768]{1,0:T(8,128)(2,1)S(1)} %get-tuple-element.113), channel_id=1, source_target_pairs={{0,4},{4,12},{8,0},{12,8},{1,5},{5,13},{9,1},{13,9},{2,6},{6,14},{... | collective-permute-start | bytes 294920 | tf_op jit(solution)/shard_map/ppermute | solution.py:374
  219.9 4.5 %collective-permute-start.45 = (bf16[64,768]{1,0:T(8,128)(2,1)S(1)}, bf16[64,768]{1,0:T(8,128)(2,1)S(1)}, u32[]{:S(2)}, u32[]{:S(2)}) collective-permute-start(bf16[64,768]{1,0:T(8,128)(2,1)S(1)} %get-tuple-element.112), channel_id=1, source_target_pairs={{0,0},{4,8},{8,4},{12,12},{1,1},{5,9},{9,5},{13,13},{2,2},{6,10},{... | collective-permute-start | bytes 294920 | tf_op jit(solution)/shard_map/ppermute | solution.py:374
  (75 other events, 612.6 us)
Sparse Core Ops, SparseCore 0:
  109.7 38.8 all-gather.4
  158.6 36.6 all-gather.6
  201.4 56.2 all-reduce.3

commit v4 on v3

v4 whole, which is shorter than its diff:
```python
import functools

import jax
import jax.numpy as jnp
from jax import lax
from jax.experimental import pallas as pl
from jax.experimental.pallas import tpu as pltpu
from jax.sharding import PartitionSpec as P

HEAD_DIM = 64
EPSILON = 1e-06
BIG_NEGATIVE = -1e30
MIB = 1024 * 1024
EXTRA_ROWS = 16
GAIN, SHIFT, OUT_BIAS, UP_BIAS, DOWN_BIAS, QV_OWN, QV_FAR, TABLE_ROWS = 0, 2, 4, 5, 6, 7, 9, 16
SQRT_HALF = 0.7071067811865476
INV_SQRT_TAU = 0.3989422804014327

f32 = jnp.float32
bf16 = jnp.bfloat16


def dot_nn(left, right):
    return lax.dot_general(left, right, (((1,), (0,)), ((), ())), preferred_element_type=f32)


def dot_nt(left, right):
    return lax.dot_general(left, right, (((1,), (1,)), ((), ())), preferred_element_type=f32)


def dot_tn(left, right):
    return lax.dot_general(left, right, (((0,), (0,)), ((), ())), preferred_element_type=f32)


def shape(dims, kind):
    return jax.ShapeDtypeStruct(dims, kind)


def run(kernel, outs, args, us, name, mib=16, after=(), grid=None, in_specs=None, out_specs=None,
        scalars=0, aliases=None):
    count = len(args)
    if in_specs is None:
        in_specs = [pl.BlockSpec(memory_space=pltpu.VMEM)] * count
    if out_specs is None:
        out_specs = [pl.BlockSpec(memory_space=pltpu.VMEM)] * len(outs)
    waits = [pl.BlockSpec(memory_space=pl.ANY)] * len(after)

    def body(*refs):
        kernel(*refs[:count], *refs[count + len(after) :])

    moved = sum(item.size * item.dtype.itemsize for item in (*args, *outs))
    return pl.pallas_call(
        body,
        out_shape=outs,
        grid_spec=pltpu.PrefetchScalarGridSpec(
            num_scalar_prefetch=scalars,
            grid=grid or (),
            in_specs=[*in_specs, *waits],
            out_specs=out_specs,
        ),
        name=name,
        input_output_aliases=aliases or {},
        compiler_params=pltpu.CompilerParams(vmem_limit_bytes=mib * MIB),
        cost_estimate=pl.CostEstimate(
            flops=int(us * 1.15e9), bytes_accessed=moved, transcendentals=0
        ),
    )(*args, *after)


def quarters(ref):
    local = ref.shape[0] // 4
    return [ref[local * number : local * (number + 1)] for number in range(4)]


def heads_forward(entry, w, table, line, same):
    local, length = w[0].shape[0], entry.shape[0] // len(same)
    bias = jnp.transpose(table[line : line + 2, :local])
    query = ((dot_nt(w[0], entry) + bias[:, 0:1]).astype(bf16) * HEAD_DIM**-0.5).astype(bf16)
    key = dot_nt(w[1], entry).astype(bf16)
    value = (dot_nt(w[2], entry) + bias[:, 1:2]).astype(bf16)
    probs, columns = [], []
    for seq, visible in enumerate(same):
        span = slice(length * seq, length * (seq + 1))
        mixed = []
        for start in range(0, local, HEAD_DIM):
            head = slice(start, start + HEAD_DIM)
            scores = jnp.where(visible, dot_tn(key[head, span], query[head, span]), BIG_NEGATIVE)
            weights = jnp.exp(scores - jnp.max(scores, 0, keepdims=True))
            weights = weights * (1.0 / jnp.sum(weights, 0, keepdims=True))
            probs.append(weights.astype(bf16))
            mixed.append(dot_nn(value[head, span], probs[-1]).astype(bf16))
        columns.append(jnp.concatenate(mixed, 0))
    return query, key, value, probs, jnp.concatenate(columns, 1)


def heads_backward(query, key, value, probs, grad_mixed):
    heads = query.shape[0] // HEAD_DIM
    length = probs[0].shape[0]
    columns = []
    for seq in range(len(probs) // heads):
        span = slice(length * seq, length * (seq + 1))
        rows = [], [], []
        for number in range(heads):
            head = slice(HEAD_DIM * number, HEAD_DIM * (number + 1))
            low = probs[heads * seq + number]
            q, k, v, upstream = (item[head, span] for item in (query, key, value, grad_mixed))
            wide = low.astype(f32)
            grads = wide * dot_tn(v, upstream)
            grads = (grads - wide * jnp.sum(grads, 0, keepdims=True)).astype(bf16)
            rows[0].append((dot_nn(k, grads) * HEAD_DIM**-0.5).astype(bf16))
            rows[1].append(dot_nt(q, grads).astype(bf16))
            rows[2].append(dot_nt(upstream, low).astype(bf16))
        columns.append([jnp.concatenate(item, 0) for item in rows])
    return [jnp.concatenate(pair, 1) for pair in zip(*columns)]


def attend_kernel(own, other, w_own, w_far, table, seg_row, seg_col, *outs):
    keep, send = outs[:2]
    rows = jnp.concatenate([own[...], other[...]], 0)
    same = seg_col[...] == seg_row[...]
    total = None
    for group, ref in enumerate((w_own, w_far)):
        *w, out = quarters(ref)
        *parts, probs, mixed = heads_forward(rows, w, table, QV_OWN + 2 * group, [same])
        if len(outs) > 2:
            for number, item in enumerate(parts):
                outs[2][group, number, : out.shape[0]] = item
            for number, item in enumerate(probs):
                outs[2][group, number, out.shape[0] :] = item
        term = dot_tn(mixed, out)
        total = term if total is None else total + term
    half = own.shape[0]
    keep[...] = own[...].astype(f32) + (total[:half] + table[OUT_BIAS : OUT_BIAS + 1])
    send[...] = total[half:].astype(bf16)


def attend_back_kernel(own, other, w_own, w_far, kept, residual, keep, send):
    half = own.shape[0] - EXTRA_ROWS
    rows = jnp.concatenate([own[:half], other[:half]], 0)
    total = None
    for group, ref in enumerate((w_own, w_far)):
        *w, out = quarters(ref)
        local = out.shape[0]
        grad_mixed = dot_nt(out, rows).astype(bf16)
        lines = [kept[group, number, :local] for number in range(3)]
        probs = [kept[group, number, local:] for number in range(3)]
        parts = heads_backward(*lines, probs, grad_mixed)
        for number, part in enumerate(parts):
            term = dot_tn(part, w[number])
            total = term if total is None else total + term
    keep[...] = total[:half] + residual[...]
    send[...] = total[half:].astype(bf16)


def standard(values):
    centred = values - jnp.mean(values, -1, keepdims=True)
    spread = lax.rsqrt(jnp.mean(centred * centred, -1, keepdims=True) + EPSILON)
    return centred * spread, spread


def norm_kernel(which, arrived, kept, table, *outs):
    summed = arrived[...].astype(f32) + kept[...]
    gain, shift = table[GAIN + which : GAIN + which + 1], table[SHIFT + which : SHIFT + which + 1]
    outs[0][...] = (standard(summed)[0] * gain + shift).astype(bf16)
    if len(outs) > 1:
        outs[1][...] = summed


def norm_grads(values, gain, upstream):
    normal, spread = standard(values)
    scaled = upstream * gain
    along = jnp.mean(scaled * normal, -1, keepdims=True)
    grad = (scaled - jnp.mean(scaled, -1, keepdims=True) - normal * along) * spread
    return grad, jnp.sum(upstream * normal, 0, keepdims=True), jnp.sum(upstream, 0, keepdims=True)


def norm_back_kernel(upstream, values, table, grad, low, gain_bias):
    result, grad_gain, grad_shift = norm_grads(
        values[...], table[GAIN + 1 : GAIN + 2], upstream[...].astype(f32)
    )
    grad[...] = result
    low[...] = result.astype(bf16)
    gain_bias[0:1] = grad_gain
    gain_bias[1:2] = grad_shift


def norm_back_sum_kernel(arrived, kept, values, table, others, grad, low):
    upstream = arrived[...].astype(f32) + kept[...]
    result, grad_gain, grad_shift = norm_grads(values[...], table[GAIN : GAIN + 1], upstream)
    rows = result.shape[0]
    grad[...] = result
    low[0:rows] = result.astype(bf16)
    small = jnp.concatenate([grad_gain, grad_shift, others[0:2]], 0)
    high = small.astype(bf16)
    rest = (small - high.astype(f32)).astype(bf16)
    blank = jnp.zeros((EXTRA_ROWS - 8, result.shape[1]), bf16)
    low[rows : rows + EXTRA_ROWS] = jnp.concatenate([high, rest, blank], 0)


def feed_kernel(one, two, three, four, weights, table, keep, send, *saved):
    part = one.shape[0]
    rows = jnp.concatenate([one[...], two[...], three[...], four[...]], 0)
    hidden = dot_nn(rows, weights[0]) + table[UP_BIAS : UP_BIAS + 1]
    phi = 0.5 * (1.0 + lax.erf(hidden * SQRT_HALF))
    if saved:
        slope = phi + hidden * (jnp.exp(-0.5 * hidden * hidden) * INV_SQRT_TAU)
        saved[0][...] = slope.astype(bf16)
    total = dot_nn((hidden * phi).astype(bf16), weights[1])
    keep[:part] = one[...].astype(f32) + (total[:part] + table[DOWN_BIAS : DOWN_BIAS + 1])
    keep[part:] = total[part : 2 * part]
    send[...] = total[2 * part :].astype(bf16)


def feed_back_kernel(one, two, three, four, slope, weights, residual, keep, send):
    part = one.shape[0]
    rows = jnp.concatenate([one[...], two[...], three[...], four[...]], 0)
    hidden = (dot_nt(rows, weights[1]) * slope[...].astype(f32)).astype(bf16)
    total = dot_nt(hidden, weights[0])
    keep[:part] = total[:part] + residual[...]
    keep[part:] = total[part : 2 * part]
    send[...] = total[2 * part :].astype(bf16)


def halves_kernel(arrived, kept, keep, send):
    part = keep.shape[0]
    total = arrived[...].astype(f32) + kept[...]
    keep[...] = total[:part]
    send[...] = total[part:].astype(bf16)


def entry_grad_kernel(arrived, kept, low):
    low[...] = (arrived[...].astype(f32) + kept[...]).astype(bf16)


def copy_kernel(source, target):
    target[...] = source[...]


def pair_kernel(*refs):
    for number, ref in enumerate(refs[:-1]):
        refs[-1][number] = ref[...]


def attend_group_kernel(one, two, three, four, w_own, table, seg_row, seg_col, lines, kept):
    entry = jnp.concatenate([one[...], two[...], three[...], four[...]], 0)
    same = [seg_col[seq] == seg_row[seq] for seq in range(2)]
    *parts, probs, mixed = heads_forward(entry, quarters(w_own)[:3], table, QV_OWN, same)
    for number, item in enumerate((*parts, mixed)):
        lines[number] = item
    for number, item in enumerate(probs):
        kept[number] = item


def unpack_kernel(total, g_w, g_out, small):
    local = g_out.shape[0]
    for number in range(3):
        g_w[number] = total[local * number : local * (number + 1)].astype(f32)
    g_out[...] = total[3 * local : 4 * local].astype(f32)
    rest = total[4 * local :].astype(f32)
    small[...] = rest + jnp.concatenate([rest[7:], rest[:7]], 0)


def attend_grads_kernel(*refs):
    lines, kept, w_own, total = refs[8:]
    out = quarters(w_own)[3]
    entry = jnp.concatenate([item[...] for item in refs[:4]], 0)
    pieces = [item[...] for item in refs[4:8]]
    part = refs[0].shape[0]
    local = out.shape[0]
    query, key, value, mixed = (lines[number] for number in range(4))
    probs = [kept[number] for number in range(kept.shape[0])]
    branch = jnp.concatenate([item[:part] for item in pieces], 0)
    grad_mixed = dot_nt(out, branch).astype(bf16)
    parts = heads_backward(query, key, value, probs, grad_mixed)
    for number, item in enumerate(parts):
        total[local * number : local * (number + 1)] = dot_nn(item, entry).astype(bf16)
    total[3 * local : 4 * local] = dot_nn(mixed, branch).astype(bf16)
    ones = jnp.ones((8, entry.shape[0]), bf16)
    blank = jnp.zeros((2, entry.shape[1] - local), f32)
    sums = jnp.concatenate([dot_nt(ones, parts[0])[:1], dot_nt(ones, parts[2])[:1]], 0)
    small = sum(item[part:].astype(f32) for item in pieces)
    sums = [jnp.concatenate([sums, blank], 1), dot_nn(ones, branch)[:1], small[:4] + small[4:8]]
    sums = jnp.concatenate(sums, 0)
    high = sums.astype(bf16)
    rest = (sums - high.astype(f32)).astype(bf16)
    blank = jnp.zeros((EXTRA_ROWS - 14, sums.shape[1]), bf16)
    total[4 * local : 4 * local + EXTRA_ROWS] = jnp.concatenate([high, rest, blank], 0)


def feed_grads_kernel(*refs):
    weights, table, g_up, g_up_b, g_down, g_down_b = refs[4:]

    @pl.when(pl.program_id(0) == 0)
    def _():
        g_up[...] = jnp.zeros_like(g_up)
        g_up_b[...] = jnp.zeros_like(g_up_b)
        g_down[...] = jnp.zeros_like(g_down)
        g_down_b[...] = jnp.zeros_like(g_down_b)

    first, grad = (jnp.concatenate([refs[i][...], refs[i + 2][...]], 0) for i in range(2))
    hidden = dot_nn(first, weights[0]) + table[UP_BIAS : UP_BIAS + 1]
    phi = 0.5 * (1.0 + lax.erf(hidden * SQRT_HALF))
    slope = phi + hidden * (jnp.exp(-0.5 * hidden * hidden) * INV_SQRT_TAU)
    act = (hidden * phi).astype(bf16)
    grad_hidden = (dot_nt(grad, weights[1]) * slope).astype(bf16)
    g_down[...] += dot_tn(act, grad)
    g_up[...] += dot_tn(first, grad_hidden)
    g_up_b[...] += jnp.sum(grad_hidden.astype(f32), 0, keepdims=True)
    g_down_b[...] += jnp.sum(grad.astype(f32), 0, keepdims=True)


def whole(item):
    return pl.BlockSpec(item.shape, lambda step: (0,) * len(item.shape))


def leading(item, count):
    rest = len(item.shape) - 1
    return pl.BlockSpec((count,) + item.shape[1:], lambda step: (step,) + (0,) * rest)


def shards(
    block_input,
    segments,
    out_grad,
    query_key_value_weight,
    b_qv,
    attention_output_weight,
    attention_out_bias,
    ln_gain,
    ln_bias,
    up_projection_weight,
    up_proj_bias,
    down_projection_weight,
    down_proj_bias,
):
    assert lax.axis_size("tensor") == 4 and block_input.shape[0] == 2
    groups = lax.axis_size("dp")
    section = lax.axis_index("section")
    place = lax.axis_index("tensor")
    a, b = place // 2, place % 2
    seqs, quarter, width = block_input.shape
    length = segments.shape[1]
    part = length // 2
    local = query_key_value_weight.shape[3]
    hidden_local = up_projection_weight.shape[2]
    heads = local // HEAD_DIM

    beside = [(i, i ^ 1) for i in range(4)]
    across = [(i, i ^ 2) for i in range(4)]
    turn = [(2 * s + c, 2 * c + s) for s in range(2) for c in range(2)]
    twist = [(2 * s + c, 2 * c + 1 - s) for s in range(2) for c in range(2)]
    untwist = [(target, source) for source, target in twist]

    def swap(value, pairs):
        return lax.ppermute(value, "tensor", pairs)

    def pieces_of(block):
        one = swap(jnp.where(b == 0, block[0], block[1]), turn)
        two = swap(jnp.where(b == 0, block[1], block[0]), untwist)
        return jnp.where(a == 0, jnp.concatenate([one, two]), jnp.concatenate([two, one]))

    def blocks_of(piece):
        one = swap(jnp.where(a == 0, piece[:quarter], piece[quarter:]), turn)
        two = swap(jnp.where(a == 0, piece[quarter:], piece[:quarter]), twist)
        return jnp.where(b == 0, jnp.stack([one, two]), jnp.stack([two, one]))

    w_own = jnp.transpose(query_key_value_weight[0], (1, 2, 0)).reshape(3 * local, width)
    w_own = jnp.concatenate([w_own, attention_output_weight[0]])
    entry_input = pieces_of(block_input)
    w_far = swap(w_own, across)
    cotangent = pieces_of(out_grad)
    weights = jnp.concatenate([up_projection_weight, down_projection_weight])

    def lines(item):
        return jnp.pad(item, ((0, 0), (0, width - item.shape[1])))

    b_own = lines(b_qv[0])
    table = [ln_gain[0], ln_bias[0], attention_out_bias, lines(up_proj_bias), down_proj_bias]
    table += [b_own, swap(b_own, across)]
    table = jnp.concatenate(table).astype(f32)
    table = jnp.pad(table, ((0, TABLE_ROWS - table.shape[0]), (0, 0)))

    seg_own = segments[0] if seqs == 1 else jnp.where(a == 0, segments[0], segments[1])
    seg_own = seg_own.astype(f32)
    seg_turned = jnp.where(b == 0, seg_own, jnp.roll(seg_own, part))
    seg_row, seg_col = seg_turned[None, :], seg_turned[:, None]
    seg_far = jnp.where(a == 0, segments[1], segments[0]).astype(f32)
    seg_far = jnp.where(b == 0, seg_far, jnp.roll(seg_far, part))
    seg_both = jnp.stack([seg_turned, seg_far])

    piece_f, piece_h = shape((part, width), f32), shape((part, width), bf16)
    pair_f, pair_h = shape((2 * part, width), f32), shape((2 * part, width), bf16)

    def forward(entry, save, before=(), after=()):
        outs = [piece_f, piece_h]
        if save:
            outs.append(shape((2, 3, local + length, length), bf16))
        args = (entry, swap(entry, beside), w_own, w_far, table, seg_row, seg_col)
        keep, branch, *kept = run(attend_kernel, outs, args, 3.0, "attend", after=before)
        args = (swap(branch, beside), keep, table)
        first, *first_res = run(
            functools.partial(norm_kernel, 0),
            [piece_h] + [piece_f] * save,
            args,
            0,
            "first_norm",
            after=after,
        )
        far = swap(first, across)
        near, far_near = swap(first, beside), swap(far, beside)
        outs = [pair_f, pair_h] + [shape((4 * part, hidden_local), bf16)] * save
        args = (first, far, near, far_near, weights, table)
        keep, send, *slope = run(feed_kernel, outs, args, 1.6, "feed")
        keep, send = run(halves_kernel, [piece_f, piece_h], (swap(send, beside), keep), 0, "halves")
        args = (swap(send, across), keep, table)
        output, *second_res = run(
            functools.partial(norm_kernel, 1),
            [piece_h] + [piece_f] * save,
            args,
            0,
            "second_norm",
        )
        if not save:
            return output
        return output, (kept, first_res[0], slope[0], second_res[0]), (first, far), branch

    def backward(upstream, saved, after=(), later=()):
        kept, first_res, slope, second_res = saved
        grad_second, grad_y, gain_bias = run(
            norm_back_kernel,
            [piece_f, piece_h, shape((2, width), f32)],
            (upstream, second_res, table),
            0,
            "second_norm_back",
            after=after,
        )
        far = swap(grad_y, across)
        near, far_near = swap(grad_y, beside), swap(far, beside)
        args = (grad_y, far, near, far_near, slope, weights, grad_second)
        keep, gate = run(feed_back_kernel, [pair_f, pair_h], args, 1.5, "feed_back")
        keep, send = run(halves_kernel, [piece_f, piece_h], (swap(gate, beside), keep), 0, "halves")
        args = (swap(send, across), keep, first_res, table, gain_bias)
        outs = [piece_f, shape((part + EXTRA_ROWS, width), bf16)]
        grad_first, branch = run(norm_back_sum_kernel, outs, args, 0, "first_norm_back")
        near = swap(branch, beside)

        args = (branch, near, w_own, w_far, *kept, grad_first)
        keep, send = run(attend_back_kernel, [piece_f, piece_h], args, 3.2, "attend_back", after=later)
        args = (swap(send, beside), keep)
        grad_entry = run(entry_grad_kernel, [piece_h], args, 0, "entry_grad")[0]
        return grad_entry, (grad_y, far), branch, near, send

    wide = groups in (2, 4)
    count = groups if wide else 1

    def gather(pair):
        mine = lax.all_gather(pair, "dp") if wide else pair[None]
        return mine, swap(mine, beside)

    sections = [(0, 1), (1, 0)]
    middle = lax.ppermute(forward(entry_input, False), "section", sections)
    entry = jnp.where(section == 0, entry_input, middle)
    entry_far = swap(entry, across)
    output, saved, first_pair, _ = forward(entry, True, (cotangent,), (entry_far,))

    entries = (entry, swap(entry, beside), entry_far, swap(entry_far, beside))

    firsts = [item.reshape(-1, width) for item in gather(jnp.stack(first_pair))]
    grad = backward(cotangent, saved, later=(firsts[0],))[0]
    layer_output = blocks_of(output)
    args = (*entries, w_own, table, seg_both[:, None, :], seg_both[:, :, None])
    outs = [shape((4, local, 2 * length), bf16), shape((2 * heads, length, length), bf16)]
    attended = run(attend_group_kernel, outs, args, 4.0, "attend_group", mib=24)
    middle = lax.ppermute(grad, "section", sections)
    grad_entry, grad_y, branch, near, token = backward(
        jnp.where(section == 1, cotangent, middle), saved, (layer_output, attended[0])
    )
    outs = [shape((2, part, width), bf16)]
    grad_y = run(pair_kernel, outs, grad_y, 0, "grad_y_pair")[0]
    grad_y = lax.all_gather(grad_y, "dp") if wide else grad_y[None]

    far = run(copy_kernel, [shape(branch.shape, bf16)], (swap(branch, across),), 0, "far", after=(token,))[0]
    total = run(
        attend_grads_kernel,
        [shape((4 * local + EXTRA_ROWS, width), bf16)],
        (*entries, branch, near, far, swap(far, beside), *attended, w_own),
        5.0,
        "attend_grads",
        mib=24,
    )[0]
    local_total = total
    total = lax.psum(total, "dp")
    grad_y = run(copy_kernel, [shape(grad_y.shape, bf16)], (grad_y,), 0, "gathered", after=(local_total,))[0]
    grads_y = [item.reshape(-1, width) for item in (grad_y, swap(grad_y, beside))]
    args = (firsts[0], grads_y[0], firsts[1], grads_y[1], weights, table)
    outs = [
        shape((width, hidden_local), f32),
        shape((1, hidden_local), f32),
        shape((hidden_local, width), f32),
        shape((1, width), f32),
    ]
    block, tall = 2 * part, firsts[0].shape[0]
    g_up, g_up_b, g_down, g_down_b = run(
        feed_grads_kernel,
        outs,
        args,
        5.0,
        "feed_grads",
        mib=56,
        grid=(tall // block,),
        in_specs=[leading(item, block) for item in args[:4]] + [whole(item) for item in args[4:]],
        out_specs=[whole(item) for item in outs],
    )
    held = run(copy_kernel, [piece_h], (grad_entry,), 0, "held", after=(g_down,))[0]
    input_grad = blocks_of(held)
    if not wide:
        g_up, g_up_b, g_down = [
            lax.psum(item.astype(bf16), "dp").astype(f32) for item in (g_up, g_up_b, g_down)
        ]
        g_down_b = lax.psum(g_down_b, "dp")
    outs = [shape((3, local, width), f32), shape((local, width), f32), shape((EXTRA_ROWS, width), f32)]
    g_w, g_out, small = run(unpack_kernel, outs, (total,), 1.0, "unpack", after=(g_down, input_grad))
    g_b, g_out_b, small = small[:2, :local], small[2:3], small[3:7]
    return (
        layer_output[None],
        input_grad[None],
        jnp.transpose(g_w, (2, 0, 1))[None],
        g_b[None],
        g_out[None],
        g_out_b,
        jnp.stack([small[0], small[2]])[None],
        jnp.stack([small[1], small[3]])[None],
        g_up[None],
        g_up_b,
        g_down[None],
        g_down_b,
    )


def solution(mesh):
    return jax.shard_map(
        shards,
        mesh=mesh,
        in_specs=(
            P("dp", "tensor", None),
            P("dp", None),
            P("dp", "tensor", None),
            P("section", None, None, "tensor"),
            P("section", None, "tensor"),
            P("section", "tensor", None),
            P("section", None),
            P("section", None, None),
            P("section", None, None),
            P("section", None, "tensor"),
            P("section", "tensor"),
            P("section", "tensor", None),
            P("section", None),
        ),
        out_specs=(
            P("section", "dp", "tensor", None),
            P("section", "dp", "tensor", None),
            P("section", None, None, "tensor"),
            P("section", None, "tensor"),
            P("section", "tensor", None),
            P("section", None),
            P("section", None, None),
            P("section", None, None),
            P("section", None, "tensor"),
            P("section", "tensor"),
            P("section", "tensor", None),
            P("section", None),
        ),
        check_vma=False,
    )
```

time: 271 us -> 267 us (0.985)
  local copies, waits for them, and re-layouts: 28.9 us -> 15.8 us
  waiting for transfers between devices: 130 us -> 138 us
    ppermute x45 -> x44, waiting for transfers between devices: 85 us -> 97.4 us  [swap(): return lax.ppermute(value, 'tensor', pairs)]
    unnamed x115 -> x85, local copies, waits for them, and re-layouts: 24.2 us -> 13.3 us
    all_gather x1, waiting for transfers between devices: 0.13 us -> 6.2 us  [shards(): grad_y = lax.all_gather(grad_y, 'dp') if wide else grad_y[None]]
    ppermute x45 -> x44, starting transfers between devices: 27.8 us -> 31.7 us  [swap(): return lax.ppermute(value, 'tensor', pairs)]
    psum x1, waiting for transfers between devices: 33.2 us -> 30 us  [shards(): total = lax.psum(total, 'dp')]
    ppermute x1, waiting for transfers between devices: 4.54 us -> 1.4 us  [shards(): middle = lax.ppermute(forward(entry_input, False), 'section', sections)]
    pallas_call x29 -> x30, Pallas kernels: 56.3 us -> 55.7 us  [run(): pl.pallas_call(body, out_shape=outs, grid_spec=pltpu.PrefetchScalarGridSp...]
  transfers between devices with their start and end apart: 50 -> 49, of which waited for: 29 -> 33; matrix products, arithmetic and copies ran while one was open for 3% -> 2% of each run, Pallas kernels for 15% -> 17%
where the time goes in v4:
time: 267 us; the launch traced here: 266 us
  waiting for transfers between devices  138 us (52%)
  Pallas kernels  55.7 us (21%)
  starting transfers between devices  35.4 us (13%)
  local copies, waits for them, and re-layouts  15.8 us (6%)
  between operations  14.5 us (5%)
  other arithmetic  5.99 us (2%)
    ppermute x44, waiting for transfers between devices, swap(): return lax.ppermute(value, 'tensor', pairs)  97.4 us
    pallas_call x30, Pallas kernels, run(): pl.pallas_call(body, out_shape=outs, grid_spec=pltpu.PrefetchScalarGridSp...  55.7 us
    ppermute x44, starting transfers between devices, swap(): return lax.ppermute(value, 'tensor', pairs)  31.7 us
    psum x1, waiting for transfers between devices, shards(): total = lax.psum(total, 'dp')  30 us
    unnamed x85, local copies, waits for them, and re-layouts  13.3 us
    all_gather x1, waiting for transfers between devices, shards(): grad_y = lax.all_gather(grad_y, 'dp') if wide else grad_y[None]  6.2 us
  transfers between devices with their start and end apart: 49, of which 33 were waited for; matrix products, arithmetic and copies ran while one was open for 2% of the time, Pallas kernels for 17%

profile of v4, /device:TPU:0, one launch (start us, length us, event | category | flops | bytes accessed | tf_op | source)
XLA Modules:
  0.0 265.8 jit_solution(7560883198733707196)
XLA Ops:
  7.9 2.9 %collective-permute-start.4 = (bf16[2,768]{1,0:T(2,128)(2,1)S(1)}, bf16[2,768]{1,0:T(2,128)(2,1)S(1)}, u32[]{:S(2)}, u32[]{:S(2)}) collective-permute-start(bf16[2,768]{1,0:T(2,128)(2,1)S(1)} %pad.10), channel_id=1, source_target_pairs={{0,8},{4,12},{8,0},{12,4},{1,9},{5,13},{9,1},{13,5},{2,10},{6,14},... | collective-permute-start | bytes 9224 | tf_op jit(solution)/shard_map/ppermute | solution.py:355
  12.5 2.4 collective-permute-start.1
  19.5 24.4 %collective-permute-done.3.refs_3_ = bf16[768,768]{1,0:T(8,128)(2,1)} collective-permute-done((bf16[768,768]{1,0:T(8,128)(2,1)S(1)}, bf16[768,768]{1,0:T(8,128)(2,1)}, u32[]{:S(2)}, u32[]{:S(2)}) %collective-permute-start.3) | collective-permute-done | bytes 1179680 | tf_op jit(solution)/shard_map/ppermute | solution.py:355
  43.9 4.7 %attend.2 = (f32[128,768]{1,0:T(8,128)S(1)}, bf16[128,768]{1,0:T(8,128)(2,1)S(1)}) custom-call(bf16[128,768]{1,0:T(8,128)(2,1)S(1)} %maximum_select_fusion.refs_0_, bf16[128,768]{1,0:T(8,128)(2,1)S(1)} %collective-permute-done.2.refs_1_, bf16[768,768]{1,0:T(8,128)(2,1)S(1)} %pad_maximum_fusion.refs_2_.refs_4_.refs_10_, ...), custom_call_target="tpu_custom_call" | custom-call | flops 3449999872 | bytes 3393536 | tf_op jit(solution)/shard_map/attend/pallas_call | solution.py:52
  51.6 5.8 %collective-permute-done.6.refs_1_ = bf16[128,768]{1,0:T(8,128)(2,1)S(1)} collective-permute-done((bf16[128,768]{1,0:T(8,128)(2,1)S(1)}, bf16[128,768]{1,0:T(8,128)(2,1)S(1)}, u32[]{:S(2)}, u32[]{:S(2)}) %collective-permute-start.6) | collective-permute-done | bytes 196640 | tf_op jit(solution)/shard_map/ppermute | solution.py:355
  63.5 5.8 %collective-permute-done.10.refs_0_ = bf16[128,768]{1,0:T(8,128)(2,1)S(1)} collective-permute-done((bf16[128,768]{1,0:T(8,128)(2,1)S(1)}, bf16[128,768]{1,0:T(8,128)(2,1)S(1)}, u32[]{:S(2)}, u32[]{:S(2)}) %collective-permute-start.10) | collective-permute-done | bytes 196640 | tf_op jit(solution)/shard_map/ppermute | solution.py:355
  71.8 2.5 collective-permute-start.14
  76.9 2.5 collective-permute-start.16
  79.4 4.7 %attend.3 = (f32[128,768]{1,0:T(8,128)S(1)}, bf16[128,768]{1,0:T(8,128)(2,1)S(1)}, bf16[2,3,448,256]{3,2,1,0:T(8,128)(2,1)S(1)}) custom-call(bf16[128,768]{1,0:T(8,128)(2,1)S(1)} %broadcast_select_fusion.1.refs_0_, bf16[128,768]{1,0:T(8,128)(2,1)S(1)} %collective-permute-done.12.refs_1_, bf16[768,768]{1,0:T(8,128)(2,1)S(1)} %pad_maximum_fusion.refs_2_.refs_4_.refs_10_, ...), custom_call_target="tpu_custom_call" | custom-call | flops 3449999872 | bytes 4769792 | tf_op jit(solution)/shard_map/attend/pallas_call | solution.py:52
  87.2 6.7 %collective-permute-done.17.refs_1_ = bf16[128,768]{1,0:T(8,128)(2,1)S(1)} collective-permute-done((bf16[128,768]{1,0:T(8,128)(2,1)S(1)}, bf16[128,768]{1,0:T(8,128)(2,1)S(1)}, u32[]{:S(2)}, u32[]{:S(2)}) %collective-permute-start.17) | collective-permute-done | bytes 196640 | tf_op jit(solution)/shard_map/ppermute | solution.py:355
  95.4 1.7 copy-done.6
  97.0 1.8 feed.3
  101.0 6.7 %collective-permute-done.21.refs_0_ = bf16[128,768]{1,0:T(8,128)(2,1)S(1)} collective-permute-done((bf16[128,768]{1,0:T(8,128)(2,1)S(1)}, bf16[128,768]{1,0:T(8,128)(2,1)S(1)}, u32[]{:S(2)}, u32[]{:S(2)}) %collective-permute-start.21) | collective-permute-done | bytes 196640 | tf_op jit(solution)/shard_map/ppermute | solution.py:355
  108.6 5.9 %collective-permute-done.24.refs_1_ = bf16[128,768]{1,0:T(8,128)(2,1)S(1)} collective-permute-done((bf16[128,768]{1,0:T(8,128)(2,1)S(1)}, bf16[128,768]{1,0:T(8,128)(2,1)S(1)}, u32[]{:S(2)}, u32[]{:S(2)}) %collective-permute-start.24) | collective-permute-done | bytes 196640 | tf_op jit(solution)/shard_map/ppermute | solution.py:355
  119.8 6.7 %collective-permute-done.28.refs_0_ = bf16[128,768]{1,0:T(8,128)(2,1)S(1)} collective-permute-done((bf16[128,768]{1,0:T(8,128)(2,1)S(1)}, bf16[128,768]{1,0:T(8,128)(2,1)S(1)}, u32[]{:S(2)}, u32[]{:S(2)}) %collective-permute-start.28) | collective-permute-done | bytes 196640 | tf_op jit(solution)/shard_map/ppermute | solution.py:355
  133.9 4.9 %attend_back.2 = (f32[128,768]{1,0:T(8,128)S(1)}, bf16[128,768]{1,0:T(8,128)(2,1)S(1)}) custom-call(bf16[144,768]{1,0:T(8,128)(2,1)} %get-tuple-element.85.refs_0_, bf16[144,768]{1,0:T(8,128)(2,1)S(1)} %collective-permute-done.29.refs_1_, bf16[768,768]{1,0:T(8,128)(2,1)S(1)} %pad_maximum_fusion.refs_2_.refs_4_.refs_10_, ...), custom_call_target="tpu_custom_call" | custom-call | flops 3680000000 | bytes 5160960 | tf_op jit(solution)/shard_map/attend_back/pallas_call | solution.py:52
  139.8 2.8 %collective-permute-start.23 = (bf16[64,768]{1,0:T(8,128)(2,1)S(1)}, bf16[64,768]{1,0:T(8,128)(2,1)S(1)}, u32[]{:S(2)}, u32[]{:S(2)}) collective-permute-start(bf16[64,768]{1,0:T(8,128)(2,1)S(1)} %get-tuple-element.113), channel_id=1, source_target_pairs={{0,4},{4,12},{8,0},{12,8},{1,5},{5,13},{9,1},{13,9},{2,6},{6,14},{... | collective-permute-start | bytes 294920 | tf_op jit(solution)/shard_map/ppermute | solution.py:355
  144.2 3.8 %attend_group.1 = (bf16[4,192,512]{2,1,0:T(8,128)(2,1)S(1)}, bf16[6,256,256]{2,1,0:T(8,128)(2,1)S(1)}) custom-call(bf16[128,768]{1,0:T(8,128)(2,1)S(1)} %broadcast_select_fusion.1.refs_0_, bf16[128,768]{1,0:T(8,128)(2,1)S(1)} %copy-done.20, bf16[128,768]{1,0:T(8,128)(2,1)S(1)} %copy-done.12, bf16[128,768]{1,0:T(8,128)(2,1)} %collective-permute-done.32.refs_3_, ...), custom_call_target="tpu_custom_call" | custom-call | flops 4600000000 | bytes 3592192 | tf_op jit(solution)/shard_map/attend_group/pallas_call | solution.py:52
  151.0 5.0 %collective-permute-done.33.refs_1_ = bf16[128,768]{1,0:T(8,128)(2,1)S(1)} collective-permute-done((bf16[128,768]{1,0:T(8,128)(2,1)S(1)}, bf16[128,768]{1,0:T(8,128)(2,1)S(1)}, u32[]{:S(2)}, u32[]{:S(2)}) %collective-permute-start.33) | collective-permute-done | bytes 196640 | tf_op jit(solution)/shard_map/ppermute | solution.py:355
  158.6 1.7 copy-done.8
  164.8 1.6 collective-permute-start.37
  166.4 5.5 %collective-permute-done.37.refs_0_ = bf16[128,768]{1,0:T(8,128)(2,1)S(1)} collective-permute-done((bf16[128,768]{1,0:T(8,128)(2,1)S(1)}, bf16[128,768]{1,0:T(8,128)(2,1)S(1)}, u32[]{:S(2)}, u32[]{:S(2)}) %collective-permute-start.37) | collective-permute-done | bytes 196640 | tf_op jit(solution)/shard_map/ppermute | solution.py:355
  172.3 1.6 collective-permute-start.40
  174.0 4.8 %attend_back.3 = (f32[128,768]{1,0:T(8,128)S(1)}, bf16[128,768]{1,0:T(8,128)(2,1)S(1)}) custom-call(bf16[144,768]{1,0:T(8,128)(2,1)S(1)} %get-tuple-element.98.refs_0_.refs_4_, bf16[144,768]{1,0:T(8,128)(2,1)S(1)} %collective-permute-done.38.refs_1_.refs_5_, bf16[768,768]{1,0:T(8,128)(2,1)S(1)} %pad_maximum_fusion.refs_2_.refs_4_.refs_10_, ...), custom_call_target="tpu_custom_call" | custom-call | flops 3680000000 | bytes 5160960 | tf_op jit(solution)/shard_map/attend_back/pallas_call | solution.py:52
  181.8 5.0 %attend_grads.1.refs_1_ = bf16[784,768]{1,0:T(8,128)(2,1)} custom-call(bf16[128,768]{1,0:T(8,128)(2,1)S(1)} %copy-done.10, bf16[128,768]{1,0:T(8,128)(2,1)S(1)} %copy-done.21, bf16[128,768]{1,0:T(8,128)(2,1)S(1)} %copy-done.13, bf16[128,768]{1,0:T(8,128)(2,1)} %collective-permute-done.32.refs_3_, bf16[144,768]{1,0:T(8,128)(2,1)S(1)} %get-tuple-element.98.refs_0_.refs_4_, ...), custom_call_target="tpu_custom_call" | custom-call | flops 5750000128 | bytes 5627904 | tf_op jit(solution)/shard_map/attend_grads/pallas_call | solution.py:52
  186.8 6.2 %all-gather.7.cloned.1.call-done = bf16[8,128,768]{2,1,0:T(8,128)(2,1)} async-done(((bf16[2,128,768]{2,1,0:T(8,128)(2,1)}), bf16[8,128,768]{2,1,0:T(8,128)(2,1)}) %all-gather.7.cloned.1.call-update) | async-done | bytes 1572880 | tf_op jit(solution)/shard_map/all_gather | solution.py:480
  195.5 3.1 %collective-permute-done.39.refs_0_ = bf16[128,768]{1,0:T(8,128)(2,1)S(1)} collective-permute-done((bf16[128,768]{1,0:T(8,128)(2,1)S(1)}, bf16[128,768]{1,0:T(8,128)(2,1)S(1)}, u32[]{:S(2)}, u32[]{:S(2)}) %collective-permute-start.39) | collective-permute-done | bytes 196640 | tf_op jit(solution)/shard_map/ppermute | solution.py:355
  198.6 15.6 %feed_grads.1 = (f32[768,768]{1,0:T(8,128)}, f32[1,768]{1,0:T(1,128)}, f32[768,768]{1,0:T(8,128)}, f32[1,768]{1,0:T(1,128)}) custom-call(bf16[1024,768]{1,0:T(8,128)(2,1)} %bitcast.18.refs_6_.refs_0_, bf16[1024,768]{1,0:T(8,128)(2,1)} %bitcast.54, bf16[1024,768]{1,0:T(8,128)(2,1)} %bitcast.25.refs_2_, bf16[1024,768]{1,0:T(8,128)(2,1)} %bitcast.26.refs_3_, ...), custom_call_target="tpu_custom_call" | custom-call | flops 5750000128 | bytes 13424640 | tf_op jit(solution)/shard_map/feed_grads/pallas_call | solution.py:52
  214.3 1.7 copy-done.1
  216.8 2.8 %collective-permute-start.45 = (bf16[64,768]{1,0:T(8,128)(2,1)S(1)}, bf16[64,768]{1,0:T(8,128)(2,1)S(1)}, u32[]{:S(2)}, u32[]{:S(2)}) collective-permute-start(bf16[64,768]{1,0:T(8,128)(2,1)S(1)} %get-tuple-element.111), channel_id=1, source_target_pairs={{0,4},{4,12},{8,0},{12,8},{1,5},{5,13},{9,1},{13,9},{2,6},{6,14},{... | collective-permute-start | bytes 294920 | tf_op jit(solution)/shard_map/ppermute | solution.py:355
  220.4 3.1 %collective-permute-done.45 = bf16[64,768]{1,0:T(8,128)(2,1)S(1)} collective-permute-done((bf16[64,768]{1,0:T(8,128)(2,1)S(1)}, bf16[64,768]{1,0:T(8,128)(2,1)S(1)}, u32[]{:S(2)}, u32[]{:S(2)}) %collective-permute-start.45) | collective-permute-done | bytes 98336 | tf_op jit(solution)/shard_map/ppermute | solution.py:355
  223.5 30.0 %all-reduce.4.cloned.1.call-done.refs_0_ = bf16[784,768]{1,0:T(8,128)(2,1)} async-done(((bf16[784,768]{1,0:T(8,128)(2,1)}), bf16[784,768]{1,0:T(8,128)(2,1)}) %all-reduce.4.cloned.1.call-update) | async-done | bytes 1204240 | tf_op jit(solution)/shard_map/psum | solution.py:492
  (217 shorter events, 67.0 us)
Async XLA Ops:
  7.2 124.3 %all-gather.5.cloned.1.call-start = ((), (), s32[]{:S(2)}) async-start(), calls=%async_computation.1 | async-start | bytes 1966080 | tf_op jit(solution)/shard_map/all_gather | solution.py:457
  7.9 10.6 %collective-permute-start.4 = (bf16[2,768]{1,0:T(2,128)(2,1)S(1)}, bf16[2,768]{1,0:T(2,128)(2,1)S(1)}, u32[]{:S(2)}, u32[]{:S(2)}) collective-permute-start(bf16[2,768]{1,0:T(2,128)(2,1)S(1)} %pad.10), channel_id=1, source_target_pairs={{0,8},{4,12},{8,0},{12,4},{1,9},{5,13},{9,1},{13,5},{2,10},{6,14},... | collective-permute-start | bytes 9224 | tf_op jit(solution)/shard_map/ppermute | solution.py:355
  11.8 5.0 %collective-permute-start = (bf16[64,768]{1,0:T(8,128)(2,1)S(1)}, bf16[64,768]{1,0:T(8,128)(2,1)S(1)}, u32[]{:S(2)}, u32[]{:S(2)}) collective-permute-start(bf16[64,768]{1,0:T(8,128)(2,1)S(1)} %get-tuple-element.116), channel_id=1, source_target_pairs={{0,0},{4,8},{8,4},{12,12},{1,1},{5,9},{9,5},{13,13},{2,2},{6,10},{... | collective-permute-start | bytes 294920 | tf_op jit(solution)/shard_map/ppermute | solution.py:355
  12.5 4.7 %collective-permute-start.1 = (bf16[64,768]{1,0:T(8,128)(2,1)S(1)}, bf16[64,768]{1,0:T(8,128)(2,1)S(1)}, u32[]{:S(2)}, u32[]{:S(2)}) collective-permute-start(bf16[64,768]{1,0:T(8,128)(2,1)S(1)} %get-tuple-element.117), channel_id=1, source_target_pairs={{4,0},{12,4},{0,8},{8,12},{5,1},{13,5},{1,9},{9,13},{6,2},{14,6},{... | collective-permute-start | bytes 294920 | tf_op jit(solution)/shard_map/ppermute | solution.py:355
  16.4 27.6 %collective-permute-start.3 = (bf16[768,768]{1,0:T(8,128)(2,1)S(1)}, bf16[768,768]{1,0:T(8,128)(2,1)}, u32[]{:S(2)}, u32[]{:S(2)}) collective-permute-start(bf16[768,768]{1,0:T(8,128)(2,1)S(1)} %pad_maximum_fusion.refs_2_.refs_4_.refs_10_), channel_id=1, source_target_pairs={{0,8},{4,12},{8,0},{12,4},{1,9},{5,13},{9,1},{13,5},{2,10},{6,14},... | collective-permute-start | bytes 3538952 | tf_op jit(solution)/shard_map/ppermute | solution.py:355
  50.4 7.0 %collective-permute-start.6 = (bf16[128,768]{1,0:T(8,128)(2,1)S(1)}, bf16[128,768]{1,0:T(8,128)(2,1)S(1)}, u32[]{:S(2)}, u32[]{:S(2)}) collective-permute-start(bf16[128,768]{1,0:T(8,128)(2,1)S(1)} %first_norm.2.refs_0_), channel_id=1, source_target_pairs={{0,8},{4,12},{8,0},{12,4},{1,9},{5,13},{9,1},{13,5},{2,10},{6,14},... | collective-permute-start | bytes 589832 | tf_op jit(solution)/shard_map/ppermute | solution.py:355
  51.6 6.0 %collective-permute-start.7 = (bf16[128,768]{1,0:T(8,128)(2,1)S(1)}, bf16[128,768]{1,0:T(8,128)(2,1)S(1)}, u32[]{:S(2)}, u32[]{:S(2)}) collective-permute-start(bf16[128,768]{1,0:T(8,128)(2,1)S(1)} %first_norm.2.refs_0_), channel_id=1, source_target_pairs={{0,4},{4,0},{8,12},{12,8},{1,5},{5,1},{9,13},{13,9},{2,6},{6,2},{1... | collective-permute-start | bytes 589832 | tf_op jit(solution)/shard_map/ppermute | solution.py:355
  62.3 7.0 %collective-permute-start.10 = (bf16[128,768]{1,0:T(8,128)(2,1)S(1)}, bf16[128,768]{1,0:T(8,128)(2,1)S(1)}, u32[]{:S(2)}, u32[]{:S(2)}) collective-permute-start(bf16[128,768]{1,0:T(8,128)(2,1)S(1)} %get-tuple-element.65), channel_id=1, source_target_pairs={{0,8},{4,12},{8,0},{12,4},{1,9},{5,13},{9,1},{13,5},{2,10},{6,14},... | collective-permute-start | bytes 589832 | tf_op jit(solution)/shard_map/ppermute | solution.py:355
  69.5 6.2 %collective-permute-start.11 = (bf16[128,768]{1,0:T(8,128)(2,1)S(1)}, bf16[128,768]{1,0:T(8,128)(2,1)S(1)}, u32[]{:S(2)}, u32[]{:S(2)}) collective-permute-start(bf16[128,768]{1,0:T(8,128)(2,1)S(1)} %second_norm.2), channel_id=1, source_target_pairs={{0,16},{16,0},{1,17},{17,1},{2,18},{18,2},{3,19},{19,3},{4,20},{20... | collective-permute-start | bytes 589832 | tf_op jit(solution)/shard_map/ppermute | solution.py:461
  71.1 4.7 %collective-permute-start.13 = (bf16[64,768]{1,0:T(8,128)(2,1)S(1)}, bf16[64,768]{1,0:T(8,128)(2,1)S(1)}, u32[]{:S(2)}, u32[]{:S(2)}) collective-permute-start(bf16[64,768]{1,0:T(8,128)(2,1)S(1)} %get-tuple-element.114), channel_id=1, source_target_pairs={{0,0},{4,8},{8,4},{12,12},{1,1},{5,9},{9,5},{13,13},{2,2},{6,10},{... | collective-permute-start | bytes 294920 | tf_op jit(solution)/shard_map/ppermute | solution.py:355
  71.8 5.1 %collective-permute-start.14 = (bf16[64,768]{1,0:T(8,128)(2,1)S(1)}, bf16[64,768]{1,0:T(8,128)(2,1)S(1)}, u32[]{:S(2)}, u32[]{:S(2)}) collective-permute-start(bf16[64,768]{1,0:T(8,128)(2,1)S(1)} %get-tuple-element.115), channel_id=1, source_target_pairs={{4,0},{12,4},{0,8},{8,12},{5,1},{13,5},{1,9},{9,13},{6,2},{14,6},{... | collective-permute-start | bytes 294920 | tf_op jit(solution)/shard_map/ppermute | solution.py:355
  76.9 8.4 %collective-permute-start.16 = (bf16[128,768]{1,0:T(8,128)(2,1)S(1)}, bf16[128,768]{1,0:T(8,128)(2,1)S(1)}, u32[]{:S(2)}, u32[]{:S(2)}) collective-permute-start(bf16[128,768]{1,0:T(8,128)(2,1)S(1)} %broadcast_select_fusion.1.refs_0_), channel_id=1, source_target_pairs={{0,8},{4,12},{8,0},{12,4},{1,9},{5,13},{9,1},{13,5},{2,10},{6,14},... | collective-permute-start | bytes 589832 | tf_op jit(solution)/shard_map/ppermute | solution.py:355
  86.9 7.0 %collective-permute-start.17 = (bf16[128,768]{1,0:T(8,128)(2,1)S(1)}, bf16[128,768]{1,0:T(8,128)(2,1)S(1)}, u32[]{:S(2)}, u32[]{:S(2)}) collective-permute-start(bf16[128,768]{1,0:T(8,128)(2,1)S(1)} %get-tuple-element.69.refs_0_), channel_id=1, source_target_pairs={{0,8},{4,12},{8,0},{12,4},{1,9},{5,13},{9,1},{13,5},{2,10},{6,14},... | collective-permute-start | bytes 589832 | tf_op jit(solution)/shard_map/ppermute | solution.py:355
  87.0 7.9 %collective-permute-start.18 = (bf16[128,768]{1,0:T(8,128)(2,1)S(1)}, bf16[128,768]{1,0:T(8,128)(2,1)S(1)}, u32[]{:S(2)}, u32[]{:S(2)}) collective-permute-start(bf16[128,768]{1,0:T(8,128)(2,1)S(1)} %get-tuple-element.69.refs_0_), channel_id=1, source_target_pairs={{0,4},{4,0},{8,12},{12,8},{1,5},{5,1},{9,13},{13,9},{2,6},{6,2},{1... | collective-permute-start | bytes 589832 | tf_op jit(solution)/shard_map/ppermute | solution.py:355
  94.7 98.2 %all-gather.7.cloned.1.call-start = ((), (), s32[]{:S(2)}) async-start(), calls=%async_computation.2 | async-start | bytes 1966080 | tf_op jit(solution)/shard_map/all_gather | solution.py:480
  100.7 7.0 %collective-permute-start.21 = (bf16[128,768]{1,0:T(8,128)(2,1)S(1)}, bf16[128,768]{1,0:T(8,128)(2,1)S(1)}, u32[]{:S(2)}, u32[]{:S(2)}) collective-permute-start(bf16[128,768]{1,0:T(8,128)(2,1)S(1)} %get-tuple-element.72), channel_id=1, source_target_pairs={{0,8},{4,12},{8,0},{12,4},{1,9},{5,13},{9,1},{13,5},{2,10},{6,14},... | collective-permute-start | bytes 589832 | tf_op jit(solution)/shard_map/ppermute | solution.py:355
  108.3 6.3 %collective-permute-start.24 = (bf16[128,768]{1,0:T(8,128)(2,1)S(1)}, bf16[128,768]{1,0:T(8,128)(2,1)S(1)}, u32[]{:S(2)}, u32[]{:S(2)}) collective-permute-start(bf16[128,768]{1,0:T(8,128)(2,1)S(1)} %get-tuple-element.76.refs_0_), channel_id=1, source_target_pairs={{0,8},{4,12},{8,0},{12,4},{1,9},{5,13},{9,1},{13,5},{2,10},{6,14},... | collective-permute-start | bytes 589832 | tf_op jit(solution)/shard_map/ppermute | solution.py:355
  108.6 5.9 %collective-permute-start.25 = (bf16[128,768]{1,0:T(8,128)(2,1)S(1)}, bf16[128,768]{1,0:T(8,128)(2,1)S(1)}, u32[]{:S(2)}, u32[]{:S(2)}) collective-permute-start(bf16[128,768]{1,0:T(8,128)(2,1)S(1)} %get-tuple-element.76.refs_0_), channel_id=1, source_target_pairs={{0,4},{4,0},{8,12},{12,8},{1,5},{5,1},{9,13},{13,9},{2,6},{6,2},{1... | collective-permute-start | bytes 589832 | tf_op jit(solution)/shard_map/ppermute | solution.py:355
  119.4 7.0 %collective-permute-start.28 = (bf16[128,768]{1,0:T(8,128)(2,1)S(1)}, bf16[128,768]{1,0:T(8,128)(2,1)S(1)}, u32[]{:S(2)}, u32[]{:S(2)}) collective-permute-start(bf16[128,768]{1,0:T(8,128)(2,1)S(1)} %get-tuple-element.81), channel_id=1, source_target_pairs={{0,8},{4,12},{8,0},{12,4},{1,9},{5,13},{9,1},{13,5},{2,10},{6,14},... | collective-permute-start | bytes 589832 | tf_op jit(solution)/shard_map/ppermute | solution.py:355
  128.4 15.7 %collective-permute-start.32 = (bf16[128,768]{1,0:T(8,128)(2,1)S(1)}, bf16[128,768]{1,0:T(8,128)(2,1)}, u32[]{:S(2)}, u32[]{:S(2)}) collective-permute-start(bf16[128,768]{1,0:T(8,128)(2,1)S(1)} %collective-permute-done.16.refs_3_.refs_2_), channel_id=1, source_target_pairs={{0,4},{4,0},{8,12},{12,8},{1,5},{5,1},{9,13},{13,9},{2,6},{6,2},{1... | collective-permute-start | bytes 589832 | tf_op jit(solution)/shard_map/ppermute | solution.py:355
  138.8 3.8 %collective-permute-start.30 = (bf16[128,768]{1,0:T(8,128)(2,1)S(1)}, bf16[128,768]{1,0:T(8,128)(2,1)S(1)}, u32[]{:S(2)}, u32[]{:S(2)}) collective-permute-start(bf16[128,768]{1,0:T(8,128)(2,1)S(1)} %get-tuple-element.88), channel_id=1, source_target_pairs={{0,4},{4,0},{8,12},{12,8},{1,5},{5,1},{9,13},{13,9},{2,6},{6,2},{1... | collective-permute-start | bytes 589832 | tf_op jit(solution)/shard_map/ppermute | solution.py:355
  138.9 9.1 %collective-permute-start.22 = (bf16[64,768]{1,0:T(8,128)(2,1)S(1)}, bf16[64,768]{1,0:T(8,128)(2,1)S(1)}, u32[]{:S(2)}, u32[]{:S(2)}) collective-permute-start(bf16[64,768]{1,0:T(8,128)(2,1)S(1)} %get-tuple-element.112), channel_id=1, source_target_pairs={{0,0},{4,8},{8,4},{12,12},{1,1},{5,9},{9,5},{13,13},{2,2},{6,10},{... | collective-permute-start | bytes 294920 | tf_op jit(solution)/shard_map/ppermute | solution.py:355
  139.8 8.3 %collective-permute-start.23 = (bf16[64,768]{1,0:T(8,128)(2,1)S(1)}, bf16[64,768]{1,0:T(8,128)(2,1)S(1)}, u32[]{:S(2)}, u32[]{:S(2)}) collective-permute-start(bf16[64,768]{1,0:T(8,128)(2,1)S(1)} %get-tuple-element.113), channel_id=1, source_target_pairs={{0,4},{4,12},{8,0},{12,8},{1,5},{5,13},{9,1},{13,9},{2,6},{6,14},{... | collective-permute-start | bytes 294920 | tf_op jit(solution)/shard_map/ppermute | solution.py:355
  142.6 6.9 %collective-permute-start.31 = (bf16[128,768]{1,0:T(8,128)(2,1)S(1)}, bf16[128,768]{1,0:T(8,128)(2,1)S(1)}, u32[]{:S(2)}, u32[]{:S(2)}) collective-permute-start(bf16[128,768]{1,0:T(8,128)(2,1)S(1)} %entry_grad.2), channel_id=1, source_target_pairs={{0,16},{16,0},{1,17},{17,1},{2,18},{18,2},{3,19},{19,3},{4,20},{20... | collective-permute-start | bytes 589832 | tf_op jit(solution)/shard_map/ppermute | solution.py:474
  149.9 6.0 %collective-permute-start.33 = (bf16[128,768]{1,0:T(8,128)(2,1)S(1)}, bf16[128,768]{1,0:T(8,128)(2,1)S(1)}, u32[]{:S(2)}, u32[]{:S(2)}) collective-permute-start(bf16[128,768]{1,0:T(8,128)(2,1)S(1)} %get-tuple-element.91.refs_0_), channel_id=1, source_target_pairs={{0,8},{4,12},{8,0},{12,4},{1,9},{5,13},{9,1},{13,5},{2,10},{6,14},... | collective-permute-start | bytes 589832 | tf_op jit(solution)/shard_map/ppermute | solution.py:355
  164.8 7.1 %collective-permute-start.37 = (bf16[128,768]{1,0:T(8,128)(2,1)S(1)}, bf16[128,768]{1,0:T(8,128)(2,1)S(1)}, u32[]{:S(2)}, u32[]{:S(2)}) collective-permute-start(bf16[128,768]{1,0:T(8,128)(2,1)S(1)} %get-tuple-element.95), channel_id=1, source_target_pairs={{0,8},{4,12},{8,0},{12,4},{1,9},{5,13},{9,1},{13,5},{2,10},{6,14},... | collective-permute-start | bytes 589832 | tf_op jit(solution)/shard_map/ppermute | solution.py:355
  172.3 7.8 %collective-permute-start.40 = (bf16[144,768]{1,0:T(8,128)(2,1)S(1)}, bf16[144,768]{1,0:T(8,128)(2,1)S(1)}, u32[]{:S(2)}, u32[]{:S(2)}) collective-permute-start(bf16[144,768]{1,0:T(8,128)(2,1)S(1)} %get-tuple-element.98.refs_0_.refs_4_), channel_id=1, source_target_pairs={{0,8},{4,12},{8,0},{12,4},{1,9},{5,13},{9,1},{13,5},{2,10},{6,14},... | collective-permute-start | bytes 663560 | tf_op jit(solution)/shard_map/ppermute | solution.py:355
  180.3 18.3 %collective-permute-start.42 = (bf16[4,2,128,768]{3,2,1,0:T(8,128)(2,1)}, bf16[4,2,128,768]{3,2,1,0:T(8,128)(2,1)}, u32[]{:S(2)}, u32[]{:S(2)}) collective-permute-start(bf16[4,2,128,768]{3,2,1,0:T(8,128)(2,1)} %bitcast.24), channel_id=1, source_target_pairs={{0,4},{4,0},{8,12},{12,8},{1,5},{5,1},{9,13},{13,9},{2,6},{6,2},{1... | collective-permute-start | bytes 4718600 | tf_op jit(solution)/shard_map/ppermute | solution.py:355
  194.5 58.9 %all-reduce.4.cloned.1.call-start = ((), (), s32[]{:S(2)}) async-start(), calls=%async_computation | async-start | bytes 2408448 | tf_op jit(solution)/shard_map/psum | solution.py:492
  194.8 3.8 %collective-permute-start.43 = (bf16[4,2,128,768]{3,2,1,0:T(8,128)(2,1)S(1)}, bf16[4,2,128,768]{3,2,1,0:T(8,128)(2,1)}, u32[]{:S(2)}, u32[]{:S(2)}) collective-permute-start(bf16[4,2,128,768]{3,2,1,0:T(8,128)(2,1)S(1)} %gathered.1), channel_id=1, source_target_pairs={{0,4},{4,0},{8,12},{12,8},{1,5},{5,1},{9,13},{13,9},{2,6},{6,2},{1... | collective-permute-start | bytes 4718600 | tf_op jit(solution)/shard_map/ppermute | solution.py:355
  216.0 4.4 %collective-permute-start.44 = (bf16[64,768]{1,0:T(8,128)(2,1)S(1)}, bf16[64,768]{1,0:T(8,128)(2,1)S(1)}, u32[]{:S(2)}, u32[]{:S(2)}) collective-permute-start(bf16[64,768]{1,0:T(8,128)(2,1)S(1)} %get-tuple-element.110), channel_id=1, source_target_pairs={{0,0},{4,8},{8,4},{12,12},{1,1},{5,9},{9,5},{13,13},{2,2},{6,10},{... | collective-permute-start | bytes 294920 | tf_op jit(solution)/shard_map/ppermute | solution.py:355
  216.8 6.6 %collective-permute-start.45 = (bf16[64,768]{1,0:T(8,128)(2,1)S(1)}, bf16[64,768]{1,0:T(8,128)(2,1)S(1)}, u32[]{:S(2)}, u32[]{:S(2)}) collective-permute-start(bf16[64,768]{1,0:T(8,128)(2,1)S(1)} %get-tuple-element.111), channel_id=1, source_target_pairs={{0,4},{4,12},{8,0},{12,8},{1,5},{5,13},{9,1},{13,9},{2,6},{6,14},{... | collective-permute-start | bytes 294920 | tf_op jit(solution)/shard_map/ppermute | solution.py:355
  (59 other events, 551.4 us)
Sparse Core Ops, SparseCore 0:
  94.9 36.6 all-gather.4
  156.9 36.0 all-gather.6
  197.7 55.6 all-reduce.3

commit v5 on v4

--- a/solution.py
+++ b/solution.py
@@ -114,12 +114,21 @@
     return [jnp.concatenate(pair, 1) for pair in zip(*columns)]
 
 
-def attend_kernel(own, other, w_own, w_far, table, seg_row, seg_col, *outs):
+def attend_own_kernel(own, other, w_own, table, seg_row, seg_col, total):
+    rows = jnp.concatenate([own[...], other[...]], 0)
+    *w, out = quarters(w_own)
+    mixed = heads_forward(rows, w, table, QV_OWN, [seg_col[...] == seg_row[...]])[-1]
+    total[...] = dot_tn(mixed, out)
+
+
+def attend_kernel(early, own, other, w_own, w_far, table, seg_row, seg_col, *outs):
     keep, send = outs[:2]
     rows = jnp.concatenate([own[...], other[...]], 0)
     same = seg_col[...] == seg_row[...]
-    total = None
+    total = w_own[...] if early else None
     for group, ref in enumerate((w_own, w_far)):
+        if early and group == 0:
+            continue
         *w, out = quarters(ref)
         *parts, probs, mixed = heads_forward(rows, w, table, QV_OWN + 2 * group, [same])
         if len(outs) > 2:
@@ -251,13 +260,17 @@
         kept[number] = item
 
 
-def unpack_kernel(total, g_w, g_out, small):
+def unpack_kernel(total, g_w, g_out, g_b, g_out_b, g_gain, g_shift):
     local = g_out.shape[0]
     for number in range(3):
         g_w[number] = total[local * number : local * (number + 1)].astype(f32)
     g_out[...] = total[3 * local : 4 * local].astype(f32)
     rest = total[4 * local :].astype(f32)
-    small[...] = rest + jnp.concatenate([rest[7:], rest[:7]], 0)
+    rest = rest[:7] + rest[7:14]
+    g_b[...] = rest[:2, :local]
+    g_out_b[...] = rest[2:3]
+    g_gain[...] = jnp.concatenate([rest[3:4], rest[5:6]], 0)
+    g_shift[...] = jnp.concatenate([rest[4:5], rest[6:7]], 0)
 
 
 def attend_grads_kernel(*refs):
@@ -395,8 +408,14 @@
         outs = [piece_f, piece_h]
         if save:
             outs.append(shape((2, 3, local + length, length), bf16))
-        args = (entry, swap(entry, beside), w_own, w_far, table, seg_row, seg_col)
-        keep, branch, *kept = run(attend_kernel, outs, args, 3.0, "attend", after=before)
+        near, first_part = swap(entry, beside), w_own
+        if not save:
+            args = (entry, near, w_own, table, seg_row, seg_col)
+            first_part = run(attend_own_kernel, [pair_f], args, 2.0, "attend_own")[0]
+        args = (entry, near, first_part, w_far, table, seg_row, seg_col)
+        keep, branch, *kept = run(
+            functools.partial(attend_kernel, not save), outs, args, 3.0, "attend", after=before
+        )
         args = (swap(branch, beside), keep, table)
         first, *first_res = run(
             functools.partial(norm_kernel, 0),
@@ -518,9 +537,12 @@
             lax.psum(item.astype(bf16), "dp").astype(f32) for item in (g_up, g_up_b, g_down)
         ]
         g_down_b = lax.psum(g_down_b, "dp")
-    outs = [shape((3, local, width), f32), shape((local, width), f32), shape((EXTRA_ROWS, width), f32)]
-    g_w, g_out, small = run(unpack_kernel, outs, (total,), 1.0, "unpack", after=(g_down, input_grad))
-    g_b, g_out_b, small = small[:2, :local], small[2:3], small[3:7]
+    outs = [shape((3, local, width), f32), shape((local, width), f32), shape((2, local), f32)]
+    outs += [shape((1, width), f32), shape((2, width), f32), shape((2, width), f32)]
+    after = (g_down, input_grad)
+    g_w, g_out, g_b, g_out_b, g_gain, g_shift = run(
+        unpack_kernel, outs, (total,), 1.0, "unpack", after=after
+    )
     return (
         layer_output[None],
         input_grad[None],
@@ -528,8 +550,8 @@
         g_b[None],
         g_out[None],
         g_out_b,
-        jnp.stack([small[0], small[2]])[None],
-        jnp.stack([small[1], small[3]])[None],
+        g_gain[None],
+        g_shift[None],
         g_up[None],
         g_up_b,
         g_down[None],

time: 267 us -> 262 us (0.981)
    pallas_call x30 -> x31, Pallas kernels: 55.7 us -> 56 us  [run(): pl.pallas_call(body, out_shape=outs, grid_spec=pltpu.PrefetchScalarGridSp...]
  transfers between devices with their start and end apart: 49 -> 49, of which waited for: 33 -> 33; matrix products, arithmetic and copies ran while one was open for 2% -> 2% of each run, Pallas kernels for 17% -> 18%
where the time goes in v5:
time: 262 us; the launch traced here: 261 us
  waiting for transfers between devices  136 us (52%)
  Pallas kernels  56 us (21%)
  starting transfers between devices  35.3 us (13%)
  local copies, waits for them, and re-layouts  15 us (6%)
  between operations  14.5 us (6%)
  other arithmetic  4.79 us (2%)
    ppermute x44, waiting for transfers between devices, swap(): return lax.ppermute(value, 'tensor', pairs)  95.7 us
    pallas_call x31, Pallas kernels, run(): pl.pallas_call(body, out_shape=outs, grid_spec=pltpu.PrefetchScalarGridSp...  56 us
    ppermute x44, starting transfers between devices, swap(): return lax.ppermute(value, 'tensor', pairs)  31.6 us
    psum x1, waiting for transfers between devices, shards(): total = lax.psum(total, 'dp')  29.3 us
    unnamed x85, local copies, waits for them, and re-layouts  13.6 us
    all_gather x1, waiting for transfers between devices, shards(): grad_y = lax.all_gather(grad_y, 'dp') if wide else grad_y[None]  6.18 us
  transfers between devices with their start and end apart: 49, of which 33 were waited for; matrix products, arithmetic and copies ran while one was open for 2% of the time, Pallas kernels for 18%

profile of v5, /device:TPU:0, one launch (start us, length us, event | category | flops | bytes accessed | tf_op | source)
XLA Modules:
  0.0 261.2 jit_solution(13940264033900524362)
XLA Ops:
  7.9 2.9 %collective-permute-start.3 = (bf16[2,768]{1,0:T(2,128)(2,1)S(1)}, bf16[2,768]{1,0:T(2,128)(2,1)S(1)}, u32[]{:S(2)}, u32[]{:S(2)}) collective-permute-start(bf16[2,768]{1,0:T(2,128)(2,1)S(1)} %pad.10), channel_id=1, source_target_pairs={{0,8},{4,12},{8,0},{12,4},{1,9},{5,13},{9,1},{13,5},{2,10},{6,14},... | collective-permute-start | bytes 9224 | tf_op jit(solution)/shard_map/ppermute | solution.py:368
  12.5 2.4 collective-permute-start.1
  19.5 1.8 attend_own.1.refs_2_
  21.3 22.6 %collective-permute-done.4.refs_3_ = bf16[768,768]{1,0:T(8,128)(2,1)} collective-permute-done((bf16[768,768]{1,0:T(8,128)(2,1)S(1)}, bf16[768,768]{1,0:T(8,128)(2,1)}, u32[]{:S(2)}, u32[]{:S(2)}) %collective-permute-start.4) | collective-permute-done | bytes 1179680 | tf_op jit(solution)/shard_map/ppermute | solution.py:368
  43.9 3.2 %attend.2 = (f32[128,768]{1,0:T(8,128)S(1)}, bf16[128,768]{1,0:T(8,128)(2,1)S(1)}) custom-call(bf16[128,768]{1,0:T(8,128)(2,1)S(1)} %maximum_select_fusion.refs_0_, bf16[128,768]{1,0:T(8,128)(2,1)S(1)} %collective-permute-done.2.refs_1_, f32[256,768]{1,0:T(8,128)S(1)} %attend_own.1.refs_2_, bf16[768,768]{1,0:T(8,128)(2,1)} %collective-permute-done.4.refs_3_, ...), custom_call_target="tpu_custom_call" | custom-call | flops 3449999872 | bytes 3000320 | tf_op jit(solution)/shard_map/attend/pallas_call | solution.py:52
  50.0 5.8 %collective-permute-done.6.refs_1_ = bf16[128,768]{1,0:T(8,128)(2,1)S(1)} collective-permute-done((bf16[128,768]{1,0:T(8,128)(2,1)S(1)}, bf16[128,768]{1,0:T(8,128)(2,1)S(1)}, u32[]{:S(2)}, u32[]{:S(2)}) %collective-permute-start.6) | collective-permute-done | bytes 196640 | tf_op jit(solution)/shard_map/ppermute | solution.py:368
  61.9 5.8 %collective-permute-done.10.refs_0_ = bf16[128,768]{1,0:T(8,128)(2,1)S(1)} collective-permute-done((bf16[128,768]{1,0:T(8,128)(2,1)S(1)}, bf16[128,768]{1,0:T(8,128)(2,1)S(1)}, u32[]{:S(2)}, u32[]{:S(2)}) %collective-permute-start.10) | collective-permute-done | bytes 196640 | tf_op jit(solution)/shard_map/ppermute | solution.py:368
  70.2 2.5 collective-permute-start.14
  75.3 2.5 collective-permute-start.16
  77.9 4.7 %attend.3 = (f32[128,768]{1,0:T(8,128)S(1)}, bf16[128,768]{1,0:T(8,128)(2,1)S(1)}, bf16[2,3,448,256]{3,2,1,0:T(8,128)(2,1)S(1)}) custom-call(bf16[128,768]{1,0:T(8,128)(2,1)S(1)} %broadcast_select_fusion.1.refs_0_, bf16[128,768]{1,0:T(8,128)(2,1)S(1)} %collective-permute-done.12.refs_1_, bf16[768,768]{1,0:T(8,128)(2,1)S(1)} %pad_maximum_fusion.refs_2_.refs_4_.refs_10_, ...), custom_call_target="tpu_custom_call" | custom-call | flops 3449999872 | bytes 4769792 | tf_op jit(solution)/shard_map/attend/pallas_call | solution.py:52
  85.7 6.7 %collective-permute-done.17.refs_1_ = bf16[128,768]{1,0:T(8,128)(2,1)S(1)} collective-permute-done((bf16[128,768]{1,0:T(8,128)(2,1)S(1)}, bf16[128,768]{1,0:T(8,128)(2,1)S(1)}, u32[]{:S(2)}, u32[]{:S(2)}) %collective-permute-start.17) | collective-permute-done | bytes 196640 | tf_op jit(solution)/shard_map/ppermute | solution.py:368
  93.8 1.7 copy-done.6
  95.5 1.8 feed.3
  99.5 6.7 %collective-permute-done.21.refs_0_ = bf16[128,768]{1,0:T(8,128)(2,1)S(1)} collective-permute-done((bf16[128,768]{1,0:T(8,128)(2,1)S(1)}, bf16[128,768]{1,0:T(8,128)(2,1)S(1)}, u32[]{:S(2)}, u32[]{:S(2)}) %collective-permute-start.21) | collective-permute-done | bytes 196640 | tf_op jit(solution)/shard_map/ppermute | solution.py:368
  107.1 5.9 %collective-permute-done.24.refs_1_ = bf16[128,768]{1,0:T(8,128)(2,1)S(1)} collective-permute-done((bf16[128,768]{1,0:T(8,128)(2,1)S(1)}, bf16[128,768]{1,0:T(8,128)(2,1)S(1)}, u32[]{:S(2)}, u32[]{:S(2)}) %collective-permute-start.24) | collective-permute-done | bytes 196640 | tf_op jit(solution)/shard_map/ppermute | solution.py:368
  118.2 6.7 %collective-permute-done.28.refs_0_ = bf16[128,768]{1,0:T(8,128)(2,1)S(1)} collective-permute-done((bf16[128,768]{1,0:T(8,128)(2,1)S(1)}, bf16[128,768]{1,0:T(8,128)(2,1)S(1)}, u32[]{:S(2)}, u32[]{:S(2)}) %collective-permute-start.28) | collective-permute-done | bytes 196640 | tf_op jit(solution)/shard_map/ppermute | solution.py:368
  132.3 4.9 %attend_back.2 = (f32[128,768]{1,0:T(8,128)S(1)}, bf16[128,768]{1,0:T(8,128)(2,1)S(1)}) custom-call(bf16[144,768]{1,0:T(8,128)(2,1)} %get-tuple-element.88.refs_0_, bf16[144,768]{1,0:T(8,128)(2,1)S(1)} %collective-permute-done.29.refs_1_, bf16[768,768]{1,0:T(8,128)(2,1)S(1)} %pad_maximum_fusion.refs_2_.refs_4_.refs_10_, ...), custom_call_target="tpu_custom_call" | custom-call | flops 3680000000 | bytes 5160960 | tf_op jit(solution)/shard_map/attend_back/pallas_call | solution.py:52
  138.2 2.8 %collective-permute-start.23 = (bf16[64,768]{1,0:T(8,128)(2,1)S(1)}, bf16[64,768]{1,0:T(8,128)(2,1)S(1)}, u32[]{:S(2)}, u32[]{:S(2)}) collective-permute-start(bf16[64,768]{1,0:T(8,128)(2,1)S(1)} %get-tuple-element.119), channel_id=1, source_target_pairs={{0,4},{4,12},{8,0},{12,8},{1,5},{5,13},{9,1},{13,9},{2,6},{6,14},{... | collective-permute-start | bytes 294920 | tf_op jit(solution)/shard_map/ppermute | solution.py:368
  142.7 3.8 %attend_group.1 = (bf16[4,192,512]{2,1,0:T(8,128)(2,1)S(1)}, bf16[6,256,256]{2,1,0:T(8,128)(2,1)S(1)}) custom-call(bf16[128,768]{1,0:T(8,128)(2,1)S(1)} %broadcast_select_fusion.1.refs_0_, bf16[128,768]{1,0:T(8,128)(2,1)S(1)} %copy-done.20, bf16[128,768]{1,0:T(8,128)(2,1)S(1)} %copy-done.12, bf16[128,768]{1,0:T(8,128)(2,1)} %collective-permute-done.32.refs_3_, ...), custom_call_target="tpu_custom_call" | custom-call | flops 4600000000 | bytes 3592192 | tf_op jit(solution)/shard_map/attend_group/pallas_call | solution.py:52
  149.5 5.0 %collective-permute-done.33.refs_1_ = bf16[128,768]{1,0:T(8,128)(2,1)S(1)} collective-permute-done((bf16[128,768]{1,0:T(8,128)(2,1)S(1)}, bf16[128,768]{1,0:T(8,128)(2,1)S(1)}, u32[]{:S(2)}, u32[]{:S(2)}) %collective-permute-start.33) | collective-permute-done | bytes 196640 | tf_op jit(solution)/shard_map/ppermute | solution.py:368
  157.0 1.7 copy-done.8
  163.2 1.6 collective-permute-start.37
  164.9 5.5 %collective-permute-done.37.refs_0_ = bf16[128,768]{1,0:T(8,128)(2,1)S(1)} collective-permute-done((bf16[128,768]{1,0:T(8,128)(2,1)S(1)}, bf16[128,768]{1,0:T(8,128)(2,1)S(1)}, u32[]{:S(2)}, u32[]{:S(2)}) %collective-permute-start.37) | collective-permute-done | bytes 196640 | tf_op jit(solution)/shard_map/ppermute | solution.py:368
  172.4 4.8 %attend_back.3 = (f32[128,768]{1,0:T(8,128)S(1)}, bf16[128,768]{1,0:T(8,128)(2,1)S(1)}) custom-call(bf16[144,768]{1,0:T(8,128)(2,1)S(1)} %get-tuple-element.101.refs_0_.refs_4_, bf16[144,768]{1,0:T(8,128)(2,1)S(1)} %collective-permute-done.38.refs_1_.refs_5_, bf16[768,768]{1,0:T(8,128)(2,1)S(1)} %pad_maximum_fusion.refs_2_.refs_4_.refs_10_, ...), custom_call_target="tpu_custom_call" | custom-call | flops 3680000000 | bytes 5160960 | tf_op jit(solution)/shard_map/attend_back/pallas_call | solution.py:52
  180.2 5.0 %attend_grads.1.refs_1_ = bf16[784,768]{1,0:T(8,128)(2,1)} custom-call(bf16[128,768]{1,0:T(8,128)(2,1)S(1)} %copy-done.10, bf16[128,768]{1,0:T(8,128)(2,1)S(1)} %copy-done.21, bf16[128,768]{1,0:T(8,128)(2,1)S(1)} %copy-done.13, bf16[128,768]{1,0:T(8,128)(2,1)} %collective-permute-done.32.refs_3_, bf16[144,768]{1,0:T(8,128)(2,1)S(1)} %get-tuple-element.101.refs_0_.refs_4_, ...), custom_call_target="tpu_custom_call" | custom-call | flops 5750000128 | bytes 5627904 | tf_op jit(solution)/shard_map/attend_grads/pallas_call | solution.py:52
  185.2 6.2 %all-gather.7.cloned.1.call-done = bf16[8,128,768]{2,1,0:T(8,128)(2,1)} async-done(((bf16[2,128,768]{2,1,0:T(8,128)(2,1)}), bf16[8,128,768]{2,1,0:T(8,128)(2,1)}) %all-gather.7.cloned.1.call-update) | async-done | bytes 1572880 | tf_op jit(solution)/shard_map/all_gather | solution.py:499
  193.9 3.2 %collective-permute-done.39.refs_0_ = bf16[128,768]{1,0:T(8,128)(2,1)S(1)} collective-permute-done((bf16[128,768]{1,0:T(8,128)(2,1)S(1)}, bf16[128,768]{1,0:T(8,128)(2,1)S(1)}, u32[]{:S(2)}, u32[]{:S(2)}) %collective-permute-start.39) | collective-permute-done | bytes 196640 | tf_op jit(solution)/shard_map/ppermute | solution.py:368
  197.1 15.6 %feed_grads.1 = (f32[768,768]{1,0:T(8,128)}, f32[1,768]{1,0:T(1,128)}, f32[768,768]{1,0:T(8,128)}, f32[1,768]{1,0:T(1,128)}) custom-call(bf16[1024,768]{1,0:T(8,128)(2,1)} %bitcast.18.refs_6_.refs_0_, bf16[1024,768]{1,0:T(8,128)(2,1)} %bitcast.51, bf16[1024,768]{1,0:T(8,128)(2,1)} %bitcast.25.refs_2_, bf16[1024,768]{1,0:T(8,128)(2,1)} %bitcast.26.refs_3_, ...), custom_call_target="tpu_custom_call" | custom-call | flops 5750000128 | bytes 13424640 | tf_op jit(solution)/shard_map/feed_grads/pallas_call | solution.py:52
  212.7 1.7 copy-done.1
  215.3 2.8 %collective-permute-start.45 = (bf16[64,768]{1,0:T(8,128)(2,1)S(1)}, bf16[64,768]{1,0:T(8,128)(2,1)S(1)}, u32[]{:S(2)}, u32[]{:S(2)}) collective-permute-start(bf16[64,768]{1,0:T(8,128)(2,1)S(1)} %get-tuple-element.117), channel_id=1, source_target_pairs={{0,4},{4,12},{8,0},{12,8},{1,5},{5,13},{9,1},{13,9},{2,6},{6,14},{... | collective-permute-start | bytes 294920 | tf_op jit(solution)/shard_map/ppermute | solution.py:368
  218.8 3.1 %collective-permute-done.45 = bf16[64,768]{1,0:T(8,128)(2,1)S(1)} collective-permute-done((bf16[64,768]{1,0:T(8,128)(2,1)S(1)}, bf16[64,768]{1,0:T(8,128)(2,1)S(1)}, u32[]{:S(2)}, u32[]{:S(2)}) %collective-permute-start.45) | collective-permute-done | bytes 98336 | tf_op jit(solution)/shard_map/ppermute | solution.py:368
  222.6 29.3 %all-reduce.4.cloned.1.call-done.refs_0_ = bf16[784,768]{1,0:T(8,128)(2,1)} async-done(((bf16[784,768]{1,0:T(8,128)(2,1)}), bf16[784,768]{1,0:T(8,128)(2,1)}) %all-reduce.4.cloned.1.call-update) | async-done | bytes 1204240 | tf_op jit(solution)/shard_map/psum | solution.py:511
  (214 shorter events, 66.1 us)
Async XLA Ops:
  7.2 122.8 %all-gather.5.cloned.1.call-start = ((), (), s32[]{:S(2)}) async-start(), calls=%async_computation.1 | async-start | bytes 1966080 | tf_op jit(solution)/shard_map/all_gather | solution.py:476
  7.9 10.6 %collective-permute-start.3 = (bf16[2,768]{1,0:T(2,128)(2,1)S(1)}, bf16[2,768]{1,0:T(2,128)(2,1)S(1)}, u32[]{:S(2)}, u32[]{:S(2)}) collective-permute-start(bf16[2,768]{1,0:T(2,128)(2,1)S(1)} %pad.10), channel_id=1, source_target_pairs={{0,8},{4,12},{8,0},{12,4},{1,9},{5,13},{9,1},{13,5},{2,10},{6,14},... | collective-permute-start | bytes 9224 | tf_op jit(solution)/shard_map/ppermute | solution.py:368
  11.8 5.0 %collective-permute-start = (bf16[64,768]{1,0:T(8,128)(2,1)S(1)}, bf16[64,768]{1,0:T(8,128)(2,1)S(1)}, u32[]{:S(2)}, u32[]{:S(2)}) collective-permute-start(bf16[64,768]{1,0:T(8,128)(2,1)S(1)} %get-tuple-element.122), channel_id=1, source_target_pairs={{0,0},{4,8},{8,4},{12,12},{1,1},{5,9},{9,5},{13,13},{2,2},{6,10},{... | collective-permute-start | bytes 294920 | tf_op jit(solution)/shard_map/ppermute | solution.py:368
  12.5 4.7 %collective-permute-start.1 = (bf16[64,768]{1,0:T(8,128)(2,1)S(1)}, bf16[64,768]{1,0:T(8,128)(2,1)S(1)}, u32[]{:S(2)}, u32[]{:S(2)}) collective-permute-start(bf16[64,768]{1,0:T(8,128)(2,1)S(1)} %get-tuple-element.123), channel_id=1, source_target_pairs={{4,0},{12,4},{0,8},{8,12},{5,1},{13,5},{1,9},{9,13},{6,2},{14,6},{... | collective-permute-start | bytes 294920 | tf_op jit(solution)/shard_map/ppermute | solution.py:368
  16.4 27.6 %collective-permute-start.4 = (bf16[768,768]{1,0:T(8,128)(2,1)S(1)}, bf16[768,768]{1,0:T(8,128)(2,1)}, u32[]{:S(2)}, u32[]{:S(2)}) collective-permute-start(bf16[768,768]{1,0:T(8,128)(2,1)S(1)} %pad_maximum_fusion.refs_2_.refs_4_.refs_10_), channel_id=1, source_target_pairs={{0,8},{4,12},{8,0},{12,4},{1,9},{5,13},{9,1},{13,5},{2,10},{6,14},... | collective-permute-start | bytes 3538952 | tf_op jit(solution)/shard_map/ppermute | solution.py:368
  48.8 7.0 %collective-permute-start.6 = (bf16[128,768]{1,0:T(8,128)(2,1)S(1)}, bf16[128,768]{1,0:T(8,128)(2,1)S(1)}, u32[]{:S(2)}, u32[]{:S(2)}) collective-permute-start(bf16[128,768]{1,0:T(8,128)(2,1)S(1)} %first_norm.2.refs_0_), channel_id=1, source_target_pairs={{0,8},{4,12},{8,0},{12,4},{1,9},{5,13},{9,1},{13,5},{2,10},{6,14},... | collective-permute-start | bytes 589832 | tf_op jit(solution)/shard_map/ppermute | solution.py:368
  50.0 6.0 %collective-permute-start.7 = (bf16[128,768]{1,0:T(8,128)(2,1)S(1)}, bf16[128,768]{1,0:T(8,128)(2,1)S(1)}, u32[]{:S(2)}, u32[]{:S(2)}) collective-permute-start(bf16[128,768]{1,0:T(8,128)(2,1)S(1)} %first_norm.2.refs_0_), channel_id=1, source_target_pairs={{0,4},{4,0},{8,12},{12,8},{1,5},{5,1},{9,13},{13,9},{2,6},{6,2},{1... | collective-permute-start | bytes 589832 | tf_op jit(solution)/shard_map/ppermute | solution.py:368
  60.7 7.0 %collective-permute-start.10 = (bf16[128,768]{1,0:T(8,128)(2,1)S(1)}, bf16[128,768]{1,0:T(8,128)(2,1)S(1)}, u32[]{:S(2)}, u32[]{:S(2)}) collective-permute-start(bf16[128,768]{1,0:T(8,128)(2,1)S(1)} %get-tuple-element.68), channel_id=1, source_target_pairs={{0,8},{4,12},{8,0},{12,4},{1,9},{5,13},{9,1},{13,5},{2,10},{6,14},... | collective-permute-start | bytes 589832 | tf_op jit(solution)/shard_map/ppermute | solution.py:368
  67.9 6.2 %collective-permute-start.11 = (bf16[128,768]{1,0:T(8,128)(2,1)S(1)}, bf16[128,768]{1,0:T(8,128)(2,1)S(1)}, u32[]{:S(2)}, u32[]{:S(2)}) collective-permute-start(bf16[128,768]{1,0:T(8,128)(2,1)S(1)} %second_norm.2), channel_id=1, source_target_pairs={{0,16},{16,0},{1,17},{17,1},{2,18},{18,2},{3,19},{19,3},{4,20},{20... | collective-permute-start | bytes 589832 | tf_op jit(solution)/shard_map/ppermute | solution.py:480
  69.6 4.7 %collective-permute-start.13 = (bf16[64,768]{1,0:T(8,128)(2,1)S(1)}, bf16[64,768]{1,0:T(8,128)(2,1)S(1)}, u32[]{:S(2)}, u32[]{:S(2)}) collective-permute-start(bf16[64,768]{1,0:T(8,128)(2,1)S(1)} %get-tuple-element.120), channel_id=1, source_target_pairs={{0,0},{4,8},{8,4},{12,12},{1,1},{5,9},{9,5},{13,13},{2,2},{6,10},{... | collective-permute-start | bytes 294920 | tf_op jit(solution)/shard_map/ppermute | solution.py:368
  70.2 5.1 %collective-permute-start.14 = (bf16[64,768]{1,0:T(8,128)(2,1)S(1)}, bf16[64,768]{1,0:T(8,128)(2,1)S(1)}, u32[]{:S(2)}, u32[]{:S(2)}) collective-permute-start(bf16[64,768]{1,0:T(8,128)(2,1)S(1)} %get-tuple-element.121), channel_id=1, source_target_pairs={{4,0},{12,4},{0,8},{8,12},{5,1},{13,5},{1,9},{9,13},{6,2},{14,6},{... | collective-permute-start | bytes 294920 | tf_op jit(solution)/shard_map/ppermute | solution.py:368
  75.3 8.4 %collective-permute-start.16 = (bf16[128,768]{1,0:T(8,128)(2,1)S(1)}, bf16[128,768]{1,0:T(8,128)(2,1)S(1)}, u32[]{:S(2)}, u32[]{:S(2)}) collective-permute-start(bf16[128,768]{1,0:T(8,128)(2,1)S(1)} %broadcast_select_fusion.1.refs_0_), channel_id=1, source_target_pairs={{0,8},{4,12},{8,0},{12,4},{1,9},{5,13},{9,1},{13,5},{2,10},{6,14},... | collective-permute-start | bytes 589832 | tf_op jit(solution)/shard_map/ppermute | solution.py:368
  85.4 7.0 %collective-permute-start.17 = (bf16[128,768]{1,0:T(8,128)(2,1)S(1)}, bf16[128,768]{1,0:T(8,128)(2,1)S(1)}, u32[]{:S(2)}, u32[]{:S(2)}) collective-permute-start(bf16[128,768]{1,0:T(8,128)(2,1)S(1)} %get-tuple-element.72.refs_0_), channel_id=1, source_target_pairs={{0,8},{4,12},{8,0},{12,4},{1,9},{5,13},{9,1},{13,5},{2,10},{6,14},... | collective-permute-start | bytes 589832 | tf_op jit(solution)/shard_map/ppermute | solution.py:368
  85.5 8.0 %collective-permute-start.18 = (bf16[128,768]{1,0:T(8,128)(2,1)S(1)}, bf16[128,768]{1,0:T(8,128)(2,1)S(1)}, u32[]{:S(2)}, u32[]{:S(2)}) collective-permute-start(bf16[128,768]{1,0:T(8,128)(2,1)S(1)} %get-tuple-element.72.refs_0_), channel_id=1, source_target_pairs={{0,4},{4,0},{8,12},{12,8},{1,5},{5,1},{9,13},{13,9},{2,6},{6,2},{1... | collective-permute-start | bytes 589832 | tf_op jit(solution)/shard_map/ppermute | solution.py:368
  93.2 98.2 %all-gather.7.cloned.1.call-start = ((), (), s32[]{:S(2)}) async-start(), calls=%async_computation.2 | async-start | bytes 1966080 | tf_op jit(solution)/shard_map/all_gather | solution.py:499
  99.1 7.0 %collective-permute-start.21 = (bf16[128,768]{1,0:T(8,128)(2,1)S(1)}, bf16[128,768]{1,0:T(8,128)(2,1)S(1)}, u32[]{:S(2)}, u32[]{:S(2)}) collective-permute-start(bf16[128,768]{1,0:T(8,128)(2,1)S(1)} %get-tuple-element.75), channel_id=1, source_target_pairs={{0,8},{4,12},{8,0},{12,4},{1,9},{5,13},{9,1},{13,5},{2,10},{6,14},... | collective-permute-start | bytes 589832 | tf_op jit(solution)/shard_map/ppermute | solution.py:368
  106.7 6.3 %collective-permute-start.24 = (bf16[128,768]{1,0:T(8,128)(2,1)S(1)}, bf16[128,768]{1,0:T(8,128)(2,1)S(1)}, u32[]{:S(2)}, u32[]{:S(2)}) collective-permute-start(bf16[128,768]{1,0:T(8,128)(2,1)S(1)} %get-tuple-element.79.refs_0_), channel_id=1, source_target_pairs={{0,8},{4,12},{8,0},{12,4},{1,9},{5,13},{9,1},{13,5},{2,10},{6,14},... | collective-permute-start | bytes 589832 | tf_op jit(solution)/shard_map/ppermute | solution.py:368
  107.1 5.9 %collective-permute-start.25 = (bf16[128,768]{1,0:T(8,128)(2,1)S(1)}, bf16[128,768]{1,0:T(8,128)(2,1)S(1)}, u32[]{:S(2)}, u32[]{:S(2)}) collective-permute-start(bf16[128,768]{1,0:T(8,128)(2,1)S(1)} %get-tuple-element.79.refs_0_), channel_id=1, source_target_pairs={{0,4},{4,0},{8,12},{12,8},{1,5},{5,1},{9,13},{13,9},{2,6},{6,2},{1... | collective-permute-start | bytes 589832 | tf_op jit(solution)/shard_map/ppermute | solution.py:368
  117.9 7.0 %collective-permute-start.28 = (bf16[128,768]{1,0:T(8,128)(2,1)S(1)}, bf16[128,768]{1,0:T(8,128)(2,1)S(1)}, u32[]{:S(2)}, u32[]{:S(2)}) collective-permute-start(bf16[128,768]{1,0:T(8,128)(2,1)S(1)} %get-tuple-element.84), channel_id=1, source_target_pairs={{0,8},{4,12},{8,0},{12,4},{1,9},{5,13},{9,1},{13,5},{2,10},{6,14},... | collective-permute-start | bytes 589832 | tf_op jit(solution)/shard_map/ppermute | solution.py:368
  126.9 15.7 %collective-permute-start.32 = (bf16[128,768]{1,0:T(8,128)(2,1)S(1)}, bf16[128,768]{1,0:T(8,128)(2,1)}, u32[]{:S(2)}, u32[]{:S(2)}) collective-permute-start(bf16[128,768]{1,0:T(8,128)(2,1)S(1)} %collective-permute-done.16.refs_3_.refs_2_), channel_id=1, source_target_pairs={{0,4},{4,0},{8,12},{12,8},{1,5},{5,1},{9,13},{13,9},{2,6},{6,2},{1... | collective-permute-start | bytes 589832 | tf_op jit(solution)/shard_map/ppermute | solution.py:368
  137.2 3.8 %collective-permute-start.30 = (bf16[128,768]{1,0:T(8,128)(2,1)S(1)}, bf16[128,768]{1,0:T(8,128)(2,1)S(1)}, u32[]{:S(2)}, u32[]{:S(2)}) collective-permute-start(bf16[128,768]{1,0:T(8,128)(2,1)S(1)} %get-tuple-element.91), channel_id=1, source_target_pairs={{0,4},{4,0},{8,12},{12,8},{1,5},{5,1},{9,13},{13,9},{2,6},{6,2},{1... | collective-permute-start | bytes 589832 | tf_op jit(solution)/shard_map/ppermute | solution.py:368
  137.3 9.1 %collective-permute-start.22 = (bf16[64,768]{1,0:T(8,128)(2,1)S(1)}, bf16[64,768]{1,0:T(8,128)(2,1)S(1)}, u32[]{:S(2)}, u32[]{:S(2)}) collective-permute-start(bf16[64,768]{1,0:T(8,128)(2,1)S(1)} %get-tuple-element.118), channel_id=1, source_target_pairs={{0,0},{4,8},{8,4},{12,12},{1,1},{5,9},{9,5},{13,13},{2,2},{6,10},{... | collective-permute-start | bytes 294920 | tf_op jit(solution)/shard_map/ppermute | solution.py:368
  138.2 8.3 %collective-permute-start.23 = (bf16[64,768]{1,0:T(8,128)(2,1)S(1)}, bf16[64,768]{1,0:T(8,128)(2,1)S(1)}, u32[]{:S(2)}, u32[]{:S(2)}) collective-permute-start(bf16[64,768]{1,0:T(8,128)(2,1)S(1)} %get-tuple-element.119), channel_id=1, source_target_pairs={{0,4},{4,12},{8,0},{12,8},{1,5},{5,13},{9,1},{13,9},{2,6},{6,14},{... | collective-permute-start | bytes 294920 | tf_op jit(solution)/shard_map/ppermute | solution.py:368
  141.1 6.9 %collective-permute-start.31 = (bf16[128,768]{1,0:T(8,128)(2,1)S(1)}, bf16[128,768]{1,0:T(8,128)(2,1)S(1)}, u32[]{:S(2)}, u32[]{:S(2)}) collective-permute-start(bf16[128,768]{1,0:T(8,128)(2,1)S(1)} %entry_grad.2), channel_id=1, source_target_pairs={{0,16},{16,0},{1,17},{17,1},{2,18},{18,2},{3,19},{19,3},{4,20},{20... | collective-permute-start | bytes 589832 | tf_op jit(solution)/shard_map/ppermute | solution.py:493
  148.4 6.0 %collective-permute-start.33 = (bf16[128,768]{1,0:T(8,128)(2,1)S(1)}, bf16[128,768]{1,0:T(8,128)(2,1)S(1)}, u32[]{:S(2)}, u32[]{:S(2)}) collective-permute-start(bf16[128,768]{1,0:T(8,128)(2,1)S(1)} %get-tuple-element.94.refs_0_), channel_id=1, source_target_pairs={{0,8},{4,12},{8,0},{12,4},{1,9},{5,13},{9,1},{13,5},{2,10},{6,14},... | collective-permute-start | bytes 589832 | tf_op jit(solution)/shard_map/ppermute | solution.py:368
  163.2 7.1 %collective-permute-start.37 = (bf16[128,768]{1,0:T(8,128)(2,1)S(1)}, bf16[128,768]{1,0:T(8,128)(2,1)S(1)}, u32[]{:S(2)}, u32[]{:S(2)}) collective-permute-start(bf16[128,768]{1,0:T(8,128)(2,1)S(1)} %get-tuple-element.98), channel_id=1, source_target_pairs={{0,8},{4,12},{8,0},{12,4},{1,9},{5,13},{9,1},{13,5},{2,10},{6,14},... | collective-permute-start | bytes 589832 | tf_op jit(solution)/shard_map/ppermute | solution.py:368
  170.8 7.8 %collective-permute-start.40 = (bf16[144,768]{1,0:T(8,128)(2,1)S(1)}, bf16[144,768]{1,0:T(8,128)(2,1)S(1)}, u32[]{:S(2)}, u32[]{:S(2)}) collective-permute-start(bf16[144,768]{1,0:T(8,128)(2,1)S(1)} %get-tuple-element.101.refs_0_.refs_4_), channel_id=1, source_target_pairs={{0,8},{4,12},{8,0},{12,4},{1,9},{5,13},{9,1},{13,5},{2,10},{6,14},... | collective-permute-start | bytes 663560 | tf_op jit(solution)/shard_map/ppermute | solution.py:368
  178.7 18.3 %collective-permute-start.42 = (bf16[4,2,128,768]{3,2,1,0:T(8,128)(2,1)}, bf16[4,2,128,768]{3,2,1,0:T(8,128)(2,1)}, u32[]{:S(2)}, u32[]{:S(2)}) collective-permute-start(bf16[4,2,128,768]{3,2,1,0:T(8,128)(2,1)} %bitcast.24), channel_id=1, source_target_pairs={{0,4},{4,0},{8,12},{12,8},{1,5},{5,1},{9,13},{13,9},{2,6},{6,2},{1... | collective-permute-start | bytes 4718600 | tf_op jit(solution)/shard_map/ppermute | solution.py:368
  193.0 58.9 %all-reduce.4.cloned.1.call-start = ((), (), s32[]{:S(2)}) async-start(), calls=%async_computation | async-start | bytes 2408448 | tf_op jit(solution)/shard_map/psum | solution.py:511
  193.3 3.8 %collective-permute-start.43 = (bf16[4,2,128,768]{3,2,1,0:T(8,128)(2,1)S(1)}, bf16[4,2,128,768]{3,2,1,0:T(8,128)(2,1)}, u32[]{:S(2)}, u32[]{:S(2)}) collective-permute-start(bf16[4,2,128,768]{3,2,1,0:T(8,128)(2,1)S(1)} %gathered.1), channel_id=1, source_target_pairs={{0,4},{4,0},{8,12},{12,8},{1,5},{5,1},{9,13},{13,9},{2,6},{6,2},{1... | collective-permute-start | bytes 4718600 | tf_op jit(solution)/shard_map/ppermute | solution.py:368
  214.5 4.4 %collective-permute-start.44 = (bf16[64,768]{1,0:T(8,128)(2,1)S(1)}, bf16[64,768]{1,0:T(8,128)(2,1)S(1)}, u32[]{:S(2)}, u32[]{:S(2)}) collective-permute-start(bf16[64,768]{1,0:T(8,128)(2,1)S(1)} %get-tuple-element.116), channel_id=1, source_target_pairs={{0,0},{4,8},{8,4},{12,12},{1,1},{5,9},{9,5},{13,13},{2,2},{6,10},{... | collective-permute-start | bytes 294920 | tf_op jit(solution)/shard_map/ppermute | solution.py:368
  215.3 6.6 %collective-permute-start.45 = (bf16[64,768]{1,0:T(8,128)(2,1)S(1)}, bf16[64,768]{1,0:T(8,128)(2,1)S(1)}, u32[]{:S(2)}, u32[]{:S(2)}) collective-permute-start(bf16[64,768]{1,0:T(8,128)(2,1)S(1)} %get-tuple-element.117), channel_id=1, source_target_pairs={{0,4},{4,12},{8,0},{12,8},{1,5},{5,13},{9,1},{13,9},{2,6},{6,14},{... | collective-permute-start | bytes 294920 | tf_op jit(solution)/shard_map/ppermute | solution.py:368
  (59 other events, 548.4 us)
Sparse Core Ops, SparseCore 0:
  93.3 36.6 all-gather.4
  155.4 36.0 all-gather.6
  196.2 55.6 all-reduce.3

commit v6 on v5

--- a/solution.py
+++ b/solution.py
@@ -508,8 +508,8 @@
         mib=24,
     )[0]
     local_total = total
-    total = lax.psum(total, "dp")
-    grad_y = run(copy_kernel, [shape(grad_y.shape, bf16)], (grad_y,), 0, "gathered", after=(local_total,))[0]
+    grad_y, local_total = lax.optimization_barrier((grad_y, local_total))
+    total = lax.psum(local_total, "dp")
     grads_y = [item.reshape(-1, width) for item in (grad_y, swap(grad_y, beside))]
     args = (firsts[0], grads_y[0], firsts[1], grads_y[1], weights, table)
     outs = [

time: 262 us -> 260 us (level)
  waiting for transfers between devices: 136 us -> 133 us
    unnamed x85 -> x79, local copies, waits for them, and re-layouts: 13.6 us -> 14.7 us
    pallas_call x31 -> x30, Pallas kernels: 56 us -> 56.1 us  [run(): pl.pallas_call(body, out_shape=outs, grid_spec=pltpu.PrefetchScalarGridSp...]
  transfers between devices with their start and end apart: 49 -> 49, of which waited for: 33 -> 34; matrix products, arithmetic and copies ran while one was open for 2% -> 2% of each run, Pallas kernels for 18% -> 19%
where the time goes in v6:
time: 260 us; the launch traced here: 259 us
  waiting for transfers between devices  133 us (51%)
  Pallas kernels  56.1 us (22%)
  starting transfers between devices  35.3 us (14%)
  local copies, waits for them, and re-layouts  16 us (6%)
  between operations  14.5 us (6%)
  other arithmetic  4.79 us (2%)
    ppermute x44, waiting for transfers between devices, swap(): return lax.ppermute(value, 'tensor', pairs)  95.9 us
    pallas_call x30, Pallas kernels, run(): pl.pallas_call(body, out_shape=outs, grid_spec=pltpu.PrefetchScalarGridSp...  56.1 us
    ppermute x44, starting transfers between devices, swap(): return lax.ppermute(value, 'tensor', pairs)  31.6 us
    psum x1, waiting for transfers between devices, shards(): total = lax.psum(local_total, 'dp')  27.3 us
    unnamed x79, local copies, waits for them, and re-layouts  14.7 us
  transfers between devices with their start and end apart: 49, of which 34 were waited for; matrix products, arithmetic and copies ran while one was open for 2% of the time, Pallas kernels for 19%

profile of v6, /device:TPU:0, one launch (start us, length us, event | category | flops | bytes accessed | tf_op | source)
XLA Modules:
  0.0 259.3 jit_solution(10134082412043493744)
XLA Ops:
  7.9 2.9 %collective-permute-start.3 = (bf16[2,768]{1,0:T(2,128)(2,1)S(1)}, bf16[2,768]{1,0:T(2,128)(2,1)S(1)}, u32[]{:S(2)}, u32[]{:S(2)}) collective-permute-start(bf16[2,768]{1,0:T(2,128)(2,1)S(1)} %pad.10), channel_id=1, source_target_pairs={{0,8},{4,12},{8,0},{12,4},{1,9},{5,13},{9,1},{13,5},{2,10},{6,14},... | collective-permute-start | bytes 9224 | tf_op jit(solution)/shard_map/ppermute | solution.py:368
  12.5 2.4 collective-permute-start.1
  19.5 1.8 attend_own.1.refs_2_
  21.3 22.6 %collective-permute-done.4.refs_3_ = bf16[768,768]{1,0:T(8,128)(2,1)} collective-permute-done((bf16[768,768]{1,0:T(8,128)(2,1)S(1)}, bf16[768,768]{1,0:T(8,128)(2,1)}, u32[]{:S(2)}, u32[]{:S(2)}) %collective-permute-start.4) | collective-permute-done | bytes 1179680 | tf_op jit(solution)/shard_map/ppermute | solution.py:368
  43.9 3.2 %attend.2 = (f32[128,768]{1,0:T(8,128)S(1)}, bf16[128,768]{1,0:T(8,128)(2,1)S(1)}) custom-call(bf16[128,768]{1,0:T(8,128)(2,1)S(1)} %maximum_select_fusion.refs_0_, bf16[128,768]{1,0:T(8,128)(2,1)S(1)} %collective-permute-done.2.refs_1_, f32[256,768]{1,0:T(8,128)S(1)} %attend_own.1.refs_2_, bf16[768,768]{1,0:T(8,128)(2,1)} %collective-permute-done.4.refs_3_, ...), custom_call_target="tpu_custom_call" | custom-call | flops 3449999872 | bytes 3000320 | tf_op jit(solution)/shard_map/attend/pallas_call | solution.py:52
  50.0 5.8 %collective-permute-done.6.refs_1_ = bf16[128,768]{1,0:T(8,128)(2,1)S(1)} collective-permute-done((bf16[128,768]{1,0:T(8,128)(2,1)S(1)}, bf16[128,768]{1,0:T(8,128)(2,1)S(1)}, u32[]{:S(2)}, u32[]{:S(2)}) %collective-permute-start.6) | collective-permute-done | bytes 196640 | tf_op jit(solution)/shard_map/ppermute | solution.py:368
  61.9 5.8 %collective-permute-done.10.refs_0_ = bf16[128,768]{1,0:T(8,128)(2,1)S(1)} collective-permute-done((bf16[128,768]{1,0:T(8,128)(2,1)S(1)}, bf16[128,768]{1,0:T(8,128)(2,1)S(1)}, u32[]{:S(2)}, u32[]{:S(2)}) %collective-permute-start.10) | collective-permute-done | bytes 196640 | tf_op jit(solution)/shard_map/ppermute | solution.py:368
  70.2 2.5 collective-permute-start.14
  75.3 2.5 collective-permute-start.16
  77.9 4.7 %attend.3 = (f32[128,768]{1,0:T(8,128)S(1)}, bf16[128,768]{1,0:T(8,128)(2,1)S(1)}, bf16[2,3,448,256]{3,2,1,0:T(8,128)(2,1)S(1)}) custom-call(bf16[128,768]{1,0:T(8,128)(2,1)S(1)} %broadcast_select_fusion.1.refs_0_, bf16[128,768]{1,0:T(8,128)(2,1)S(1)} %collective-permute-done.12.refs_1_, bf16[768,768]{1,0:T(8,128)(2,1)S(1)} %pad_maximum_fusion.refs_2_.refs_4_.refs_10_, ...), custom_call_target="tpu_custom_call" | custom-call | flops 3449999872 | bytes 4769792 | tf_op jit(solution)/shard_map/attend/pallas_call | solution.py:52
  85.7 6.7 %collective-permute-done.17.refs_1_ = bf16[128,768]{1,0:T(8,128)(2,1)S(1)} collective-permute-done((bf16[128,768]{1,0:T(8,128)(2,1)S(1)}, bf16[128,768]{1,0:T(8,128)(2,1)S(1)}, u32[]{:S(2)}, u32[]{:S(2)}) %collective-permute-start.17) | collective-permute-done | bytes 196640 | tf_op jit(solution)/shard_map/ppermute | solution.py:368
  93.8 1.7 copy-done.4
  95.5 1.8 feed.3
  99.5 6.7 %collective-permute-done.21.refs_0_ = bf16[128,768]{1,0:T(8,128)(2,1)S(1)} collective-permute-done((bf16[128,768]{1,0:T(8,128)(2,1)S(1)}, bf16[128,768]{1,0:T(8,128)(2,1)S(1)}, u32[]{:S(2)}, u32[]{:S(2)}) %collective-permute-start.21) | collective-permute-done | bytes 196640 | tf_op jit(solution)/shard_map/ppermute | solution.py:368
  107.1 5.9 %collective-permute-done.24.refs_1_ = bf16[128,768]{1,0:T(8,128)(2,1)S(1)} collective-permute-done((bf16[128,768]{1,0:T(8,128)(2,1)S(1)}, bf16[128,768]{1,0:T(8,128)(2,1)S(1)}, u32[]{:S(2)}, u32[]{:S(2)}) %collective-permute-start.24) | collective-permute-done | bytes 196640 | tf_op jit(solution)/shard_map/ppermute | solution.py:368
  118.2 6.7 %collective-permute-done.28.refs_0_ = bf16[128,768]{1,0:T(8,128)(2,1)S(1)} collective-permute-done((bf16[128,768]{1,0:T(8,128)(2,1)S(1)}, bf16[128,768]{1,0:T(8,128)(2,1)S(1)}, u32[]{:S(2)}, u32[]{:S(2)}) %collective-permute-start.28) | collective-permute-done | bytes 196640 | tf_op jit(solution)/shard_map/ppermute | solution.py:368
  132.3 4.9 %attend_back.2 = (f32[128,768]{1,0:T(8,128)S(1)}, bf16[128,768]{1,0:T(8,128)(2,1)S(1)}) custom-call(bf16[144,768]{1,0:T(8,128)(2,1)} %get-tuple-element.90.refs_0_, bf16[144,768]{1,0:T(8,128)(2,1)S(1)} %collective-permute-done.29.refs_1_, bf16[768,768]{1,0:T(8,128)(2,1)S(1)} %pad_maximum_fusion.refs_2_.refs_4_.refs_10_, ...), custom_call_target="tpu_custom_call" | custom-call | flops 3680000000 | bytes 5160960 | tf_op jit(solution)/shard_map/attend_back/pallas_call | solution.py:52
  138.0 2.8 %collective-permute-start.23 = (bf16[64,768]{1,0:T(8,128)(2,1)S(1)}, bf16[64,768]{1,0:T(8,128)(2,1)S(1)}, u32[]{:S(2)}, u32[]{:S(2)}) collective-permute-start(bf16[64,768]{1,0:T(8,128)(2,1)S(1)} %get-tuple-element.123), channel_id=1, source_target_pairs={{0,4},{4,12},{8,0},{12,8},{1,5},{5,13},{9,1},{13,9},{2,6},{6,14},{... | collective-permute-start | bytes 294920 | tf_op jit(solution)/shard_map/ppermute | solution.py:368
  142.4 3.8 %attend_group.1 = (bf16[4,192,512]{2,1,0:T(8,128)(2,1)S(1)}, bf16[6,256,256]{2,1,0:T(8,128)(2,1)S(1)}) custom-call(bf16[128,768]{1,0:T(8,128)(2,1)S(1)} %broadcast_select_fusion.1.refs_0_, bf16[128,768]{1,0:T(8,128)(2,1)S(1)} %copy-done.16, bf16[128,768]{1,0:T(8,128)(2,1)S(1)} %copy-done.8, bf16[128,768]{1,0:T(8,128)(2,1)} %collective-permute-done.32.refs_3_, ...), custom_call_target="tpu_custom_call" | custom-call | flops 4600000000 | bytes 3592192 | tf_op jit(solution)/shard_map/attend_group/pallas_call | solution.py:52
  149.9 5.0 %collective-permute-done.33.refs_1_ = bf16[128,768]{1,0:T(8,128)(2,1)S(1)} collective-permute-done((bf16[128,768]{1,0:T(8,128)(2,1)S(1)}, bf16[128,768]{1,0:T(8,128)(2,1)S(1)}, u32[]{:S(2)}, u32[]{:S(2)}) %collective-permute-start.33) | collective-permute-done | bytes 196640 | tf_op jit(solution)/shard_map/ppermute | solution.py:368
  157.8 1.7 copy-done.6
  166.6 5.5 %collective-permute-done.37.refs_0_ = bf16[128,768]{1,0:T(8,128)(2,1)S(1)} collective-permute-done((bf16[128,768]{1,0:T(8,128)(2,1)S(1)}, bf16[128,768]{1,0:T(8,128)(2,1)S(1)}, u32[]{:S(2)}, u32[]{:S(2)}) %collective-permute-start.37) | collective-permute-done | bytes 196640 | tf_op jit(solution)/shard_map/ppermute | solution.py:368
  172.6 1.6 collective-permute-start.40
  174.2 4.8 %attend_back.3 = (f32[128,768]{1,0:T(8,128)S(1)}, bf16[128,768]{1,0:T(8,128)(2,1)S(1)}) custom-call(bf16[144,768]{1,0:T(8,128)(2,1)S(1)} %get-tuple-element.103.refs_0_.refs_4_, bf16[144,768]{1,0:T(8,128)(2,1)S(1)} %collective-permute-done.38.refs_1_.refs_5_, bf16[768,768]{1,0:T(8,128)(2,1)S(1)} %pad_maximum_fusion.refs_2_.refs_4_.refs_10_, ...), custom_call_target="tpu_custom_call" | custom-call | flops 3680000000 | bytes 5160960 | tf_op jit(solution)/shard_map/attend_back/pallas_call | solution.py:52
  182.0 5.0 %attend_grads.1 = bf16[784,768]{1,0:T(8,128)(2,1)} custom-call(bf16[128,768]{1,0:T(8,128)(2,1)S(1)} %broadcast_select_fusion.1.refs_0_, bf16[128,768]{1,0:T(8,128)(2,1)S(1)} %copy-done.17, bf16[128,768]{1,0:T(8,128)(2,1)S(1)} %copy-done.9, bf16[128,768]{1,0:T(8,128)(2,1)} %collective-permute-done.32.refs_3_, ...), custom_call_target="tpu_custom_call" | custom-call | flops 5750000128 | bytes 5627904 | tf_op jit(solution)/shard_map/attend_grads/pallas_call | solution.py:52
  187.0 4.9 %all-gather.7.cloned.1.call-done = bf16[8,128,768]{2,1,0:T(8,128)(2,1)} async-done(((bf16[2,128,768]{2,1,0:T(8,128)(2,1)}), bf16[8,128,768]{2,1,0:T(8,128)(2,1)}) %all-gather.7.cloned.1.call-update) | async-done | bytes 1572880 | tf_op jit(solution)/shard_map/all_gather | solution.py:499
  192.4 2.8 %collective-permute-done.39.refs_0_ = bf16[128,768]{1,0:T(8,128)(2,1)S(1)} collective-permute-done((bf16[128,768]{1,0:T(8,128)(2,1)S(1)}, bf16[128,768]{1,0:T(8,128)(2,1)S(1)}, u32[]{:S(2)}, u32[]{:S(2)}) %collective-permute-start.39) | collective-permute-done | bytes 196640 | tf_op jit(solution)/shard_map/ppermute | solution.py:368
  196.9 15.8 %feed_grads.1 = (f32[768,768]{1,0:T(8,128)}, f32[1,768]{1,0:T(1,128)}, f32[768,768]{1,0:T(8,128)}, f32[1,768]{1,0:T(1,128)}) custom-call(bf16[1024,768]{1,0:T(8,128)(2,1)} %bitcast.18.refs_6_.refs_0_, bf16[1024,768]{1,0:T(8,128)(2,1)} %bitcast.67, bf16[1024,768]{1,0:T(8,128)(2,1)} %bitcast.25.refs_2_, bf16[1024,768]{1,0:T(8,128)(2,1)} %bitcast.68, ...), custom_call_target="tpu_custom_call" | custom-call | flops 5750000128 | bytes 13424640 | tf_op jit(solution)/shard_map/feed_grads/pallas_call | solution.py:52
  212.8 1.7 copy-done.1
  215.3 2.8 %collective-permute-start.45 = (bf16[64,768]{1,0:T(8,128)(2,1)S(1)}, bf16[64,768]{1,0:T(8,128)(2,1)S(1)}, u32[]{:S(2)}, u32[]{:S(2)}) collective-permute-start(bf16[64,768]{1,0:T(8,128)(2,1)S(1)} %get-tuple-element.121), channel_id=1, source_target_pairs={{0,4},{4,12},{8,0},{12,8},{1,5},{5,13},{9,1},{13,9},{2,6},{6,14},{... | collective-permute-start | bytes 294920 | tf_op jit(solution)/shard_map/ppermute | solution.py:368
  218.8 3.1 %collective-permute-done.45 = bf16[64,768]{1,0:T(8,128)(2,1)S(1)} collective-permute-done((bf16[64,768]{1,0:T(8,128)(2,1)S(1)}, bf16[64,768]{1,0:T(8,128)(2,1)S(1)}, u32[]{:S(2)}, u32[]{:S(2)}) %collective-permute-start.45) | collective-permute-done | bytes 98336 | tf_op jit(solution)/shard_map/ppermute | solution.py:368
  222.6 27.3 %all-reduce.4.cloned.1.call-done.refs_0_ = bf16[784,768]{1,0:T(8,128)(2,1)} async-done(((bf16[784,768]{1,0:T(8,128)(2,1)}), bf16[784,768]{1,0:T(8,128)(2,1)}) %all-reduce.4.cloned.1.call-update) | async-done | bytes 1204240 | tf_op jit(solution)/shard_map/psum | solution.py:512
  (207 shorter events, 67.7 us)
Async XLA Ops:
  7.2 122.8 %all-gather.5.cloned.1.call-start = ((), (), s32[]{:S(2)}) async-start(), calls=%async_computation.1 | async-start | bytes 1966080 | tf_op jit(solution)/shard_map/all_gather | solution.py:476
  7.9 10.6 %collective-permute-start.3 = (bf16[2,768]{1,0:T(2,128)(2,1)S(1)}, bf16[2,768]{1,0:T(2,128)(2,1)S(1)}, u32[]{:S(2)}, u32[]{:S(2)}) collective-permute-start(bf16[2,768]{1,0:T(2,128)(2,1)S(1)} %pad.10), channel_id=1, source_target_pairs={{0,8},{4,12},{8,0},{12,4},{1,9},{5,13},{9,1},{13,5},{2,10},{6,14},... | collective-permute-start | bytes 9224 | tf_op jit(solution)/shard_map/ppermute | solution.py:368
  11.8 5.0 %collective-permute-start = (bf16[64,768]{1,0:T(8,128)(2,1)S(1)}, bf16[64,768]{1,0:T(8,128)(2,1)S(1)}, u32[]{:S(2)}, u32[]{:S(2)}) collective-permute-start(bf16[64,768]{1,0:T(8,128)(2,1)S(1)} %get-tuple-element.126), channel_id=1, source_target_pairs={{0,0},{4,8},{8,4},{12,12},{1,1},{5,9},{9,5},{13,13},{2,2},{6,10},{... | collective-permute-start | bytes 294920 | tf_op jit(solution)/shard_map/ppermute | solution.py:368
  12.5 4.7 %collective-permute-start.1 = (bf16[64,768]{1,0:T(8,128)(2,1)S(1)}, bf16[64,768]{1,0:T(8,128)(2,1)S(1)}, u32[]{:S(2)}, u32[]{:S(2)}) collective-permute-start(bf16[64,768]{1,0:T(8,128)(2,1)S(1)} %get-tuple-element.127), channel_id=1, source_target_pairs={{4,0},{12,4},{0,8},{8,12},{5,1},{13,5},{1,9},{9,13},{6,2},{14,6},{... | collective-permute-start | bytes 294920 | tf_op jit(solution)/shard_map/ppermute | solution.py:368
  16.4 27.6 %collective-permute-start.4 = (bf16[768,768]{1,0:T(8,128)(2,1)S(1)}, bf16[768,768]{1,0:T(8,128)(2,1)}, u32[]{:S(2)}, u32[]{:S(2)}) collective-permute-start(bf16[768,768]{1,0:T(8,128)(2,1)S(1)} %pad_maximum_fusion.refs_2_.refs_4_.refs_10_), channel_id=1, source_target_pairs={{0,8},{4,12},{8,0},{12,4},{1,9},{5,13},{9,1},{13,5},{2,10},{6,14},... | collective-permute-start | bytes 3538952 | tf_op jit(solution)/shard_map/ppermute | solution.py:368
  48.8 7.0 %collective-permute-start.6 = (bf16[128,768]{1,0:T(8,128)(2,1)S(1)}, bf16[128,768]{1,0:T(8,128)(2,1)S(1)}, u32[]{:S(2)}, u32[]{:S(2)}) collective-permute-start(bf16[128,768]{1,0:T(8,128)(2,1)S(1)} %first_norm.2.refs_0_), channel_id=1, source_target_pairs={{0,8},{4,12},{8,0},{12,4},{1,9},{5,13},{9,1},{13,5},{2,10},{6,14},... | collective-permute-start | bytes 589832 | tf_op jit(solution)/shard_map/ppermute | solution.py:368
  50.0 6.0 %collective-permute-start.7 = (bf16[128,768]{1,0:T(8,128)(2,1)S(1)}, bf16[128,768]{1,0:T(8,128)(2,1)S(1)}, u32[]{:S(2)}, u32[]{:S(2)}) collective-permute-start(bf16[128,768]{1,0:T(8,128)(2,1)S(1)} %first_norm.2.refs_0_), channel_id=1, source_target_pairs={{0,4},{4,0},{8,12},{12,8},{1,5},{5,1},{9,13},{13,9},{2,6},{6,2},{1... | collective-permute-start | bytes 589832 | tf_op jit(solution)/shard_map/ppermute | solution.py:368
  60.7 7.0 %collective-permute-start.10 = (bf16[128,768]{1,0:T(8,128)(2,1)S(1)}, bf16[128,768]{1,0:T(8,128)(2,1)S(1)}, u32[]{:S(2)}, u32[]{:S(2)}) collective-permute-start(bf16[128,768]{1,0:T(8,128)(2,1)S(1)} %get-tuple-element.70), channel_id=1, source_target_pairs={{0,8},{4,12},{8,0},{12,4},{1,9},{5,13},{9,1},{13,5},{2,10},{6,14},... | collective-permute-start | bytes 589832 | tf_op jit(solution)/shard_map/ppermute | solution.py:368
  67.9 6.2 %collective-permute-start.11 = (bf16[128,768]{1,0:T(8,128)(2,1)S(1)}, bf16[128,768]{1,0:T(8,128)(2,1)S(1)}, u32[]{:S(2)}, u32[]{:S(2)}) collective-permute-start(bf16[128,768]{1,0:T(8,128)(2,1)S(1)} %second_norm.2), channel_id=1, source_target_pairs={{0,16},{16,0},{1,17},{17,1},{2,18},{18,2},{3,19},{19,3},{4,20},{20... | collective-permute-start | bytes 589832 | tf_op jit(solution)/shard_map/ppermute | solution.py:480
  69.6 4.7 %collective-permute-start.13 = (bf16[64,768]{1,0:T(8,128)(2,1)S(1)}, bf16[64,768]{1,0:T(8,128)(2,1)S(1)}, u32[]{:S(2)}, u32[]{:S(2)}) collective-permute-start(bf16[64,768]{1,0:T(8,128)(2,1)S(1)} %get-tuple-element.124), channel_id=1, source_target_pairs={{0,0},{4,8},{8,4},{12,12},{1,1},{5,9},{9,5},{13,13},{2,2},{6,10},{... | collective-permute-start | bytes 294920 | tf_op jit(solution)/shard_map/ppermute | solution.py:368
  70.2 5.1 %collective-permute-start.14 = (bf16[64,768]{1,0:T(8,128)(2,1)S(1)}, bf16[64,768]{1,0:T(8,128)(2,1)S(1)}, u32[]{:S(2)}, u32[]{:S(2)}) collective-permute-start(bf16[64,768]{1,0:T(8,128)(2,1)S(1)} %get-tuple-element.125), channel_id=1, source_target_pairs={{4,0},{12,4},{0,8},{8,12},{5,1},{13,5},{1,9},{9,13},{6,2},{14,6},{... | collective-permute-start | bytes 294920 | tf_op jit(solution)/shard_map/ppermute | solution.py:368
  74.2 3.7 %collective-permute-start.12 = (bf16[128,768]{1,0:T(8,128)(2,1)S(1)}, bf16[128,768]{1,0:T(8,128)(2,1)S(1)}, u32[]{:S(2)}, u32[]{:S(2)}) collective-permute-start(bf16[128,768]{1,0:T(8,128)(2,1)S(1)} %broadcast_select_fusion.1.refs_0_), channel_id=1, source_target_pairs={{0,4},{4,0},{8,12},{12,8},{1,5},{5,1},{9,13},{13,9},{2,6},{6,2},{1... | collective-permute-start | bytes 589832 | tf_op jit(solution)/shard_map/ppermute | solution.py:368
  75.3 8.4 %collective-permute-start.16 = (bf16[128,768]{1,0:T(8,128)(2,1)S(1)}, bf16[128,768]{1,0:T(8,128)(2,1)S(1)}, u32[]{:S(2)}, u32[]{:S(2)}) collective-permute-start(bf16[128,768]{1,0:T(8,128)(2,1)S(1)} %broadcast_select_fusion.1.refs_0_), channel_id=1, source_target_pairs={{0,8},{4,12},{8,0},{12,4},{1,9},{5,13},{9,1},{13,5},{2,10},{6,14},... | collective-permute-start | bytes 589832 | tf_op jit(solution)/shard_map/ppermute | solution.py:368
  85.4 7.0 %collective-permute-start.17 = (bf16[128,768]{1,0:T(8,128)(2,1)S(1)}, bf16[128,768]{1,0:T(8,128)(2,1)S(1)}, u32[]{:S(2)}, u32[]{:S(2)}) collective-permute-start(bf16[128,768]{1,0:T(8,128)(2,1)S(1)} %get-tuple-element.74.refs_0_), channel_id=1, source_target_pairs={{0,8},{4,12},{8,0},{12,4},{1,9},{5,13},{9,1},{13,5},{2,10},{6,14},... | collective-permute-start | bytes 589832 | tf_op jit(solution)/shard_map/ppermute | solution.py:368
  85.5 8.0 %collective-permute-start.18 = (bf16[128,768]{1,0:T(8,128)(2,1)S(1)}, bf16[128,768]{1,0:T(8,128)(2,1)S(1)}, u32[]{:S(2)}, u32[]{:S(2)}) collective-permute-start(bf16[128,768]{1,0:T(8,128)(2,1)S(1)} %get-tuple-element.74.refs_0_), channel_id=1, source_target_pairs={{0,4},{4,0},{8,12},{12,8},{1,5},{5,1},{9,13},{13,9},{2,6},{6,2},{1... | collective-permute-start | bytes 589832 | tf_op jit(solution)/shard_map/ppermute | solution.py:368
  93.2 98.7 %all-gather.7.cloned.1.call-start = ((), (), s32[]{:S(2)}) async-start(), calls=%async_computation.2 | async-start | bytes 1966080 | tf_op jit(solution)/shard_map/all_gather | solution.py:499
  99.1 7.0 %collective-permute-start.21 = (bf16[128,768]{1,0:T(8,128)(2,1)S(1)}, bf16[128,768]{1,0:T(8,128)(2,1)S(1)}, u32[]{:S(2)}, u32[]{:S(2)}) collective-permute-start(bf16[128,768]{1,0:T(8,128)(2,1)S(1)} %get-tuple-element.77), channel_id=1, source_target_pairs={{0,8},{4,12},{8,0},{12,4},{1,9},{5,13},{9,1},{13,5},{2,10},{6,14},... | collective-permute-start | bytes 589832 | tf_op jit(solution)/shard_map/ppermute | solution.py:368
  106.7 6.3 %collective-permute-start.24 = (bf16[128,768]{1,0:T(8,128)(2,1)S(1)}, bf16[128,768]{1,0:T(8,128)(2,1)S(1)}, u32[]{:S(2)}, u32[]{:S(2)}) collective-permute-start(bf16[128,768]{1,0:T(8,128)(2,1)S(1)} %get-tuple-element.81.refs_0_), channel_id=1, source_target_pairs={{0,8},{4,12},{8,0},{12,4},{1,9},{5,13},{9,1},{13,5},{2,10},{6,14},... | collective-permute-start | bytes 589832 | tf_op jit(solution)/shard_map/ppermute | solution.py:368
  107.1 5.9 %collective-permute-start.25 = (bf16[128,768]{1,0:T(8,128)(2,1)S(1)}, bf16[128,768]{1,0:T(8,128)(2,1)S(1)}, u32[]{:S(2)}, u32[]{:S(2)}) collective-permute-start(bf16[128,768]{1,0:T(8,128)(2,1)S(1)} %get-tuple-element.81.refs_0_), channel_id=1, source_target_pairs={{0,4},{4,0},{8,12},{12,8},{1,5},{5,1},{9,13},{13,9},{2,6},{6,2},{1... | collective-permute-start | bytes 589832 | tf_op jit(solution)/shard_map/ppermute | solution.py:368
  117.9 7.0 %collective-permute-start.28 = (bf16[128,768]{1,0:T(8,128)(2,1)S(1)}, bf16[128,768]{1,0:T(8,128)(2,1)S(1)}, u32[]{:S(2)}, u32[]{:S(2)}) collective-permute-start(bf16[128,768]{1,0:T(8,128)(2,1)S(1)} %get-tuple-element.86), channel_id=1, source_target_pairs={{0,8},{4,12},{8,0},{12,4},{1,9},{5,13},{9,1},{13,5},{2,10},{6,14},... | collective-permute-start | bytes 589832 | tf_op jit(solution)/shard_map/ppermute | solution.py:368
  126.9 15.5 %collective-permute-start.32 = (bf16[128,768]{1,0:T(8,128)(2,1)S(1)}, bf16[128,768]{1,0:T(8,128)(2,1)}, u32[]{:S(2)}, u32[]{:S(2)}) collective-permute-start(bf16[128,768]{1,0:T(8,128)(2,1)S(1)} %collective-permute-done.16.refs_3_.refs_2_), channel_id=1, source_target_pairs={{0,4},{4,0},{8,12},{12,8},{1,5},{5,1},{9,13},{13,9},{2,6},{6,2},{1... | collective-permute-start | bytes 589832 | tf_op jit(solution)/shard_map/ppermute | solution.py:368
  137.3 8.9 %collective-permute-start.22 = (bf16[64,768]{1,0:T(8,128)(2,1)S(1)}, bf16[64,768]{1,0:T(8,128)(2,1)S(1)}, u32[]{:S(2)}, u32[]{:S(2)}) collective-permute-start(bf16[64,768]{1,0:T(8,128)(2,1)S(1)} %get-tuple-element.122), channel_id=1, source_target_pairs={{0,0},{4,8},{8,4},{12,12},{1,1},{5,9},{9,5},{13,13},{2,2},{6,10},{... | collective-permute-start | bytes 294920 | tf_op jit(solution)/shard_map/ppermute | solution.py:368
  138.0 8.3 %collective-permute-start.23 = (bf16[64,768]{1,0:T(8,128)(2,1)S(1)}, bf16[64,768]{1,0:T(8,128)(2,1)S(1)}, u32[]{:S(2)}, u32[]{:S(2)}) collective-permute-start(bf16[64,768]{1,0:T(8,128)(2,1)S(1)} %get-tuple-element.123), channel_id=1, source_target_pairs={{0,4},{4,12},{8,0},{12,8},{1,5},{5,13},{9,1},{13,9},{2,6},{6,14},{... | collective-permute-start | bytes 294920 | tf_op jit(solution)/shard_map/ppermute | solution.py:368
  140.9 6.9 %collective-permute-start.31 = (bf16[128,768]{1,0:T(8,128)(2,1)S(1)}, bf16[128,768]{1,0:T(8,128)(2,1)S(1)}, u32[]{:S(2)}, u32[]{:S(2)}) collective-permute-start(bf16[128,768]{1,0:T(8,128)(2,1)S(1)} %entry_grad.2), channel_id=1, source_target_pairs={{0,16},{16,0},{1,17},{17,1},{2,18},{18,2},{3,19},{19,3},{4,20},{20... | collective-permute-start | bytes 589832 | tf_op jit(solution)/shard_map/ppermute | solution.py:493
  148.9 6.0 %collective-permute-start.33 = (bf16[128,768]{1,0:T(8,128)(2,1)S(1)}, bf16[128,768]{1,0:T(8,128)(2,1)S(1)}, u32[]{:S(2)}, u32[]{:S(2)}) collective-permute-start(bf16[128,768]{1,0:T(8,128)(2,1)S(1)} %get-tuple-element.96.refs_0_), channel_id=1, source_target_pairs={{0,8},{4,12},{8,0},{12,4},{1,9},{5,13},{9,1},{13,5},{2,10},{6,14},... | collective-permute-start | bytes 589832 | tf_op jit(solution)/shard_map/ppermute | solution.py:368
  155.7 94.3 %all-reduce.4.cloned.1.call-start = ((), (), s32[]{:S(2)}) async-start(), calls=%async_computation | async-start | bytes 2408448 | tf_op jit(solution)/shard_map/psum | solution.py:512
  165.0 7.1 %collective-permute-start.37 = (bf16[128,768]{1,0:T(8,128)(2,1)S(1)}, bf16[128,768]{1,0:T(8,128)(2,1)S(1)}, u32[]{:S(2)}, u32[]{:S(2)}) collective-permute-start(bf16[128,768]{1,0:T(8,128)(2,1)S(1)} %get-tuple-element.100), channel_id=1, source_target_pairs={{0,8},{4,12},{8,0},{12,4},{1,9},{5,13},{9,1},{13,5},{2,10},{6,14},... | collective-permute-start | bytes 589832 | tf_op jit(solution)/shard_map/ppermute | solution.py:368
  172.6 7.8 %collective-permute-start.40 = (bf16[144,768]{1,0:T(8,128)(2,1)S(1)}, bf16[144,768]{1,0:T(8,128)(2,1)S(1)}, u32[]{:S(2)}, u32[]{:S(2)}) collective-permute-start(bf16[144,768]{1,0:T(8,128)(2,1)S(1)} %get-tuple-element.103.refs_0_.refs_4_), channel_id=1, source_target_pairs={{0,8},{4,12},{8,0},{12,4},{1,9},{5,13},{9,1},{13,5},{2,10},{6,14},... | collective-permute-start | bytes 663560 | tf_op jit(solution)/shard_map/ppermute | solution.py:368
  180.5 14.8 %collective-permute-start.42 = (bf16[4,2,128,768]{3,2,1,0:T(8,128)(2,1)}, bf16[4,2,128,768]{3,2,1,0:T(8,128)(2,1)}, u32[]{:S(2)}, u32[]{:S(2)}) collective-permute-start(bf16[4,2,128,768]{3,2,1,0:T(8,128)(2,1)} %bitcast.24), channel_id=1, source_target_pairs={{0,4},{4,0},{8,12},{12,8},{1,5},{5,1},{9,13},{13,9},{2,6},{6,2},{1... | collective-permute-start | bytes 4718600 | tf_op jit(solution)/shard_map/ppermute | solution.py:368
  191.9 3.9 %collective-permute-start.43 = (bf16[4,2,128,768]{3,2,1,0:T(8,128)(2,1)}, bf16[4,2,128,768]{3,2,1,0:T(8,128)(2,1)S(1)}, u32[]{:S(2)}, u32[]{:S(2)}) collective-permute-start(bf16[4,2,128,768]{3,2,1,0:T(8,128)(2,1)} %bitcast.66), channel_id=1, source_target_pairs={{0,4},{4,0},{8,12},{12,8},{1,5},{5,1},{9,13},{13,9},{2,6},{6,2},{1... | collective-permute-start | bytes 4718600 | tf_op jit(solution)/shard_map/ppermute | solution.py:368
  214.5 4.3 %collective-permute-start.44 = (bf16[64,768]{1,0:T(8,128)(2,1)S(1)}, bf16[64,768]{1,0:T(8,128)(2,1)S(1)}, u32[]{:S(2)}, u32[]{:S(2)}) collective-permute-start(bf16[64,768]{1,0:T(8,128)(2,1)S(1)} %get-tuple-element.120), channel_id=1, source_target_pairs={{0,0},{4,8},{8,4},{12,12},{1,1},{5,9},{9,5},{13,13},{2,2},{6,10},{... | collective-permute-start | bytes 294920 | tf_op jit(solution)/shard_map/ppermute | solution.py:368
  215.3 6.6 %collective-permute-start.45 = (bf16[64,768]{1,0:T(8,128)(2,1)S(1)}, bf16[64,768]{1,0:T(8,128)(2,1)S(1)}, u32[]{:S(2)}, u32[]{:S(2)}) collective-permute-start(bf16[64,768]{1,0:T(8,128)(2,1)S(1)} %get-tuple-element.121), channel_id=1, source_target_pairs={{0,4},{4,12},{8,0},{12,8},{1,5},{5,13},{9,1},{13,9},{2,6},{6,14},{... | collective-permute-start | bytes 294920 | tf_op jit(solution)/shard_map/ppermute | solution.py:368
  (56 other events, 466.8 us)
Sparse Core Ops, SparseCore 0:
  93.3 36.6 all-gather.4
  155.8 36.0 all-gather.6
  194.3 55.6 all-reduce.3

commit v7 on v6

--- a/solution.py
+++ b/solution.py
@@ -485,11 +485,11 @@
     entries = (entry, swap(entry, beside), entry_far, swap(entry_far, beside))
 
     firsts = [item.reshape(-1, width) for item in gather(jnp.stack(first_pair))]
-    grad = backward(cotangent, saved, later=(firsts[0],))[0]
+    grad = backward(cotangent, saved)[0]
     layer_output = blocks_of(output)
     args = (*entries, w_own, table, seg_both[:, None, :], seg_both[:, :, None])
     outs = [shape((4, local, 2 * length), bf16), shape((2 * heads, length, length), bf16)]
-    attended = run(attend_group_kernel, outs, args, 4.0, "attend_group", mib=24)
+    attended = run(attend_group_kernel, outs, args, 4.0, "attend_group", mib=24, after=(firsts[0],))
     middle = lax.ppermute(grad, "section", sections)
     grad_entry, grad_y, branch, near, token = backward(
         jnp.where(section == 1, cotangent, middle), saved, (layer_output, attended[0])

time: 260 us -> 258 us (level)
  Pallas kernels: 56.1 us -> 50.1 us
  other arithmetic: 4.79 us -> 8.7 us
  local copies, waits for them, and re-layouts: 16 us -> 19 us
    pallas_call x30, Pallas kernels: 56.1 us -> 50.1 us  [run(): pl.pallas_call(body, out_shape=outs, grid_spec=pltpu.PrefetchScalarGridSp...]
    unnamed x79 -> x91, local copies, waits for them, and re-layouts: 14.7 us -> 17.6 us
    all_gather x1, waiting for transfers between devices: 4.88 us -> 7.56 us  [shards(): grad_y = lax.all_gather(grad_y, 'dp') if wide else grad_y[None]]
  transfers between devices with their start and end apart: 49 -> 49, of which waited for: 34 -> 33; matrix products, arithmetic and copies ran while one was open for 2% -> 3% of each run, Pallas kernels for 19% -> 16%
where the time goes in v7:
time: 258 us
  waiting for transfers between devices  132 us (51%)
  Pallas kernels  50.1 us (19%)
  starting transfers between devices  33.5 us (13%)
  local copies, waits for them, and re-layouts  19 us (7%)
  between operations  14.5 us (6%)
  other arithmetic  8.7 us (3%)
    ppermute x44, waiting for transfers between devices, swap(): return lax.ppermute(value, 'tensor', pairs)  96.2 us
    pallas_call x30, Pallas kernels, run(): pl.pallas_call(body, out_shape=outs, grid_spec=pltpu.PrefetchScalarGridSp...  50.1 us
    ppermute x44, starting transfers between devices, swap(): return lax.ppermute(value, 'tensor', pairs)  31 us
    psum x1, waiting for transfers between devices, shards(): total = lax.psum(local_total, 'dp')  27.4 us
    unnamed x91, local copies, waits for them, and re-layouts  17.6 us
    all_gather x1, waiting for transfers between devices, shards(): grad_y = lax.all_gather(grad_y, 'dp') if wide else grad_y[None]  7.56 us
  transfers between devices with their start and end apart: 49, of which 33 were waited for; matrix products, arithmetic and copies ran while one was open for 3% of the time, Pallas kernels for 16%

profile of v7, /device:TPU:0, one launch (start us, length us, event | category | flops | bytes accessed | tf_op | source)
XLA Modules:
  0.0 257.8 jit_solution(14752922005876183951)
XLA Ops:
  7.9 2.9 %collective-permute-start.3 = (bf16[2,768]{1,0:T(2,128)(2,1)S(1)}, bf16[2,768]{1,0:T(2,128)(2,1)S(1)}, u32[]{:S(2)}, u32[]{:S(2)}) collective-permute-start(bf16[2,768]{1,0:T(2,128)(2,1)S(1)} %pad.10), channel_id=1, source_target_pairs={{0,8},{4,12},{8,0},{12,4},{1,9},{5,13},{9,1},{13,5},{2,10},{6,14},... | collective-permute-start | bytes 9224 | tf_op jit(solution)/shard_map/ppermute | solution.py:368
  12.5 2.4 collective-permute-start.1
  19.5 1.8 attend_own.1.refs_2_
  21.3 22.5 %collective-permute-done.4.refs_3_ = bf16[768,768]{1,0:T(8,128)(2,1)S(1)} collective-permute-done((bf16[768,768]{1,0:T(8,128)(2,1)S(1)}, bf16[768,768]{1,0:T(8,128)(2,1)S(1)}, u32[]{:S(2)}, u32[]{:S(2)}) %collective-permute-start.4) | collective-permute-done | bytes 1179680 | tf_op jit(solution)/shard_map/ppermute | solution.py:368
  43.8 1.8 attend.2
  48.6 5.8 %collective-permute-done.6.refs_1_ = bf16[128,768]{1,0:T(8,128)(2,1)S(1)} collective-permute-done((bf16[128,768]{1,0:T(8,128)(2,1)S(1)}, bf16[128,768]{1,0:T(8,128)(2,1)S(1)}, u32[]{:S(2)}, u32[]{:S(2)}) %collective-permute-start.6) | collective-permute-done | bytes 196640 | tf_op jit(solution)/shard_map/ppermute | solution.py:368
  60.4 5.8 %collective-permute-done.10.refs_0_ = bf16[128,768]{1,0:T(8,128)(2,1)S(1)} collective-permute-done((bf16[128,768]{1,0:T(8,128)(2,1)S(1)}, bf16[128,768]{1,0:T(8,128)(2,1)S(1)}, u32[]{:S(2)}, u32[]{:S(2)}) %collective-permute-start.10) | collective-permute-done | bytes 196640 | tf_op jit(solution)/shard_map/ppermute | solution.py:368
  72.9 1.8 collective-permute-done.14
  74.7 2.5 collective-permute-start.16
  77.3 3.4 %attend.3 = (f32[128,768]{1,0:T(8,128)S(1)}, bf16[128,768]{1,0:T(8,128)(2,1)S(1)}, bf16[2,3,448,256]{3,2,1,0:T(8,128)(2,1)S(1)}) custom-call(bf16[128,768]{1,0:T(8,128)(2,1)S(1)} %broadcast_select_fusion.1.refs_0_, bf16[128,768]{1,0:T(8,128)(2,1)S(1)} %collective-permute-done.12.refs_1_, bf16[768,768]{1,0:T(8,128)(2,1)S(1)} %pad_maximum_fusion.refs_2_.refs_4_.refs_10_, ...), custom_call_target="tpu_custom_call" | custom-call | flops 3449999872 | bytes 4769792 | tf_op jit(solution)/shard_map/attend/pallas_call | solution.py:52
  83.7 6.7 %collective-permute-done.17.refs_1_ = bf16[128,768]{1,0:T(8,128)(2,1)S(1)} collective-permute-done((bf16[128,768]{1,0:T(8,128)(2,1)S(1)}, bf16[128,768]{1,0:T(8,128)(2,1)S(1)}, u32[]{:S(2)}, u32[]{:S(2)}) %collective-permute-start.17) | collective-permute-done | bytes 196640 | tf_op jit(solution)/shard_map/ppermute | solution.py:368
  96.7 6.7 %collective-permute-done.21.refs_0_ = bf16[128,768]{1,0:T(8,128)(2,1)S(1)} collective-permute-done((bf16[128,768]{1,0:T(8,128)(2,1)S(1)}, bf16[128,768]{1,0:T(8,128)(2,1)S(1)}, u32[]{:S(2)}, u32[]{:S(2)}) %collective-permute-start.21) | collective-permute-done | bytes 196640 | tf_op jit(solution)/shard_map/ppermute | solution.py:368
  104.3 5.8 %collective-permute-done.24.refs_1_ = bf16[128,768]{1,0:T(8,128)(2,1)S(1)} collective-permute-done((bf16[128,768]{1,0:T(8,128)(2,1)S(1)}, bf16[128,768]{1,0:T(8,128)(2,1)S(1)}, u32[]{:S(2)}, u32[]{:S(2)}) %collective-permute-start.24) | collective-permute-done | bytes 196640 | tf_op jit(solution)/shard_map/ppermute | solution.py:368
  112.7 2.3 feed_back.2
  115.1 1.8 collective-permute-done.27.refs_0_
  117.4 6.7 %collective-permute-done.28.refs_0_ = bf16[128,768]{1,0:T(8,128)(2,1)S(1)} collective-permute-done((bf16[128,768]{1,0:T(8,128)(2,1)S(1)}, bf16[128,768]{1,0:T(8,128)(2,1)S(1)}, u32[]{:S(2)}, u32[]{:S(2)}) %collective-permute-start.28) | collective-permute-done | bytes 196640 | tf_op jit(solution)/shard_map/ppermute | solution.py:368
  128.3 4.1 %attend_back.2 = (f32[128,768]{1,0:T(8,128)S(1)}, bf16[128,768]{1,0:T(8,128)(2,1)}) custom-call(bf16[144,768]{1,0:T(8,128)(2,1)S(1)} %get-tuple-element.90.refs_0_, bf16[144,768]{1,0:T(8,128)(2,1)S(1)} %collective-permute-done.29.refs_1_, bf16[768,768]{1,0:T(8,128)(2,1)S(1)} %pad_maximum_fusion.refs_2_.refs_4_.refs_10_, bf16[768,768]{1,0:T(8,128)(2,1)S(1)} %copy-done.17, ...), custom_call_target="tpu_custom_call" | custom-call | flops 3680000000 | bytes 5160960 | tf_op jit(solution)/shard_map/attend_back/pallas_call | solution.py:52
  139.6 2.8 %attend_group.1 = (bf16[4,192,512]{2,1,0:T(8,128)(2,1)S(1)}, bf16[6,256,256]{2,1,0:T(8,128)(2,1)S(1)}) custom-call(bf16[128,768]{1,0:T(8,128)(2,1)S(1)} %copy-done.10, bf16[128,768]{1,0:T(8,128)(2,1)S(1)} %copy-done.22, bf16[128,768]{1,0:T(8,128)(2,1)S(1)} %copy-done.13, bf16[128,768]{1,0:T(8,128)(2,1)S(1)} %copy-done.25, ...), custom_call_target="tpu_custom_call" | custom-call | flops 4600000000 | bytes 3592192 | tf_op jit(solution)/shard_map/attend_group/pallas_call | solution.py:52
  144.7 1.8 collective-permute-start.33
  146.5 5.1 %collective-permute-done.33.refs_1_ = bf16[128,768]{1,0:T(8,128)(2,1)S(1)} collective-permute-done((bf16[128,768]{1,0:T(8,128)(2,1)S(1)}, bf16[128,768]{1,0:T(8,128)(2,1)S(1)}, u32[]{:S(2)}, u32[]{:S(2)}) %collective-permute-start.33) | collective-permute-done | bytes 196640 | tf_op jit(solution)/shard_map/ppermute | solution.py:368
  161.8 1.8 collective-permute-start.37
  163.6 5.3 %collective-permute-done.37.refs_0_ = bf16[128,768]{1,0:T(8,128)(2,1)S(1)} collective-permute-done((bf16[128,768]{1,0:T(8,128)(2,1)S(1)}, bf16[128,768]{1,0:T(8,128)(2,1)S(1)}, u32[]{:S(2)}, u32[]{:S(2)}) %collective-permute-start.37) | collective-permute-done | bytes 196640 | tf_op jit(solution)/shard_map/ppermute | solution.py:368
  169.3 1.8 collective-permute-start.40
  171.2 3.4 %attend_back.3 = (f32[128,768]{1,0:T(8,128)S(1)}, bf16[128,768]{1,0:T(8,128)(2,1)S(1)}) custom-call(bf16[144,768]{1,0:T(8,128)(2,1)S(1)} %get-tuple-element.103.refs_0_.refs_4_, bf16[144,768]{1,0:T(8,128)(2,1)S(1)} %collective-permute-done.38.refs_1_.refs_5_, bf16[768,768]{1,0:T(8,128)(2,1)S(1)} %pad_maximum_fusion.refs_2_.refs_4_.refs_10_, ...), custom_call_target="tpu_custom_call" | custom-call | flops 3680000000 | bytes 5160960 | tf_op jit(solution)/shard_map/attend_back/pallas_call | solution.py:52
  174.6 2.5 collective-permute-done.40.refs_0_
  178.7 4.1 %attend_grads.1 = bf16[784,768]{1,0:T(8,128)(2,1)} custom-call(bf16[128,768]{1,0:T(8,128)(2,1)S(1)} %copy-done.11, bf16[128,768]{1,0:T(8,128)(2,1)S(1)} %copy-done.23, bf16[128,768]{1,0:T(8,128)(2,1)S(1)} %copy-done.14, bf16[128,768]{1,0:T(8,128)(2,1)S(1)} %copy-done.26, bf16[144,768]{1,0:T(8,128)(2,1)S(1)} %get-tuple-element.103.refs_0_.refs_4_, ...), custom_call_target="tpu_custom_call" | custom-call | flops 5750000128 | bytes 5627904 | tf_op jit(solution)/shard_map/attend_grads/pallas_call | solution.py:52
  182.8 7.6 %all-gather.7.cloned.1.call-done = bf16[8,128,768]{2,1,0:T(8,128)(2,1)} async-done(((bf16[2,128,768]{2,1,0:T(8,128)(2,1)}), bf16[8,128,768]{2,1,0:T(8,128)(2,1)}) %all-gather.7.cloned.1.call-update) | async-done | bytes 1572880 | tf_op jit(solution)/shard_map/all_gather | solution.py:499
  190.9 2.8 %collective-permute-done.39.refs_0_ = bf16[128,768]{1,0:T(8,128)(2,1)S(1)} collective-permute-done((bf16[128,768]{1,0:T(8,128)(2,1)S(1)}, bf16[128,768]{1,0:T(8,128)(2,1)S(1)}, u32[]{:S(2)}, u32[]{:S(2)}) %collective-permute-start.39) | collective-permute-done | bytes 196640 | tf_op jit(solution)/shard_map/ppermute | solution.py:368
  195.4 15.8 %feed_grads.1 = (f32[768,768]{1,0:T(8,128)}, f32[1,768]{1,0:T(1,128)}, f32[768,768]{1,0:T(8,128)}, f32[1,768]{1,0:T(1,128)}) custom-call(bf16[1024,768]{1,0:T(8,128)(2,1)} %bitcast.21.refs_8_.refs_0_, bf16[1024,768]{1,0:T(8,128)(2,1)} %bitcast.63, bf16[1024,768]{1,0:T(8,128)(2,1)} %bitcast.25.refs_2_, bf16[1024,768]{1,0:T(8,128)(2,1)} %bitcast.64, ...), custom_call_target="tpu_custom_call" | custom-call | flops 5750000128 | bytes 13424640 | tf_op jit(solution)/shard_map/feed_grads/pallas_call | solution.py:52
  213.8 2.8 %collective-permute-start.45 = (bf16[64,768]{1,0:T(8,128)(2,1)S(1)}, bf16[64,768]{1,0:T(8,128)(2,1)S(1)}, u32[]{:S(2)}, u32[]{:S(2)}) collective-permute-start(bf16[64,768]{1,0:T(8,128)(2,1)S(1)} %get-tuple-element.121), channel_id=1, source_target_pairs={{0,4},{4,12},{8,0},{12,8},{1,5},{5,13},{9,1},{13,9},{2,6},{6,14},{... | collective-permute-start | bytes 294920 | tf_op jit(solution)/shard_map/ppermute | solution.py:368
  218.3 2.1 collective-permute-done.45
  221.1 27.4 %all-reduce.4.cloned.1.call-done.refs_0_ = bf16[784,768]{1,0:T(8,128)(2,1)} async-done(((bf16[784,768]{1,0:T(8,128)(2,1)}), bf16[784,768]{1,0:T(8,128)(2,1)}) %all-reduce.4.cloned.1.call-update) | async-done | bytes 1204240 | tf_op jit(solution)/shard_map/psum | solution.py:512
  (219 shorter events, 71.4 us)
Async XLA Ops:
  7.2 128.7 %all-gather.5.cloned.1.call-start = ((), (), s32[]{:S(2)}) async-start(), calls=%async_computation.1 | async-start | bytes 1966080 | tf_op jit(solution)/shard_map/all_gather | solution.py:476
  7.9 10.6 %collective-permute-start.3 = (bf16[2,768]{1,0:T(2,128)(2,1)S(1)}, bf16[2,768]{1,0:T(2,128)(2,1)S(1)}, u32[]{:S(2)}, u32[]{:S(2)}) collective-permute-start(bf16[2,768]{1,0:T(2,128)(2,1)S(1)} %pad.10), channel_id=1, source_target_pairs={{0,8},{4,12},{8,0},{12,4},{1,9},{5,13},{9,1},{13,5},{2,10},{6,14},... | collective-permute-start | bytes 9224 | tf_op jit(solution)/shard_map/ppermute | solution.py:368
  11.8 5.0 %collective-permute-start = (bf16[64,768]{1,0:T(8,128)(2,1)S(1)}, bf16[64,768]{1,0:T(8,128)(2,1)S(1)}, u32[]{:S(2)}, u32[]{:S(2)}) collective-permute-start(bf16[64,768]{1,0:T(8,128)(2,1)S(1)} %get-tuple-element.126), channel_id=1, source_target_pairs={{0,0},{4,8},{8,4},{12,12},{1,1},{5,9},{9,5},{13,13},{2,2},{6,10},{... | collective-permute-start | bytes 294920 | tf_op jit(solution)/shard_map/ppermute | solution.py:368
  12.5 4.7 %collective-permute-start.1 = (bf16[64,768]{1,0:T(8,128)(2,1)S(1)}, bf16[64,768]{1,0:T(8,128)(2,1)S(1)}, u32[]{:S(2)}, u32[]{:S(2)}) collective-permute-start(bf16[64,768]{1,0:T(8,128)(2,1)S(1)} %get-tuple-element.127), channel_id=1, source_target_pairs={{4,0},{12,4},{0,8},{8,12},{5,1},{13,5},{1,9},{9,13},{6,2},{14,6},{... | collective-permute-start | bytes 294920 | tf_op jit(solution)/shard_map/ppermute | solution.py:368
  16.4 27.5 %collective-permute-start.4 = (bf16[768,768]{1,0:T(8,128)(2,1)S(1)}, bf16[768,768]{1,0:T(8,128)(2,1)S(1)}, u32[]{:S(2)}, u32[]{:S(2)}) collective-permute-start(bf16[768,768]{1,0:T(8,128)(2,1)S(1)} %pad_maximum_fusion.refs_2_.refs_4_.refs_10_), channel_id=1, source_target_pairs={{0,8},{4,12},{8,0},{12,4},{1,9},{5,13},{9,1},{13,5},{2,10},{6,14},... | collective-permute-start | bytes 3538952 | tf_op jit(solution)/shard_map/ppermute | solution.py:368
  47.4 7.0 %collective-permute-start.6 = (bf16[128,768]{1,0:T(8,128)(2,1)S(1)}, bf16[128,768]{1,0:T(8,128)(2,1)S(1)}, u32[]{:S(2)}, u32[]{:S(2)}) collective-permute-start(bf16[128,768]{1,0:T(8,128)(2,1)S(1)} %first_norm.2.refs_0_), channel_id=1, source_target_pairs={{0,8},{4,12},{8,0},{12,4},{1,9},{5,13},{9,1},{13,5},{2,10},{6,14},... | collective-permute-start | bytes 589832 | tf_op jit(solution)/shard_map/ppermute | solution.py:368
  48.6 6.0 %collective-permute-start.7 = (bf16[128,768]{1,0:T(8,128)(2,1)S(1)}, bf16[128,768]{1,0:T(8,128)(2,1)S(1)}, u32[]{:S(2)}, u32[]{:S(2)}) collective-permute-start(bf16[128,768]{1,0:T(8,128)(2,1)S(1)} %first_norm.2.refs_0_), channel_id=1, source_target_pairs={{0,4},{4,0},{8,12},{12,8},{1,5},{5,1},{9,13},{13,9},{2,6},{6,2},{1... | collective-permute-start | bytes 589832 | tf_op jit(solution)/shard_map/ppermute | solution.py:368
  59.2 7.0 %collective-permute-start.10 = (bf16[128,768]{1,0:T(8,128)(2,1)S(1)}, bf16[128,768]{1,0:T(8,128)(2,1)S(1)}, u32[]{:S(2)}, u32[]{:S(2)}) collective-permute-start(bf16[128,768]{1,0:T(8,128)(2,1)S(1)} %get-tuple-element.70), channel_id=1, source_target_pairs={{0,8},{4,12},{8,0},{12,4},{1,9},{5,13},{9,1},{13,5},{2,10},{6,14},... | collective-permute-start | bytes 589832 | tf_op jit(solution)/shard_map/ppermute | solution.py:368
  66.5 6.3 %collective-permute-start.11 = (bf16[128,768]{1,0:T(8,128)(2,1)S(1)}, bf16[128,768]{1,0:T(8,128)(2,1)}, u32[]{:S(2)}, u32[]{:S(2)}) collective-permute-start(bf16[128,768]{1,0:T(8,128)(2,1)S(1)} %second_norm.2), channel_id=1, source_target_pairs={{0,16},{16,0},{1,17},{17,1},{2,18},{18,2},{3,19},{19,3},{4,20},{20... | collective-permute-start | bytes 589832 | tf_op jit(solution)/shard_map/ppermute | solution.py:480
  68.7 4.2 %collective-permute-start.13 = (bf16[64,768]{1,0:T(8,128)(2,1)}, bf16[64,768]{1,0:T(8,128)(2,1)S(1)}, u32[]{:S(2)}, u32[]{:S(2)}) collective-permute-start(bf16[64,768]{1,0:T(8,128)(2,1)} %get-tuple-element.124), channel_id=1, source_target_pairs={{0,0},{4,8},{8,4},{12,12},{1,1},{5,9},{9,5},{13,13},{2,2},{6,10},{... | collective-permute-start | bytes 294920 | tf_op jit(solution)/shard_map/ppermute | solution.py:368
  70.3 4.4 %collective-permute-start.14 = (bf16[64,768]{1,0:T(8,128)(2,1)S(1)}, bf16[64,768]{1,0:T(8,128)(2,1)S(1)}, u32[]{:S(2)}, u32[]{:S(2)}) collective-permute-start(bf16[64,768]{1,0:T(8,128)(2,1)S(1)} %get-tuple-element.125), channel_id=1, source_target_pairs={{4,0},{12,4},{0,8},{8,12},{5,1},{13,5},{1,9},{9,13},{6,2},{14,6},{... | collective-permute-start | bytes 294920 | tf_op jit(solution)/shard_map/ppermute | solution.py:368
  72.8 4.5 %collective-permute-start.12 = (bf16[128,768]{1,0:T(8,128)(2,1)S(1)}, bf16[128,768]{1,0:T(8,128)(2,1)S(1)}, u32[]{:S(2)}, u32[]{:S(2)}) collective-permute-start(bf16[128,768]{1,0:T(8,128)(2,1)S(1)} %broadcast_select_fusion.1.refs_0_), channel_id=1, source_target_pairs={{0,4},{4,0},{8,12},{12,8},{1,5},{5,1},{9,13},{13,9},{2,6},{6,2},{1... | collective-permute-start | bytes 589832 | tf_op jit(solution)/shard_map/ppermute | solution.py:368
  74.7 7.7 %collective-permute-start.16 = (bf16[128,768]{1,0:T(8,128)(2,1)S(1)}, bf16[128,768]{1,0:T(8,128)(2,1)S(1)}, u32[]{:S(2)}, u32[]{:S(2)}) collective-permute-start(bf16[128,768]{1,0:T(8,128)(2,1)S(1)} %broadcast_select_fusion.1.refs_0_), channel_id=1, source_target_pairs={{0,8},{4,12},{8,0},{12,4},{1,9},{5,13},{9,1},{13,5},{2,10},{6,14},... | collective-permute-start | bytes 589832 | tf_op jit(solution)/shard_map/ppermute | solution.py:368
  83.4 7.0 %collective-permute-start.17 = (bf16[128,768]{1,0:T(8,128)(2,1)S(1)}, bf16[128,768]{1,0:T(8,128)(2,1)S(1)}, u32[]{:S(2)}, u32[]{:S(2)}) collective-permute-start(bf16[128,768]{1,0:T(8,128)(2,1)S(1)} %get-tuple-element.74.refs_0_), channel_id=1, source_target_pairs={{0,8},{4,12},{8,0},{12,4},{1,9},{5,13},{9,1},{13,5},{2,10},{6,14},... | collective-permute-start | bytes 589832 | tf_op jit(solution)/shard_map/ppermute | solution.py:368
  83.5 6.9 %collective-permute-start.18 = (bf16[128,768]{1,0:T(8,128)(2,1)S(1)}, bf16[128,768]{1,0:T(8,128)(2,1)S(1)}, u32[]{:S(2)}, u32[]{:S(2)}) collective-permute-start(bf16[128,768]{1,0:T(8,128)(2,1)S(1)} %get-tuple-element.74.refs_0_), channel_id=1, source_target_pairs={{0,4},{4,0},{8,12},{12,8},{1,5},{5,1},{9,13},{13,9},{2,6},{6,2},{1... | collective-permute-start | bytes 589832 | tf_op jit(solution)/shard_map/ppermute | solution.py:368
  95.5 94.9 %all-gather.7.cloned.1.call-start = ((), (), s32[]{:S(2)}) async-start(), calls=%async_computation.2 | async-start | bytes 1966080 | tf_op jit(solution)/shard_map/all_gather | solution.py:499
  96.3 7.0 %collective-permute-start.21 = (bf16[128,768]{1,0:T(8,128)(2,1)S(1)}, bf16[128,768]{1,0:T(8,128)(2,1)S(1)}, u32[]{:S(2)}, u32[]{:S(2)}) collective-permute-start(bf16[128,768]{1,0:T(8,128)(2,1)S(1)} %get-tuple-element.77), channel_id=1, source_target_pairs={{0,8},{4,12},{8,0},{12,4},{1,9},{5,13},{9,1},{13,5},{2,10},{6,14},... | collective-permute-start | bytes 589832 | tf_op jit(solution)/shard_map/ppermute | solution.py:368
  103.9 6.2 %collective-permute-start.24 = (bf16[128,768]{1,0:T(8,128)(2,1)S(1)}, bf16[128,768]{1,0:T(8,128)(2,1)S(1)}, u32[]{:S(2)}, u32[]{:S(2)}) collective-permute-start(bf16[128,768]{1,0:T(8,128)(2,1)S(1)} %get-tuple-element.81.refs_0_), channel_id=1, source_target_pairs={{0,8},{4,12},{8,0},{12,4},{1,9},{5,13},{9,1},{13,5},{2,10},{6,14},... | collective-permute-start | bytes 589832 | tf_op jit(solution)/shard_map/ppermute | solution.py:368
  104.3 5.8 %collective-permute-start.25 = (bf16[128,768]{1,0:T(8,128)(2,1)S(1)}, bf16[128,768]{1,0:T(8,128)(2,1)S(1)}, u32[]{:S(2)}, u32[]{:S(2)}) collective-permute-start(bf16[128,768]{1,0:T(8,128)(2,1)S(1)} %get-tuple-element.81.refs_0_), channel_id=1, source_target_pairs={{0,4},{4,0},{8,12},{12,8},{1,5},{5,1},{9,13},{13,9},{2,6},{6,2},{1... | collective-permute-start | bytes 589832 | tf_op jit(solution)/shard_map/ppermute | solution.py:368
  117.0 7.0 %collective-permute-start.28 = (bf16[128,768]{1,0:T(8,128)(2,1)S(1)}, bf16[128,768]{1,0:T(8,128)(2,1)S(1)}, u32[]{:S(2)}, u32[]{:S(2)}) collective-permute-start(bf16[128,768]{1,0:T(8,128)(2,1)S(1)} %get-tuple-element.86), channel_id=1, source_target_pairs={{0,8},{4,12},{8,0},{12,4},{1,9},{5,13},{9,1},{13,5},{2,10},{6,14},... | collective-permute-start | bytes 589832 | tf_op jit(solution)/shard_map/ppermute | solution.py:368
  117.3 17.8 %collective-permute-start.32 = (bf16[128,768]{1,0:T(8,128)(2,1)}, bf16[128,768]{1,0:T(8,128)(2,1)S(1)}, u32[]{:S(2)}, u32[]{:S(2)}) collective-permute-start(bf16[128,768]{1,0:T(8,128)(2,1)} %copy-done.12), channel_id=1, source_target_pairs={{0,4},{4,0},{8,12},{12,8},{1,5},{5,1},{9,13},{13,9},{2,6},{6,2},{1... | collective-permute-start | bytes 589832 | tf_op jit(solution)/shard_map/ppermute | solution.py:368
  124.5 8.1 %collective-permute-start.22 = (bf16[64,768]{1,0:T(8,128)(2,1)S(1)}, bf16[64,768]{1,0:T(8,128)(2,1)}, u32[]{:S(2)}, u32[]{:S(2)}) collective-permute-start(bf16[64,768]{1,0:T(8,128)(2,1)S(1)} %get-tuple-element.122), channel_id=1, source_target_pairs={{0,0},{4,8},{8,4},{12,12},{1,1},{5,9},{9,5},{13,13},{2,2},{6,10},{... | collective-permute-start | bytes 294920 | tf_op jit(solution)/shard_map/ppermute | solution.py:368
  125.8 6.8 %collective-permute-start.23 = (bf16[64,768]{1,0:T(8,128)(2,1)S(1)}, bf16[64,768]{1,0:T(8,128)(2,1)}, u32[]{:S(2)}, u32[]{:S(2)}) collective-permute-start(bf16[64,768]{1,0:T(8,128)(2,1)S(1)} %get-tuple-element.123), channel_id=1, source_target_pairs={{0,4},{4,12},{8,0},{12,8},{1,5},{5,13},{9,1},{13,9},{2,6},{6,14},{... | collective-permute-start | bytes 294920 | tf_op jit(solution)/shard_map/ppermute | solution.py:368
  134.8 7.7 %collective-permute-start.31 = (bf16[128,768]{1,0:T(8,128)(2,1)}, bf16[128,768]{1,0:T(8,128)(2,1)}, u32[]{:S(2)}, u32[]{:S(2)}) collective-permute-start(bf16[128,768]{1,0:T(8,128)(2,1)} %entry_grad.2), channel_id=1, source_target_pairs={{0,16},{16,0},{1,17},{17,1},{2,18},{18,2},{3,19},{19,3},{4,20},{20... | collective-permute-start | bytes 589832 | tf_op jit(solution)/shard_map/ppermute | solution.py:493
  144.7 6.9 %collective-permute-start.33 = (bf16[128,768]{1,0:T(8,128)(2,1)S(1)}, bf16[128,768]{1,0:T(8,128)(2,1)S(1)}, u32[]{:S(2)}, u32[]{:S(2)}) collective-permute-start(bf16[128,768]{1,0:T(8,128)(2,1)S(1)} %get-tuple-element.96.refs_0_), channel_id=1, source_target_pairs={{0,8},{4,12},{8,0},{12,4},{1,9},{5,13},{9,1},{13,5},{2,10},{6,14},... | collective-permute-start | bytes 589832 | tf_op jit(solution)/shard_map/ppermute | solution.py:368
  152.5 96.0 %all-reduce.4.cloned.1.call-start = ((), (), s32[]{:S(2)}) async-start(), calls=%async_computation | async-start | bytes 2408448 | tf_op jit(solution)/shard_map/psum | solution.py:512
  161.8 7.1 %collective-permute-start.37 = (bf16[128,768]{1,0:T(8,128)(2,1)S(1)}, bf16[128,768]{1,0:T(8,128)(2,1)S(1)}, u32[]{:S(2)}, u32[]{:S(2)}) collective-permute-start(bf16[128,768]{1,0:T(8,128)(2,1)S(1)} %get-tuple-element.100), channel_id=1, source_target_pairs={{0,8},{4,12},{8,0},{12,4},{1,9},{5,13},{9,1},{13,5},{2,10},{6,14},... | collective-permute-start | bytes 589832 | tf_op jit(solution)/shard_map/ppermute | solution.py:368
  169.3 7.8 %collective-permute-start.40 = (bf16[144,768]{1,0:T(8,128)(2,1)S(1)}, bf16[144,768]{1,0:T(8,128)(2,1)S(1)}, u32[]{:S(2)}, u32[]{:S(2)}) collective-permute-start(bf16[144,768]{1,0:T(8,128)(2,1)S(1)} %get-tuple-element.103.refs_0_.refs_4_), channel_id=1, source_target_pairs={{0,8},{4,12},{8,0},{12,4},{1,9},{5,13},{9,1},{13,5},{2,10},{6,14},... | collective-permute-start | bytes 663560 | tf_op jit(solution)/shard_map/ppermute | solution.py:368
  177.2 16.5 %collective-permute-start.42 = (bf16[4,2,128,768]{3,2,1,0:T(8,128)(2,1)}, bf16[4,2,128,768]{3,2,1,0:T(8,128)(2,1)}, u32[]{:S(2)}, u32[]{:S(2)}) collective-permute-start(bf16[4,2,128,768]{3,2,1,0:T(8,128)(2,1)} %bitcast.24), channel_id=1, source_target_pairs={{0,4},{4,0},{8,12},{12,8},{1,5},{5,1},{9,13},{13,9},{2,6},{6,2},{1... | collective-permute-start | bytes 4718600 | tf_op jit(solution)/shard_map/ppermute | solution.py:368
  190.4 3.9 %collective-permute-start.43 = (bf16[4,2,128,768]{3,2,1,0:T(8,128)(2,1)}, bf16[4,2,128,768]{3,2,1,0:T(8,128)(2,1)S(1)}, u32[]{:S(2)}, u32[]{:S(2)}) collective-permute-start(bf16[4,2,128,768]{3,2,1,0:T(8,128)(2,1)} %bitcast.62), channel_id=1, source_target_pairs={{0,4},{4,0},{8,12},{12,8},{1,5},{5,1},{9,13},{13,9},{2,6},{6,2},{1... | collective-permute-start | bytes 4718600 | tf_op jit(solution)/shard_map/ppermute | solution.py:368
  213.0 5.3 %collective-permute-start.44 = (bf16[64,768]{1,0:T(8,128)(2,1)S(1)}, bf16[64,768]{1,0:T(8,128)(2,1)S(1)}, u32[]{:S(2)}, u32[]{:S(2)}) collective-permute-start(bf16[64,768]{1,0:T(8,128)(2,1)S(1)} %get-tuple-element.120), channel_id=1, source_target_pairs={{0,0},{4,8},{8,4},{12,12},{1,1},{5,9},{9,5},{13,13},{2,2},{6,10},{... | collective-permute-start | bytes 294920 | tf_op jit(solution)/shard_map/ppermute | solution.py:368
  213.8 6.6 %collective-permute-start.45 = (bf16[64,768]{1,0:T(8,128)(2,1)S(1)}, bf16[64,768]{1,0:T(8,128)(2,1)S(1)}, u32[]{:S(2)}, u32[]{:S(2)}) collective-permute-start(bf16[64,768]{1,0:T(8,128)(2,1)S(1)} %get-tuple-element.121), channel_id=1, source_target_pairs={{0,4},{4,12},{8,0},{12,8},{1,5},{5,13},{9,1},{13,9},{2,6},{6,14},{... | collective-permute-start | bytes 294920 | tf_op jit(solution)/shard_map/ppermute | solution.py:368
  (62 other events, 485.2 us)
Sparse Core Ops, SparseCore 0:
  95.6 36.4 all-gather.4
  152.6 37.7 all-gather.6
  192.8 55.6 all-reduce.3

commit v8 on v7

--- a/solution.py
+++ b/solution.py
@@ -260,17 +260,22 @@
         kept[number] = item
 
 
-def unpack_kernel(total, g_w, g_out, g_b, g_out_b, g_gain, g_shift):
-    local = g_out.shape[0]
-    for number in range(3):
-        g_w[number] = total[local * number : local * (number + 1)].astype(f32)
-    g_out[...] = total[3 * local : 4 * local].astype(f32)
-    rest = total[4 * local :].astype(f32)
-    rest = rest[:7] + rest[7:14]
-    g_b[...] = rest[:2, :local]
-    g_out_b[...] = rest[2:3]
-    g_gain[...] = jnp.concatenate([rest[3:4], rest[5:6]], 0)
-    g_shift[...] = jnp.concatenate([rest[4:5], rest[6:7]], 0)
+def unpack_kernel(total, tail, g_w, g_out, g_b, g_out_b, g_gain, g_shift):
+    step = pl.program_id(0)
+
+    @pl.when(step < 3)
+    def _():
+        g_w[0] = total[...].astype(f32)
+
+    @pl.when(step == 3)
+    def _():
+        g_out[...] = total[...].astype(f32)
+        rest = tail[...].astype(f32)
+        rest = rest[:7] + rest[7:14]
+        g_b[...] = rest[:2, : g_b.shape[1]]
+        g_out_b[...] = rest[2:3]
+        g_gain[...] = jnp.concatenate([rest[3:4], rest[5:6]], 0)
+        g_shift[...] = jnp.concatenate([rest[4:5], rest[6:7]], 0)
 
 
 def attend_grads_kernel(*refs):
@@ -541,7 +546,20 @@
     outs += [shape((1, width), f32), shape((2, width), f32), shape((2, width), f32)]
     after = (g_down, input_grad)
     g_w, g_out, g_b, g_out_b, g_gain, g_shift = run(
-        unpack_kernel, outs, (total,), 1.0, "unpack", after=after
+        unpack_kernel,
+        outs,
+        (total, total),
+        1.0,
+        "unpack",
+        mib=56,
+        after=after,
+        grid=(4,),
+        in_specs=[
+            pl.BlockSpec((local, width), lambda i: (i, 0)),
+            pl.BlockSpec((EXTRA_ROWS, width), lambda i: (4 * local // EXTRA_ROWS, 0)),
+        ],
+        out_specs=[pl.BlockSpec((1, local, width), lambda i: (jnp.minimum(i, 2), 0, 0))]
+        + [whole(item) for item in outs[1:]],
     )
     return (
         layer_output[None],

time: 258 us -> 260 us (level)
  Pallas kernels: 50.1 us -> 54.4 us
    pallas_call x30, Pallas kernels: 50.1 us -> 54.4 us  [run(): pl.pallas_call(body, out_shape=outs, grid_spec=pltpu.PrefetchScalarGridSp...]
    unnamed x91 -> x93, local copies, waits for them, and re-layouts: 17.6 us -> 16.4 us
  transfers between devices with their start and end apart: 49 -> 49, of which waited for: 33 -> 34; matrix products, arithmetic and copies ran while one was open for 3% -> 3% of each run, Pallas kernels for 16% -> 17%
where the time goes in v8:
time: 260 us; the launch traced here: 259 us
  waiting for transfers between devices  131 us (50%)
  Pallas kernels  54.4 us (21%)
  starting transfers between devices  33.8 us (13%)
  local copies, waits for them, and re-layouts  17.7 us (7%)
  between operations  14.5 us (6%)
  other arithmetic  7.41 us (3%)
    ppermute x44, waiting for transfers between devices, swap(): return lax.ppermute(value, 'tensor', pairs)  97.3 us
    pallas_call x30, Pallas kernels, run(): pl.pallas_call(body, out_shape=outs, grid_spec=pltpu.PrefetchScalarGridSp...  54.4 us
    ppermute x44, starting transfers between devices, swap(): return lax.ppermute(value, 'tensor', pairs)  31.3 us
    psum x1, waiting for transfers between devices, shards(): total = lax.psum(local_total, 'dp')  26.6 us
    unnamed x93, local copies, waits for them, and re-layouts  16.4 us
    all_gather x1, waiting for transfers between devices, shards(): grad_y = lax.all_gather(grad_y, 'dp') if wide else grad_y[None]  5.66 us
  transfers between devices with their start and end apart: 49, of which 34 were waited for; matrix products, arithmetic and copies ran while one was open for 3% of the time, Pallas kernels for 17%

profile of v8, /device:TPU:0, one launch (start us, length us, event | category | flops | bytes accessed | tf_op | source)
XLA Modules:
  0.0 259.2 jit_solution(6184736557999957283)
XLA Ops:
  7.9 2.9 %collective-permute-start.3 = (bf16[2,768]{1,0:T(2,128)(2,1)S(1)}, bf16[2,768]{1,0:T(2,128)(2,1)S(1)}, u32[]{:S(2)}, u32[]{:S(2)}) collective-permute-start(bf16[2,768]{1,0:T(2,128)(2,1)S(1)} %pad.10), channel_id=1, source_target_pairs={{0,8},{4,12},{8,0},{12,4},{1,9},{5,13},{9,1},{13,5},{2,10},{6,14},... | collective-permute-start | bytes 9224 | tf_op jit(solution)/shard_map/ppermute | solution.py:373
  12.5 2.4 collective-permute-start.1
  21.3 22.5 %collective-permute-done.4.refs_3_ = bf16[768,768]{1,0:T(8,128)(2,1)S(1)} collective-permute-done((bf16[768,768]{1,0:T(8,128)(2,1)S(1)}, bf16[768,768]{1,0:T(8,128)(2,1)S(1)}, u32[]{:S(2)}, u32[]{:S(2)}) %collective-permute-start.4) | collective-permute-done | bytes 1179680 | tf_op jit(solution)/shard_map/ppermute | solution.py:373
  43.8 1.8 attend.2
  48.6 5.8 %collective-permute-done.6.refs_1_ = bf16[128,768]{1,0:T(8,128)(2,1)S(1)} collective-permute-done((bf16[128,768]{1,0:T(8,128)(2,1)S(1)}, bf16[128,768]{1,0:T(8,128)(2,1)S(1)}, u32[]{:S(2)}, u32[]{:S(2)}) %collective-permute-start.6) | collective-permute-done | bytes 196640 | tf_op jit(solution)/shard_map/ppermute | solution.py:373
  60.5 5.8 %collective-permute-done.10.refs_0_ = bf16[128,768]{1,0:T(8,128)(2,1)S(1)} collective-permute-done((bf16[128,768]{1,0:T(8,128)(2,1)S(1)}, bf16[128,768]{1,0:T(8,128)(2,1)S(1)}, u32[]{:S(2)}, u32[]{:S(2)}) %collective-permute-start.10) | collective-permute-done | bytes 196640 | tf_op jit(solution)/shard_map/ppermute | solution.py:373
  68.8 2.5 collective-permute-start.14
  74.9 2.7 %collective-permute-start.16 = (bf16[128,768]{1,0:T(8,128)(2,1)S(1)}, bf16[128,768]{1,0:T(8,128)(2,1)S(1)}, u32[]{:S(2)}, u32[]{:S(2)}) collective-permute-start(bf16[128,768]{1,0:T(8,128)(2,1)S(1)} %broadcast_select_fusion.1.refs_0_), channel_id=1, source_target_pairs={{0,8},{4,12},{8,0},{12,4},{1,9},{5,13},{9,1},{13,5},{2,10},{6,14},... | collective-permute-start | bytes 589832 | tf_op jit(solution)/shard_map/ppermute | solution.py:373
  77.6 3.4 %attend.3 = (f32[128,768]{1,0:T(8,128)S(1)}, bf16[128,768]{1,0:T(8,128)(2,1)S(1)}, bf16[2,3,448,256]{3,2,1,0:T(8,128)(2,1)S(1)}) custom-call(bf16[128,768]{1,0:T(8,128)(2,1)S(1)} %broadcast_select_fusion.1.refs_0_, bf16[128,768]{1,0:T(8,128)(2,1)S(1)} %collective-permute-done.12.refs_1_, bf16[768,768]{1,0:T(8,128)(2,1)S(1)} %pad_maximum_fusion.refs_2_.refs_4_.refs_10_, ...), custom_call_target="tpu_custom_call" | custom-call | flops 3449999872 | bytes 4769792 | tf_op jit(solution)/shard_map/attend/pallas_call | solution.py:52
  84.0 6.7 %collective-permute-done.17.refs_1_ = bf16[128,768]{1,0:T(8,128)(2,1)S(1)} collective-permute-done((bf16[128,768]{1,0:T(8,128)(2,1)S(1)}, bf16[128,768]{1,0:T(8,128)(2,1)S(1)}, u32[]{:S(2)}, u32[]{:S(2)}) %collective-permute-start.17) | collective-permute-done | bytes 196640 | tf_op jit(solution)/shard_map/ppermute | solution.py:373
  97.0 6.7 %collective-permute-done.21.refs_0_ = bf16[128,768]{1,0:T(8,128)(2,1)S(1)} collective-permute-done((bf16[128,768]{1,0:T(8,128)(2,1)S(1)}, bf16[128,768]{1,0:T(8,128)(2,1)S(1)}, u32[]{:S(2)}, u32[]{:S(2)}) %collective-permute-start.21) | collective-permute-done | bytes 196640 | tf_op jit(solution)/shard_map/ppermute | solution.py:373
  104.6 5.8 %collective-permute-done.24.refs_1_ = bf16[128,768]{1,0:T(8,128)(2,1)S(1)} collective-permute-done((bf16[128,768]{1,0:T(8,128)(2,1)S(1)}, bf16[128,768]{1,0:T(8,128)(2,1)S(1)}, u32[]{:S(2)}, u32[]{:S(2)}) %collective-permute-start.24) | collective-permute-done | bytes 196640 | tf_op jit(solution)/shard_map/ppermute | solution.py:373
  113.0 2.3 feed_back.2
  115.4 1.8 collective-permute-done.27.refs_0_
  117.7 6.6 %collective-permute-done.28.refs_0_ = bf16[128,768]{1,0:T(8,128)(2,1)S(1)} collective-permute-done((bf16[128,768]{1,0:T(8,128)(2,1)S(1)}, bf16[128,768]{1,0:T(8,128)(2,1)S(1)}, u32[]{:S(2)}, u32[]{:S(2)}) %collective-permute-start.28) | collective-permute-done | bytes 196640 | tf_op jit(solution)/shard_map/ppermute | solution.py:373
  128.6 4.1 %attend_back.2 = (f32[128,768]{1,0:T(8,128)S(1)}, bf16[128,768]{1,0:T(8,128)(2,1)}) custom-call(bf16[144,768]{1,0:T(8,128)(2,1)S(1)} %get-tuple-element.90.refs_0_, bf16[144,768]{1,0:T(8,128)(2,1)S(1)} %collective-permute-done.29.refs_1_, bf16[768,768]{1,0:T(8,128)(2,1)S(1)} %pad_maximum_fusion.refs_2_.refs_4_.refs_10_, bf16[768,768]{1,0:T(8,128)(2,1)S(1)} %copy-done.17, ...), custom_call_target="tpu_custom_call" | custom-call | flops 3680000000 | bytes 5160960 | tf_op jit(solution)/shard_map/attend_back/pallas_call | solution.py:52
  138.3 3.8 %attend_group.1 = (bf16[4,192,512]{2,1,0:T(8,128)(2,1)S(1)}, bf16[6,256,256]{2,1,0:T(8,128)(2,1)S(1)}) custom-call(bf16[128,768]{1,0:T(8,128)(2,1)S(1)} %copy-done.9, bf16[128,768]{1,0:T(8,128)(2,1)S(1)} %copy-done.22, bf16[128,768]{1,0:T(8,128)(2,1)S(1)} %copy-done.12, bf16[128,768]{1,0:T(8,128)(2,1)} %collective-permute-done.32.refs_3_, ...), custom_call_target="tpu_custom_call" | custom-call | flops 4600000000 | bytes 3592192 | tf_op jit(solution)/shard_map/attend_group/pallas_call | solution.py:52
  144.4 2.0 collective-permute-start.33
  146.4 4.9 %collective-permute-done.33.refs_1_ = bf16[128,768]{1,0:T(8,128)(2,1)S(1)} collective-permute-done((bf16[128,768]{1,0:T(8,128)(2,1)S(1)}, bf16[128,768]{1,0:T(8,128)(2,1)S(1)}, u32[]{:S(2)}, u32[]{:S(2)}) %collective-permute-start.33) | collective-permute-done | bytes 196640 | tf_op jit(solution)/shard_map/ppermute | solution.py:373
  163.0 1.8 collective-permute-start.37
  164.8 5.3 %collective-permute-done.37.refs_0_ = bf16[128,768]{1,0:T(8,128)(2,1)S(1)} collective-permute-done((bf16[128,768]{1,0:T(8,128)(2,1)S(1)}, bf16[128,768]{1,0:T(8,128)(2,1)S(1)}, u32[]{:S(2)}, u32[]{:S(2)}) %collective-permute-start.37) | collective-permute-done | bytes 196640 | tf_op jit(solution)/shard_map/ppermute | solution.py:373
  170.6 1.8 collective-permute-start.40
  172.4 3.5 %attend_back.3 = (f32[128,768]{1,0:T(8,128)S(1)}, bf16[128,768]{1,0:T(8,128)(2,1)S(1)}) custom-call(bf16[144,768]{1,0:T(8,128)(2,1)S(1)} %get-tuple-element.103.refs_0_.refs_4_, bf16[144,768]{1,0:T(8,128)(2,1)S(1)} %collective-permute-done.38.refs_1_.refs_5_, bf16[768,768]{1,0:T(8,128)(2,1)S(1)} %pad_maximum_fusion.refs_2_.refs_4_.refs_10_, ...), custom_call_target="tpu_custom_call" | custom-call | flops 3680000000 | bytes 5160960 | tf_op jit(solution)/shard_map/attend_back/pallas_call | solution.py:52
  175.9 2.5 collective-permute-done.40.refs_0_
  180.0 5.0 %attend_grads.1 = bf16[784,768]{1,0:T(8,128)(2,1)} custom-call(bf16[128,768]{1,0:T(8,128)(2,1)S(1)} %copy-done.10, bf16[128,768]{1,0:T(8,128)(2,1)S(1)} %copy-done.23, bf16[128,768]{1,0:T(8,128)(2,1)S(1)} %copy-done.13, bf16[128,768]{1,0:T(8,128)(2,1)} %collective-permute-done.32.refs_3_, bf16[144,768]{1,0:T(8,128)(2,1)S(1)} %get-tuple-element.103.refs_0_.refs_4_, ...), custom_call_target="tpu_custom_call" | custom-call | flops 5750000128 | bytes 5627904 | tf_op jit(solution)/shard_map/attend_grads/pallas_call | solution.py:52
  185.0 5.7 %all-gather.7.cloned.1.call-done = bf16[8,128,768]{2,1,0:T(8,128)(2,1)} async-done(((bf16[2,128,768]{2,1,0:T(8,128)(2,1)}), bf16[8,128,768]{2,1,0:T(8,128)(2,1)}) %all-gather.7.cloned.1.call-update) | async-done | bytes 1572880 | tf_op jit(solution)/shard_map/all_gather | solution.py:504
  191.2 2.8 %collective-permute-done.39.refs_0_ = bf16[128,768]{1,0:T(8,128)(2,1)S(1)} collective-permute-done((bf16[128,768]{1,0:T(8,128)(2,1)S(1)}, bf16[128,768]{1,0:T(8,128)(2,1)S(1)}, u32[]{:S(2)}, u32[]{:S(2)}) %collective-permute-start.39) | collective-permute-done | bytes 196640 | tf_op jit(solution)/shard_map/ppermute | solution.py:373
  195.7 15.8 %feed_grads.1 = (f32[768,768]{1,0:T(8,128)}, f32[1,768]{1,0:T(1,128)}, f32[768,768]{1,0:T(8,128)}, f32[1,768]{1,0:T(1,128)}) custom-call(bf16[1024,768]{1,0:T(8,128)(2,1)} %bitcast.21.refs_8_.refs_0_, bf16[1024,768]{1,0:T(8,128)(2,1)} %bitcast.68, bf16[1024,768]{1,0:T(8,128)(2,1)} %bitcast.25.refs_2_, bf16[1024,768]{1,0:T(8,128)(2,1)} %bitcast.69, ...), custom_call_target="tpu_custom_call" | custom-call | flops 5750000128 | bytes 13424640 | tf_op jit(solution)/shard_map/feed_grads/pallas_call | solution.py:52
  214.1 2.8 %collective-permute-start.45 = (bf16[64,768]{1,0:T(8,128)(2,1)S(1)}, bf16[64,768]{1,0:T(8,128)(2,1)S(1)}, u32[]{:S(2)}, u32[]{:S(2)}) collective-permute-start(bf16[64,768]{1,0:T(8,128)(2,1)S(1)} %get-tuple-element.121), channel_id=1, source_target_pairs={{0,4},{4,12},{8,0},{12,8},{1,5},{5,13},{9,1},{13,9},{2,6},{6,14},{... | collective-permute-start | bytes 294920 | tf_op jit(solution)/shard_map/ppermute | solution.py:373
  217.6 3.1 %collective-permute-done.45 = bf16[64,768]{1,0:T(8,128)(2,1)S(1)} collective-permute-done((bf16[64,768]{1,0:T(8,128)(2,1)S(1)}, bf16[64,768]{1,0:T(8,128)(2,1)S(1)}, u32[]{:S(2)}, u32[]{:S(2)}) %collective-permute-start.45) | collective-permute-done | bytes 98336 | tf_op jit(solution)/shard_map/ppermute | solution.py:373
  222.1 26.6 %all-reduce.4.cloned.1.call-done.refs_0_.refs_1_ = bf16[784,768]{1,0:T(8,128)(2,1)} async-done(((bf16[784,768]{1,0:T(8,128)(2,1)}), bf16[784,768]{1,0:T(8,128)(2,1)}) %all-reduce.4.cloned.1.call-update) | async-done | bytes 1204240 | tf_op jit(solution)/shard_map/psum | solution.py:517
  248.8 3.9 %unpack.1 = (f32[3,192,768]{2,1,0:T(8,128)}, f32[192,768]{1,0:T(8,128)}, f32[2,192]{1,0:T(2,128)}, f32[1,768]{1,0:T(1,128)}, f32[2,768]{1,0:T(2,128)}, /*index=5*/f32[2,768]{1,0:T(2,128)}) custom-call(bf16[784,768]{1,0:T(8,128)(2,1)} %all-reduce.4.cloned.1.call-done.refs_0_.refs_1_, bf16[784,768]{1,0:T(8,128)(2,1)} %all-reduce.4.cloned.1.call-done.refs_0_.refs_1_, ...), custom_call_target="tpu_custom_call" | custom-call | flops 1150000000 | bytes 4784640 | tf_op jit(solution)/shard_map/unpack/pallas_call | solution.py:52
  (221 shorter events, 69.6 us)
Async XLA Ops:
  7.2 128.3 %all-gather.5.cloned.1.call-start = ((), (), s32[]{:S(2)}) async-start(), calls=%async_computation.1 | async-start | bytes 1966080 | tf_op jit(solution)/shard_map/all_gather | solution.py:481
  7.9 10.6 %collective-permute-start.3 = (bf16[2,768]{1,0:T(2,128)(2,1)S(1)}, bf16[2,768]{1,0:T(2,128)(2,1)S(1)}, u32[]{:S(2)}, u32[]{:S(2)}) collective-permute-start(bf16[2,768]{1,0:T(2,128)(2,1)S(1)} %pad.10), channel_id=1, source_target_pairs={{0,8},{4,12},{8,0},{12,4},{1,9},{5,13},{9,1},{13,5},{2,10},{6,14},... | collective-permute-start | bytes 9224 | tf_op jit(solution)/shard_map/ppermute | solution.py:373
  11.8 5.0 %collective-permute-start = (bf16[64,768]{1,0:T(8,128)(2,1)S(1)}, bf16[64,768]{1,0:T(8,128)(2,1)S(1)}, u32[]{:S(2)}, u32[]{:S(2)}) collective-permute-start(bf16[64,768]{1,0:T(8,128)(2,1)S(1)} %get-tuple-element.126), channel_id=1, source_target_pairs={{0,0},{4,8},{8,4},{12,12},{1,1},{5,9},{9,5},{13,13},{2,2},{6,10},{... | collective-permute-start | bytes 294920 | tf_op jit(solution)/shard_map/ppermute | solution.py:373
  12.5 4.7 %collective-permute-start.1 = (bf16[64,768]{1,0:T(8,128)(2,1)S(1)}, bf16[64,768]{1,0:T(8,128)(2,1)S(1)}, u32[]{:S(2)}, u32[]{:S(2)}) collective-permute-start(bf16[64,768]{1,0:T(8,128)(2,1)S(1)} %get-tuple-element.127), channel_id=1, source_target_pairs={{4,0},{12,4},{0,8},{8,12},{5,1},{13,5},{1,9},{9,13},{6,2},{14,6},{... | collective-permute-start | bytes 294920 | tf_op jit(solution)/shard_map/ppermute | solution.py:373
  16.4 27.5 %collective-permute-start.4 = (bf16[768,768]{1,0:T(8,128)(2,1)S(1)}, bf16[768,768]{1,0:T(8,128)(2,1)S(1)}, u32[]{:S(2)}, u32[]{:S(2)}) collective-permute-start(bf16[768,768]{1,0:T(8,128)(2,1)S(1)} %pad_maximum_fusion.refs_2_.refs_4_.refs_10_), channel_id=1, source_target_pairs={{0,8},{4,12},{8,0},{12,4},{1,9},{5,13},{9,1},{13,5},{2,10},{6,14},... | collective-permute-start | bytes 3538952 | tf_op jit(solution)/shard_map/ppermute | solution.py:373
  47.4 7.0 %collective-permute-start.6 = (bf16[128,768]{1,0:T(8,128)(2,1)S(1)}, bf16[128,768]{1,0:T(8,128)(2,1)S(1)}, u32[]{:S(2)}, u32[]{:S(2)}) collective-permute-start(bf16[128,768]{1,0:T(8,128)(2,1)S(1)} %first_norm.2.refs_0_), channel_id=1, source_target_pairs={{0,8},{4,12},{8,0},{12,4},{1,9},{5,13},{9,1},{13,5},{2,10},{6,14},... | collective-permute-start | bytes 589832 | tf_op jit(solution)/shard_map/ppermute | solution.py:373
  48.6 6.0 %collective-permute-start.7 = (bf16[128,768]{1,0:T(8,128)(2,1)S(1)}, bf16[128,768]{1,0:T(8,128)(2,1)S(1)}, u32[]{:S(2)}, u32[]{:S(2)}) collective-permute-start(bf16[128,768]{1,0:T(8,128)(2,1)S(1)} %first_norm.2.refs_0_), channel_id=1, source_target_pairs={{0,4},{4,0},{8,12},{12,8},{1,5},{5,1},{9,13},{13,9},{2,6},{6,2},{1... | collective-permute-start | bytes 589832 | tf_op jit(solution)/shard_map/ppermute | solution.py:373
  59.3 7.0 %collective-permute-start.10 = (bf16[128,768]{1,0:T(8,128)(2,1)S(1)}, bf16[128,768]{1,0:T(8,128)(2,1)S(1)}, u32[]{:S(2)}, u32[]{:S(2)}) collective-permute-start(bf16[128,768]{1,0:T(8,128)(2,1)S(1)} %get-tuple-element.70), channel_id=1, source_target_pairs={{0,8},{4,12},{8,0},{12,4},{1,9},{5,13},{9,1},{13,5},{2,10},{6,14},... | collective-permute-start | bytes 589832 | tf_op jit(solution)/shard_map/ppermute | solution.py:373
  66.5 6.2 %collective-permute-start.11 = (bf16[128,768]{1,0:T(8,128)(2,1)S(1)}, bf16[128,768]{1,0:T(8,128)(2,1)S(1)}, u32[]{:S(2)}, u32[]{:S(2)}) collective-permute-start(bf16[128,768]{1,0:T(8,128)(2,1)S(1)} %second_norm.2), channel_id=1, source_target_pairs={{0,16},{16,0},{1,17},{17,1},{2,18},{18,2},{3,19},{19,3},{4,20},{20... | collective-permute-start | bytes 589832 | tf_op jit(solution)/shard_map/ppermute | solution.py:485
  68.1 4.7 %collective-permute-start.13 = (bf16[64,768]{1,0:T(8,128)(2,1)S(1)}, bf16[64,768]{1,0:T(8,128)(2,1)S(1)}, u32[]{:S(2)}, u32[]{:S(2)}) collective-permute-start(bf16[64,768]{1,0:T(8,128)(2,1)S(1)} %get-tuple-element.124), channel_id=1, source_target_pairs={{0,0},{4,8},{8,4},{12,12},{1,1},{5,9},{9,5},{13,13},{2,2},{6,10},{... | collective-permute-start | bytes 294920 | tf_op jit(solution)/shard_map/ppermute | solution.py:373
  68.8 5.1 %collective-permute-start.14 = (bf16[64,768]{1,0:T(8,128)(2,1)S(1)}, bf16[64,768]{1,0:T(8,128)(2,1)}, u32[]{:S(2)}, u32[]{:S(2)}) collective-permute-start(bf16[64,768]{1,0:T(8,128)(2,1)S(1)} %get-tuple-element.125), channel_id=1, source_target_pairs={{4,0},{12,4},{0,8},{8,12},{5,1},{13,5},{1,9},{9,13},{6,2},{14,6},{... | collective-permute-start | bytes 294920 | tf_op jit(solution)/shard_map/ppermute | solution.py:373
  72.7 4.8 %collective-permute-start.12 = (bf16[128,768]{1,0:T(8,128)(2,1)S(1)}, bf16[128,768]{1,0:T(8,128)(2,1)S(1)}, u32[]{:S(2)}, u32[]{:S(2)}) collective-permute-start(bf16[128,768]{1,0:T(8,128)(2,1)S(1)} %broadcast_select_fusion.1.refs_0_), channel_id=1, source_target_pairs={{0,4},{4,0},{8,12},{12,8},{1,5},{5,1},{9,13},{13,9},{2,6},{6,2},{1... | collective-permute-start | bytes 589832 | tf_op jit(solution)/shard_map/ppermute | solution.py:373
  74.9 8.0 %collective-permute-start.16 = (bf16[128,768]{1,0:T(8,128)(2,1)S(1)}, bf16[128,768]{1,0:T(8,128)(2,1)S(1)}, u32[]{:S(2)}, u32[]{:S(2)}) collective-permute-start(bf16[128,768]{1,0:T(8,128)(2,1)S(1)} %broadcast_select_fusion.1.refs_0_), channel_id=1, source_target_pairs={{0,8},{4,12},{8,0},{12,4},{1,9},{5,13},{9,1},{13,5},{2,10},{6,14},... | collective-permute-start | bytes 589832 | tf_op jit(solution)/shard_map/ppermute | solution.py:373
  83.7 7.0 %collective-permute-start.17 = (bf16[128,768]{1,0:T(8,128)(2,1)S(1)}, bf16[128,768]{1,0:T(8,128)(2,1)S(1)}, u32[]{:S(2)}, u32[]{:S(2)}) collective-permute-start(bf16[128,768]{1,0:T(8,128)(2,1)S(1)} %get-tuple-element.74.refs_0_), channel_id=1, source_target_pairs={{0,8},{4,12},{8,0},{12,4},{1,9},{5,13},{9,1},{13,5},{2,10},{6,14},... | collective-permute-start | bytes 589832 | tf_op jit(solution)/shard_map/ppermute | solution.py:373
  83.8 6.9 %collective-permute-start.18 = (bf16[128,768]{1,0:T(8,128)(2,1)S(1)}, bf16[128,768]{1,0:T(8,128)(2,1)S(1)}, u32[]{:S(2)}, u32[]{:S(2)}) collective-permute-start(bf16[128,768]{1,0:T(8,128)(2,1)S(1)} %get-tuple-element.74.refs_0_), channel_id=1, source_target_pairs={{0,4},{4,0},{8,12},{12,8},{1,5},{5,1},{9,13},{13,9},{2,6},{6,2},{1... | collective-permute-start | bytes 589832 | tf_op jit(solution)/shard_map/ppermute | solution.py:373
  95.8 94.9 %all-gather.7.cloned.1.call-start = ((), (), s32[]{:S(2)}) async-start(), calls=%async_computation.2 | async-start | bytes 1966080 | tf_op jit(solution)/shard_map/all_gather | solution.py:504
  96.6 7.0 %collective-permute-start.21 = (bf16[128,768]{1,0:T(8,128)(2,1)S(1)}, bf16[128,768]{1,0:T(8,128)(2,1)S(1)}, u32[]{:S(2)}, u32[]{:S(2)}) collective-permute-start(bf16[128,768]{1,0:T(8,128)(2,1)S(1)} %get-tuple-element.77), channel_id=1, source_target_pairs={{0,8},{4,12},{8,0},{12,4},{1,9},{5,13},{9,1},{13,5},{2,10},{6,14},... | collective-permute-start | bytes 589832 | tf_op jit(solution)/shard_map/ppermute | solution.py:373
  104.2 6.2 %collective-permute-start.24 = (bf16[128,768]{1,0:T(8,128)(2,1)S(1)}, bf16[128,768]{1,0:T(8,128)(2,1)S(1)}, u32[]{:S(2)}, u32[]{:S(2)}) collective-permute-start(bf16[128,768]{1,0:T(8,128)(2,1)S(1)} %get-tuple-element.81.refs_0_), channel_id=1, source_target_pairs={{0,8},{4,12},{8,0},{12,4},{1,9},{5,13},{9,1},{13,5},{2,10},{6,14},... | collective-permute-start | bytes 589832 | tf_op jit(solution)/shard_map/ppermute | solution.py:373
  104.6 5.8 %collective-permute-start.25 = (bf16[128,768]{1,0:T(8,128)(2,1)S(1)}, bf16[128,768]{1,0:T(8,128)(2,1)S(1)}, u32[]{:S(2)}, u32[]{:S(2)}) collective-permute-start(bf16[128,768]{1,0:T(8,128)(2,1)S(1)} %get-tuple-element.81.refs_0_), channel_id=1, source_target_pairs={{0,4},{4,0},{8,12},{12,8},{1,5},{5,1},{9,13},{13,9},{2,6},{6,2},{1... | collective-permute-start | bytes 589832 | tf_op jit(solution)/shard_map/ppermute | solution.py:373
  117.3 7.0 %collective-permute-start.28 = (bf16[128,768]{1,0:T(8,128)(2,1)S(1)}, bf16[128,768]{1,0:T(8,128)(2,1)S(1)}, u32[]{:S(2)}, u32[]{:S(2)}) collective-permute-start(bf16[128,768]{1,0:T(8,128)(2,1)S(1)} %get-tuple-element.86), channel_id=1, source_target_pairs={{0,8},{4,12},{8,0},{12,4},{1,9},{5,13},{9,1},{13,5},{2,10},{6,14},... | collective-permute-start | bytes 589832 | tf_op jit(solution)/shard_map/ppermute | solution.py:373
  117.6 17.8 %collective-permute-start.32 = (bf16[128,768]{1,0:T(8,128)(2,1)}, bf16[128,768]{1,0:T(8,128)(2,1)}, u32[]{:S(2)}, u32[]{:S(2)}) collective-permute-start(bf16[128,768]{1,0:T(8,128)(2,1)} %copy-done.11), channel_id=1, source_target_pairs={{0,4},{4,0},{8,12},{12,8},{1,5},{5,1},{9,13},{13,9},{2,6},{6,2},{1... | collective-permute-start | bytes 589832 | tf_op jit(solution)/shard_map/ppermute | solution.py:373
  124.8 8.1 %collective-permute-start.22 = (bf16[64,768]{1,0:T(8,128)(2,1)S(1)}, bf16[64,768]{1,0:T(8,128)(2,1)S(1)}, u32[]{:S(2)}, u32[]{:S(2)}) collective-permute-start(bf16[64,768]{1,0:T(8,128)(2,1)S(1)} %get-tuple-element.122), channel_id=1, source_target_pairs={{0,0},{4,8},{8,4},{12,12},{1,1},{5,9},{9,5},{13,13},{2,2},{6,10},{... | collective-permute-start | bytes 294920 | tf_op jit(solution)/shard_map/ppermute | solution.py:373
  125.5 7.4 %collective-permute-start.23 = (bf16[64,768]{1,0:T(8,128)(2,1)S(1)}, bf16[64,768]{1,0:T(8,128)(2,1)S(1)}, u32[]{:S(2)}, u32[]{:S(2)}) collective-permute-start(bf16[64,768]{1,0:T(8,128)(2,1)S(1)} %get-tuple-element.123), channel_id=1, source_target_pairs={{0,4},{4,12},{8,0},{12,8},{1,5},{5,13},{9,1},{13,9},{2,6},{6,14},{... | collective-permute-start | bytes 294920 | tf_op jit(solution)/shard_map/ppermute | solution.py:373
  135.1 7.3 %collective-permute-start.31 = (bf16[128,768]{1,0:T(8,128)(2,1)}, bf16[128,768]{1,0:T(8,128)(2,1)}, u32[]{:S(2)}, u32[]{:S(2)}) collective-permute-start(bf16[128,768]{1,0:T(8,128)(2,1)} %entry_grad.2), channel_id=1, source_target_pairs={{0,16},{16,0},{1,17},{17,1},{2,18},{18,2},{3,19},{19,3},{4,20},{20... | collective-permute-start | bytes 589832 | tf_op jit(solution)/shard_map/ppermute | solution.py:498
  144.4 6.9 %collective-permute-start.33 = (bf16[128,768]{1,0:T(8,128)(2,1)S(1)}, bf16[128,768]{1,0:T(8,128)(2,1)S(1)}, u32[]{:S(2)}, u32[]{:S(2)}) collective-permute-start(bf16[128,768]{1,0:T(8,128)(2,1)S(1)} %get-tuple-element.96.refs_0_), channel_id=1, source_target_pairs={{0,8},{4,12},{8,0},{12,4},{1,9},{5,13},{9,1},{13,5},{2,10},{6,14},... | collective-permute-start | bytes 589832 | tf_op jit(solution)/shard_map/ppermute | solution.py:373
  152.8 96.0 %all-reduce.4.cloned.1.call-start = ((), (), s32[]{:S(2)}) async-start(), calls=%async_computation | async-start | bytes 2408448 | tf_op jit(solution)/shard_map/psum | solution.py:517
  163.0 7.1 %collective-permute-start.37 = (bf16[128,768]{1,0:T(8,128)(2,1)S(1)}, bf16[128,768]{1,0:T(8,128)(2,1)S(1)}, u32[]{:S(2)}, u32[]{:S(2)}) collective-permute-start(bf16[128,768]{1,0:T(8,128)(2,1)S(1)} %get-tuple-element.100), channel_id=1, source_target_pairs={{0,8},{4,12},{8,0},{12,4},{1,9},{5,13},{9,1},{13,5},{2,10},{6,14},... | collective-permute-start | bytes 589832 | tf_op jit(solution)/shard_map/ppermute | solution.py:373
  170.6 7.8 %collective-permute-start.40 = (bf16[144,768]{1,0:T(8,128)(2,1)S(1)}, bf16[144,768]{1,0:T(8,128)(2,1)S(1)}, u32[]{:S(2)}, u32[]{:S(2)}) collective-permute-start(bf16[144,768]{1,0:T(8,128)(2,1)S(1)} %get-tuple-element.103.refs_0_.refs_4_), channel_id=1, source_target_pairs={{0,8},{4,12},{8,0},{12,4},{1,9},{5,13},{9,1},{13,5},{2,10},{6,14},... | collective-permute-start | bytes 663560 | tf_op jit(solution)/shard_map/ppermute | solution.py:373
  178.5 15.5 %collective-permute-start.42 = (bf16[4,2,128,768]{3,2,1,0:T(8,128)(2,1)}, bf16[4,2,128,768]{3,2,1,0:T(8,128)(2,1)}, u32[]{:S(2)}, u32[]{:S(2)}) collective-permute-start(bf16[4,2,128,768]{3,2,1,0:T(8,128)(2,1)} %bitcast.24), channel_id=1, source_target_pairs={{0,4},{4,0},{8,12},{12,8},{1,5},{5,1},{9,13},{13,9},{2,6},{6,2},{1... | collective-permute-start | bytes 4718600 | tf_op jit(solution)/shard_map/ppermute | solution.py:373
  190.7 3.9 %collective-permute-start.43 = (bf16[4,2,128,768]{3,2,1,0:T(8,128)(2,1)}, bf16[4,2,128,768]{3,2,1,0:T(8,128)(2,1)S(1)}, u32[]{:S(2)}, u32[]{:S(2)}) collective-permute-start(bf16[4,2,128,768]{3,2,1,0:T(8,128)(2,1)} %bitcast.67), channel_id=1, source_target_pairs={{0,4},{4,0},{8,12},{12,8},{1,5},{5,1},{9,13},{13,9},{2,6},{6,2},{1... | collective-permute-start | bytes 4718600 | tf_op jit(solution)/shard_map/ppermute | solution.py:373
  213.3 4.3 %collective-permute-start.44 = (bf16[64,768]{1,0:T(8,128)(2,1)S(1)}, bf16[64,768]{1,0:T(8,128)(2,1)S(1)}, u32[]{:S(2)}, u32[]{:S(2)}) collective-permute-start(bf16[64,768]{1,0:T(8,128)(2,1)S(1)} %get-tuple-element.120), channel_id=1, source_target_pairs={{0,0},{4,8},{8,4},{12,12},{1,1},{5,9},{9,5},{13,13},{2,2},{6,10},{... | collective-permute-start | bytes 294920 | tf_op jit(solution)/shard_map/ppermute | solution.py:373
  214.1 6.6 %collective-permute-start.45 = (bf16[64,768]{1,0:T(8,128)(2,1)S(1)}, bf16[64,768]{1,0:T(8,128)(2,1)S(1)}, u32[]{:S(2)}, u32[]{:S(2)}) collective-permute-start(bf16[64,768]{1,0:T(8,128)(2,1)S(1)} %get-tuple-element.121), channel_id=1, source_target_pairs={{0,4},{4,12},{8,0},{12,8},{1,5},{5,13},{9,1},{13,9},{2,6},{6,14},{... | collective-permute-start | bytes 294920 | tf_op jit(solution)/shard_map/ppermute | solution.py:373
  (63 other events, 453.2 us)
Sparse Core Ops, SparseCore 0:
  95.9 36.4 all-gather.4
  152.9 37.7 all-gather.6
  193.1 55.6 all-reduce.3
